TPU v7x, 32 devices: a whole 2x2x4 slice. The times are simulated.
32 devices in a mesh: pts: 8 (over y, x, core), blk: 4 (over z).
Axes of the slice: x: 2, y: 2, z: 4, core: 2. Of those that a mesh axis runs over, the one named last changes fastest.
Arguments:
- snapshots: bfloat16 [3072, 4, 8192], P('blk', None, 'pts'), may hold values from -8 to 8
- freq_index: int32 [32], replicated, may hold values from 2 to 383, as said below
- weight_class: int32 [8192], P('pts'), may hold values from 0 to 7
- class_weight: float32 [8], replicated, may hold values from 0.25 to 4
Outputs:
- csd: float32 [32, 2, 8, 8], P('blk')
- eigval: float32 [32], P('blk')
- modes: float32 [32, 2, 4, 8192], P('blk', None, None, 'pts')
Inputs may be any that keep to these rules, and one draw needn't show every extreme that they name: `freq_index`: 32 distinct bins; both 2 and 383 are always among them.
All inputs are finite; a program needn't handle non-finite values.
Results may differ from a plain program's by a relative error of at most 0.0018.
Values may be sent and summed in bfloat16 or wider, within the bound.
No kernel may reach another device: no remote copies, remote signals or barrier semaphores. Data moves between devices by JAX's collectives and lax.ppermute only.
A program may use at most 64 MiB of HBM per device.

v0:
```python
import math

import jax
import jax.numpy as jnp
from jax import lax
from jax.sharding import PartitionSpec as P

NFFT = 768
ITERS = 3


def from_behind(x, axis, by):
    devices = lax.axis_size(axis)
    pairs = [(i, i + by) for i in range(devices) if 0 <= i + by < devices]
    return lax.ppermute(x, axis, pairs)


def transform_table(freq_index):
    times = jnp.arange(NFFT, dtype=jnp.int32)
    phase = freq_index[:, None] * times[None, :] % NFFT
    angle = 2.0 * math.pi / NFFT * phase.astype(jnp.float32)
    window = 0.5 - 0.5 * jnp.cos(2.0 * math.pi / NFFT * times.astype(jnp.float32))
    real_part = window[None, :] * jnp.cos(angle)
    imag_part = -window[None, :] * jnp.sin(angle)
    stacked = jnp.stack([real_part, imag_part], axis=1)
    return stacked.reshape(2 * freq_index.shape[0], NFFT).astype(jnp.bfloat16)


def point_weights(weight_class, class_weight):
    classes = jnp.arange(class_weight.shape[0], dtype=jnp.int32)
    picked = jnp.where(
        weight_class[:, None] == classes[None, :], class_weight[None, :], jnp.float32(0.0)
    )
    return jnp.sum(picked, axis=1)


def apply_csd(real_mat, imag_mat, vec_re, vec_im):
    highest = lax.Precision.HIGHEST
    out_re = jnp.einsum("fab,fb->fa", real_mat, vec_re, precision=highest) - jnp.einsum(
        "fab,fb->fa", imag_mat, vec_im, precision=highest
    )
    out_im = jnp.einsum("fab,fb->fa", real_mat, vec_im, precision=highest) + jnp.einsum(
        "fab,fb->fa", imag_mat, vec_re, precision=highest
    )
    return (out_re, out_im)


def on_device(snapshots, freq_index, weight_class, class_weight):
    row_count, var_count, local_points = snapshots.shape
    features = var_count * local_points
    half_len = NFFT // 2
    block_count = row_count // half_len
    freq_count = freq_index.shape[0]
    halves = snapshots.reshape(block_count, half_len, features)
    transform = transform_table(freq_index)
    first_part = transform[:, :half_len]
    second_part = transform[:, half_len:]
    leading = jnp.einsum("ht,btp->bhp", first_part, halves, preferred_element_type=jnp.float32)
    following = from_behind(halves[0], "blk", -1)
    ahead = jnp.concatenate([halves[1:], following[None]], axis=0)
    trailing = jnp.einsum("ht,btp->bhp", second_part, ahead, preferred_element_type=jnp.float32)
    summed = leading + trailing
    qhat = summed.astype(jnp.bfloat16).reshape(block_count, freq_count, 2, features)
    spectra = lax.all_to_all(qhat, "blk", split_axis=1, concat_axis=0, tiled=True)
    wpoint = point_weights(weight_class, class_weight)
    wfeat = jnp.tile(wpoint, var_count)
    qweighted = (spectra.astype(jnp.float32) * wfeat).astype(jnp.bfloat16)
    partial_gram = jnp.einsum(
        "bfcp,efdp->fbced", spectra, qweighted, preferred_element_type=jnp.float32
    )
    gram = lax.psum(partial_gram, "pts")
    total_points = local_points * lax.axis_size("pts")
    scaling = 1.0 / (var_count * total_points * (3.0 * NFFT / 8.0))
    real_mat = scaling * (gram[:, :, 0, :, 0] + gram[:, :, 1, :, 1])
    imag_mat = scaling * (gram[:, :, 0, :, 1] - gram[:, :, 1, :, 0])
    csd = jnp.stack([real_mat, imag_mat], axis=1)
    local_freqs = spectra.shape[1]
    all_blocks = spectra.shape[0]
    vec_re = jnp.full((local_freqs, all_blocks), 1.0 / math.sqrt(all_blocks), jnp.float32)
    vec_im = jnp.zeros((local_freqs, all_blocks), jnp.float32)
    for iteration in range(ITERS):
        out_re, out_im = apply_csd(real_mat, imag_mat, vec_re, vec_im)
        length = jnp.sqrt(jnp.sum(out_re * out_re + out_im * out_im, axis=1, keepdims=True))
        vec_re, vec_im = (out_re / length, out_im / length)
    out_re, out_im = apply_csd(real_mat, imag_mat, vec_re, vec_im)
    eigval = jnp.sum(vec_re * out_re + vec_im * out_im, axis=1)
    coef = jnp.stack(
        [jnp.stack([vec_re, vec_im], axis=-1), jnp.stack([-vec_im, vec_re], axis=-1)], axis=2
    ).astype(jnp.bfloat16)
    phi = jnp.einsum("bfcp,fbck->fkp", spectra, coef, preferred_element_type=jnp.float32)
    local_sq = jnp.sum(wfeat[None, None, :] * phi * phi, axis=(1, 2))
    normsq = lax.psum(local_sq, "pts")
    modes = phi * jnp.sqrt(var_count * total_points / normsq)[:, None, None]
    return (csd, eigval, modes.reshape(local_freqs, 2, var_count, local_points))


def solution(mesh):
    in_specs = (P("blk", None, "pts"), P(), P("pts"), P())
    out_specs = (P("blk", None, None, None), P("blk"), P("blk", None, None, "pts"))
    return jax.shard_map(
        on_device, mesh=mesh, in_specs=in_specs, out_specs=out_specs, check_vma=False
    )
```

profile of v0, /device:TPU:0, one launch (start us, length us, event | category | flops | bytes accessed | tf_op | source)
XLA Modules:
  0.0 164.7 jit_solution(10753900440236154036)
XLA Ops:
  0.6 4.5 %fusion.66 = (bf16[384,4,1024]{2,1,0:T(4,128)(2,1)S(1)}, bf16[384,4,1024]{2,1,0:T(4,128)(2,1)S(1)}) fusion(bf16[768,4,1024]{2,1,0:T(4,128)(2,1)} %param.4), kind=kLoop, calls=%fused_computation.97 | loop fusion | bytes 12582912 | tf_op jit(solution)/shard_map/slice | solution.py:60
  5.2 3.0 %copy.76 = bf16[48,8,4,1024]{3,1,2,0:T(8,128)(2,1)} copy(bf16[48,8,4,1024]{3,2,1,0:T(4,128)(2,1)S(1)} %bitcast.177) | data formatting | bytes 6291456
  8.2 1.4 collective-permute-start
  9.6 11.1 %reshape.220 = bf16[2,384,4096]{2,1,0:T(8,128)(2,1)} reshape(bf16[768,4,1024]{2,1,0:T(4,128)(2,1)} %param.4) | data formatting | bytes 12582912 | tf_op jit(solution)/shard_map/reshape | solution.py:54
  20.8 0.5 multiply_convert_fusion.2
  21.4 4.0 %slice.30 = bf16[1,384,4096]{2,1,0:T(8,128)(2,1)} reshape(bf16[384,4,1024]{2,1,0:T(4,128)(2,1)S(1)} %get-tuple-element.31) | data formatting | bytes 6291456 | tf_op jit(solution)/shard_map/slice | solution.py:60
  25.4 4.2 %convolution_bitcast_fusion = f32[2,64,4096]{2,1,0:T(8,128)S(1)} fusion(bf16[2,384,4096]{2,1,0:T(8,128)(2,1)} %reshape.220, bf16[64,768]{1,0:T(8,128)(2,1)S(1)} %convert_element_type.42), kind=kOutput, calls=%fused_computation.5 | convolution fusion | flops 402653184 | bytes 8437760 | tf_op jit(solution)/shard_map/ht,btp->bhp/dot_general | solution.py:58
  29.6 52.1 %collective-permute-done = bf16[384,4096]{1,0:T(8,128)(2,1)} collective-permute-done((bf16[384,4096]{1,0:T(8,128)(2,1)}, bf16[384,4096]{1,0:T(8,128)(2,1)}, u32[]{:S(2)}, u32[]{:S(2)}) %collective-permute-start) | collective-permute-done | bytes 3145760 | tf_op jit(solution)/shard_map/ppermute | solution.py:15
  81.7 3.1 %fusion.10 = bf16[2,64,4096]{2,1,0:T(8,128)(2,1)S(1)} fusion(f32[2,64,4096]{2,1,0:T(8,128)S(1)} %convolution_bitcast_fusion, bf16[1,384,4096]{2,1,0:T(8,128)(2,1)} %bitcast.2, bf16[1,384,4096]{2,1,0:T(8,128)(2,1)S(1)} %copy-done, bf16[64,768]{1,0:T(8,128)(2,1)S(1)} %convert_element_type.42), kind=kOutput, calls=%fused_computation.7 | convolution fusion | flops 416284672 | bytes 9486336 | tf_op jit(solution)/shard_map/ht,btp->bhp/dot_general | solution.py:61
  84.8 0.7 reshape.221
  85.5 2.2 %copy.39 = bf16[2,32,2,4096]{3,2,0,1:T(2,128)(2,1)} copy(bf16[2,32,2,4096]{3,2,1,0:T(2,128)(2,1)S(1)} %reshape.221) | data formatting | bytes 2097152 | tf_op jit(solution)/shard_map/reshape | solution.py:63
  87.7 4.0 %all-to-all-start = ((bf16[2,32,2,4096]{3,2,0,1:T(2,128)(2,1)}), bf16[2,32,2,4096]{3,2,0,1:T(2,128)(2,1)S(1)}, u32[]{:S(2)}, u32[]{:S(2)}) async-start(bf16[2,32,2,4096]{3,2,0,1:T(2,128)(2,1)} %copy.39), calls=%async_computation | async-start | bytes 2097152 | tf_op jit(solution)/shard_map/all_to_all | solution.py:64
  91.9 24.8 %all-to-all-done = bf16[2,32,2,4096]{3,2,0,1:T(2,128)(2,1)S(1)} async-done(((bf16[2,32,2,4096]{3,2,0,1:T(2,128)(2,1)}), bf16[2,32,2,4096]{3,2,0,1:T(2,128)(2,1)S(1)}, u32[]{:S(2)}, u32[]{:S(2)}) %all-to-all-start) | async-done | bytes 1048608 | tf_op jit(solution)/shard_map/all_to_all | solution.py:64
  116.7 1.3 copy.80
  118.0 0.4 all_to_all.16
  118.5 0.4 reshape.226
  118.9 2.4 %fusion.14 = f32[8,8,2,8,2]{3,1,4,2,0:T(8,128)S(1)} fusion(bf16[8,8,2,4096]{3,0,2,1:T(8,128)(2,1)S(1)} %all_to_all.16, bf16[8,8,2,4096,1]{3,0,2,1,4:T(8,128)(2,1)S(1)} %reshape.226, f32[4096]{0:T(1024)S(1)} %bitcast.209), kind=kOutput, calls=%fused_computation.11 | convolution fusion | flops 18350080 | bytes 2121728 | tf_op jit(solution)/shard_map/bfcp,efdp->fbced/dot_general | solution.py:68
  121.3 24.6 %psum.14 = f32[8,8,2,8,2]{3,1,4,2,0:T(8,128)S(1)} all-reduce(f32[8,8,2,8,2]{3,1,4,2,0:T(8,128)S(1)} %fusion.14), channel_id=1, replica_groups=mesh['pts'=8,'blk'=4] {'pts'}, use_global_device_ids=true, to_apply=%region_1.2 | all-reduce | flops 2048 | bytes 16384 | tf_op jit(solution)/shard_map/psum | solution.py:71
  146.2 0.2 fusion.55
  146.4 0.2 fusion.41
  146.6 0.2 fusion.39
  147.0 0.2 fusion.51
  147.4 0.2 fusion.35
  148.0 0.2 fusion.47
  148.4 0.2 fusion.31
  148.6 0.2 fusion.49
  149.0 0.2 fusion.45
  149.8 0.6 fusion.62
  150.5 0.5 fusion.18
  151.0 11.9 %psum.15 = f32[8]{0:T(128)S(1)} all-reduce(f32[8]{0:T(128)S(1)} %get-tuple-element.45), channel_id=1, replica_groups=mesh['pts'=8,'blk'=4] {'pts'}, use_global_device_ids=true, to_apply=%region_7.8 | all-reduce | flops 8 | bytes 64 | tf_op jit(solution)/shard_map/psum | solution.py:92
  163.0 1.0 reshape.222
  164.0 0.6 copy.46
  (43 shorter events, 2.5 us)
Async XLA Ops:
  8.2 12.5 %copy-start.2 = (s32[32]{0:T(128)S(1)}, s32[32]{0:T(128)}, u32[]{:S(2)}) copy-start(s32[32]{0:T(128)} %param.5) | copy-start | bytes 388
  8.2 73.5 %collective-permute-start = (bf16[384,4096]{1,0:T(8,128)(2,1)}, bf16[384,4096]{1,0:T(8,128)(2,1)}, u32[]{:S(2)}, u32[]{:S(2)}) collective-permute-start(bf16[384,4096]{1,0:T(8,128)(2,1)} %bitcast.78), channel_id=1, source_target_pairs={{1,0},{2,1},{3,2},{5,4},{6,5},{7,6},{9,8},{10,9},{11,10},{13,12},{... | collective-permute-start | bytes 9437192 | tf_op jit(solution)/shard_map/ppermute | solution.py:15
  25.4 56.2 %copy-start = (bf16[1,384,4096]{2,1,0:T(8,128)(2,1)S(1)}, bf16[1,384,4096]{2,1,0:T(8,128)(2,1)}, u32[]{:S(2)}) copy-start(bf16[1,384,4096]{2,1,0:T(8,128)(2,1)} %slice.30) | copy-start | bytes 9437188
  84.8 6.9 %copy-start.1 = (s32[1024]{0:T(1024)S(1)}, s32[1024]{0:T(1024)}, u32[]{:S(2)}) copy-start(s32[1024]{0:T(1024)} %param.6) | copy-start | bytes 12292
  84.8 6.9 %copy-start.3 = (f32[8]{0:T(128)S(1)}, f32[8]{0:T(128)}, u32[]{:S(2)}) copy-start(f32[8]{0:T(128)} %param.7) | copy-start | bytes 100
  87.7 28.9 %all-to-all-start = ((bf16[2,32,2,4096]{3,2,0,1:T(2,128)(2,1)}), bf16[2,32,2,4096]{3,2,0,1:T(2,128)(2,1)S(1)}, u32[]{:S(2)}, u32[]{:S(2)}) async-start(bf16[2,32,2,4096]{3,2,0,1:T(2,128)(2,1)} %copy.39), calls=%async_computation | async-start | bytes 2097152 | tf_op jit(solution)/shard_map/all_to_all | solution.py:64
where the time goes:
time: 165 us
  waiting for transfers between devices  76.9 us (47%)
  blocking collectives  36.5 us (22%)
  local copies, waits for them, and re-layouts  29.6 us (18%)
  matrix products  13.2 us (8%)
  starting transfers between devices  5.44 us (3%)
  other arithmetic  2.06 us (1%)
    ppermute x1, waiting for transfers between devices, from_behind(): return lax.ppermute(x, axis, pairs)  52.1 us
    all_to_all x1, waiting for transfers between devices, on_device(): lax.all_to_all(qhat, 'blk', split_axis=1, concat_axis=0, tiled=True)  24.8 us
    psum x1, blocking collectives, on_device(): gram = lax.psum(partial_gram, 'pts')  24.6 us
    psum x1, blocking collectives, on_device(): normsq = lax.psum(local_sq, 'pts')  11.9 us
    reshape x1, local copies, waits for them, and re-layouts, on_device(): halves = snapshots.reshape(block_count, half_len, features)  11.1 us
    slice x2, local copies, waits for them, and re-layouts, on_device(): ahead = jnp.concatenate([halves[1:], following[None]], axis=0)  8.58 us
    dot_general x1, matrix products, on_device(): jnp.einsum('ht,btp->bhp', first_part, halves, preferred_element_type=jnp....  4.16 us
    all_to_all x1, starting transfers between devices, on_device(): lax.all_to_all(qhat, 'blk', split_axis=1, concat_axis=0, tiled=True)  4.03 us
  transfers between devices with their start and end apart: 2, of which 2 were waited for; matrix products, arithmetic and copies ran while one was open for 12% of the time, Pallas kernels for 0%

commit v1 on v0

v1 whole, which is shorter than its diff:
```python
import functools
import math

import jax
import jax.numpy as jnp
from jax import lax
from jax.experimental import pallas as pl
from jax.experimental.pallas import tpu as pltpu
from jax.sharding import PartitionSpec as P

NFFT = 768
HALF = NFFT // 2
ITERS = 3
LANES = 128
VMEM_LIMIT = 48 * 1024 * 1024
F32 = jnp.float32
BF16 = jnp.bfloat16


def iota(shape, axis):
    return lax.broadcasted_iota(jnp.int32, shape, axis)


def mm(a, b):
    return jnp.dot(a, b, preferred_element_type=F32)


def split3(x):
    high = x.astype(BF16)
    rest = x - high.astype(F32)
    mid = rest.astype(BF16)
    low = (rest - mid.astype(F32)).astype(BF16)
    return (high, mid, low)


def one_hot(condition):
    return jnp.where(condition, 1.0, 0.0).astype(BF16)


def transform_table(freq_rows, group):
    times = jnp.arange(NFFT, dtype=jnp.int32)
    phase = freq_rows[:, None] * times[None, :] % NFFT
    angle = 2.0 * math.pi / NFFT * phase.astype(F32)
    window = 0.5 - 0.5 * jnp.cos(2.0 * math.pi / NFFT * times.astype(F32))
    real_part = window[None, :] * jnp.cos(angle)
    imag_part = -window[None, :] * jnp.sin(angle)
    slots = freq_rows.shape[0] // group
    stacked = jnp.stack(
        [real_part.reshape(slots, group, NFFT), imag_part.reshape(slots, group, NFFT)], axis=1
    )
    return stacked.reshape(2 * freq_rows.shape[0], NFFT).astype(BF16)


def spread(rows, var_count):
    width = HALF * var_count
    pick = one_hot(iota((HALF, width), 1) // var_count == iota((HALF, width), 0))
    wide = mm(rows, pick)
    owner = iota(wide.shape, 1) % var_count
    return jnp.concatenate(
        [jnp.where(owner == v, wide, 0.0).astype(BF16) for v in range(var_count)], axis=0
    )


def load_copies(x_hbm, held, sems):
    return [
        pltpu.make_async_copy(x_hbm.at[:, :, pl.ds(j * LANES, LANES)], held.at[j], sems.at[j])
        for j in range(held.shape[0])
    ]


def columns(held, j, half, var_count):
    rows = HALF * var_count
    parts = [
        held.at[j + i].reshape(2 * rows, LANES)[half * rows : (half + 1) * rows, :]
        for i in range(2)
    ]
    return jnp.concatenate(parts, axis=1)


def halo_kernel(down_rows, up_rows, var_count, points, tab, x_hbm, down, up, held, sems):
    copies = load_copies(x_hbm, held, sems)
    for copy in copies:
        copy.start()
    down_lhs = spread(tab[down_rows[0] : down_rows[1], HALF:], var_count)
    up_lhs = spread(tab[up_rows[0] : up_rows[1], :HALF], var_count)
    count = down_rows[1] - down_rows[0]
    for j in range(0, held.shape[0], 2):
        copies[j].wait()
        copies[j + 1].wait()
        for half, lhs, out in ((0, down_lhs, down), (1, up_lhs, up)):
            got = mm(lhs, columns(held, j, half, var_count))
            for v in range(var_count):
                out[:, v * points + j * LANES : v * points + (j + 2) * LANES] = got[
                    v * count : (v + 1) * count
                ]


def block_kernel(slots, keep, var_count, points, tab, x_hbm, *refs):
    outs, (held, sems) = (refs[: -2], refs[-2:])
    even = outs[:slots]
    lead = outs[slots : slots + len(keep)]
    trail = outs[slots + len(keep) :]
    group = even[0].shape[0]
    copies = load_copies(x_hbm, held, sems)
    for copy in copies:
        copy.start()
    lead_tab = tab[:, :HALF]
    trail_tab = tab[:, HALF:]
    lead_lhs = spread(lead_tab, var_count)
    trail_lhs = spread(trail_tab, var_count)
    keep_rows = jnp.concatenate([lead_tab[s * group : (s + 1) * group] for s in keep], axis=0)
    keep_lhs = spread(keep_rows, var_count)
    half_slots = len(trail)
    own_lhs = spread(trail_tab[: half_slots * group], var_count)
    for j in range(0, held.shape[0], 2):
        copies[j].wait()
        copies[j + 1].wait()
        first = columns(held, j, 0, var_count)
        second = columns(held, j, 1, var_count)
        whole = mm(lead_lhs, first) + mm(trail_lhs, second)
        kept = mm(keep_lhs, second)
        own = mm(own_lhs, first)
        for value, targets in ((whole, even), (kept, lead), (own, trail)):
            total = len(targets) * group
            for v in range(var_count):
                for s, target in enumerate(targets):
                    low = v * total + s * group
                    target[:, v * points + j * LANES : v * points + (j + 2) * LANES] = value[
                        low : low + group
                    ].astype(target.dtype)


def join_kernel(half_slots, group, *refs):
    lead = refs[:half_slots]
    trail = refs[half_slots : 2 * half_slots]
    from_above, from_below = refs[2 * half_slots : 2 * half_slots + 2]
    outs = refs[2 * half_slots + 2 :]
    for i in range(half_slots):
        above = (i + half_slots - 1) % half_slots
        outs[i][...] = (
            lead[i][...] + from_above[above * group : (above + 1) * group, :]
        ).astype(BF16)
        outs[half_slots + i][...] = (
            trail[i][...] + from_below[i * group : (i + 1) * group, :]
        ).astype(BF16)


def gram_kernel(slots, group, var_count, points, weights, classes, *refs):
    half_slots = slots // 2
    even = refs[:slots]
    above = refs[slots : slots + half_slots]
    below = refs[slots + half_slots : 2 * slots]
    last = refs[2 * slots : 2 * slots + half_slots]
    packed, spectra, sems = refs[2 * slots + half_slots :]
    blocks = 2 * slots
    me = lax.axis_index("blk")

    def place(source, block, sem):
        return pltpu.make_async_copy(source, spectra.at[pl.ds(block * group, group), :], sem)

    copies = []
    for s in range(slots):
        copies.append(place(even[s], 2 * ((me + slots - s) % slots), sems.at[s]))
    for copy in copies:
        copy.start()
    offsets = [0] + list(range(half_slots + 1, slots))
    for i, s in enumerate(offsets):
        copy = place(above[i], 2 * ((me + slots - s) % slots) + 1, sems.at[slots + i])
        copy.start()
        copies.append(copy)
    for i in range(half_slots):
        block = (2 * ((me + slots - i) % slots) + blocks - 1) % blocks
        sem = sems.at[slots + half_slots + i]

        @pl.when(me == i)
        def _():
            place(last[i], block, sem).start()

        @pl.when(me != i)
        def _():
            place(below[i], block, sem).start()

        copies.append(place(below[i], block, sem))
    picked = jnp.zeros(classes.shape, F32)
    for k in range(weights.shape[0]):
        picked = picked + jnp.where(classes[...] == k, weights[k], jnp.float32(0.0))
    wide = jnp.concatenate([picked] * var_count, axis=1)
    for copy in copies:
        copy.wait()
    left = spectra[...]
    right = (left.astype(F32) * wide).astype(BF16)
    gram = lax.dot_general(
        left, right, (((1,), (1,)), ((), ())), preferred_element_type=F32
    )
    size = blocks * group
    freqs = group // 2
    same = iota((size, size), 0) % freqs == iota((size, size), 1) % freqs
    gram = jnp.where(same, gram, 0.0).reshape(blocks, 2, freqs, size)
    rows_re = gram[:, 0].reshape(blocks * freqs, size)
    rows_im = gram[:, 1].reshape(blocks * freqs, size)
    width = 2 * blocks * blocks
    row, lane = (iota((size, width), 0), iota((size, width), 1))
    fits = row // group == lane % blocks
    row_part = row // freqs % 2
    lane_part = lane // blocks % 2
    from_re = one_hot(fits & (row_part == lane_part))
    sign = jnp.where(lane_part == 0, 1.0, -1.0)
    from_im = jnp.where(fits & (row_part != lane_part), sign, 0.0).astype(BF16)
    total = jnp.zeros((blocks * freqs, width), F32)
    for part_re, part_im in zip(split3(rows_re), split3(rows_im)):
        total = total + (mm(part_re, from_re) + mm(part_im, from_im))
    mine = iota((freqs, width), 1) // (2 * blocks)
    out = jnp.zeros((freqs, width), F32)
    for b in range(blocks):
        out = out + jnp.where(mine == b, total[b * freqs : (b + 1) * freqs], 0.0)
    packed[...] = out


def mode_kernel(blocks, var_count, points, scaling, feature_count, a_ref, b_ref, spectra, csd, eig, modes):
    raw = a_ref[...] + b_ref[...]
    freqs, width = raw.shape
    group = 2 * freqs
    size = blocks * group
    mat = scaling * raw
    lane_part = iota((freqs, width), 1) // blocks % 2
    is_re = lane_part == 0
    gather = one_hot(
        iota((width, width), 0) // (2 * blocks) == iota((width, width), 1) % blocks
    )

    def apply(matrix, vec_re, vec_im):
        top = matrix * jnp.where(is_re, vec_re, -vec_im)
        bottom = matrix * jnp.where(is_re, vec_im, vec_re)
        both = jnp.concatenate([top, bottom], axis=0)
        parts = jnp.concatenate([p.astype(F32) for p in split3(both)], axis=0).astype(BF16)
        got = mm(parts, gather)
        got = got[: 2 * freqs] + got[2 * freqs : 4 * freqs] + got[4 * freqs :]
        return (got[:freqs], got[freqs:])

    def over_blocks(x):
        return jnp.sum(x, axis=1, keepdims=True) * jnp.float32(1.0 / (2 * blocks))

    vec_re = jnp.full((freqs, width), 1.0 / math.sqrt(blocks), F32)
    vec_im = jnp.zeros((freqs, width), F32)
    for _ in range(ITERS):
        out_re, out_im = apply(mat, vec_re, vec_im)
        length = jnp.sqrt(over_blocks(out_re * out_re + out_im * out_im))
        vec_re, vec_im = (out_re / length, out_im / length)
    out_re, out_im = apply(mat, vec_re, vec_im)
    value = over_blocks(vec_re * out_re + vec_im * out_im)
    diagonal = iota((freqs, freqs), 0) == iota((freqs, freqs), 1)
    eig[...] = jnp.sum(
        jnp.where(diagonal, jnp.broadcast_to(value, (freqs, freqs)), 0.0), axis=0, keepdims=True
    )
    low_re = vec_re.astype(BF16)
    low_im = vec_im.astype(BF16)
    out_re, out_im = apply(raw, low_re.astype(F32), low_im.astype(F32))
    normsq = over_blocks(low_re.astype(F32) * out_re + low_im.astype(F32) * out_im)
    scale = jnp.sqrt(jnp.float32(feature_count) / normsq)
    row, lane = (iota((width, size), 0), iota((width, size), 1))
    expand = one_hot(row == lane // group)
    wide = mm(jnp.concatenate([vec_re, vec_im], axis=0).astype(BF16), expand)
    wide_re, wide_im = (wide[:freqs], wide[freqs:])
    part = iota((freqs, size), 1) // freqs % 2
    mine = iota((freqs, size), 1) % freqs == iota((freqs, size), 0)
    coef_re = jnp.where(mine, jnp.where(part == 0, wide_re, -wide_im), 0.0)
    coef_im = jnp.where(mine, jnp.where(part == 0, wide_im, wide_re), 0.0)
    rows = 2 * var_count
    upper = iota((rows, size), 0) < var_count
    var = iota((rows, size), 0) % var_count
    tall = []
    for f in range(freqs):
        both = jnp.where(
            upper,
            jnp.broadcast_to(coef_re[f : f + 1], (rows, size)),
            jnp.broadcast_to(coef_im[f : f + 1], (rows, size)),
        )
        tall.append(
            jnp.concatenate([jnp.where(var == v, both, 0.0) for v in range(var_count)], axis=1)
        )
    coef = jnp.concatenate(tall, axis=0).astype(BF16)
    stacked = jnp.concatenate(
        [spectra[:, v * points : (v + 1) * points] for v in range(var_count)], axis=0
    )
    phi = mm(coef, stacked)
    for f in range(freqs):
        block = phi[f * rows : (f + 1) * rows] * scale[f : f + 1, :]
        for k in range(2):
            modes[f, k] = block[k * var_count : (k + 1) * var_count]
    tiles = jnp.concatenate(
        [
            jnp.where(
                iota((blocks, width), 1) // (2 * blocks) == iota((blocks, width), 0),
                jnp.broadcast_to(mat[f : f + 1], (blocks, width)),
                0.0,
            )
            for f in range(freqs)
        ],
        axis=0,
    )
    for k in range(2):
        row, lane = (iota((width, blocks), 0), iota((width, blocks), 1))
        fold = one_hot(row % (2 * blocks) == lane + k * blocks)
        got = jnp.zeros((freqs * blocks, blocks), F32)
        for piece in split3(tiles):
            got = got + mm(piece, fold)
        for f in range(freqs):
            csd[f, k] = got[f * blocks : (f + 1) * blocks]


def call(kernel, outs, ins, inputs, scratch, flops, moved):
    vmem = pl.BlockSpec(memory_space=pltpu.VMEM)
    return pl.pallas_call(
        kernel,
        out_shape=outs,
        in_specs=ins,
        out_specs=jax.tree.map(lambda _: vmem, outs),
        scratch_shapes=scratch,
        compiler_params=pltpu.CompilerParams(vmem_limit_bytes=VMEM_LIMIT),
        cost_estimate=pl.CostEstimate(flops=flops, bytes_accessed=moved, transcendentals=0),
    )(*inputs)


def on_device(snapshots, freq_index, weight_class, class_weight):
    row_count, var_count, points = snapshots.shape
    features = var_count * points
    slots = lax.axis_size("blk")
    half_slots = slots // 2
    me = lax.axis_index("blk")
    freqs = freq_index.shape[0] // slots
    group = 2 * freqs
    blocks = 2 * slots
    vmem = pl.BlockSpec(memory_space=pltpu.VMEM)
    smem = pl.BlockSpec(memory_space=pltpu.SMEM)
    hbm = pl.BlockSpec(memory_space=pl.ANY)
    shape = jax.ShapeDtypeStruct
    held = [
        pltpu.VMEM((points // LANES, row_count, var_count, LANES), BF16),
        pltpu.SemaphoreType.DMA((points // LANES,)),
    ]

    turned = lax.dynamic_slice(
        jnp.concatenate([freq_index, freq_index]), (me * freqs,), (freq_index.shape[0],)
    )
    table = transform_table(turned, freqs)
    down_rows = (half_slots * group, slots * group)
    up_rows = (group, (half_slots + 1) * group)
    wide = half_slots * group
    halo = [shape((wide, features), F32)] * 2
    down, up = call(
        functools.partial(halo_kernel, down_rows, up_rows, var_count, points),
        halo,
        [vmem, hbm],
        (table, snapshots),
        held,
        2 * 2 * wide * HALF * features * var_count,
        2 * row_count * features,
    )
    below = [(i, i + 1) for i in range(slots - 1)]
    from_above = lax.ppermute(down, "blk", [(b, a) for a, b in below])
    from_below = lax.ppermute(up, "blk", below)

    keep = [0] + list(range(half_slots + 1, slots))
    piece = shape((group, features), BF16)
    wide_piece = shape((group, features), F32)
    table, _ = lax.optimization_barrier((table, down))
    pieces = call(
        functools.partial(block_kernel, slots, keep, var_count, points),
        [piece] * slots + [wide_piece] * (2 * half_slots),
        [vmem, hbm],
        (table, snapshots),
        held,
        2 * 3 * slots * group * HALF * features * var_count,
        2 * row_count * features,
    )
    even = pieces[:slots]

    def shift(x, s, pairs=None):
        pairs = [(i, (i + s) % slots) for i in range(slots)]
        return lax.ppermute(x, "blk", pairs)

    even = [even[0]] + [shift(even[s], s) for s in range(1, slots)]
    last = [
        lax.ppermute(
            up[i * group : (i + 1) * group].astype(BF16), "blk", [(slots - 1, i)]
        )
        for i in range(half_slots)
    ]
    odd = call(
        functools.partial(join_kernel, half_slots, group),
        [piece] * slots,
        [vmem] * (slots + 2),
        (*pieces[slots:], from_above, from_below),
        [],
        slots * group * features,
        10 * slots * group * features,
    )
    above = [odd[0]] + [shift(odd[i], s) for i, s in enumerate(keep) if i]
    under = [odd[half_slots]]
    for i in range(1, half_slots):
        pairs = [(a, (a + i) % slots) for a in range(1, slots)]
        under.append(lax.ppermute(odd[half_slots + i], "blk", pairs))
    width = 2 * blocks * blocks
    packed, spectra = call(
        functools.partial(gram_kernel, slots, group, var_count, points),
        [shape((freqs, width), F32), shape((blocks * group, features), BF16)],
        [smem, vmem] + [hbm] * (2 * slots + half_slots),
        (class_weight, weight_class.reshape(1, points), *even, *above, *under, *last),
        [pltpu.SemaphoreType.DMA((2 * slots,))],
        2 * (blocks * group) ** 2 * features,
        4 * blocks * group * features,
    )
    devices = lax.axis_size("pts")
    step = 1
    other = None
    while step < devices:
        if other is not None:
            packed = packed + other
        other = lax.ppermute(packed, "pts", [(i, i ^ step) for i in range(devices)])
        step *= 2
    total_features = features * devices
    csd, eigval, modes = call(
        functools.partial(
            mode_kernel,
            blocks,
            var_count,
            points,
            1.0 / (total_features * (3.0 * NFFT / 8.0)),
            total_features,
        ),
        [
            shape((freqs, 2, blocks, blocks), F32),
            shape((1, freqs), F32),
            shape((freqs, 2, var_count, points), F32),
        ],
        [vmem] * 3,
        (packed, other, spectra),
        [],
        2 * 2 * blocks * group * group * features,
        2 * blocks * group * features,
    )
    return (csd, eigval.reshape(freqs), modes)


def solution(mesh):
    in_specs = (P("blk", None, "pts"), P(), P("pts"), P())
    out_specs = (P("blk", None, None, None), P("blk"), P("blk", None, None, "pts"))
    return jax.shard_map(
        on_device, mesh=mesh, in_specs=in_specs, out_specs=out_specs, check_vma=False
    )
```

time: 165 us -> 58.2 us (0.35)
  waiting for transfers between devices: 76.9 us -> 18.3 us
  blocking collectives: 36.5 us -> 0 us
  local copies, waits for them, and re-layouts: 29.6 us -> 0.19 us
  starting transfers between devices: 5.44 us -> 23 us
  Pallas kernels: 0 us -> 14.1 us
  matrix products: 13.2 us -> 0 us
    psum x2 -> x0, blocking collectives: 36.5 us -> none  [the longest x1 24.6 us: on_device(): gram = lax.psum(partial_gram, 'pts')]
    ppermute x1 -> x12, waiting for transfers between devices: 52.1 us -> 18.3 us  [the longest x4 8.61 us: shift(): return lax.ppermute(x, 'blk', pairs)]
    all_to_all x1 -> x0, waiting for transfers between devices: 24.8 us -> none  [on_device(): lax.all_to_all(qhat, 'blk', split_axis=1, concat_axis=0, tiled=True)]
    ppermute x1 -> x12, starting transfers between devices: 1.41 us -> 23 us  [the longest x4 9.85 us: shift(): return lax.ppermute(x, 'blk', pairs)]
    reshape x4 -> x0, local copies, waits for them, and re-layouts: 14.9 us -> none  [the longest x1 11.1 us: on_device(): halves = snapshots.reshape(block_count, half_len, features)]
    pallas_call x0 -> x5, Pallas kernels: none -> 14.1 us  [call(): pl.pallas_call(kernel, out_shape=outs, in_specs=ins, out_specs=jax.tree.m...]
    dot_general x20 -> x0, matrix products: 13.2 us -> none  [the longest x1 4.16 us: on_device(): jnp.einsum('ht,btp->bhp', first_part, halves, preferred_element_type=jnp....]
    slice x2 -> x1, local copies, waits for them, and re-layouts: 8.58 us -> 0.02 us  [on_device(): up[i * group:(i + 1) * group].astype(BF16)]
  transfers between devices with their start and end apart: 2 -> 12, of which waited for: 2 -> 8; matrix products, arithmetic and copies ran while one was open for 12% -> 0% of each run, Pallas kernels for 0% -> 10%
where the time goes in v1:
time: 58.2 us; the launch traced here: 57.8 us
  starting transfers between devices  23 us (40%)
  waiting for transfers between devices  18.3 us (31%)
  Pallas kernels  14.1 us (24%)
  other arithmetic  1.39 us (2%)
  between operations  0.78 us (1%)
    pallas_call x5, Pallas kernels, call(): pl.pallas_call(kernel, out_shape=outs, in_specs=ins, out_specs=jax.tree.m...  14.1 us
    ppermute x4, starting transfers between devices, shift(): return lax.ppermute(x, 'blk', pairs)  9.85 us
    ppermute x4, waiting for transfers between devices, shift(): return lax.ppermute(x, 'blk', pairs)  8.61 us
    ppermute x1, starting transfers between devices, on_device(): from_below = lax.ppermute(up, 'blk', below)  5.61 us
    ppermute x3, waiting for transfers between devices, on_device(): other = lax.ppermute(packed, 'pts', [(i, i ^ step) for i in range(devices)])  5.39 us
    ppermute x3, starting transfers between devices, on_device(): other = lax.ppermute(packed, 'pts', [(i, i ^ step) for i in range(devices)])  3.05 us
    ppermute x1, waiting for transfers between devices, on_device(): under.append(lax.ppermute(odd[half_slots + i], 'blk', pairs))  3.01 us
    ppermute x2, starting transfers between devices, on_device(): lax.ppermute(up[i * group:(i + 1) * group].astype(BF16), 'blk', [(slots -...  1.96 us
  transfers between devices with their start and end apart: 12, of which 8 were waited for; matrix products, arithmetic and copies ran while one was open for 0% of the time, Pallas kernels for 10%

profile of v1, /device:TPU:0, one launch (start us, length us, event | category | flops | bytes accessed | tf_op | source)
XLA Modules:
  0.0 57.8 jit_solution(6183032910340505329)
XLA Ops:
  0.7 0.8 %pad_add_fusion = s32[64]{0:T(128)S(1)} fusion(s32[32]{0:T(128)} %param.5), kind=kLoop, calls=%fused_computation.12 | loop fusion | flops 64 | bytes 384 | tf_op jit(solution)/shard_map/concatenate | solution.py:343
  1.5 0.1 dynamic_slice.3
  1.6 0.1 mul.108
  1.7 0.5 multiply_convert_fusion.1
  2.2 3.6 %shard_map.67 = (f32[32,4096]{1,0:T(8,128)S(1)}, f32[32,4096]{1,0:T(8,128)S(1)}) custom-call(bf16[64,768]{1,0:T(8,128)(2,1)S(1)} %bitcast.3, bf16[768,4,1024]{2,1,0:T(4,128)(2,1)} %x_hbm.3), custom_call_target="tpu_custom_call" | custom-call | flops 805306368 | bytes 6291456 | tf_op jit(solution)/shard_map/pallas_call | solution.py:313
  5.8 0.0 copy-start
  5.8 0.0 copy-start.1
  5.8 1.3 %collective-permute-start.3 = (f32[32,4096]{1,0:T(8,128)S(1)}, f32[32,4096]{1,0:T(8,128)S(1)}, u32[]{:S(2)}, u32[]{:S(2)}) collective-permute-start(f32[32,4096]{1,0:T(8,128)S(1)} %get-tuple-element.23), channel_id=1, source_target_pairs={{1,0},{2,1},{3,2},{5,4},{6,5},{7,6},{9,8},{10,9},{11,10},{13,12},{... | collective-permute-start | bytes 1572872 | tf_op jit(solution)/shard_map/ppermute | solution.py:360
  7.1 5.6 %collective-permute-start.4 = (f32[32,4096]{1,0:T(8,128)S(1)}, f32[32,4096]{1,0:T(8,128)S(1)}, u32[]{:S(2)}, u32[]{:S(2)}) collective-permute-start(f32[32,4096]{1,0:T(8,128)S(1)} %get-tuple-element.33), channel_id=1, source_target_pairs={{0,1},{1,2},{2,3},{4,5},{5,6},{6,7},{8,9},{9,10},{10,11},{12,13},{... | collective-permute-start | bytes 1572872 | tf_op jit(solution)/shard_map/ppermute | solution.py:361
  12.8 0.7 %collective-permute-start.8 = (bf16[16,4096]{1,0:T(8,128)(2,1)S(1)}, bf16[16,4096]{1,0:T(8,128)(2,1)S(1)}, u32[]{:S(2)}, u32[]{:S(2)}) collective-permute-start(bf16[16,4096]{1,0:T(8,128)(2,1)S(1)} %get-tuple-element.43), channel_id=1, source_target_pairs={{3,1},{7,5},{11,9},{15,13},{19,17},{23,21},{27,25},{31,29}} | collective-permute-start | bytes 393224 | tf_op jit(solution)/shard_map/ppermute | solution.py:384
  13.5 1.3 %collective-permute-start.7 = (bf16[16,4096]{1,0:T(8,128)(2,1)S(1)}, bf16[16,4096]{1,0:T(8,128)(2,1)S(1)}, u32[]{:S(2)}, u32[]{:S(2)}) collective-permute-start(bf16[16,4096]{1,0:T(8,128)(2,1)S(1)} %get-tuple-element.44), channel_id=1, source_target_pairs={{3,0},{7,4},{11,8},{15,12},{19,16},{23,20},{27,24},{31,28}} | collective-permute-start | bytes 393224 | tf_op jit(solution)/shard_map/ppermute | solution.py:384
  14.8 5.8 %shard_map.68 = (bf16[16,4096]{1,0:T(8,128)(2,1)S(1)}, bf16[16,4096]{1,0:T(8,128)(2,1)S(1)}, bf16[16,4096]{1,0:T(8,128)(2,1)S(1)}, bf16[16,4096]{1,0:T(8,128)(2,...) custom-call(bf16[64,768]{1,0:T(8,128)(2,1)S(1)} %bitcast.4, ...), custom_call_target="tpu_custom_call" | custom-call | flops 2415919104 | bytes 6291456 | tf_op jit(solution)/shard_map/pallas_call | solution.py:313
  20.6 2.0 %collective-permute-start = (bf16[16,4096]{1,0:T(8,128)(2,1)S(1)}, bf16[16,4096]{1,0:T(8,128)(2,1)S(1)}, u32[]{:S(2)}, u32[]{:S(2)}) collective-permute-start(bf16[16,4096]{1,0:T(8,128)(2,1)S(1)} %get-tuple-element.26), channel_id=1, source_target_pairs={{0,1},{1,2},{2,3},{3,0},{4,5},{5,6},{6,7},{7,4},{8,9},{9,10},{10,1... | collective-permute-start | bytes 393224 | tf_op jit(solution)/shard_map/ppermute | solution.py:380
  22.6 0.0 collective-permute-done.3.refs_4_
  22.7 4.1 %collective-permute-start.1 = (bf16[16,4096]{1,0:T(8,128)(2,1)S(1)}, bf16[16,4096]{1,0:T(8,128)(2,1)S(1)}, u32[]{:S(2)}, u32[]{:S(2)}) collective-permute-start(bf16[16,4096]{1,0:T(8,128)(2,1)S(1)} %get-tuple-element.27), channel_id=1, source_target_pairs={{0,2},{1,3},{2,0},{3,1},{4,6},{5,7},{6,4},{7,5},{8,10},{9,11},{10,... | collective-permute-start | bytes 393224 | tf_op jit(solution)/shard_map/ppermute | solution.py:380
  26.8 2.4 %collective-permute-start.2 = (bf16[16,4096]{1,0:T(8,128)(2,1)S(1)}, bf16[16,4096]{1,0:T(8,128)(2,1)S(1)}, u32[]{:S(2)}, u32[]{:S(2)}) collective-permute-start(bf16[16,4096]{1,0:T(8,128)(2,1)S(1)} %get-tuple-element.28), channel_id=1, source_target_pairs={{0,3},{1,0},{2,1},{3,2},{4,7},{5,4},{6,5},{7,6},{8,11},{9,8},{10,9... | collective-permute-start | bytes 393224 | tf_op jit(solution)/shard_map/ppermute | solution.py:380
  29.2 0.1 shard_map.69
  29.3 1.3 %collective-permute-start.5 = (bf16[16,4096]{1,0:T(8,128)(2,1)S(1)}, bf16[16,4096]{1,0:T(8,128)(2,1)S(1)}, u32[]{:S(2)}, u32[]{:S(2)}) collective-permute-start(bf16[16,4096]{1,0:T(8,128)(2,1)S(1)} %get-tuple-element.35), channel_id=1, source_target_pairs={{0,3},{1,0},{2,1},{3,2},{4,7},{5,4},{6,5},{7,6},{8,11},{9,8},{10,9... | collective-permute-start | bytes 393224 | tf_op jit(solution)/shard_map/ppermute | solution.py:380
  30.6 1.2 %collective-permute-done.7.refs_8_ = bf16[16,4096]{1,0:T(8,128)(2,1)S(1)} collective-permute-done((bf16[16,4096]{1,0:T(8,128)(2,1)S(1)}, bf16[16,4096]{1,0:T(8,128)(2,1)S(1)}, u32[]{:S(2)}, u32[]{:S(2)}) %collective-permute-start.7) | collective-permute-done | bytes 131104 | tf_op jit(solution)/shard_map/ppermute | solution.py:384
  31.8 1.3 %collective-permute-start.6 = (bf16[16,4096]{1,0:T(8,128)(2,1)S(1)}, bf16[16,4096]{1,0:T(8,128)(2,1)S(1)}, u32[]{:S(2)}, u32[]{:S(2)}) collective-permute-start(bf16[16,4096]{1,0:T(8,128)(2,1)S(1)} %get-tuple-element.37), channel_id=1, source_target_pairs={{1,2},{2,3},{3,0},{5,6},{6,7},{7,4},{9,10},{10,11},{11,8},{13,14},... | collective-permute-start | bytes 393224 | tf_op jit(solution)/shard_map/ppermute | solution.py:402
  33.1 1.5 %collective-permute-done.refs_1_ = bf16[16,4096]{1,0:T(8,128)(2,1)S(1)} collective-permute-done((bf16[16,4096]{1,0:T(8,128)(2,1)S(1)}, bf16[16,4096]{1,0:T(8,128)(2,1)S(1)}, u32[]{:S(2)}, u32[]{:S(2)}) %collective-permute-start) | collective-permute-done | bytes 131104 | tf_op jit(solution)/shard_map/ppermute | solution.py:380
  34.6 4.5 %collective-permute-done.1.refs_2_ = bf16[16,4096]{1,0:T(8,128)(2,1)S(1)} collective-permute-done((bf16[16,4096]{1,0:T(8,128)(2,1)S(1)}, bf16[16,4096]{1,0:T(8,128)(2,1)S(1)}, u32[]{:S(2)}, u32[]{:S(2)}) %collective-permute-start.1) | collective-permute-done | bytes 131104 | tf_op jit(solution)/shard_map/ppermute | solution.py:380
  39.1 2.6 %collective-permute-done.5.refs_5_ = bf16[16,4096]{1,0:T(8,128)(2,1)S(1)} collective-permute-done((bf16[16,4096]{1,0:T(8,128)(2,1)S(1)}, bf16[16,4096]{1,0:T(8,128)(2,1)S(1)}, u32[]{:S(2)}, u32[]{:S(2)}) %collective-permute-start.5) | collective-permute-done | bytes 131104 | tf_op jit(solution)/shard_map/ppermute | solution.py:380
  41.7 3.0 %collective-permute-done.6.refs_7_ = bf16[16,4096]{1,0:T(8,128)(2,1)S(1)} collective-permute-done((bf16[16,4096]{1,0:T(8,128)(2,1)S(1)}, bf16[16,4096]{1,0:T(8,128)(2,1)S(1)}, u32[]{:S(2)}, u32[]{:S(2)}) %collective-permute-start.6) | collective-permute-done | bytes 131104 | tf_op jit(solution)/shard_map/ppermute | solution.py:402
  44.7 2.8 %shard_map.70 = (f32[8,128]{1,0:T(8,128)S(1)}, bf16[128,4096]{1,0:T(8,128)(2,1)S(1)}) custom-call(f32[8]{0:T(128)S(1)} %copy-done.1, s32[1,1024]{1,0:T(1,128)S(1)} %bitcast.5, bf16[16,4096]{1,0:T(8,128)(2,1)S(1)} %get-tuple-element.25.refs_0_, bf16[16,4096]{1,0:T(8,128)(2,1)S(1)} %collective-permute-done.refs_1_, ...), custom_call_target="tpu_custom_call" | custom-call | flops 134217728 | bytes 2097152 | tf_op jit(solution)/shard_map/pallas_call | solution.py:313
  47.5 0.1 collective-permute-start.9
  47.6 1.2 %collective-permute-done.9 = f32[8,128]{1,0:T(8,128)S(1)} collective-permute-done((f32[8,128]{1,0:T(8,128)S(1)}, f32[8,128]{1,0:T(8,128)S(1)}, u32[]{:S(2)}, u32[]{:S(2)}) %collective-permute-start.9) | collective-permute-done | bytes 4128 | tf_op jit(solution)/shard_map/ppermute | solution.py:419
  48.7 1.5 %collective-permute-start.10 = (f32[8,128]{1,0:T(8,128)S(1)}, f32[8,128]{1,0:T(8,128)S(1)}, u32[]{:S(2)}, u32[]{:S(2)}) collective-permute-start(f32[8,128]{1,0:T(8,128)S(1)} %add.28), channel_id=1, source_target_pairs={{0,8},{4,12},{8,0},{12,4},{16,24},{20,28},{24,16},{28,20},{1,9},{5... | collective-permute-start | bytes 12296 | tf_op jit(solution)/shard_map/ppermute | solution.py:419
  50.2 2.1 %collective-permute-done.10 = f32[8,128]{1,0:T(8,128)S(1)} collective-permute-done((f32[8,128]{1,0:T(8,128)S(1)}, f32[8,128]{1,0:T(8,128)S(1)}, u32[]{:S(2)}, u32[]{:S(2)}) %collective-permute-start.10) | collective-permute-done | bytes 4128 | tf_op jit(solution)/shard_map/ppermute | solution.py:419
  52.3 1.5 %collective-permute-start.11 = (f32[8,128]{1,0:T(8,128)S(1)}, f32[8,128]{1,0:T(8,128)S(1)}, u32[]{:S(2)}, u32[]{:S(2)}) collective-permute-start(f32[8,128]{1,0:T(8,128)S(1)} %add.29.a_ref), channel_id=1, source_target_pairs={{0,16},{4,20},{8,24},{12,28},{16,0},{20,4},{24,8},{28,12},{1,17},{... | collective-permute-start | bytes 12296 | tf_op jit(solution)/shard_map/ppermute | solution.py:419
  53.8 2.1 %collective-permute-done.11.b_ref = f32[8,128]{1,0:T(8,128)S(1)} collective-permute-done((f32[8,128]{1,0:T(8,128)S(1)}, f32[8,128]{1,0:T(8,128)S(1)}, u32[]{:S(2)}, u32[]{:S(2)}) %collective-permute-start.11) | collective-permute-done | bytes 4128 | tf_op jit(solution)/shard_map/ppermute | solution.py:419
  55.9 1.8 %shard_map.71 = (f32[8,2,8,8]{3,2,1,0:T(8,128)}, f32[1,8]{1,0:T(1,128)}, f32[8,2,4,1024]{3,2,1,0:T(4,128)}) custom-call(f32[8,128]{1,0:T(8,128)S(1)} %add.29.a_ref, f32[8,128]{1,0:T(8,128)S(1)} %collective-permute-done.11.b_ref, bf16[128,4096]{1,0:T(8,128)(2,1)S(1)} %get-tuple-element.39.spectra), custom_call_target="tpu_custom_call" | custom-call | flops 33554432 | bytes 1048576 | tf_op jit(solution)/shard_map/pallas_call | solution.py:313
  (11 shorter events, 0.1 us)
Async XLA Ops:
  5.8 38.9 %copy-start = (s32[1024]{0:T(1024)S(1)}, s32[1024]{0:T(1024)}, u32[]{:S(2)}) copy-start(s32[1024]{0:T(1024)} %param.6) | copy-start | bytes 12292
  5.8 38.9 %copy-start.1 = (f32[8]{0:T(128)S(1)}, f32[8]{0:T(128)}, u32[]{:S(2)}) copy-start(f32[8]{0:T(128)} %weights.1) | copy-start | bytes 100
  5.8 16.9 %collective-permute-start.3 = (f32[32,4096]{1,0:T(8,128)S(1)}, f32[32,4096]{1,0:T(8,128)S(1)}, u32[]{:S(2)}, u32[]{:S(2)}) collective-permute-start(f32[32,4096]{1,0:T(8,128)S(1)} %get-tuple-element.23), channel_id=1, source_target_pairs={{1,0},{2,1},{3,2},{5,4},{6,5},{7,6},{9,8},{10,9},{11,10},{13,12},{... | collective-permute-start | bytes 1572872 | tf_op jit(solution)/shard_map/ppermute | solution.py:360
  7.1 19.7 %collective-permute-start.4 = (f32[32,4096]{1,0:T(8,128)S(1)}, f32[32,4096]{1,0:T(8,128)S(1)}, u32[]{:S(2)}, u32[]{:S(2)}) collective-permute-start(f32[32,4096]{1,0:T(8,128)S(1)} %get-tuple-element.33), channel_id=1, source_target_pairs={{0,1},{1,2},{2,3},{4,5},{5,6},{6,7},{8,9},{9,10},{10,11},{12,13},{... | collective-permute-start | bytes 1572872 | tf_op jit(solution)/shard_map/ppermute | solution.py:361
  12.8 16.5 %collective-permute-start.8 = (bf16[16,4096]{1,0:T(8,128)(2,1)S(1)}, bf16[16,4096]{1,0:T(8,128)(2,1)S(1)}, u32[]{:S(2)}, u32[]{:S(2)}) collective-permute-start(bf16[16,4096]{1,0:T(8,128)(2,1)S(1)} %get-tuple-element.43), channel_id=1, source_target_pairs={{3,1},{7,5},{11,9},{15,13},{19,17},{23,21},{27,25},{31,29}} | collective-permute-start | bytes 393224 | tf_op jit(solution)/shard_map/ppermute | solution.py:384
  13.5 18.3 %collective-permute-start.7 = (bf16[16,4096]{1,0:T(8,128)(2,1)S(1)}, bf16[16,4096]{1,0:T(8,128)(2,1)S(1)}, u32[]{:S(2)}, u32[]{:S(2)}) collective-permute-start(bf16[16,4096]{1,0:T(8,128)(2,1)S(1)} %get-tuple-element.44), channel_id=1, source_target_pairs={{3,0},{7,4},{11,8},{15,12},{19,16},{23,20},{27,24},{31,28}} | collective-permute-start | bytes 393224 | tf_op jit(solution)/shard_map/ppermute | solution.py:384
  20.6 14.0 %collective-permute-start = (bf16[16,4096]{1,0:T(8,128)(2,1)S(1)}, bf16[16,4096]{1,0:T(8,128)(2,1)S(1)}, u32[]{:S(2)}, u32[]{:S(2)}) collective-permute-start(bf16[16,4096]{1,0:T(8,128)(2,1)S(1)} %get-tuple-element.26), channel_id=1, source_target_pairs={{0,1},{1,2},{2,3},{3,0},{4,5},{5,6},{6,7},{7,4},{8,9},{9,10},{10,1... | collective-permute-start | bytes 393224 | tf_op jit(solution)/shard_map/ppermute | solution.py:380
  22.7 16.4 %collective-permute-start.1 = (bf16[16,4096]{1,0:T(8,128)(2,1)S(1)}, bf16[16,4096]{1,0:T(8,128)(2,1)S(1)}, u32[]{:S(2)}, u32[]{:S(2)}) collective-permute-start(bf16[16,4096]{1,0:T(8,128)(2,1)S(1)} %get-tuple-element.27), channel_id=1, source_target_pairs={{0,2},{1,3},{2,0},{3,1},{4,6},{5,7},{6,4},{7,5},{8,10},{9,11},{10,... | collective-permute-start | bytes 393224 | tf_op jit(solution)/shard_map/ppermute | solution.py:380
  26.8 12.3 %collective-permute-start.2 = (bf16[16,4096]{1,0:T(8,128)(2,1)S(1)}, bf16[16,4096]{1,0:T(8,128)(2,1)S(1)}, u32[]{:S(2)}, u32[]{:S(2)}) collective-permute-start(bf16[16,4096]{1,0:T(8,128)(2,1)S(1)} %get-tuple-element.28), channel_id=1, source_target_pairs={{0,3},{1,0},{2,1},{3,2},{4,7},{5,4},{6,5},{7,6},{8,11},{9,8},{10,9... | collective-permute-start | bytes 393224 | tf_op jit(solution)/shard_map/ppermute | solution.py:380
  29.3 12.4 %collective-permute-start.5 = (bf16[16,4096]{1,0:T(8,128)(2,1)S(1)}, bf16[16,4096]{1,0:T(8,128)(2,1)S(1)}, u32[]{:S(2)}, u32[]{:S(2)}) collective-permute-start(bf16[16,4096]{1,0:T(8,128)(2,1)S(1)} %get-tuple-element.35), channel_id=1, source_target_pairs={{0,3},{1,0},{2,1},{3,2},{4,7},{5,4},{6,5},{7,6},{8,11},{9,8},{10,9... | collective-permute-start | bytes 393224 | tf_op jit(solution)/shard_map/ppermute | solution.py:380
  31.8 12.9 %collective-permute-start.6 = (bf16[16,4096]{1,0:T(8,128)(2,1)S(1)}, bf16[16,4096]{1,0:T(8,128)(2,1)S(1)}, u32[]{:S(2)}, u32[]{:S(2)}) collective-permute-start(bf16[16,4096]{1,0:T(8,128)(2,1)S(1)} %get-tuple-element.37), channel_id=1, source_target_pairs={{1,2},{2,3},{3,0},{5,6},{6,7},{7,4},{9,10},{10,11},{11,8},{13,14},... | collective-permute-start | bytes 393224 | tf_op jit(solution)/shard_map/ppermute | solution.py:402
  47.5 1.2 %collective-permute-start.9 = (f32[8,128]{1,0:T(8,128)S(1)}, f32[8,128]{1,0:T(8,128)S(1)}, u32[]{:S(2)}, u32[]{:S(2)}) collective-permute-start(f32[8,128]{1,0:T(8,128)S(1)} %get-tuple-element.38), channel_id=1, source_target_pairs={{0,4},{4,0},{8,12},{12,8},{16,20},{20,16},{24,28},{28,24},{1,5},{5... | collective-permute-start | bytes 12296 | tf_op jit(solution)/shard_map/ppermute | solution.py:419
  48.7 3.6 %collective-permute-start.10 = (f32[8,128]{1,0:T(8,128)S(1)}, f32[8,128]{1,0:T(8,128)S(1)}, u32[]{:S(2)}, u32[]{:S(2)}) collective-permute-start(f32[8,128]{1,0:T(8,128)S(1)} %add.28), channel_id=1, source_target_pairs={{0,8},{4,12},{8,0},{12,4},{16,24},{20,28},{24,16},{28,20},{1,9},{5... | collective-permute-start | bytes 12296 | tf_op jit(solution)/shard_map/ppermute | solution.py:419
  52.3 3.6 %collective-permute-start.11 = (f32[8,128]{1,0:T(8,128)S(1)}, f32[8,128]{1,0:T(8,128)S(1)}, u32[]{:S(2)}, u32[]{:S(2)}) collective-permute-start(f32[8,128]{1,0:T(8,128)S(1)} %add.29.a_ref), channel_id=1, source_target_pairs={{0,16},{4,20},{8,24},{12,28},{16,0},{20,4},{24,8},{28,12},{1,17},{... | collective-permute-start | bytes 12296 | tf_op jit(solution)/shard_map/ppermute | solution.py:419

commit v2 on v1

--- a/solution.py
+++ b/solution.py
@@ -37,18 +37,37 @@
     return jnp.where(condition, 1.0, 0.0).astype(BF16)
 
 
-def transform_table(freq_rows, group):
-    times = jnp.arange(NFFT, dtype=jnp.int32)
-    phase = freq_rows[:, None] * times[None, :] % NFFT
-    angle = 2.0 * math.pi / NFFT * phase.astype(F32)
+def modulo(x, n):
+    return jnp.where(x < 0, x + n, x)
+
+
+def block_of(slot, me, slots):
+    half_slots = slots // 2
+    above = slot - slots
+    below = above - half_slots
+    even = 2 * modulo(me - slot, slots)
+    upper = 2 * modulo(me - jnp.where(above == 0, 0, above + half_slots), slots) + 1
+    lower = modulo(2 * modulo(me - below, slots) - 1, 2 * slots)
+    return jnp.where(slot < slots, even, jnp.where(below < 0, upper, lower))
+
+
+def transform_rows(freqs, me, wanted, slots, group, start):
+    count = group // 2
+    times = start + iota((count, HALF), 1)
     window = 0.5 - 0.5 * jnp.cos(2.0 * math.pi / NFFT * times.astype(F32))
-    real_part = window[None, :] * jnp.cos(angle)
-    imag_part = -window[None, :] * jnp.sin(angle)
-    slots = freq_rows.shape[0] // group
-    stacked = jnp.stack(
-        [real_part.reshape(slots, group, NFFT), imag_part.reshape(slots, group, NFFT)], axis=1
-    )
-    return stacked.reshape(2 * freq_rows.shape[0], NFFT).astype(BF16)
+    row = iota((count, HALF), 0)
+    out = []
+    for s in wanted:
+        owner = lax.rem(me + s, slots)
+        freq = jnp.zeros((count, HALF), jnp.int32)
+        for f in range(count):
+            freq = jnp.where(row == f, freqs[owner * count + f], freq)
+        product = freq * times
+        thirds = ((product >> 8) * 21846) >> 16
+        angle = 2.0 * math.pi / NFFT * (product - NFFT * thirds).astype(F32)
+        out.append(window * jnp.cos(angle))
+        out.append(-window * jnp.sin(angle))
+    return jnp.concatenate(out, axis=0).astype(BF16)
 
 
 def spread(rows, var_count):
@@ -56,78 +75,86 @@
     pick = one_hot(iota((HALF, width), 1) // var_count == iota((HALF, width), 0))
     wide = mm(rows, pick)
     owner = iota(wide.shape, 1) % var_count
-    return jnp.concatenate(
-        [jnp.where(owner == v, wide, 0.0).astype(BF16) for v in range(var_count)], axis=0
-    )
+    return [jnp.where(owner == v, wide, 0.0).astype(BF16) for v in range(var_count)]
 
 
 def load_copies(x_hbm, held, sems):
+    rows = held.shape[1]
     return [
-        pltpu.make_async_copy(x_hbm.at[:, :, pl.ds(j * LANES, LANES)], held.at[j], sems.at[j])
+        pltpu.make_async_copy(
+            x_hbm.at[pl.ds(0, rows), :, pl.ds(j * LANES, LANES)], held.at[j], sems.at[j]
+        )
         for j in range(held.shape[0])
     ]
 
 
 def columns(held, j, half, var_count):
     rows = HALF * var_count
+    total = held.shape[1] * var_count
     parts = [
-        held.at[j + i].reshape(2 * rows, LANES)[half * rows : (half + 1) * rows, :]
+        held.at[j + i].reshape(total, LANES)[half * rows : (half + 1) * rows, :]
         for i in range(2)
     ]
     return jnp.concatenate(parts, axis=1)
 
 
-def halo_kernel(down_rows, up_rows, var_count, points, tab, x_hbm, down, up, held, sems):
+def down_kernel(slots, group, var_count, points, freqs, x_hbm, down, lhs, held, sems):
     copies = load_copies(x_hbm, held, sems)
     for copy in copies:
         copy.start()
-    down_lhs = spread(tab[down_rows[0] : down_rows[1], HALF:], var_count)
-    up_lhs = spread(tab[up_rows[0] : up_rows[1], :HALF], var_count)
-    count = down_rows[1] - down_rows[0]
+    me = lax.axis_index("blk")
+    count = down.shape[0]
+    rows = transform_rows(freqs, me, range(slots // 2, slots), slots, group, HALF)
+    for v, part in enumerate(spread(rows, var_count)):
+        lhs[v * count : (v + 1) * count, :] = part
     for j in range(0, held.shape[0], 2):
         copies[j].wait()
         copies[j + 1].wait()
-        for half, lhs, out in ((0, down_lhs, down), (1, up_lhs, up)):
-            got = mm(lhs, columns(held, j, half, var_count))
-            for v in range(var_count):
-                out[:, v * points + j * LANES : v * points + (j + 2) * LANES] = got[
-                    v * count : (v + 1) * count
-                ]
-
-
-def block_kernel(slots, keep, var_count, points, tab, x_hbm, *refs):
-    outs, (held, sems) = (refs[: -2], refs[-2:])
-    even = outs[:slots]
-    lead = outs[slots : slots + len(keep)]
-    trail = outs[slots + len(keep) :]
+        got = mm(lhs[...], columns(held, j, 0, var_count))
+        for v in range(var_count):
+            down[:, v * points + j * LANES : v * points + (j + 2) * LANES] = got[
+                v * count : (v + 1) * count
+            ]
+
+
+def block_kernel(slots, keep, var_count, points, freqs, x_hbm, _, *refs):
+    outs, (lhs, held, sems) = (refs[:-3], refs[-3:])
+    half_slots = slots // 2
+    up = outs[0]
+    even = outs[1 : 1 + slots]
+    lead = outs[1 + slots : 1 + slots + half_slots]
+    trail = outs[1 + slots + half_slots :]
     group = even[0].shape[0]
     copies = load_copies(x_hbm, held, sems)
     for copy in copies:
         copy.start()
-    lead_tab = tab[:, :HALF]
-    trail_tab = tab[:, HALF:]
-    lead_lhs = spread(lead_tab, var_count)
-    trail_lhs = spread(trail_tab, var_count)
-    keep_rows = jnp.concatenate([lead_tab[s * group : (s + 1) * group] for s in keep], axis=0)
-    keep_lhs = spread(keep_rows, var_count)
-    half_slots = len(trail)
-    own_lhs = spread(trail_tab[: half_slots * group], var_count)
+    me = lax.axis_index("blk")
+    full = slots * group
+    lead_rows = transform_rows(freqs, me, range(slots), slots, group, 0)
+    trail_rows = transform_rows(freqs, me, range(slots), slots, group, HALF)
+    both = spread(jnp.concatenate([lead_rows, trail_rows], axis=0), var_count)
+    for v, part in enumerate(both):
+        lhs[2 * v * full : 2 * (v + 1) * full, :] = part
+    short = full + half_slots * group
     for j in range(0, held.shape[0], 2):
         copies[j].wait()
         copies[j + 1].wait()
-        first = columns(held, j, 0, var_count)
-        second = columns(held, j, 1, var_count)
-        whole = mm(lead_lhs, first) + mm(trail_lhs, second)
-        kept = mm(keep_lhs, second)
-        own = mm(own_lhs, first)
-        for value, targets in ((whole, even), (kept, lead), (own, trail)):
-            total = len(targets) * group
-            for v in range(var_count):
-                for s, target in enumerate(targets):
-                    low = v * total + s * group
-                    target[:, v * points + j * LANES : v * points + (j + 2) * LANES] = value[
-                        low : low + group
-                    ].astype(target.dtype)
+        wanted = [lhs[2 * v * full : 2 * v * full + short, :] for v in range(var_count)]
+        first = mm(jnp.concatenate(wanted, axis=0), columns(held, j, 0, var_count))
+        second = mm(lhs[...], columns(held, j, 1, var_count))
+        for v in range(var_count):
+            low = v * points + j * LANES
+            high = low + 2 * LANES
+            top = first[v * short : (v + 1) * short]
+            bottom = second[2 * v * full : 2 * (v + 1) * full]
+            whole = (top[:full] + bottom[full:]).astype(BF16)
+            for s in range(slots):
+                even[s][:, low:high] = whole[s * group : (s + 1) * group]
+            up[:, low:high] = bottom[group : group + half_slots * group]
+            for s, target in zip(keep, lead):
+                target[:, low:high] = bottom[s * group : (s + 1) * group]
+            for s, target in enumerate(trail):
+                target[:, low:high] = top[full + s * group : full + (s + 1) * group]
 
 
 def join_kernel(half_slots, group, *refs):
@@ -145,49 +172,25 @@
         ).astype(BF16)
 
 
+def gather_pieces(refs, slots, me):
+    half_slots = slots // 2
+    found = [ref[...] for ref in refs[: slots + half_slots]]
+    for i in range(half_slots):
+        below = refs[slots + half_slots + i][...]
+        last = refs[2 * slots + i][...]
+        found.append(jnp.where(me == i, last, below))
+    return found
+
+
 def gram_kernel(slots, group, var_count, points, weights, classes, *refs):
-    half_slots = slots // 2
-    even = refs[:slots]
-    above = refs[slots : slots + half_slots]
-    below = refs[slots + half_slots : 2 * slots]
-    last = refs[2 * slots : 2 * slots + half_slots]
-    packed, spectra, sems = refs[2 * slots + half_slots :]
+    packed = refs[-1]
     blocks = 2 * slots
     me = lax.axis_index("blk")
-
-    def place(source, block, sem):
-        return pltpu.make_async_copy(source, spectra.at[pl.ds(block * group, group), :], sem)
-
-    copies = []
-    for s in range(slots):
-        copies.append(place(even[s], 2 * ((me + slots - s) % slots), sems.at[s]))
-    for copy in copies:
-        copy.start()
-    offsets = [0] + list(range(half_slots + 1, slots))
-    for i, s in enumerate(offsets):
-        copy = place(above[i], 2 * ((me + slots - s) % slots) + 1, sems.at[slots + i])
-        copy.start()
-        copies.append(copy)
-    for i in range(half_slots):
-        block = (2 * ((me + slots - i) % slots) + blocks - 1) % blocks
-        sem = sems.at[slots + half_slots + i]
-
-        @pl.when(me == i)
-        def _():
-            place(last[i], block, sem).start()
-
-        @pl.when(me != i)
-        def _():
-            place(below[i], block, sem).start()
-
-        copies.append(place(below[i], block, sem))
     picked = jnp.zeros(classes.shape, F32)
     for k in range(weights.shape[0]):
         picked = picked + jnp.where(classes[...] == k, weights[k], jnp.float32(0.0))
     wide = jnp.concatenate([picked] * var_count, axis=1)
-    for copy in copies:
-        copy.wait()
-    left = spectra[...]
+    left = jnp.concatenate(gather_pieces(refs[:-1], slots, me), axis=0)
     right = (left.astype(F32) * wide).astype(BF16)
     gram = lax.dot_general(
         left, right, (((1,), (1,)), ((), ())), preferred_element_type=F32
@@ -200,7 +203,7 @@
     rows_im = gram[:, 1].reshape(blocks * freqs, size)
     width = 2 * blocks * blocks
     row, lane = (iota((size, width), 0), iota((size, width), 1))
-    fits = row // group == lane % blocks
+    fits = block_of(row // group, me, slots) == lane % blocks
     row_part = row // freqs % 2
     lane_part = lane // blocks % 2
     from_re = one_hot(fits & (row_part == lane_part))
@@ -212,11 +215,16 @@
     mine = iota((freqs, width), 1) // (2 * blocks)
     out = jnp.zeros((freqs, width), F32)
     for b in range(blocks):
-        out = out + jnp.where(mine == b, total[b * freqs : (b + 1) * freqs], 0.0)
+        block = block_of(jnp.int32(b), me, slots)
+        out = out + jnp.where(mine == block, total[b * freqs : (b + 1) * freqs], 0.0)
     packed[...] = out
 
 
-def mode_kernel(blocks, var_count, points, scaling, feature_count, a_ref, b_ref, spectra, csd, eig, modes):
+def mode_kernel(slots, var_count, points, scaling, feature_count, a_ref, b_ref, *refs):
+    csd, eig, modes = refs[-3:]
+    blocks = 2 * slots
+    me = lax.axis_index("blk")
+    spectra = gather_pieces(refs[:-3], slots, me)
     raw = a_ref[...] + b_ref[...]
     freqs, width = raw.shape
     group = 2 * freqs
@@ -258,7 +266,7 @@
     normsq = over_blocks(low_re.astype(F32) * out_re + low_im.astype(F32) * out_im)
     scale = jnp.sqrt(jnp.float32(feature_count) / normsq)
     row, lane = (iota((width, size), 0), iota((width, size), 1))
-    expand = one_hot(row == lane // group)
+    expand = one_hot(row == block_of(lane // group, me, slots))
     wide = mm(jnp.concatenate([vec_re, vec_im], axis=0).astype(BF16), expand)
     wide_re, wide_im = (wide[:freqs], wide[freqs:])
     part = iota((freqs, size), 1) // freqs % 2
@@ -280,7 +288,12 @@
         )
     coef = jnp.concatenate(tall, axis=0).astype(BF16)
     stacked = jnp.concatenate(
-        [spectra[:, v * points : (v + 1) * points] for v in range(var_count)], axis=0
+        [
+            piece[:, v * points : (v + 1) * points]
+            for v in range(var_count)
+            for piece in spectra
+        ],
+        axis=0,
     )
     phi = mm(coef, stacked)
     for f in range(freqs):
@@ -334,45 +347,39 @@
     smem = pl.BlockSpec(memory_space=pltpu.SMEM)
     hbm = pl.BlockSpec(memory_space=pl.ANY)
     shape = jax.ShapeDtypeStruct
-    held = [
-        pltpu.VMEM((points // LANES, row_count, var_count, LANES), BF16),
-        pltpu.SemaphoreType.DMA((points // LANES,)),
-    ]
-
-    turned = lax.dynamic_slice(
-        jnp.concatenate([freq_index, freq_index]), (me * freqs,), (freq_index.shape[0],)
-    )
-    table = transform_table(turned, freqs)
-    down_rows = (half_slots * group, slots * group)
-    up_rows = (group, (half_slots + 1) * group)
+
+    def scratch(rows, halves):
+        return [
+            pltpu.VMEM((rows * var_count, HALF * var_count), BF16),
+            pltpu.VMEM((points // LANES, halves * HALF, var_count, LANES), BF16),
+            pltpu.SemaphoreType.DMA((points // LANES,)),
+        ]
+
     wide = half_slots * group
-    halo = [shape((wide, features), F32)] * 2
-    down, up = call(
-        functools.partial(halo_kernel, down_rows, up_rows, var_count, points),
-        halo,
-        [vmem, hbm],
-        (table, snapshots),
-        held,
-        2 * 2 * wide * HALF * features * var_count,
-        2 * row_count * features,
+    down = call(
+        functools.partial(down_kernel, slots, group, var_count, points),
+        shape((wide, features), F32),
+        [smem, hbm],
+        (freq_index, snapshots),
+        scratch(wide, 1),
+        2 * wide * HALF * features * var_count,
+        row_count * features,
     )
     below = [(i, i + 1) for i in range(slots - 1)]
     from_above = lax.ppermute(down, "blk", [(b, a) for a, b in below])
-    from_below = lax.ppermute(up, "blk", below)
-
     keep = [0] + list(range(half_slots + 1, slots))
     piece = shape((group, features), BF16)
     wide_piece = shape((group, features), F32)
-    table, _ = lax.optimization_barrier((table, down))
-    pieces = call(
+    up, *pieces = call(
         functools.partial(block_kernel, slots, keep, var_count, points),
-        [piece] * slots + [wide_piece] * (2 * half_slots),
-        [vmem, hbm],
-        (table, snapshots),
-        held,
-        2 * 3 * slots * group * HALF * features * var_count,
+        [shape((wide, features), F32)] + [piece] * slots + [wide_piece] * (2 * half_slots),
+        [smem, hbm, hbm],
+        (freq_index, snapshots, down),
+        scratch(2 * slots * group, 2),
+        2 * 4 * slots * group * HALF * features * var_count,
         2 * row_count * features,
     )
+    from_below = lax.ppermute(up, "blk", below)
     even = pieces[:slots]
 
     def shift(x, s, pairs=None):
@@ -401,12 +408,13 @@
         pairs = [(a, (a + i) % slots) for a in range(1, slots)]
         under.append(lax.ppermute(odd[half_slots + i], "blk", pairs))
     width = 2 * blocks * blocks
-    packed, spectra = call(
+    spectra = (*even, *above, *under, *last)
+    packed = call(
         functools.partial(gram_kernel, slots, group, var_count, points),
-        [shape((freqs, width), F32), shape((blocks * group, features), BF16)],
-        [smem, vmem] + [hbm] * (2 * slots + half_slots),
-        (class_weight, weight_class.reshape(1, points), *even, *above, *under, *last),
-        [pltpu.SemaphoreType.DMA((2 * slots,))],
+        shape((freqs, width), F32),
+        [smem, vmem] + [vmem] * len(spectra),
+        (class_weight, weight_class.reshape(1, points), *spectra),
+        [],
         2 * (blocks * group) ** 2 * features,
         4 * blocks * group * features,
     )
@@ -422,7 +430,7 @@
     csd, eigval, modes = call(
         functools.partial(
             mode_kernel,
-            blocks,
+            slots,
             var_count,
             points,
             1.0 / (total_features * (3.0 * NFFT / 8.0)),
@@ -433,8 +441,8 @@
             shape((1, freqs), F32),
             shape((freqs, 2, var_count, points), F32),
         ],
-        [vmem] * 3,
-        (packed, other, spectra),
+        [vmem] * (2 + len(spectra)),
+        (packed, other, *spectra),
         [],
         2 * 2 * blocks * group * group * features,
         2 * blocks * group * features,

time: 58.2 us -> 64.1 us (1.10)
  waiting for transfers between devices: 18.3 us -> 24.6 us
  other arithmetic: 1.39 us -> 0.04 us
  Pallas kernels: 14.1 us -> 14.8 us
    ppermute x1, waiting for transfers between devices: 0.01 us -> 11.9 us  [on_device(): from_below = lax.ppermute(up, 'blk', below)]
    ppermute x4, waiting for transfers between devices: 8.61 us -> 0.58 us  [shift(): return lax.ppermute(x, 'blk', pairs)]
    ppermute x1, starting transfers between devices: 5.61 us -> 2.63 us  [on_device(): from_below = lax.ppermute(up, 'blk', below)]
    ppermute x4, starting transfers between devices: 9.85 us -> 12.8 us  [shift(): return lax.ppermute(x, 'blk', pairs)]
    ppermute x1, waiting for transfers between devices: 3.01 us -> 4.31 us  [on_device(): under.append(lax.ppermute(odd[half_slots + i], 'blk', pairs))]
    ppermute x2, waiting for transfers between devices: 1.22 us -> 2.45 us  [on_device(): lax.ppermute(up[i * group:(i + 1) * group].astype(BF16), 'blk', [(slots -...]
    concatenate x1 -> x0, other arithmetic: 0.81 us -> none  [on_device(): jnp.concatenate([freq_index, freq_index])]
    pallas_call x5, Pallas kernels: 14.1 us -> 14.8 us  [call(): pl.pallas_call(kernel, out_shape=outs, in_specs=ins, out_specs=jax.tree.m...]
  transfers between devices with their start and end apart: 12 -> 12, of which waited for: 8 -> 7; matrix products, arithmetic and copies ran while one was open for 0% -> 0% of each run, Pallas kernels for 10% -> 13%
where the time goes in v2:
time: 64.1 us; the launch traced here: 63.9 us
  waiting for transfers between devices  24.6 us (38%)
  starting transfers between devices  23 us (36%)
  Pallas kernels  14.8 us (23%)
  between operations  0.78 us (1%)
  local copies, waits for them, and re-layouts  0.68 us (1%)
    pallas_call x5, Pallas kernels, call(): pl.pallas_call(kernel, out_shape=outs, in_specs=ins, out_specs=jax.tree.m...  14.8 us
    ppermute x4, starting transfers between devices, shift(): return lax.ppermute(x, 'blk', pairs)  12.8 us
    ppermute x1, waiting for transfers between devices, on_device(): from_below = lax.ppermute(up, 'blk', below)  11.9 us
    ppermute x3, waiting for transfers between devices, on_device(): other = lax.ppermute(packed, 'pts', [(i, i ^ step) for i in range(devices)])  5.36 us
    ppermute x1, waiting for transfers between devices, on_device(): under.append(lax.ppermute(odd[half_slots + i], 'blk', pairs))  4.31 us
    ppermute x3, starting transfers between devices, on_device(): other = lax.ppermute(packed, 'pts', [(i, i ^ step) for i in range(devices)])  3.05 us
    ppermute x1, starting transfers between devices, on_device(): from_below = lax.ppermute(up, 'blk', below)  2.63 us
    ppermute x2, waiting for transfers between devices, on_device(): lax.ppermute(up[i * group:(i + 1) * group].astype(BF16), 'blk', [(slots -...  2.45 us
  transfers between devices with their start and end apart: 12, of which 7 were waited for; matrix products, arithmetic and copies ran while one was open for 0% of the time, Pallas kernels for 13%

profile of v2, /device:TPU:0, one launch (start us, length us, event | category | flops | bytes accessed | tf_op | source)
XLA Modules:
  0.0 63.9 jit_solution(18047369267785067693)
XLA Ops:
  0.6 0.6 %copy-done.1 = s32[32]{0:T(128)S(1)} copy-done((s32[32]{0:T(128)S(1)}, s32[32]{0:T(128)}, u32[]{:S(2)}) %copy-start.1) | copy-done | bytes 152
  1.3 3.2 %shard_map.67._ = f32[32,4096]{1,0:T(8,128)S(1)} custom-call(s32[32]{0:T(128)S(1)} %copy-done.1, bf16[768,4,1024]{2,1,0:T(4,128)(2,1)} %x_hbm.3), custom_call_target="tpu_custom_call" | custom-call | flops 402653184 | bytes 3145728 | tf_op jit(solution)/shard_map/pallas_call | solution.py:326
  4.5 0.0 copy-start
  4.5 0.0 copy-start.2
  4.5 1.3 %collective-permute-start.3 = (f32[32,4096]{1,0:T(8,128)S(1)}, f32[32,4096]{1,0:T(8,128)S(1)}, u32[]{:S(2)}, u32[]{:S(2)}) collective-permute-start(f32[32,4096]{1,0:T(8,128)S(1)} %shard_map.67._), channel_id=1, source_target_pairs={{1,0},{2,1},{3,2},{5,4},{6,5},{7,6},{9,8},{10,9},{11,10},{13,12},{... | collective-permute-start | bytes 1572872 | tf_op jit(solution)/shard_map/ppermute | solution.py:369
  5.8 8.4 %shard_map.68 = (f32[32,4096]{1,0:T(8,128)S(1)}, bf16[16,4096]{1,0:T(8,128)(2,1)S(1)}, bf16[16,4096]{1,0:T(8,128)(2,1)S(1)}, bf16[16,4096]{1,0:T(8,128)(2,1)S(1)...) custom-call(s32[32]{0:T(128)S(1)} %copy-done.1, ...), custom_call_target="tpu_custom_call" | custom-call | flops 3221225472 | bytes 6291456 | tf_op jit(solution)/shard_map/pallas_call | solution.py:326
  14.2 3.7 %collective-permute-start = (bf16[16,4096]{1,0:T(8,128)(2,1)S(1)}, bf16[16,4096]{1,0:T(8,128)(2,1)S(1)}, u32[]{:S(2)}, u32[]{:S(2)}) collective-permute-start(bf16[16,4096]{1,0:T(8,128)(2,1)S(1)} %get-tuple-element.20), channel_id=1, source_target_pairs={{0,1},{1,2},{2,3},{3,0},{4,5},{5,6},{6,7},{7,4},{8,9},{9,10},{10,1... | collective-permute-start | bytes 393224 | tf_op jit(solution)/shard_map/ppermute | solution.py:387
  17.9 3.1 %collective-permute-start.1 = (bf16[16,4096]{1,0:T(8,128)(2,1)S(1)}, bf16[16,4096]{1,0:T(8,128)(2,1)S(1)}, u32[]{:S(2)}, u32[]{:S(2)}) collective-permute-start(bf16[16,4096]{1,0:T(8,128)(2,1)S(1)} %get-tuple-element.21), channel_id=1, source_target_pairs={{0,2},{1,3},{2,0},{3,1},{4,6},{5,7},{6,4},{7,5},{8,10},{9,11},{10,... | collective-permute-start | bytes 393224 | tf_op jit(solution)/shard_map/ppermute | solution.py:387
  21.0 1.3 %collective-permute-start.2 = (bf16[16,4096]{1,0:T(8,128)(2,1)S(1)}, bf16[16,4096]{1,0:T(8,128)(2,1)S(1)}, u32[]{:S(2)}, u32[]{:S(2)}) collective-permute-start(bf16[16,4096]{1,0:T(8,128)(2,1)S(1)} %get-tuple-element.22), channel_id=1, source_target_pairs={{0,3},{1,0},{2,1},{3,2},{4,7},{5,4},{6,5},{7,6},{8,11},{9,8},{10,9... | collective-permute-start | bytes 393224 | tf_op jit(solution)/shard_map/ppermute | solution.py:387
  22.3 2.6 %collective-permute-start.4 = (f32[32,4096]{1,0:T(8,128)S(1)}, f32[32,4096]{1,0:T(8,128)S(1)}, u32[]{:S(2)}, u32[]{:S(2)}) collective-permute-start(f32[32,4096]{1,0:T(8,128)S(1)} %get-tuple-element.27), channel_id=1, source_target_pairs={{0,1},{1,2},{2,3},{4,5},{5,6},{6,7},{8,9},{9,10},{10,11},{12,13},{... | collective-permute-start | bytes 1572872 | tf_op jit(solution)/shard_map/ppermute | solution.py:382
  25.0 0.0 collective-permute-done.3.refs_4_
  25.0 0.7 %collective-permute-start.8 = (bf16[16,4096]{1,0:T(8,128)(2,1)S(1)}, bf16[16,4096]{1,0:T(8,128)(2,1)S(1)}, u32[]{:S(2)}, u32[]{:S(2)}) collective-permute-start(bf16[16,4096]{1,0:T(8,128)(2,1)S(1)} %get-tuple-element.35), channel_id=1, source_target_pairs={{3,1},{7,5},{11,9},{15,13},{19,17},{23,21},{27,25},{31,29}} | collective-permute-start | bytes 393224 | tf_op jit(solution)/shard_map/ppermute | solution.py:391
  25.7 11.9 %collective-permute-done.4.refs_5_ = f32[32,4096]{1,0:T(8,128)S(1)} collective-permute-done((f32[32,4096]{1,0:T(8,128)S(1)}, f32[32,4096]{1,0:T(8,128)S(1)}, u32[]{:S(2)}, u32[]{:S(2)}) %collective-permute-start.4) | collective-permute-done | bytes 524320 | tf_op jit(solution)/shard_map/ppermute | solution.py:382
  37.6 1.3 %collective-permute-start.7 = (bf16[16,4096]{1,0:T(8,128)(2,1)S(1)}, bf16[16,4096]{1,0:T(8,128)(2,1)S(1)}, u32[]{:S(2)}, u32[]{:S(2)}) collective-permute-start(bf16[16,4096]{1,0:T(8,128)(2,1)S(1)} %get-tuple-element.36), channel_id=1, source_target_pairs={{3,0},{7,4},{11,8},{15,12},{19,16},{23,20},{27,24},{31,28}} | collective-permute-start | bytes 393224 | tf_op jit(solution)/shard_map/ppermute | solution.py:391
  38.9 0.1 shard_map.69
  39.0 0.0 collective-permute-done.refs_1_
  39.0 4.7 %collective-permute-start.5 = (bf16[16,4096]{1,0:T(8,128)(2,1)S(1)}, bf16[16,4096]{1,0:T(8,128)(2,1)S(1)}, u32[]{:S(2)}, u32[]{:S(2)}) collective-permute-start(bf16[16,4096]{1,0:T(8,128)(2,1)S(1)} %get-tuple-element.29), channel_id=1, source_target_pairs={{0,3},{1,0},{2,1},{3,2},{4,7},{5,4},{6,5},{7,6},{8,11},{9,8},{10,9... | collective-permute-start | bytes 393224 | tf_op jit(solution)/shard_map/ppermute | solution.py:387
  43.7 0.0 collective-permute-done.1.refs_2_
  43.7 1.3 %collective-permute-start.6 = (bf16[16,4096]{1,0:T(8,128)(2,1)S(1)}, bf16[16,4096]{1,0:T(8,128)(2,1)S(1)}, u32[]{:S(2)}, u32[]{:S(2)}) collective-permute-start(bf16[16,4096]{1,0:T(8,128)(2,1)S(1)} %get-tuple-element.31), channel_id=1, source_target_pairs={{1,2},{2,3},{3,0},{5,6},{6,7},{7,4},{9,10},{10,11},{11,8},{13,14},... | collective-permute-start | bytes 393224 | tf_op jit(solution)/shard_map/ppermute | solution.py:409
  45.0 0.0 collective-permute-done.2.refs_3_
  45.0 0.0 collective-permute-done.8.refs_9_
  45.0 2.5 %collective-permute-done.7.refs_8_ = bf16[16,4096]{1,0:T(8,128)(2,1)S(1)} collective-permute-done((bf16[16,4096]{1,0:T(8,128)(2,1)S(1)}, bf16[16,4096]{1,0:T(8,128)(2,1)S(1)}, u32[]{:S(2)}, u32[]{:S(2)}) %collective-permute-start.7) | collective-permute-done | bytes 131104 | tf_op jit(solution)/shard_map/ppermute | solution.py:391
  47.5 0.6 collective-permute-done.5.refs_5_
  48.0 4.3 %collective-permute-done.6.refs_7_ = bf16[16,4096]{1,0:T(8,128)(2,1)S(1)} collective-permute-done((bf16[16,4096]{1,0:T(8,128)(2,1)S(1)}, bf16[16,4096]{1,0:T(8,128)(2,1)S(1)}, u32[]{:S(2)}, u32[]{:S(2)}) %collective-permute-start.6) | collective-permute-done | bytes 131104 | tf_op jit(solution)/shard_map/ppermute | solution.py:409
  52.3 1.3 %shard_map.70 = f32[8,128]{1,0:T(8,128)S(1)} custom-call(f32[8]{0:T(128)S(1)} %copy-done.2, s32[1,1024]{1,0:T(1,128)S(1)} %bitcast.2, bf16[16,4096]{1,0:T(8,128)(2,1)S(1)} %get-tuple-element.19.refs_0_, bf16[16,4096]{1,0:T(8,128)(2,1)S(1)} %collective-permute-done.refs_1_, bf16[16,4096]{1,0:T(8,128)(2,1)S(1)} %collective-permute-done.1.refs_2_, ...), custom_call_target="tpu_custom_call" | custom-call | flops 134217728 | bytes 2097152 | tf_op jit(solution)/shard_map/pallas_call | solution.py:326
  53.6 0.0 collective-permute-start.9
  53.7 1.2 %collective-permute-done.9 = f32[8,128]{1,0:T(8,128)S(1)} collective-permute-done((f32[8,128]{1,0:T(8,128)S(1)}, f32[8,128]{1,0:T(8,128)S(1)}, u32[]{:S(2)}, u32[]{:S(2)}) %collective-permute-start.9) | collective-permute-done | bytes 4128 | tf_op jit(solution)/shard_map/ppermute | solution.py:427
  54.8 1.5 %collective-permute-start.10 = (f32[8,128]{1,0:T(8,128)S(1)}, f32[8,128]{1,0:T(8,128)S(1)}, u32[]{:S(2)}, u32[]{:S(2)}) collective-permute-start(f32[8,128]{1,0:T(8,128)S(1)} %add.6), channel_id=1, source_target_pairs={{0,8},{4,12},{8,0},{12,4},{16,24},{20,28},{24,16},{28,20},{1,9},{5... | collective-permute-start | bytes 12296 | tf_op jit(solution)/shard_map/ppermute | solution.py:427
  56.3 2.1 %collective-permute-done.10 = f32[8,128]{1,0:T(8,128)S(1)} collective-permute-done((f32[8,128]{1,0:T(8,128)S(1)}, f32[8,128]{1,0:T(8,128)S(1)}, u32[]{:S(2)}, u32[]{:S(2)}) %collective-permute-start.10) | collective-permute-done | bytes 4128 | tf_op jit(solution)/shard_map/ppermute | solution.py:427
  58.4 1.5 %collective-permute-start.11 = (f32[8,128]{1,0:T(8,128)S(1)}, f32[8,128]{1,0:T(8,128)S(1)}, u32[]{:S(2)}, u32[]{:S(2)}) collective-permute-start(f32[8,128]{1,0:T(8,128)S(1)} %add.7.a_ref), channel_id=1, source_target_pairs={{0,16},{4,20},{8,24},{12,28},{16,0},{20,4},{24,8},{28,12},{1,17},{... | collective-permute-start | bytes 12296 | tf_op jit(solution)/shard_map/ppermute | solution.py:427
  59.9 2.1 %collective-permute-done.11.b_ref = f32[8,128]{1,0:T(8,128)S(1)} collective-permute-done((f32[8,128]{1,0:T(8,128)S(1)}, f32[8,128]{1,0:T(8,128)S(1)}, u32[]{:S(2)}, u32[]{:S(2)}) %collective-permute-start.11) | collective-permute-done | bytes 4128 | tf_op jit(solution)/shard_map/ppermute | solution.py:427
  62.0 1.8 %shard_map.71 = (f32[8,2,8,8]{3,2,1,0:T(8,128)}, f32[1,8]{1,0:T(1,128)}, f32[8,2,4,1024]{3,2,1,0:T(4,128)}) custom-call(f32[8,128]{1,0:T(8,128)S(1)} %add.7.a_ref, f32[8,128]{1,0:T(8,128)S(1)} %collective-permute-done.11.b_ref, bf16[16,4096]{1,0:T(8,128)(2,1)S(1)} %get-tuple-element.19.refs_0_, bf16[16,4096]{1,0:T(8,128)(2,1)S(1)} %collective-permute-done.refs_1_, ...), custom_call_target="tpu_custom_call" | custom-call | flops 33554432 | bytes 1048576 | tf_op jit(solution)/shard_map/pallas_call | solution.py:326
  (7 shorter events, 0.1 us)
Async XLA Ops:
  0.6 0.7 %copy-start.1 = (s32[32]{0:T(128)S(1)}, s32[32]{0:T(128)}, u32[]{:S(2)}) copy-start(s32[32]{0:T(128)} %freqs.3) | copy-start | bytes 388
  4.5 47.9 %copy-start = (s32[1024]{0:T(1024)S(1)}, s32[1024]{0:T(1024)}, u32[]{:S(2)}) copy-start(s32[1024]{0:T(1024)} %param.6) | copy-start | bytes 12292
  4.5 47.9 %copy-start.2 = (f32[8]{0:T(128)S(1)}, f32[8]{0:T(128)}, u32[]{:S(2)}) copy-start(f32[8]{0:T(128)} %weights.1) | copy-start | bytes 100
  4.5 20.5 %collective-permute-start.3 = (f32[32,4096]{1,0:T(8,128)S(1)}, f32[32,4096]{1,0:T(8,128)S(1)}, u32[]{:S(2)}, u32[]{:S(2)}) collective-permute-start(f32[32,4096]{1,0:T(8,128)S(1)} %shard_map.67._), channel_id=1, source_target_pairs={{1,0},{2,1},{3,2},{5,4},{6,5},{7,6},{9,8},{10,9},{11,10},{13,12},{... | collective-permute-start | bytes 1572872 | tf_op jit(solution)/shard_map/ppermute | solution.py:369
  14.2 24.8 %collective-permute-start = (bf16[16,4096]{1,0:T(8,128)(2,1)S(1)}, bf16[16,4096]{1,0:T(8,128)(2,1)S(1)}, u32[]{:S(2)}, u32[]{:S(2)}) collective-permute-start(bf16[16,4096]{1,0:T(8,128)(2,1)S(1)} %get-tuple-element.20), channel_id=1, source_target_pairs={{0,1},{1,2},{2,3},{3,0},{4,5},{5,6},{6,7},{7,4},{8,9},{9,10},{10,1... | collective-permute-start | bytes 393224 | tf_op jit(solution)/shard_map/ppermute | solution.py:387
  17.9 25.8 %collective-permute-start.1 = (bf16[16,4096]{1,0:T(8,128)(2,1)S(1)}, bf16[16,4096]{1,0:T(8,128)(2,1)S(1)}, u32[]{:S(2)}, u32[]{:S(2)}) collective-permute-start(bf16[16,4096]{1,0:T(8,128)(2,1)S(1)} %get-tuple-element.21), channel_id=1, source_target_pairs={{0,2},{1,3},{2,0},{3,1},{4,6},{5,7},{6,4},{7,5},{8,10},{9,11},{10,... | collective-permute-start | bytes 393224 | tf_op jit(solution)/shard_map/ppermute | solution.py:387
  21.0 24.0 %collective-permute-start.2 = (bf16[16,4096]{1,0:T(8,128)(2,1)S(1)}, bf16[16,4096]{1,0:T(8,128)(2,1)S(1)}, u32[]{:S(2)}, u32[]{:S(2)}) collective-permute-start(bf16[16,4096]{1,0:T(8,128)(2,1)S(1)} %get-tuple-element.22), channel_id=1, source_target_pairs={{0,3},{1,0},{2,1},{3,2},{4,7},{5,4},{6,5},{7,6},{8,11},{9,8},{10,9... | collective-permute-start | bytes 393224 | tf_op jit(solution)/shard_map/ppermute | solution.py:387
  22.3 15.3 %collective-permute-start.4 = (f32[32,4096]{1,0:T(8,128)S(1)}, f32[32,4096]{1,0:T(8,128)S(1)}, u32[]{:S(2)}, u32[]{:S(2)}) collective-permute-start(f32[32,4096]{1,0:T(8,128)S(1)} %get-tuple-element.27), channel_id=1, source_target_pairs={{0,1},{1,2},{2,3},{4,5},{5,6},{6,7},{8,9},{9,10},{10,11},{12,13},{... | collective-permute-start | bytes 1572872 | tf_op jit(solution)/shard_map/ppermute | solution.py:382
  25.0 20.0 %collective-permute-start.8 = (bf16[16,4096]{1,0:T(8,128)(2,1)S(1)}, bf16[16,4096]{1,0:T(8,128)(2,1)S(1)}, u32[]{:S(2)}, u32[]{:S(2)}) collective-permute-start(bf16[16,4096]{1,0:T(8,128)(2,1)S(1)} %get-tuple-element.35), channel_id=1, source_target_pairs={{3,1},{7,5},{11,9},{15,13},{19,17},{23,21},{27,25},{31,29}} | collective-permute-start | bytes 393224 | tf_op jit(solution)/shard_map/ppermute | solution.py:391
  37.6 9.9 %collective-permute-start.7 = (bf16[16,4096]{1,0:T(8,128)(2,1)S(1)}, bf16[16,4096]{1,0:T(8,128)(2,1)S(1)}, u32[]{:S(2)}, u32[]{:S(2)}) collective-permute-start(bf16[16,4096]{1,0:T(8,128)(2,1)S(1)} %get-tuple-element.36), channel_id=1, source_target_pairs={{3,0},{7,4},{11,8},{15,12},{19,16},{23,20},{27,24},{31,28}} | collective-permute-start | bytes 393224 | tf_op jit(solution)/shard_map/ppermute | solution.py:391
  39.0 9.0 %collective-permute-start.5 = (bf16[16,4096]{1,0:T(8,128)(2,1)S(1)}, bf16[16,4096]{1,0:T(8,128)(2,1)S(1)}, u32[]{:S(2)}, u32[]{:S(2)}) collective-permute-start(bf16[16,4096]{1,0:T(8,128)(2,1)S(1)} %get-tuple-element.29), channel_id=1, source_target_pairs={{0,3},{1,0},{2,1},{3,2},{4,7},{5,4},{6,5},{7,6},{8,11},{9,8},{10,9... | collective-permute-start | bytes 393224 | tf_op jit(solution)/shard_map/ppermute | solution.py:387
  43.7 8.6 %collective-permute-start.6 = (bf16[16,4096]{1,0:T(8,128)(2,1)S(1)}, bf16[16,4096]{1,0:T(8,128)(2,1)S(1)}, u32[]{:S(2)}, u32[]{:S(2)}) collective-permute-start(bf16[16,4096]{1,0:T(8,128)(2,1)S(1)} %get-tuple-element.31), channel_id=1, source_target_pairs={{1,2},{2,3},{3,0},{5,6},{6,7},{7,4},{9,10},{10,11},{11,8},{13,14},... | collective-permute-start | bytes 393224 | tf_op jit(solution)/shard_map/ppermute | solution.py:409
  53.6 1.2 %collective-permute-start.9 = (f32[8,128]{1,0:T(8,128)S(1)}, f32[8,128]{1,0:T(8,128)S(1)}, u32[]{:S(2)}, u32[]{:S(2)}) collective-permute-start(f32[8,128]{1,0:T(8,128)S(1)} %shard_map.70), channel_id=1, source_target_pairs={{0,4},{4,0},{8,12},{12,8},{16,20},{20,16},{24,28},{28,24},{1,5},{5... | collective-permute-start | bytes 12296 | tf_op jit(solution)/shard_map/ppermute | solution.py:427
  54.8 3.6 %collective-permute-start.10 = (f32[8,128]{1,0:T(8,128)S(1)}, f32[8,128]{1,0:T(8,128)S(1)}, u32[]{:S(2)}, u32[]{:S(2)}) collective-permute-start(f32[8,128]{1,0:T(8,128)S(1)} %add.6), channel_id=1, source_target_pairs={{0,8},{4,12},{8,0},{12,4},{16,24},{20,28},{24,16},{28,20},{1,9},{5... | collective-permute-start | bytes 12296 | tf_op jit(solution)/shard_map/ppermute | solution.py:427
  58.4 3.6 %collective-permute-start.11 = (f32[8,128]{1,0:T(8,128)S(1)}, f32[8,128]{1,0:T(8,128)S(1)}, u32[]{:S(2)}, u32[]{:S(2)}) collective-permute-start(f32[8,128]{1,0:T(8,128)S(1)} %add.7.a_ref), channel_id=1, source_target_pairs={{0,16},{4,20},{8,24},{12,28},{16,0},{20,4},{24,8},{28,12},{1,17},{... | collective-permute-start | bytes 12296 | tf_op jit(solution)/shard_map/ppermute | solution.py:427

commit v3 on v2

--- a/solution.py
+++ b/solution.py
@@ -12,7 +12,7 @@
 HALF = NFFT // 2
 ITERS = 3
 LANES = 128
-VMEM_LIMIT = 48 * 1024 * 1024
+VMEM_LIMIT = 32 * 1024 * 1024
 F32 = jnp.float32
 BF16 = jnp.bfloat16
 
@@ -45,28 +45,43 @@
     half_slots = slots // 2
     above = slot - slots
     below = above - half_slots
-    even = 2 * modulo(me - slot, slots)
+    even = 2 * slot
     upper = 2 * modulo(me - jnp.where(above == 0, 0, above + half_slots), slots) + 1
     lower = modulo(2 * modulo(me - below, slots) - 1, 2 * slots)
     return jnp.where(slot < slots, even, jnp.where(below < 0, upper, lower))
 
 
-def transform_rows(freqs, me, wanted, slots, group, start):
+def trig(phase):
+    quarter = ((phase + NFFT // 8) * 1366) >> 18
+    angle = (2.0 * math.pi / NFFT) * (phase - (NFFT // 4) * quarter).astype(F32)
+    x = angle * angle
+    cos = 1.0 + x * (-1.0 / 2 + x * (1.0 / 24 + x * (-1.0 / 720 + x * (1.0 / 40320))))
+    sin = 1.0 + x * (-1.0 / 6 + x * (1.0 / 120 + x * (-1.0 / 5040 + x * (1.0 / 362880))))
+    sin = angle * sin
+    odd = (quarter & 1) != 0
+    real_part = jnp.where(odd, sin, cos)
+    imag_part = jnp.where(odd, cos, sin)
+    real_part = jnp.where(((quarter + 1) & 2) != 0, -real_part, real_part)
+    imag_part = jnp.where((quarter & 2) != 0, -imag_part, imag_part)
+    return (real_part, imag_part)
+
+
+def transform_rows(freqs, me, slots, group, start):
     count = group // 2
     times = start + iota((count, HALF), 1)
-    window = 0.5 - 0.5 * jnp.cos(2.0 * math.pi / NFFT * times.astype(F32))
+    window = 0.5 - 0.5 * trig(times)[0]
     row = iota((count, HALF), 0)
     out = []
-    for s in wanted:
+    for s in range(slots):
         owner = lax.rem(me + s, slots)
         freq = jnp.zeros((count, HALF), jnp.int32)
         for f in range(count):
             freq = jnp.where(row == f, freqs[owner * count + f], freq)
         product = freq * times
-        thirds = ((product >> 8) * 21846) >> 16
-        angle = 2.0 * math.pi / NFFT * (product - NFFT * thirds).astype(F32)
-        out.append(window * jnp.cos(angle))
-        out.append(-window * jnp.sin(angle))
+        turns = ((product >> 8) * 21846) >> 16
+        real_part, imag_part = trig(product - NFFT * turns)
+        out.append(window * real_part)
+        out.append(-window * imag_part)
     return jnp.concatenate(out, axis=0).astype(BF16)
 
 
@@ -78,107 +93,112 @@
     return [jnp.where(owner == v, wide, 0.0).astype(BF16) for v in range(var_count)]
 
 
-def load_copies(x_hbm, held, sems):
-    rows = held.shape[1]
-    return [
-        pltpu.make_async_copy(
-            x_hbm.at[pl.ds(0, rows), :, pl.ds(j * LANES, LANES)], held.at[j], sems.at[j]
-        )
-        for j in range(held.shape[0])
-    ]
-
-
 def columns(held, j, half, var_count):
     rows = HALF * var_count
-    total = held.shape[1] * var_count
     parts = [
-        held.at[j + i].reshape(total, LANES)[half * rows : (half + 1) * rows, :]
+        held.at[j + i].reshape(2 * rows, LANES)[half * rows : (half + 1) * rows, :]
         for i in range(2)
     ]
     return jnp.concatenate(parts, axis=1)
 
 
-def down_kernel(slots, group, var_count, points, freqs, x_hbm, down, lhs, held, sems):
-    copies = load_copies(x_hbm, held, sems)
+def halo_kernel(slots, group, var_count, points, freqs, x_hbm, inner, outer, lhs, held, sems):
+    copies = [
+        pltpu.make_async_copy(x_hbm.at[:, :, pl.ds(j * LANES, LANES)], held.at[j], sems.at[j])
+        for j in range(held.shape[0])
+    ]
     for copy in copies:
         copy.start()
     me = lax.axis_index("blk")
-    count = down.shape[0]
-    rows = transform_rows(freqs, me, range(slots // 2, slots), slots, group, HALF)
-    for v, part in enumerate(spread(rows, var_count)):
-        lhs[v * count : (v + 1) * count, :] = part
+    odd = lax.rem(me, 2) == 1
+    full = slots * group
+    wide = full // 2
+    rows = [transform_rows(freqs, me, slots, group, start) for start in (0, HALF)]
+    for v, part in enumerate(spread(jnp.concatenate(rows, axis=0), var_count)):
+        lhs[2 * v * full : 2 * (v + 1) * full, :] = part
+
+    def some(low):
+        return jnp.concatenate(
+            [lhs[2 * v * full + low : 2 * v * full + low + wide, :] for v in range(var_count)],
+            axis=0,
+        )
+
     for j in range(0, held.shape[0], 2):
         copies[j].wait()
         copies[j + 1].wait()
-        got = mm(lhs[...], columns(held, j, 0, var_count))
+        down = mm(some(full + wide), columns(held, j, 0, var_count))
+        up = mm(some(group), columns(held, j, 1, var_count))
         for v in range(var_count):
-            down[:, v * points + j * LANES : v * points + (j + 2) * LANES] = got[
-                v * count : (v + 1) * count
-            ]
-
-
-def block_kernel(slots, keep, var_count, points, freqs, x_hbm, _, *refs):
-    outs, (lhs, held, sems) = (refs[:-3], refs[-3:])
+            low = v * points + j * LANES
+            lower = down[v * wide : (v + 1) * wide]
+            upper = up[v * wide : (v + 1) * wide]
+            inner[:, low : low + 2 * LANES] = jnp.where(odd, upper, lower)
+            outer[:, low : low + 2 * LANES] = jnp.where(odd, lower, upper)
+
+
+def block_kernel(slots, keep, var_count, points, lhs, held, *outs):
     half_slots = slots // 2
-    up = outs[0]
-    even = outs[1 : 1 + slots]
-    lead = outs[1 + slots : 1 + slots + half_slots]
-    trail = outs[1 + slots + half_slots :]
-    group = even[0].shape[0]
-    copies = load_copies(x_hbm, held, sems)
-    for copy in copies:
-        copy.start()
+    even = outs[0]
+    lead = outs[1 : 1 + half_slots]
+    trail = outs[1 + half_slots :]
+    full = even.shape[0]
+    group = full // slots
+    short = full + half_slots * group
     me = lax.axis_index("blk")
-    full = slots * group
-    lead_rows = transform_rows(freqs, me, range(slots), slots, group, 0)
-    trail_rows = transform_rows(freqs, me, range(slots), slots, group, HALF)
-    both = spread(jnp.concatenate([lead_rows, trail_rows], axis=0), var_count)
-    for v, part in enumerate(both):
-        lhs[2 * v * full : 2 * (v + 1) * full, :] = part
-    short = full + half_slots * group
+
+    def some(v, low, high):
+        return lhs[2 * v * full + low : 2 * v * full + high, :]
+
     for j in range(0, held.shape[0], 2):
-        copies[j].wait()
-        copies[j + 1].wait()
-        wanted = [lhs[2 * v * full : 2 * v * full + short, :] for v in range(var_count)]
-        first = mm(jnp.concatenate(wanted, axis=0), columns(held, j, 0, var_count))
-        second = mm(lhs[...], columns(held, j, 1, var_count))
+        parts = [some(v, 0, short) for v in range(var_count)]
+        first = mm(jnp.concatenate(parts, axis=0), columns(held, j, 0, var_count))
+        parts = []
+        for v in range(var_count):
+            parts.append(some(v, full, 2 * full))
+            parts.extend(some(v, s * group, (s + 1) * group) for s in keep)
+        second = mm(jnp.concatenate(parts, axis=0), columns(held, j, 1, var_count))
         for v in range(var_count):
             low = v * points + j * LANES
             high = low + 2 * LANES
             top = first[v * short : (v + 1) * short]
-            bottom = second[2 * v * full : 2 * (v + 1) * full]
-            whole = (top[:full] + bottom[full:]).astype(BF16)
+            bottom = second[v * short : (v + 1) * short]
+            whole = (top[:full] + bottom[:full]).astype(BF16)
             for s in range(slots):
-                even[s][:, low:high] = whole[s * group : (s + 1) * group]
-            up[:, low:high] = bottom[group : group + half_slots * group]
-            for s, target in zip(keep, lead):
-                target[:, low:high] = bottom[s * group : (s + 1) * group]
-            for s, target in enumerate(trail):
-                target[:, low:high] = top[full + s * group : full + (s + 1) * group]
+                owner = pl.multiple_of(lax.rem(me + s, slots) * group, group)
+                even[pl.ds(owner, group), low:high] = whole[s * group : (s + 1) * group]
+            for i in range(half_slots):
+                rows = slice(full + i * group, full + (i + 1) * group)
+                lead[i][:, low:high] = bottom[rows]
+                trail[i][:, low:high] = top[rows]
 
 
 def join_kernel(half_slots, group, *refs):
     lead = refs[:half_slots]
     trail = refs[half_slots : 2 * half_slots]
-    from_above, from_below = refs[2 * half_slots : 2 * half_slots + 2]
+    inner, outer = refs[2 * half_slots : 2 * half_slots + 2]
     outs = refs[2 * half_slots + 2 :]
+    odd = lax.rem(lax.axis_index("blk"), 2) == 1
     for i in range(half_slots):
         above = (i + half_slots - 1) % half_slots
-        outs[i][...] = (
-            lead[i][...] + from_above[above * group : (above + 1) * group, :]
-        ).astype(BF16)
-        outs[half_slots + i][...] = (
-            trail[i][...] + from_below[i * group : (i + 1) * group, :]
-        ).astype(BF16)
+        rows = slice(above * group, (above + 1) * group)
+        from_above = jnp.where(odd, inner[rows, :], outer[rows, :])
+        outs[i][...] = (lead[i][...] + from_above).astype(BF16)
+        rows = slice(i * group, (i + 1) * group)
+        from_below = jnp.where(odd, outer[rows, :], inner[rows, :])
+        outs[half_slots + i][...] = (trail[i][...] + from_below).astype(BF16)
 
 
 def gather_pieces(refs, slots, me):
     half_slots = slots // 2
-    found = [ref[...] for ref in refs[: slots + half_slots]]
+    even, above, below, last = (
+        refs[0],
+        refs[1 : 1 + half_slots],
+        refs[1 + half_slots : 1 + slots],
+        refs[1 + slots :],
+    )
+    found = [even[...]] + [ref[...] for ref in above]
     for i in range(half_slots):
-        below = refs[slots + half_slots + i][...]
-        last = refs[2 * slots + i][...]
-        found.append(jnp.where(me == i, last, below))
+        found.append(jnp.where(me == i, last[i][...], below[i][...]))
     return found
 
 
@@ -345,51 +365,47 @@
     blocks = 2 * slots
     vmem = pl.BlockSpec(memory_space=pltpu.VMEM)
     smem = pl.BlockSpec(memory_space=pltpu.SMEM)
-    hbm = pl.BlockSpec(memory_space=pl.ANY)
+    hbm = pl.BlockSpec(memory_space=pltpu.HBM)
     shape = jax.ShapeDtypeStruct
 
-    def scratch(rows, halves):
-        return [
-            pltpu.VMEM((rows * var_count, HALF * var_count), BF16),
-            pltpu.VMEM((points // LANES, halves * HALF, var_count, LANES), BF16),
-            pltpu.SemaphoreType.DMA((points // LANES,)),
-        ]
-
     wide = half_slots * group
-    down = call(
-        functools.partial(down_kernel, slots, group, var_count, points),
-        shape((wide, features), F32),
+    groups = points // LANES
+    inner, outer, lhs, held = call(
+        functools.partial(halo_kernel, slots, group, var_count, points),
+        [
+            shape((wide, features), F32),
+            shape((wide, features), F32),
+            shape((2 * slots * group * var_count, HALF * var_count), BF16),
+            shape((groups, row_count, var_count, LANES), BF16),
+        ],
         [smem, hbm],
-        (freq_index, snapshots),
-        scratch(wide, 1),
-        2 * wide * HALF * features * var_count,
-        row_count * features,
-    )
-    below = [(i, i + 1) for i in range(slots - 1)]
-    from_above = lax.ppermute(down, "blk", [(b, a) for a, b in below])
+        (freq_index, pltpu.with_memory_space_constraint(snapshots, pltpu.HBM)),
+        [pltpu.SemaphoreType.DMA((groups,))],
+        2 * 2 * wide * HALF * features * var_count,
+        2 * row_count * features,
+    )
+
+    def swap(x, first):
+        pairs = [(i, i + 1) for i in range(first, slots - 1, 2)]
+        return lax.ppermute(x, "blk", pairs + [(b, a) for a, b in pairs])
+
+    swapped = (swap(inner, 1), swap(outer, 0))
     keep = [0] + list(range(half_slots + 1, slots))
     piece = shape((group, features), BF16)
     wide_piece = shape((group, features), F32)
-    up, *pieces = call(
+    pieces = call(
         functools.partial(block_kernel, slots, keep, var_count, points),
-        [shape((wide, features), F32)] + [piece] * slots + [wide_piece] * (2 * half_slots),
-        [smem, hbm, hbm],
-        (freq_index, snapshots, down),
-        scratch(2 * slots * group, 2),
-        2 * 4 * slots * group * HALF * features * var_count,
+        [shape((slots * group, features), BF16)] + [wide_piece] * (2 * half_slots),
+        [vmem, vmem],
+        (lhs, held),
+        [],
+        2 * 3 * slots * group * HALF * features * var_count,
         2 * row_count * features,
     )
-    from_below = lax.ppermute(up, "blk", below)
-    even = pieces[:slots]
-
-    def shift(x, s, pairs=None):
-        pairs = [(i, (i + s) % slots) for i in range(slots)]
-        return lax.ppermute(x, "blk", pairs)
-
-    even = [even[0]] + [shift(even[s], s) for s in range(1, slots)]
+    even = lax.all_to_all(pieces[0], "blk", split_axis=0, concat_axis=0, tiled=True)
     last = [
         lax.ppermute(
-            up[i * group : (i + 1) * group].astype(BF16), "blk", [(slots - 1, i)]
+            inner[i * group : (i + 1) * group].astype(BF16), "blk", [(slots - 1, i)]
         )
         for i in range(half_slots)
     ]
@@ -397,18 +413,19 @@
         functools.partial(join_kernel, half_slots, group),
         [piece] * slots,
         [vmem] * (slots + 2),
-        (*pieces[slots:], from_above, from_below),
+        (*pieces[1:], *swapped),
         [],
         slots * group * features,
         10 * slots * group * features,
     )
-    above = [odd[0]] + [shift(odd[i], s) for i, s in enumerate(keep) if i]
-    under = [odd[half_slots]]
-    for i in range(1, half_slots):
-        pairs = [(a, (a + i) % slots) for a in range(1, slots)]
-        under.append(lax.ppermute(odd[half_slots + i], "blk", pairs))
+
+    def shift(x, s, first):
+        return lax.ppermute(x, "blk", [(i, (i + s) % slots) for i in range(first, slots)])
+
+    above = [odd[0]] + [shift(odd[i], s, 0) for i, s in enumerate(keep) if i]
+    under = [odd[half_slots]] + [shift(odd[half_slots + i], i, 1) for i in range(1, half_slots)]
     width = 2 * blocks * blocks
-    spectra = (*even, *above, *under, *last)
+    spectra = (even, *above, *under, *last)
     packed = call(
         functools.partial(gram_kernel, slots, group, var_count, points),
         shape((freqs, width), F32),

time: 64.1 us -> 65.4 us (1.020)
  waiting for transfers between devices: 24.6 us -> 34.5 us
  starting transfers between devices: 23 us -> 18.2 us
  Pallas kernels: 14.8 us -> 11 us
    ppermute x9 -> x6, starting transfers between devices: 19.9 us -> 8.81 us  [the longest x2 4.15 us: shift(): lax.ppermute(x, 'blk', [(i, (i + s) % slots) for i in range(first, slots)])]
    ppermute x9 -> x6, waiting for transfers between devices: 19.2 us -> 29.1 us  [the longest x2 17.3 us: swap(): return lax.ppermute(x, 'blk', pairs + [(b, a) for a, b in pairs])]
    all_to_all x0 -> x1, starting transfers between devices: none -> 6.32 us  [on_device(): lax.all_to_all(pieces[0], 'blk', split_axis=0, concat_axis=0, tiled=True)]
    pallas_call x5, Pallas kernels: 14.8 us -> 11 us  [call(): pl.pallas_call(kernel, out_shape=outs, in_specs=ins, out_specs=jax.tree.m...]
  transfers between devices with their start and end apart: 12 -> 10, of which waited for: 7 -> 7; matrix products, arithmetic and copies ran while one was open for 0% -> 0% of each run, Pallas kernels for 13% -> 0%
where the time goes in v3:
time: 65.4 us; the launch traced here: 65.1 us
  waiting for transfers between devices  34.5 us (53%)
  starting transfers between devices  18.2 us (28%)
  Pallas kernels  11 us (17%)
  between operations  0.75 us (1%)
  local copies, waits for them, and re-layouts  0.68 us (1%)
    ppermute x2, waiting for transfers between devices, swap(): return lax.ppermute(x, 'blk', pairs + [(b, a) for a, b in pairs])  17.3 us
    pallas_call x5, Pallas kernels, call(): pl.pallas_call(kernel, out_shape=outs, in_specs=ins, out_specs=jax.tree.m...  11 us
    ppermute x2, waiting for transfers between devices, shift(): lax.ppermute(x, 'blk', [(i, (i + s) % slots) for i in range(first, slots)])  8.62 us
    all_to_all x1, starting transfers between devices, on_device(): lax.all_to_all(pieces[0], 'blk', split_axis=0, concat_axis=0, tiled=True)  6.32 us
    ppermute x3, waiting for transfers between devices, on_device(): other = lax.ppermute(packed, 'pts', [(i, i ^ step) for i in range(devices)])  5.36 us
    ppermute x2, starting transfers between devices, shift(): lax.ppermute(x, 'blk', [(i, (i + s) % slots) for i in range(first, slots)])  4.15 us
    ppermute x2, waiting for transfers between devices, on_device(): lax.ppermute(inner[i * group:(i + 1) * group].astype(BF16), 'blk', [(slot...  3.25 us
    ppermute x3, starting transfers between devices, on_device(): other = lax.ppermute(packed, 'pts', [(i, i ^ step) for i in range(devices)])  3.06 us
  transfers between devices with their start and end apart: 10, of which 7 were waited for; matrix products, arithmetic and copies ran while one was open for 0% of the time, Pallas kernels for 0%

profile of v3, /device:TPU:0, one launch (start us, length us, event | category | flops | bytes accessed | tf_op | source)
XLA Modules:
  0.0 65.1 jit_solution(12442162532546301274)
XLA Ops:
  0.6 0.0 copy-start.1
  0.6 0.6 copy-done.1
  1.3 4.1 %shard_map.67 = (f32[32,4096]{1,0:T(8,128)S(1)}, f32[32,4096]{1,0:T(8,128)S(1)}, bf16[512,1536]{1,0:T(8,128)(2,1)S(1)}, bf16[8,768,4,128]{3,2,1,0:T(4,128)(2,1)S(1)}) custom-call(s32[32]{0:T(128)S(1)} %copy-done.1, bf16[768,4,1024]{2,1,0:T(4,128)(2,1)} %x_hbm.1), custom_call_target="tpu_custom_call" | custom-call | flops 805306368 | bytes 6291456 | tf_op jit(solution)/shard_map/pallas_call | solution.py:346
  5.4 0.0 copy-start
  5.4 0.0 copy-start.2
  5.4 3.7 %shard_map.68 = (bf16[64,4096]{1,0:T(8,128)(2,1)}, f32[16,4096]{1,0:T(8,128)S(1)}, f32[16,4096]{1,0:T(8,128)S(1)}, f32[16,4096]{1,0:T(8,128)S(1)}, f32[16,4096]{1,0:T(8,128)S(1)}) custom-call(bf16[512,1536]{1,0:T(8,128)(2,1)S(1)} %get-tuple-element.19.lhs, bf16[8,768,4,128]{3,2,1,0:T(4,128)(2,1)S(1)} %get-tuple-element.20.held), custom_call_target="tpu_custom_call" | custom-call | flops 2415919104 | bytes 6291456 | tf_op jit(solution)/shard_map/pallas_call | solution.py:346
  9.1 6.3 %all-to-all-start = ((bf16[4,16,4096]{2,1,0:T(8,128)(2,1)}), bf16[4,16,4096]{2,1,0:T(8,128)(2,1)S(1)}, u32[]{:S(2)}, u32[]{:S(2)}) async-start(bf16[4,16,4096]{2,1,0:T(8,128)(2,1)} %bitcast.1), calls=%async_computation | async-start | bytes 1048576 | tf_op jit(solution)/shard_map/all_to_all | solution.py:405
  15.4 2.0 %collective-permute-start.1 = (f32[32,4096]{1,0:T(8,128)S(1)}, f32[32,4096]{1,0:T(8,128)S(1)}, u32[]{:S(2)}, u32[]{:S(2)}) collective-permute-start(f32[32,4096]{1,0:T(8,128)S(1)} %get-tuple-element.27), channel_id=1, source_target_pairs={{0,1},{2,3},{1,0},{3,2},{4,5},{6,7},{5,4},{7,6},{8,9},{10,11},{9,8... | collective-permute-start | bytes 1572872 | tf_op jit(solution)/shard_map/ppermute | solution.py:390
  17.4 0.7 %collective-permute-start = (f32[32,4096]{1,0:T(8,128)S(1)}, f32[32,4096]{1,0:T(8,128)S(1)}, u32[]{:S(2)}, u32[]{:S(2)}) collective-permute-start(f32[32,4096]{1,0:T(8,128)S(1)} %get-tuple-element.26), channel_id=1, source_target_pairs={{1,2},{2,1},{5,6},{6,5},{9,10},{10,9},{13,14},{14,13},{17,18},{18,... | collective-permute-start | bytes 1572872 | tf_op jit(solution)/shard_map/ppermute | solution.py:390
  18.2 0.7 %collective-permute-start.5 = (bf16[16,4096]{1,0:T(8,128)(2,1)S(1)}, bf16[16,4096]{1,0:T(8,128)(2,1)S(1)}, u32[]{:S(2)}, u32[]{:S(2)}) collective-permute-start(bf16[16,4096]{1,0:T(8,128)(2,1)S(1)} %get-tuple-element.35), channel_id=1, source_target_pairs={{3,1},{7,5},{11,9},{15,13},{19,17},{23,21},{27,25},{31,29}} | collective-permute-start | bytes 393224 | tf_op jit(solution)/shard_map/ppermute | solution.py:407
  18.9 1.3 %collective-permute-start.4 = (bf16[16,4096]{1,0:T(8,128)(2,1)S(1)}, bf16[16,4096]{1,0:T(8,128)(2,1)S(1)}, u32[]{:S(2)}, u32[]{:S(2)}) collective-permute-start(bf16[16,4096]{1,0:T(8,128)(2,1)S(1)} %get-tuple-element.36), channel_id=1, source_target_pairs={{3,0},{7,4},{11,8},{15,12},{19,16},{23,20},{27,24},{31,28}} | collective-permute-start | bytes 393224 | tf_op jit(solution)/shard_map/ppermute | solution.py:407
  20.2 17.3 %collective-permute-done.1.refs_5_ = f32[32,4096]{1,0:T(8,128)S(1)} collective-permute-done((f32[32,4096]{1,0:T(8,128)S(1)}, f32[32,4096]{1,0:T(8,128)S(1)}, u32[]{:S(2)}, u32[]{:S(2)}) %collective-permute-start.1) | collective-permute-done | bytes 524320 | tf_op jit(solution)/shard_map/ppermute | solution.py:390
  37.4 0.0 collective-permute-done.refs_4_
  37.4 0.1 shard_map.69
  37.6 2.9 %collective-permute-start.2 = (bf16[16,4096]{1,0:T(8,128)(2,1)S(1)}, bf16[16,4096]{1,0:T(8,128)(2,1)S(1)}, u32[]{:S(2)}, u32[]{:S(2)}) collective-permute-start(bf16[16,4096]{1,0:T(8,128)(2,1)S(1)} %get-tuple-element.29), channel_id=1, source_target_pairs={{0,3},{1,0},{2,1},{3,2},{4,7},{5,4},{6,5},{7,6},{8,11},{9,8},{10,9... | collective-permute-start | bytes 393224 | tf_op jit(solution)/shard_map/ppermute | solution.py:423
  40.4 1.3 %collective-permute-start.3 = (bf16[16,4096]{1,0:T(8,128)(2,1)S(1)}, bf16[16,4096]{1,0:T(8,128)(2,1)S(1)}, u32[]{:S(2)}, u32[]{:S(2)}) collective-permute-start(bf16[16,4096]{1,0:T(8,128)(2,1)S(1)} %get-tuple-element.31), channel_id=1, source_target_pairs={{1,2},{2,3},{3,0},{5,6},{6,7},{7,4},{9,10},{10,11},{11,8},{13,14},... | collective-permute-start | bytes 393224 | tf_op jit(solution)/shard_map/ppermute | solution.py:423
  41.7 0.0 collective-permute-done.5.refs_6_
  41.7 3.3 %collective-permute-done.4.refs_5_ = bf16[16,4096]{1,0:T(8,128)(2,1)S(1)} collective-permute-done((bf16[16,4096]{1,0:T(8,128)(2,1)S(1)}, bf16[16,4096]{1,0:T(8,128)(2,1)S(1)}, u32[]{:S(2)}, u32[]{:S(2)}) %collective-permute-start.4) | collective-permute-done | bytes 131104 | tf_op jit(solution)/shard_map/ppermute | solution.py:407
  45.0 6.7 %collective-permute-done.2.refs_2_ = bf16[16,4096]{1,0:T(8,128)(2,1)S(1)} collective-permute-done((bf16[16,4096]{1,0:T(8,128)(2,1)S(1)}, bf16[16,4096]{1,0:T(8,128)(2,1)S(1)}, u32[]{:S(2)}, u32[]{:S(2)}) %collective-permute-start.2) | collective-permute-done | bytes 131104 | tf_op jit(solution)/shard_map/ppermute | solution.py:423
  51.7 1.9 %collective-permute-done.3.refs_4_ = bf16[16,4096]{1,0:T(8,128)(2,1)S(1)} collective-permute-done((bf16[16,4096]{1,0:T(8,128)(2,1)S(1)}, bf16[16,4096]{1,0:T(8,128)(2,1)S(1)}, u32[]{:S(2)}, u32[]{:S(2)}) %collective-permute-start.3) | collective-permute-done | bytes 131104 | tf_op jit(solution)/shard_map/ppermute | solution.py:423
  53.6 0.0 all-to-all-done
  53.6 0.0 copy-done
  53.6 0.0 copy-done.2
  53.6 1.3 %shard_map.70 = f32[8,128]{1,0:T(8,128)S(1)} custom-call(f32[8]{0:T(128)S(1)} %copy-done.2, s32[1,1024]{1,0:T(1,128)S(1)} %bitcast.6, bf16[64,4096]{1,0:T(8,128)(2,1)S(1)} %bitcast.4, bf16[16,4096]{1,0:T(8,128)(2,1)S(1)} %get-tuple-element.28.refs_1_, bf16[16,4096]{1,0:T(8,128)(2,1)S(1)} %collective-permute-done.2.refs_2_, ...), custom_call_target="tpu_custom_call" | custom-call | flops 134217728 | bytes 2097152 | tf_op jit(solution)/shard_map/pallas_call | solution.py:346
  54.9 0.0 collective-permute-start.6
  54.9 1.2 %collective-permute-done.6 = f32[8,128]{1,0:T(8,128)S(1)} collective-permute-done((f32[8,128]{1,0:T(8,128)S(1)}, f32[8,128]{1,0:T(8,128)S(1)}, u32[]{:S(2)}, u32[]{:S(2)}) %collective-permute-start.6) | collective-permute-done | bytes 4128 | tf_op jit(solution)/shard_map/ppermute | solution.py:444
  56.1 1.5 %collective-permute-start.7 = (f32[8,128]{1,0:T(8,128)S(1)}, f32[8,128]{1,0:T(8,128)S(1)}, u32[]{:S(2)}, u32[]{:S(2)}) collective-permute-start(f32[8,128]{1,0:T(8,128)S(1)} %add.6), channel_id=1, source_target_pairs={{0,8},{4,12},{8,0},{12,4},{16,24},{20,28},{24,16},{28,20},{1,9},{5... | collective-permute-start | bytes 12296 | tf_op jit(solution)/shard_map/ppermute | solution.py:444
  57.6 2.1 %collective-permute-done.7 = f32[8,128]{1,0:T(8,128)S(1)} collective-permute-done((f32[8,128]{1,0:T(8,128)S(1)}, f32[8,128]{1,0:T(8,128)S(1)}, u32[]{:S(2)}, u32[]{:S(2)}) %collective-permute-start.7) | collective-permute-done | bytes 4128 | tf_op jit(solution)/shard_map/ppermute | solution.py:444
  59.7 1.5 %collective-permute-start.8 = (f32[8,128]{1,0:T(8,128)S(1)}, f32[8,128]{1,0:T(8,128)S(1)}, u32[]{:S(2)}, u32[]{:S(2)}) collective-permute-start(f32[8,128]{1,0:T(8,128)S(1)} %add.7.a_ref), channel_id=1, source_target_pairs={{0,16},{4,20},{8,24},{12,28},{16,0},{20,4},{24,8},{28,12},{1,17},{... | collective-permute-start | bytes 12296 | tf_op jit(solution)/shard_map/ppermute | solution.py:444
  61.2 2.1 %collective-permute-done.8.b_ref = f32[8,128]{1,0:T(8,128)S(1)} collective-permute-done((f32[8,128]{1,0:T(8,128)S(1)}, f32[8,128]{1,0:T(8,128)S(1)}, u32[]{:S(2)}, u32[]{:S(2)}) %collective-permute-start.8) | collective-permute-done | bytes 4128 | tf_op jit(solution)/shard_map/ppermute | solution.py:444
  63.3 1.8 %shard_map.71 = (f32[8,2,8,8]{3,2,1,0:T(8,128)}, f32[1,8]{1,0:T(1,128)}, f32[8,2,4,1024]{3,2,1,0:T(4,128)}) custom-call(f32[8,128]{1,0:T(8,128)S(1)} %add.7.a_ref, f32[8,128]{1,0:T(8,128)S(1)} %collective-permute-done.8.b_ref, bf16[64,4096]{1,0:T(8,128)(2,1)S(1)} %bitcast.5, bf16[16,4096]{1,0:T(8,128)(2,1)S(1)} %get-tuple-element.28.refs_1_, ...), custom_call_target="tpu_custom_call" | custom-call | flops 33554432 | bytes 1048576 | tf_op jit(solution)/shard_map/pallas_call | solution.py:346
  (4 shorter events, 0.1 us)
Async XLA Ops:
  0.6 0.7 %copy-start.1 = (s32[32]{0:T(128)S(1)}, s32[32]{0:T(128)}, u32[]{:S(2)}) copy-start(s32[32]{0:T(128)} %freqs.1) | copy-start | bytes 388
  5.4 48.2 %copy-start = (s32[1024]{0:T(1024)S(1)}, s32[1024]{0:T(1024)}, u32[]{:S(2)}) copy-start(s32[1024]{0:T(1024)} %param.6) | copy-start | bytes 12292
  5.4 48.2 %copy-start.2 = (f32[8]{0:T(128)S(1)}, f32[8]{0:T(128)}, u32[]{:S(2)}) copy-start(f32[8]{0:T(128)} %weights.1) | copy-start | bytes 100
  9.1 44.5 %all-to-all-start = ((bf16[4,16,4096]{2,1,0:T(8,128)(2,1)}), bf16[4,16,4096]{2,1,0:T(8,128)(2,1)S(1)}, u32[]{:S(2)}, u32[]{:S(2)}) async-start(bf16[4,16,4096]{2,1,0:T(8,128)(2,1)} %bitcast.1), calls=%async_computation | async-start | bytes 1048576 | tf_op jit(solution)/shard_map/all_to_all | solution.py:405
  15.4 22.0 %collective-permute-start.1 = (f32[32,4096]{1,0:T(8,128)S(1)}, f32[32,4096]{1,0:T(8,128)S(1)}, u32[]{:S(2)}, u32[]{:S(2)}) collective-permute-start(f32[32,4096]{1,0:T(8,128)S(1)} %get-tuple-element.27), channel_id=1, source_target_pairs={{0,1},{2,3},{1,0},{3,2},{4,5},{6,7},{5,4},{7,6},{8,9},{10,11},{9,8... | collective-permute-start | bytes 1572872 | tf_op jit(solution)/shard_map/ppermute | solution.py:390
  17.4 20.0 %collective-permute-start = (f32[32,4096]{1,0:T(8,128)S(1)}, f32[32,4096]{1,0:T(8,128)S(1)}, u32[]{:S(2)}, u32[]{:S(2)}) collective-permute-start(f32[32,4096]{1,0:T(8,128)S(1)} %get-tuple-element.26), channel_id=1, source_target_pairs={{1,2},{2,1},{5,6},{6,5},{9,10},{10,9},{13,14},{14,13},{17,18},{18,... | collective-permute-start | bytes 1572872 | tf_op jit(solution)/shard_map/ppermute | solution.py:390
  18.2 23.5 %collective-permute-start.5 = (bf16[16,4096]{1,0:T(8,128)(2,1)S(1)}, bf16[16,4096]{1,0:T(8,128)(2,1)S(1)}, u32[]{:S(2)}, u32[]{:S(2)}) collective-permute-start(bf16[16,4096]{1,0:T(8,128)(2,1)S(1)} %get-tuple-element.35), channel_id=1, source_target_pairs={{3,1},{7,5},{11,9},{15,13},{19,17},{23,21},{27,25},{31,29}} | collective-permute-start | bytes 393224 | tf_op jit(solution)/shard_map/ppermute | solution.py:407
  18.9 26.1 %collective-permute-start.4 = (bf16[16,4096]{1,0:T(8,128)(2,1)S(1)}, bf16[16,4096]{1,0:T(8,128)(2,1)S(1)}, u32[]{:S(2)}, u32[]{:S(2)}) collective-permute-start(bf16[16,4096]{1,0:T(8,128)(2,1)S(1)} %get-tuple-element.36), channel_id=1, source_target_pairs={{3,0},{7,4},{11,8},{15,12},{19,16},{23,20},{27,24},{31,28}} | collective-permute-start | bytes 393224 | tf_op jit(solution)/shard_map/ppermute | solution.py:407
  37.6 14.2 %collective-permute-start.2 = (bf16[16,4096]{1,0:T(8,128)(2,1)S(1)}, bf16[16,4096]{1,0:T(8,128)(2,1)S(1)}, u32[]{:S(2)}, u32[]{:S(2)}) collective-permute-start(bf16[16,4096]{1,0:T(8,128)(2,1)S(1)} %get-tuple-element.29), channel_id=1, source_target_pairs={{0,3},{1,0},{2,1},{3,2},{4,7},{5,4},{6,5},{7,6},{8,11},{9,8},{10,9... | collective-permute-start | bytes 393224 | tf_op jit(solution)/shard_map/ppermute | solution.py:423
  40.4 13.2 %collective-permute-start.3 = (bf16[16,4096]{1,0:T(8,128)(2,1)S(1)}, bf16[16,4096]{1,0:T(8,128)(2,1)S(1)}, u32[]{:S(2)}, u32[]{:S(2)}) collective-permute-start(bf16[16,4096]{1,0:T(8,128)(2,1)S(1)} %get-tuple-element.31), channel_id=1, source_target_pairs={{1,2},{2,3},{3,0},{5,6},{6,7},{7,4},{9,10},{10,11},{11,8},{13,14},... | collective-permute-start | bytes 393224 | tf_op jit(solution)/shard_map/ppermute | solution.py:423
  54.9 1.2 %collective-permute-start.6 = (f32[8,128]{1,0:T(8,128)S(1)}, f32[8,128]{1,0:T(8,128)S(1)}, u32[]{:S(2)}, u32[]{:S(2)}) collective-permute-start(f32[8,128]{1,0:T(8,128)S(1)} %shard_map.70), channel_id=1, source_target_pairs={{0,4},{4,0},{8,12},{12,8},{16,20},{20,16},{24,28},{28,24},{1,5},{5... | collective-permute-start | bytes 12296 | tf_op jit(solution)/shard_map/ppermute | solution.py:444
  56.1 3.6 %collective-permute-start.7 = (f32[8,128]{1,0:T(8,128)S(1)}, f32[8,128]{1,0:T(8,128)S(1)}, u32[]{:S(2)}, u32[]{:S(2)}) collective-permute-start(f32[8,128]{1,0:T(8,128)S(1)} %add.6), channel_id=1, source_target_pairs={{0,8},{4,12},{8,0},{12,4},{16,24},{20,28},{24,16},{28,20},{1,9},{5... | collective-permute-start | bytes 12296 | tf_op jit(solution)/shard_map/ppermute | solution.py:444
  59.7 3.6 %collective-permute-start.8 = (f32[8,128]{1,0:T(8,128)S(1)}, f32[8,128]{1,0:T(8,128)S(1)}, u32[]{:S(2)}, u32[]{:S(2)}) collective-permute-start(f32[8,128]{1,0:T(8,128)S(1)} %add.7.a_ref), channel_id=1, source_target_pairs={{0,16},{4,20},{8,24},{12,28},{16,0},{20,4},{24,8},{28,12},{1,17},{... | collective-permute-start | bytes 12296 | tf_op jit(solution)/shard_map/ppermute | solution.py:444

commit v4 on v3

--- a/solution.py
+++ b/solution.py
@@ -45,7 +45,7 @@
     half_slots = slots // 2
     above = slot - slots
     below = above - half_slots
-    even = 2 * slot
+    even = 2 * modulo(me - slot, slots)
     upper = 2 * modulo(me - jnp.where(above == 0, 0, above + half_slots), slots) + 1
     lower = modulo(2 * modulo(me - below, slots) - 1, 2 * slots)
     return jnp.where(slot < slots, even, jnp.where(below < 0, upper, lower))
@@ -138,13 +138,12 @@
 
 def block_kernel(slots, keep, var_count, points, lhs, held, *outs):
     half_slots = slots // 2
-    even = outs[0]
-    lead = outs[1 : 1 + half_slots]
-    trail = outs[1 + half_slots :]
-    full = even.shape[0]
-    group = full // slots
+    even = outs[:slots]
+    lead = outs[slots : slots + half_slots]
+    trail = outs[slots + half_slots :]
+    group = even[0].shape[0]
+    full = slots * group
     short = full + half_slots * group
-    me = lax.axis_index("blk")
 
     def some(v, low, high):
         return lhs[2 * v * full + low : 2 * v * full + high, :]
@@ -164,8 +163,7 @@
             bottom = second[v * short : (v + 1) * short]
             whole = (top[:full] + bottom[:full]).astype(BF16)
             for s in range(slots):
-                owner = pl.multiple_of(lax.rem(me + s, slots) * group, group)
-                even[pl.ds(owner, group), low:high] = whole[s * group : (s + 1) * group]
+                even[s][:, low:high] = whole[s * group : (s + 1) * group]
             for i in range(half_slots):
                 rows = slice(full + i * group, full + (i + 1) * group)
                 lead[i][:, low:high] = bottom[rows]
@@ -176,8 +174,10 @@
     lead = refs[:half_slots]
     trail = refs[half_slots : 2 * half_slots]
     inner, outer = refs[2 * half_slots : 2 * half_slots + 2]
-    outs = refs[2 * half_slots + 2 :]
-    odd = lax.rem(lax.axis_index("blk"), 2) == 1
+    last = refs[2 * half_slots + 2 : 3 * half_slots + 2]
+    outs = refs[3 * half_slots + 2 :]
+    me = lax.axis_index("blk")
+    odd = lax.rem(me, 2) == 1
     for i in range(half_slots):
         above = (i + half_slots - 1) % half_slots
         rows = slice(above * group, (above + 1) * group)
@@ -185,20 +185,21 @@
         outs[i][...] = (lead[i][...] + from_above).astype(BF16)
         rows = slice(i * group, (i + 1) * group)
         from_below = jnp.where(odd, outer[rows, :], inner[rows, :])
-        outs[half_slots + i][...] = (trail[i][...] + from_below).astype(BF16)
+        joined = (trail[i][...] + from_below).astype(BF16)
+        if i == 0:
+            outs[half_slots][...] = jnp.where(me == 0, last[0][...], joined)
+        else:
+            outs[half_slots + i][...] = joined
+            outs[2 * half_slots + i - 1][...] = last[i][...]
 
 
 def gather_pieces(refs, slots, me):
     half_slots = slots // 2
-    even, above, below, last = (
-        refs[0],
-        refs[1 : 1 + half_slots],
-        refs[1 + half_slots : 1 + slots],
-        refs[1 + slots :],
-    )
-    found = [even[...]] + [ref[...] for ref in above]
-    for i in range(half_slots):
-        found.append(jnp.where(me == i, last[i][...], below[i][...]))
+    found = [ref[...] for ref in refs[: slots + half_slots + 1]]
+    for i in range(1, half_slots):
+        below = refs[slots + half_slots + i][...]
+        last = refs[2 * slots + i - 1][...]
+        found.append(jnp.where(me == i, last, below))
     return found
 
 
@@ -389,20 +390,25 @@
         pairs = [(i, i + 1) for i in range(first, slots - 1, 2)]
         return lax.ppermute(x, "blk", pairs + [(b, a) for a, b in pairs])
 
-    swapped = (swap(inner, 1), swap(outer, 0))
+    from_outer = swap(outer, 0)
+    swapped = (swap(inner, 1), from_outer)
     keep = [0] + list(range(half_slots + 1, slots))
     piece = shape((group, features), BF16)
     wide_piece = shape((group, features), F32)
     pieces = call(
         functools.partial(block_kernel, slots, keep, var_count, points),
-        [shape((slots * group, features), BF16)] + [wide_piece] * (2 * half_slots),
+        [piece] * slots + [wide_piece] * (2 * half_slots),
         [vmem, vmem],
         (lhs, held),
         [],
         2 * 3 * slots * group * HALF * features * var_count,
         2 * row_count * features,
     )
-    even = lax.all_to_all(pieces[0], "blk", split_axis=0, concat_axis=0, tiled=True)
+
+    def shift(x, s, first):
+        return lax.ppermute(x, "blk", [(i, (i + s) % slots) for i in range(first, slots)])
+
+    even = [pieces[0]] + [shift(pieces[s], s, 0) for s in range(1, slots)]
     last = [
         lax.ppermute(
             inner[i * group : (i + 1) * group].astype(BF16), "blk", [(slots - 1, i)]
@@ -411,21 +417,18 @@
     ]
     odd = call(
         functools.partial(join_kernel, half_slots, group),
-        [piece] * slots,
-        [vmem] * (slots + 2),
-        (*pieces[1:], *swapped),
+        [piece] * (slots + half_slots - 1),
+        [vmem] * (slots + 2 + half_slots),
+        (*pieces[slots:], *swapped, *last),
         [],
         slots * group * features,
         10 * slots * group * features,
     )
 
-    def shift(x, s, first):
-        return lax.ppermute(x, "blk", [(i, (i + s) % slots) for i in range(first, slots)])
-
     above = [odd[0]] + [shift(odd[i], s, 0) for i, s in enumerate(keep) if i]
     under = [odd[half_slots]] + [shift(odd[half_slots + i], i, 1) for i in range(1, half_slots)]
     width = 2 * blocks * blocks
-    spectra = (even, *above, *under, *last)
+    spectra = (*even, *above, *under, *odd[slots:])
     packed = call(
         functools.partial(gram_kernel, slots, group, var_count, points),
         shape((freqs, width), F32),

time: 65.4 us -> 56.5 us (0.86); the launches traced: 65.1 us -> 55.5 us
  waiting for transfers between devices: 34.5 us -> 24.9 us
  Pallas kernels: 11 us -> 10.2 us
  starting transfers between devices: 18.2 us -> 19 us
    ppermute x2, waiting for transfers between devices: 17.3 us -> 0.01 us  [swap(): return lax.ppermute(x, 'blk', pairs + [(b, a) for a, b in pairs])]
    all_to_all x1 -> x0, starting transfers between devices: 6.32 us -> none  [on_device(): lax.all_to_all(pieces[0], 'blk', split_axis=0, concat_axis=0, tiled=True)]
    ppermute x2 -> x5, starting transfers between devices: 4.15 us -> 10.1 us  [shift(): lax.ppermute(x, 'blk', [(i, (i + s) % slots) for i in range(first, slots)])]
    ppermute x2 -> x5, waiting for transfers between devices: 8.62 us -> 12.9 us  [shift(): lax.ppermute(x, 'blk', [(i, (i + s) % slots) for i in range(first, slots)])]
    ppermute x2, waiting for transfers between devices: 3.25 us -> 6.61 us  [on_device(): lax.ppermute(inner[i * group:(i + 1) * group].astype(BF16), 'blk', [(slot...]
    ppermute x2, starting transfers between devices: 2.71 us -> 3.9 us  [swap(): return lax.ppermute(x, 'blk', pairs + [(b, a) for a, b in pairs])]
    pallas_call x5, Pallas kernels: 11 us -> 10.2 us  [call(): pl.pallas_call(kernel, out_shape=outs, in_specs=ins, out_specs=jax.tree.m...]
  transfers between devices with their start and end apart: 10 -> 12, of which waited for: 7 -> 7; matrix products, arithmetic and copies ran while one was open for 0% -> 0% of each run, Pallas kernels for 0% -> 5%
where the time goes in v4:
time: 56.5 us; the launch traced here: 55.5 us
  waiting for transfers between devices  24.9 us (44%)
  starting transfers between devices  19 us (34%)
  Pallas kernels  10.2 us (18%)
  between operations  0.73 us (1%)
  local copies, waits for them, and re-layouts  0.68 us (1%)
    ppermute x5, waiting for transfers between devices, shift(): lax.ppermute(x, 'blk', [(i, (i + s) % slots) for i in range(first, slots)])  12.9 us
    pallas_call x5, Pallas kernels, call(): pl.pallas_call(kernel, out_shape=outs, in_specs=ins, out_specs=jax.tree.m...  10.2 us
    ppermute x5, starting transfers between devices, shift(): lax.ppermute(x, 'blk', [(i, (i + s) % slots) for i in range(first, slots)])  10.1 us
    ppermute x2, waiting for transfers between devices, on_device(): lax.ppermute(inner[i * group:(i + 1) * group].astype(BF16), 'blk', [(slot...  6.61 us
    ppermute x3, waiting for transfers between devices, on_device(): other = lax.ppermute(packed, 'pts', [(i, i ^ step) for i in range(devices)])  5.35 us
    ppermute x2, starting transfers between devices, swap(): return lax.ppermute(x, 'blk', pairs + [(b, a) for a, b in pairs])  3.9 us
    ppermute x3, starting transfers between devices, on_device(): other = lax.ppermute(packed, 'pts', [(i, i ^ step) for i in range(devices)])  3.07 us
    ppermute x2, starting transfers between devices, on_device(): lax.ppermute(inner[i * group:(i + 1) * group].astype(BF16), 'blk', [(slot...  1.96 us
  transfers between devices with their start and end apart: 12, of which 7 were waited for; matrix products, arithmetic and copies ran while one was open for 0% of the time, Pallas kernels for 5%

profile of v4, /device:TPU:0, one launch (start us, length us, event | category | flops | bytes accessed | tf_op | source)
XLA Modules:
  0.0 55.5 jit_solution(9131693998145215160)
XLA Ops:
  0.6 0.0 copy-start.1
  0.6 0.6 %copy-done.1 = s32[32]{0:T(128)S(1)} copy-done((s32[32]{0:T(128)S(1)}, s32[32]{0:T(128)}, u32[]{:S(2)}) %copy-start.1) | copy-done | bytes 152
  1.3 4.1 %shard_map.67 = (f32[32,4096]{1,0:T(8,128)S(1)}, f32[32,4096]{1,0:T(8,128)S(1)}, bf16[512,1536]{1,0:T(8,128)(2,1)S(1)}, bf16[8,768,4,128]{3,2,1,0:T(4,128)(2,1)S(1)}) custom-call(s32[32]{0:T(128)S(1)} %copy-done.1, bf16[768,4,1024]{2,1,0:T(4,128)(2,1)} %x_hbm.1), custom_call_target="tpu_custom_call" | custom-call | flops 805306368 | bytes 6291456 | tf_op jit(solution)/shard_map/pallas_call | solution.py:347
  5.4 3.1 %collective-permute-start.4 = (f32[32,4096]{1,0:T(8,128)S(1)}, f32[32,4096]{1,0:T(8,128)S(1)}, u32[]{:S(2)}, u32[]{:S(2)}) collective-permute-start(f32[32,4096]{1,0:T(8,128)S(1)} %get-tuple-element.34), channel_id=1, source_target_pairs={{0,1},{2,3},{1,0},{3,2},{4,5},{6,7},{5,4},{7,6},{8,9},{10,11},{9,8... | collective-permute-start | bytes 1572872 | tf_op jit(solution)/shard_map/ppermute | solution.py:391
  8.5 0.8 %collective-permute-start.3 = (f32[32,4096]{1,0:T(8,128)S(1)}, f32[32,4096]{1,0:T(8,128)S(1)}, u32[]{:S(2)}, u32[]{:S(2)}) collective-permute-start(f32[32,4096]{1,0:T(8,128)S(1)} %get-tuple-element.33), channel_id=1, source_target_pairs={{1,2},{2,1},{5,6},{6,5},{9,10},{10,9},{13,14},{14,13},{17,18},{18,... | collective-permute-start | bytes 1572872 | tf_op jit(solution)/shard_map/ppermute | solution.py:391
  9.4 0.7 %collective-permute-start.6 = (bf16[16,4096]{1,0:T(8,128)(2,1)S(1)}, bf16[16,4096]{1,0:T(8,128)(2,1)S(1)}, u32[]{:S(2)}, u32[]{:S(2)}) collective-permute-start(bf16[16,4096]{1,0:T(8,128)(2,1)S(1)} %get-tuple-element.43), channel_id=1, source_target_pairs={{3,1},{7,5},{11,9},{15,13},{19,17},{23,21},{27,25},{31,29}} | collective-permute-start | bytes 393224 | tf_op jit(solution)/shard_map/ppermute | solution.py:413
  10.0 1.3 %collective-permute-start.5 = (bf16[16,4096]{1,0:T(8,128)(2,1)S(1)}, bf16[16,4096]{1,0:T(8,128)(2,1)S(1)}, u32[]{:S(2)}, u32[]{:S(2)}) collective-permute-start(bf16[16,4096]{1,0:T(8,128)(2,1)S(1)} %get-tuple-element.44), channel_id=1, source_target_pairs={{3,0},{7,4},{11,8},{15,12},{19,16},{23,20},{27,24},{31,28}} | collective-permute-start | bytes 393224 | tf_op jit(solution)/shard_map/ppermute | solution.py:413
  11.3 2.9 %shard_map.68 = (bf16[16,4096]{1,0:T(8,128)(2,1)S(1)}, bf16[16,4096]{1,0:T(8,128)(2,1)S(1)}, bf16[16,4096]{1,0:T(8,128)(2,1)S(1)}, bf16[16,4096]{1,0:T(8,128)(2,...) custom-call(bf16[512,1536]{1,0:T(8,128)(2,1)S(1)} %get-tuple-element., ...), custom_call_target="tpu_custom_call" | custom-call | flops 2415919104 | bytes 6291456 | tf_op jit(solution)/shard_map/pallas_call | solution.py:347
  14.2 4.4 %collective-permute-start = (bf16[16,4096]{1,0:T(8,128)(2,1)S(1)}, bf16[16,4096]{1,0:T(8,128)(2,1)S(1)}, u32[]{:S(2)}, u32[]{:S(2)}) collective-permute-start(bf16[16,4096]{1,0:T(8,128)(2,1)S(1)} %get-tuple-element.26), channel_id=1, source_target_pairs={{0,1},{1,2},{2,3},{3,0},{4,5},{5,6},{6,7},{7,4},{8,9},{9,10},{10,1... | collective-permute-start | bytes 393224 | tf_op jit(solution)/shard_map/ppermute | solution.py:409
  18.7 0.0 collective-permute-done.6.refs_7_
  18.7 4.2 %collective-permute-start.1 = (bf16[16,4096]{1,0:T(8,128)(2,1)S(1)}, bf16[16,4096]{1,0:T(8,128)(2,1)S(1)}, u32[]{:S(2)}, u32[]{:S(2)}) collective-permute-start(bf16[16,4096]{1,0:T(8,128)(2,1)S(1)} %get-tuple-element.27), channel_id=1, source_target_pairs={{0,2},{1,3},{2,0},{3,1},{4,6},{5,7},{6,4},{7,5},{8,10},{9,11},{10,... | collective-permute-start | bytes 393224 | tf_op jit(solution)/shard_map/ppermute | solution.py:409
  22.8 6.6 %collective-permute-done.5.refs_6_ = bf16[16,4096]{1,0:T(8,128)(2,1)S(1)} collective-permute-done((bf16[16,4096]{1,0:T(8,128)(2,1)S(1)}, bf16[16,4096]{1,0:T(8,128)(2,1)S(1)}, u32[]{:S(2)}, u32[]{:S(2)}) %collective-permute-start.5) | collective-permute-done | bytes 131104 | tf_op jit(solution)/shard_map/ppermute | solution.py:413
  29.5 0.1 collective-permute-start.2
  29.6 0.0 collective-permute-done.4.refs_5_
  29.6 0.0 collective-permute-done.3.refs_4_
  29.6 0.2 shard_map.69
  29.7 0.1 collective-permute-start.7
  29.8 1.3 %collective-permute-start.8 = (bf16[16,4096]{1,0:T(8,128)(2,1)S(1)}, bf16[16,4096]{1,0:T(8,128)(2,1)S(1)}, u32[]{:S(2)}, u32[]{:S(2)}) collective-permute-start(bf16[16,4096]{1,0:T(8,128)(2,1)S(1)} %get-tuple-element.38), channel_id=1, source_target_pairs={{1,2},{2,3},{3,0},{5,6},{6,7},{7,4},{9,10},{10,11},{11,8},{13,14},... | collective-permute-start | bytes 393224 | tf_op jit(solution)/shard_map/ppermute | solution.py:409
  31.1 1.2 %collective-permute-done.refs_1_ = bf16[16,4096]{1,0:T(8,128)(2,1)S(1)} collective-permute-done((bf16[16,4096]{1,0:T(8,128)(2,1)S(1)}, bf16[16,4096]{1,0:T(8,128)(2,1)S(1)}, u32[]{:S(2)}, u32[]{:S(2)}) %collective-permute-start) | collective-permute-done | bytes 131104 | tf_op jit(solution)/shard_map/ppermute | solution.py:409
  32.3 9.1 %collective-permute-done.1.refs_2_ = bf16[16,4096]{1,0:T(8,128)(2,1)S(1)} collective-permute-done((bf16[16,4096]{1,0:T(8,128)(2,1)S(1)}, bf16[16,4096]{1,0:T(8,128)(2,1)S(1)}, u32[]{:S(2)}, u32[]{:S(2)}) %collective-permute-start.1) | collective-permute-done | bytes 131104 | tf_op jit(solution)/shard_map/ppermute | solution.py:409
  41.3 0.0 collective-permute-done.2.refs_3_
  41.3 2.7 %collective-permute-done.7.refs_5_ = bf16[16,4096]{1,0:T(8,128)(2,1)S(1)} collective-permute-done((bf16[16,4096]{1,0:T(8,128)(2,1)S(1)}, bf16[16,4096]{1,0:T(8,128)(2,1)S(1)}, u32[]{:S(2)}, u32[]{:S(2)}) %collective-permute-start.7) | collective-permute-done | bytes 131104 | tf_op jit(solution)/shard_map/ppermute | solution.py:409
  44.0 0.0 collective-permute-done.8.refs_7_
  44.0 0.0 copy-done
  44.0 1.2 %shard_map.70 = f32[8,128]{1,0:T(8,128)S(1)} custom-call(f32[8]{0:T(128)S(1)} %copy-done.2, s32[1,1024]{1,0:T(1,128)S(1)} %bitcast.2, bf16[16,4096]{1,0:T(8,128)(2,1)S(1)} %get-tuple-element.25.refs_0_, bf16[16,4096]{1,0:T(8,128)(2,1)S(1)} %collective-permute-done.refs_1_, bf16[16,4096]{1,0:T(8,128)(2,1)S(1)} %collective-permute-done.1.refs_2_, ...), custom_call_target="tpu_custom_call" | custom-call | flops 134217728 | bytes 2097152 | tf_op jit(solution)/shard_map/pallas_call | solution.py:347
  45.3 0.0 collective-permute-start.9
  45.3 1.2 %collective-permute-done.9 = f32[8,128]{1,0:T(8,128)S(1)} collective-permute-done((f32[8,128]{1,0:T(8,128)S(1)}, f32[8,128]{1,0:T(8,128)S(1)}, u32[]{:S(2)}, u32[]{:S(2)}) %collective-permute-start.9) | collective-permute-done | bytes 4128 | tf_op jit(solution)/shard_map/ppermute | solution.py:447
  46.5 1.5 %collective-permute-start.10 = (f32[8,128]{1,0:T(8,128)S(1)}, f32[8,128]{1,0:T(8,128)S(1)}, u32[]{:S(2)}, u32[]{:S(2)}) collective-permute-start(f32[8,128]{1,0:T(8,128)S(1)} %add.6), channel_id=1, source_target_pairs={{0,8},{4,12},{8,0},{12,4},{16,24},{20,28},{24,16},{28,20},{1,9},{5... | collective-permute-start | bytes 12296 | tf_op jit(solution)/shard_map/ppermute | solution.py:447
  48.0 2.1 %collective-permute-done.10 = f32[8,128]{1,0:T(8,128)S(1)} collective-permute-done((f32[8,128]{1,0:T(8,128)S(1)}, f32[8,128]{1,0:T(8,128)S(1)}, u32[]{:S(2)}, u32[]{:S(2)}) %collective-permute-start.10) | collective-permute-done | bytes 4128 | tf_op jit(solution)/shard_map/ppermute | solution.py:447
  50.1 1.5 %collective-permute-start.11 = (f32[8,128]{1,0:T(8,128)S(1)}, f32[8,128]{1,0:T(8,128)S(1)}, u32[]{:S(2)}, u32[]{:S(2)}) collective-permute-start(f32[8,128]{1,0:T(8,128)S(1)} %add.7.a_ref), channel_id=1, source_target_pairs={{0,16},{4,20},{8,24},{12,28},{16,0},{20,4},{24,8},{28,12},{1,17},{... | collective-permute-start | bytes 12296 | tf_op jit(solution)/shard_map/ppermute | solution.py:447
  51.6 2.1 %collective-permute-done.11.b_ref = f32[8,128]{1,0:T(8,128)S(1)} collective-permute-done((f32[8,128]{1,0:T(8,128)S(1)}, f32[8,128]{1,0:T(8,128)S(1)}, u32[]{:S(2)}, u32[]{:S(2)}) %collective-permute-start.11) | collective-permute-done | bytes 4128 | tf_op jit(solution)/shard_map/ppermute | solution.py:447
  53.7 1.8 %shard_map.71 = (f32[8,2,8,8]{3,2,1,0:T(8,128)}, f32[1,8]{1,0:T(1,128)}, f32[8,2,4,1024]{3,2,1,0:T(4,128)}) custom-call(f32[8,128]{1,0:T(8,128)S(1)} %add.7.a_ref, f32[8,128]{1,0:T(8,128)S(1)} %collective-permute-done.11.b_ref, bf16[16,4096]{1,0:T(8,128)(2,1)S(1)} %get-tuple-element.25.refs_0_, bf16[16,4096]{1,0:T(8,128)(2,1)S(1)} %collective-permute-done.refs_1_, ...), custom_call_target="tpu_custom_call" | custom-call | flops 33554432 | bytes 1048576 | tf_op jit(solution)/shard_map/pallas_call | solution.py:347
  (7 shorter events, 0.1 us)
Async XLA Ops:
  0.6 0.7 %copy-start.1 = (s32[32]{0:T(128)S(1)}, s32[32]{0:T(128)}, u32[]{:S(2)}) copy-start(s32[32]{0:T(128)} %freqs.1) | copy-start | bytes 388
  5.4 24.2 %collective-permute-start.4 = (f32[32,4096]{1,0:T(8,128)S(1)}, f32[32,4096]{1,0:T(8,128)S(1)}, u32[]{:S(2)}, u32[]{:S(2)}) collective-permute-start(f32[32,4096]{1,0:T(8,128)S(1)} %get-tuple-element.34), channel_id=1, source_target_pairs={{0,1},{2,3},{1,0},{3,2},{4,5},{6,7},{5,4},{7,6},{8,9},{10,11},{9,8... | collective-permute-start | bytes 1572872 | tf_op jit(solution)/shard_map/ppermute | solution.py:391
  8.5 35.5 %copy-start = (s32[1024]{0:T(1024)S(1)}, s32[1024]{0:T(1024)}, u32[]{:S(2)}) copy-start(s32[1024]{0:T(1024)} %param.6) | copy-start | bytes 12292
  8.5 35.5 %copy-start.2 = (f32[8]{0:T(128)S(1)}, f32[8]{0:T(128)}, u32[]{:S(2)}) copy-start(f32[8]{0:T(128)} %weights.1) | copy-start | bytes 100
  8.5 21.1 %collective-permute-start.3 = (f32[32,4096]{1,0:T(8,128)S(1)}, f32[32,4096]{1,0:T(8,128)S(1)}, u32[]{:S(2)}, u32[]{:S(2)}) collective-permute-start(f32[32,4096]{1,0:T(8,128)S(1)} %get-tuple-element.33), channel_id=1, source_target_pairs={{1,2},{2,1},{5,6},{6,5},{9,10},{10,9},{13,14},{14,13},{17,18},{18,... | collective-permute-start | bytes 1572872 | tf_op jit(solution)/shard_map/ppermute | solution.py:391
  9.4 9.3 %collective-permute-start.6 = (bf16[16,4096]{1,0:T(8,128)(2,1)S(1)}, bf16[16,4096]{1,0:T(8,128)(2,1)S(1)}, u32[]{:S(2)}, u32[]{:S(2)}) collective-permute-start(bf16[16,4096]{1,0:T(8,128)(2,1)S(1)} %get-tuple-element.43), channel_id=1, source_target_pairs={{3,1},{7,5},{11,9},{15,13},{19,17},{23,21},{27,25},{31,29}} | collective-permute-start | bytes 393224 | tf_op jit(solution)/shard_map/ppermute | solution.py:413
  10.0 19.4 %collective-permute-start.5 = (bf16[16,4096]{1,0:T(8,128)(2,1)S(1)}, bf16[16,4096]{1,0:T(8,128)(2,1)S(1)}, u32[]{:S(2)}, u32[]{:S(2)}) collective-permute-start(bf16[16,4096]{1,0:T(8,128)(2,1)S(1)} %get-tuple-element.44), channel_id=1, source_target_pairs={{3,0},{7,4},{11,8},{15,12},{19,16},{23,20},{27,24},{31,28}} | collective-permute-start | bytes 393224 | tf_op jit(solution)/shard_map/ppermute | solution.py:413
  14.2 18.0 %collective-permute-start = (bf16[16,4096]{1,0:T(8,128)(2,1)S(1)}, bf16[16,4096]{1,0:T(8,128)(2,1)S(1)}, u32[]{:S(2)}, u32[]{:S(2)}) collective-permute-start(bf16[16,4096]{1,0:T(8,128)(2,1)S(1)} %get-tuple-element.26), channel_id=1, source_target_pairs={{0,1},{1,2},{2,3},{3,0},{4,5},{5,6},{6,7},{7,4},{8,9},{9,10},{10,1... | collective-permute-start | bytes 393224 | tf_op jit(solution)/shard_map/ppermute | solution.py:409
  18.7 22.7 %collective-permute-start.1 = (bf16[16,4096]{1,0:T(8,128)(2,1)S(1)}, bf16[16,4096]{1,0:T(8,128)(2,1)S(1)}, u32[]{:S(2)}, u32[]{:S(2)}) collective-permute-start(bf16[16,4096]{1,0:T(8,128)(2,1)S(1)} %get-tuple-element.27), channel_id=1, source_target_pairs={{0,2},{1,3},{2,0},{3,1},{4,6},{5,7},{6,4},{7,5},{8,10},{9,11},{10,... | collective-permute-start | bytes 393224 | tf_op jit(solution)/shard_map/ppermute | solution.py:409
  29.5 11.9 %collective-permute-start.2 = (bf16[16,4096]{1,0:T(8,128)(2,1)S(1)}, bf16[16,4096]{1,0:T(8,128)(2,1)S(1)}, u32[]{:S(2)}, u32[]{:S(2)}) collective-permute-start(bf16[16,4096]{1,0:T(8,128)(2,1)S(1)} %get-tuple-element.28), channel_id=1, source_target_pairs={{0,3},{1,0},{2,1},{3,2},{4,7},{5,4},{6,5},{7,6},{8,11},{9,8},{10,9... | collective-permute-start | bytes 393224 | tf_op jit(solution)/shard_map/ppermute | solution.py:409
  29.7 14.3 %collective-permute-start.7 = (bf16[16,4096]{1,0:T(8,128)(2,1)S(1)}, bf16[16,4096]{1,0:T(8,128)(2,1)S(1)}, u32[]{:S(2)}, u32[]{:S(2)}) collective-permute-start(bf16[16,4096]{1,0:T(8,128)(2,1)S(1)} %get-tuple-element.36), channel_id=1, source_target_pairs={{0,3},{1,0},{2,1},{3,2},{4,7},{5,4},{6,5},{7,6},{8,11},{9,8},{10,9... | collective-permute-start | bytes 393224 | tf_op jit(solution)/shard_map/ppermute | solution.py:409
  29.8 14.2 %collective-permute-start.8 = (bf16[16,4096]{1,0:T(8,128)(2,1)S(1)}, bf16[16,4096]{1,0:T(8,128)(2,1)S(1)}, u32[]{:S(2)}, u32[]{:S(2)}) collective-permute-start(bf16[16,4096]{1,0:T(8,128)(2,1)S(1)} %get-tuple-element.38), channel_id=1, source_target_pairs={{1,2},{2,3},{3,0},{5,6},{6,7},{7,4},{9,10},{10,11},{11,8},{13,14},... | collective-permute-start | bytes 393224 | tf_op jit(solution)/shard_map/ppermute | solution.py:409
  45.3 1.2 %collective-permute-start.9 = (f32[8,128]{1,0:T(8,128)S(1)}, f32[8,128]{1,0:T(8,128)S(1)}, u32[]{:S(2)}, u32[]{:S(2)}) collective-permute-start(f32[8,128]{1,0:T(8,128)S(1)} %shard_map.70), channel_id=1, source_target_pairs={{0,4},{4,0},{8,12},{12,8},{16,20},{20,16},{24,28},{28,24},{1,5},{5... | collective-permute-start | bytes 12296 | tf_op jit(solution)/shard_map/ppermute | solution.py:447
  46.5 3.6 %collective-permute-start.10 = (f32[8,128]{1,0:T(8,128)S(1)}, f32[8,128]{1,0:T(8,128)S(1)}, u32[]{:S(2)}, u32[]{:S(2)}) collective-permute-start(f32[8,128]{1,0:T(8,128)S(1)} %add.6), channel_id=1, source_target_pairs={{0,8},{4,12},{8,0},{12,4},{16,24},{20,28},{24,16},{28,20},{1,9},{5... | collective-permute-start | bytes 12296 | tf_op jit(solution)/shard_map/ppermute | solution.py:447
  50.1 3.6 %collective-permute-start.11 = (f32[8,128]{1,0:T(8,128)S(1)}, f32[8,128]{1,0:T(8,128)S(1)}, u32[]{:S(2)}, u32[]{:S(2)}) collective-permute-start(f32[8,128]{1,0:T(8,128)S(1)} %add.7.a_ref), channel_id=1, source_target_pairs={{0,16},{4,20},{8,24},{12,28},{16,0},{20,4},{24,8},{28,12},{1,17},{... | collective-permute-start | bytes 12296 | tf_op jit(solution)/shard_map/ppermute | solution.py:447

commit v5 on v4

--- a/solution.py
+++ b/solution.py
@@ -102,13 +102,17 @@
     return jnp.concatenate(parts, axis=1)
 
 
-def halo_kernel(slots, group, var_count, points, freqs, x_hbm, inner, outer, lhs, held, sems):
-    copies = [
-        pltpu.make_async_copy(x_hbm.at[:, :, pl.ds(j * LANES, LANES)], held.at[j], sems.at[j])
-        for j in range(held.shape[0])
-    ]
-    for copy in copies:
-        copy.start()
+def halo_kernel(slots, group, var_count, points, freqs, x_hbm, inner, outer, lhs, held, *refs):
+    last, sems = (refs[:-1], refs[-1])
+    copies = []
+    for j in range(held.shape[0]):
+        for i in range(2):
+            rows = pl.ds(i * HALF, HALF)
+            copy = pltpu.make_async_copy(
+                x_hbm.at[rows, :, pl.ds(j * LANES, LANES)], held.at[j, rows], sems.at[j, i]
+            )
+            copy.start()
+            copies.append(copy)
     me = lax.axis_index("blk")
     odd = lax.rem(me, 2) == 1
     full = slots * group
@@ -124,8 +128,8 @@
         )
 
     for j in range(0, held.shape[0], 2):
-        copies[j].wait()
-        copies[j + 1].wait()
+        for copy in copies[2 * j : 2 * j + 4]:
+            copy.wait()
         down = mm(some(full + wide), columns(held, j, 0, var_count))
         up = mm(some(group), columns(held, j, 1, var_count))
         for v in range(var_count):
@@ -134,6 +138,8 @@
             upper = up[v * wide : (v + 1) * wide]
             inner[:, low : low + 2 * LANES] = jnp.where(odd, upper, lower)
             outer[:, low : low + 2 * LANES] = jnp.where(odd, lower, upper)
+            for i, target in enumerate(last):
+                target[:, low : low + 2 * LANES] = upper[i * group : (i + 1) * group].astype(BF16)
 
 
 def block_kernel(slots, keep, var_count, points, lhs, held, *outs):
@@ -241,12 +247,14 @@
     packed[...] = out
 
 
-def mode_kernel(slots, var_count, points, scaling, feature_count, a_ref, b_ref, *refs):
+def mode_kernel(slots, var_count, points, scaling, feature_count, sums, *refs):
     csd, eig, modes = refs[-3:]
     blocks = 2 * slots
     me = lax.axis_index("blk")
     spectra = gather_pieces(refs[:-3], slots, me)
-    raw = a_ref[...] + b_ref[...]
+    raw = sums[0]
+    for i in range(1, sums.shape[0]):
+        raw = raw + sums[i]
     freqs, width = raw.shape
     group = 2 * freqs
     size = blocks * group
@@ -371,17 +379,18 @@
 
     wide = half_slots * group
     groups = points // LANES
-    inner, outer, lhs, held = call(
+    inner, outer, lhs, held, *last = call(
         functools.partial(halo_kernel, slots, group, var_count, points),
         [
             shape((wide, features), F32),
             shape((wide, features), F32),
             shape((2 * slots * group * var_count, HALF * var_count), BF16),
             shape((groups, row_count, var_count, LANES), BF16),
-        ],
+        ]
+        + [shape((group, features), BF16)] * half_slots,
         [smem, hbm],
         (freq_index, pltpu.with_memory_space_constraint(snapshots, pltpu.HBM)),
-        [pltpu.SemaphoreType.DMA((groups,))],
+        [pltpu.SemaphoreType.DMA((groups, 2))],
         2 * 2 * wide * HALF * features * var_count,
         2 * row_count * features,
     )
@@ -409,12 +418,7 @@
         return lax.ppermute(x, "blk", [(i, (i + s) % slots) for i in range(first, slots)])
 
     even = [pieces[0]] + [shift(pieces[s], s, 0) for s in range(1, slots)]
-    last = [
-        lax.ppermute(
-            inner[i * group : (i + 1) * group].astype(BF16), "blk", [(slots - 1, i)]
-        )
-        for i in range(half_slots)
-    ]
+    last = [lax.ppermute(x, "blk", [(slots - 1, i)]) for i, x in enumerate(last)]
     odd = call(
         functools.partial(join_kernel, half_slots, group),
         [piece] * (slots + half_slots - 1),
@@ -439,13 +443,7 @@
         4 * blocks * group * features,
     )
     devices = lax.axis_size("pts")
-    step = 1
-    other = None
-    while step < devices:
-        if other is not None:
-            packed = packed + other
-        other = lax.ppermute(packed, "pts", [(i, i ^ step) for i in range(devices)])
-        step *= 2
+    packed = lax.all_gather(packed, "pts")
     total_features = features * devices
     csd, eigval, modes = call(
         functools.partial(
@@ -461,8 +459,8 @@
             shape((1, freqs), F32),
             shape((freqs, 2, var_count, points), F32),
         ],
-        [vmem] * (2 + len(spectra)),
-        (packed, other, *spectra),
+        [vmem] * (1 + len(spectra)),
+        (packed, *spectra),
         [],
         2 * 2 * blocks * group * group * features,
         2 * blocks * group * features,

time: 56.5 us -> 57.7 us (1.021)
  blocking collectives: 0 us -> 9.08 us
  starting transfers between devices: 19 us -> 14.3 us
  waiting for transfers between devices: 24.9 us -> 21.7 us
    all_gather x0 -> x1, blocking collectives: none -> 9.08 us  [on_device(): packed = lax.all_gather(packed, 'pts')]
    ppermute x5, starting transfers between devices: 10.1 us -> 5.8 us  [shift(): lax.ppermute(x, 'blk', [(i, (i + s) % slots) for i in range(first, slots)])]
    ppermute x5, waiting for transfers between devices: 12.9 us -> 9.63 us  [shift(): lax.ppermute(x, 'blk', [(i, (i + s) % slots) for i in range(first, slots)])]
    ppermute x5 -> x2, starting transfers between devices: 5.03 us -> 1.95 us  [on_device(): lax.ppermute(x, 'blk', [(slots - 1, i)])]
    ppermute x2, starting transfers between devices: 3.9 us -> 6.57 us  [swap(): return lax.ppermute(x, 'blk', pairs + [(b, a) for a, b in pairs])]
    ppermute x5 -> x2, waiting for transfers between devices: 12 us -> 12 us  [on_device(): lax.ppermute(x, 'blk', [(slots - 1, i)])]
  transfers between devices with their start and end apart: 12 -> 9, of which waited for: 7 -> 5; matrix products, arithmetic and copies ran while one was open for 0% -> 0% of each run, Pallas kernels for 5% -> 5%
where the time goes in v5:
time: 57.7 us; the launch traced here: 56.8 us
  waiting for transfers between devices  21.7 us (38%)
  starting transfers between devices  14.3 us (25%)
  Pallas kernels  10.4 us (18%)
  blocking collectives  9.08 us (16%)
  between operations  0.73 us (1%)
  local copies, waits for them, and re-layouts  0.66 us (1%)
    ppermute x2, waiting for transfers between devices, on_device(): lax.ppermute(x, 'blk', [(slots - 1, i)])  12 us
    pallas_call x5, Pallas kernels, call(): pl.pallas_call(kernel, out_shape=outs, in_specs=ins, out_specs=jax.tree.m...  10.4 us
    ppermute x5, waiting for transfers between devices, shift(): lax.ppermute(x, 'blk', [(i, (i + s) % slots) for i in range(first, slots)])  9.63 us
    all_gather x1, blocking collectives, on_device(): packed = lax.all_gather(packed, 'pts')  9.08 us
    ppermute x2, starting transfers between devices, swap(): return lax.ppermute(x, 'blk', pairs + [(b, a) for a, b in pairs])  6.57 us
    ppermute x5, starting transfers between devices, shift(): lax.ppermute(x, 'blk', [(i, (i + s) % slots) for i in range(first, slots)])  5.8 us
    ppermute x2, starting transfers between devices, on_device(): lax.ppermute(x, 'blk', [(slots - 1, i)])  1.95 us
  transfers between devices with their start and end apart: 9, of which 5 were waited for; matrix products, arithmetic and copies ran while one was open for 0% of the time, Pallas kernels for 5%

profile of v5, /device:TPU:0, one launch (start us, length us, event | category | flops | bytes accessed | tf_op | source)
XLA Modules:
  0.0 56.8 jit_solution(7001998903812554518)
XLA Ops:
  0.6 0.0 copy-start.1
  0.6 0.6 %copy-done.1 = s32[32]{0:T(128)S(1)} copy-done((s32[32]{0:T(128)S(1)}, s32[32]{0:T(128)}, u32[]{:S(2)}) %copy-start.1) | copy-done | bytes 152
  1.3 4.3 %shard_map.67 = (f32[32,4096]{1,0:T(8,128)S(1)}, f32[32,4096]{1,0:T(8,128)S(1)}, bf16[512,1536]{1,0:T(8,128)(2,1)S(1)}, bf16[8,768,4,128]{3,2,1,0:T(4,128)(2,1)S...) custom-call(s32[32]{0:T(128)S(1)} %copy-done.1, bf16[768,4,1024]{2,1,0:T(4,128)(2,1)} %x_hbm.1), custom_call_target="tpu_custom_call" | custom-call | flops 805306368 | bytes 6291456 | tf_op jit(solution)/shard_map/pallas_call | solution.py:355
  5.6 0.0 copy-start
  5.6 0.0 copy-start.2
  5.6 0.7 %collective-permute-start.3 = (f32[32,4096]{1,0:T(8,128)S(1)}, f32[32,4096]{1,0:T(8,128)S(1)}, u32[]{:S(2)}, u32[]{:S(2)}) collective-permute-start(f32[32,4096]{1,0:T(8,128)S(1)} %get-tuple-element.35), channel_id=1, source_target_pairs={{1,2},{2,1},{5,6},{6,5},{9,10},{10,9},{13,14},{14,13},{17,18},{18,... | collective-permute-start | bytes 1572872 | tf_op jit(solution)/shard_map/ppermute | solution.py:400
  6.3 5.9 %collective-permute-start.4 = (f32[32,4096]{1,0:T(8,128)S(1)}, f32[32,4096]{1,0:T(8,128)S(1)}, u32[]{:S(2)}, u32[]{:S(2)}) collective-permute-start(f32[32,4096]{1,0:T(8,128)S(1)} %get-tuple-element.36), channel_id=1, source_target_pairs={{0,1},{2,3},{1,0},{3,2},{4,5},{6,7},{5,4},{7,6},{8,9},{10,11},{9,8... | collective-permute-start | bytes 1572872 | tf_op jit(solution)/shard_map/ppermute | solution.py:400
  12.2 1.3 %collective-permute-start.5 = (bf16[16,4096]{1,0:T(8,128)(2,1)S(1)}, bf16[16,4096]{1,0:T(8,128)(2,1)S(1)}, u32[]{:S(2)}, u32[]{:S(2)}) collective-permute-start(bf16[16,4096]{1,0:T(8,128)(2,1)S(1)} %get-tuple-element.37), channel_id=1, source_target_pairs={{3,0},{7,4},{11,8},{15,12},{19,16},{23,20},{27,24},{31,28}} | collective-permute-start | bytes 393224 | tf_op jit(solution)/shard_map/ppermute | solution.py:421
  13.5 0.7 %collective-permute-start.6 = (bf16[16,4096]{1,0:T(8,128)(2,1)S(1)}, bf16[16,4096]{1,0:T(8,128)(2,1)S(1)}, u32[]{:S(2)}, u32[]{:S(2)}) collective-permute-start(bf16[16,4096]{1,0:T(8,128)(2,1)S(1)} %get-tuple-element.38), channel_id=1, source_target_pairs={{3,1},{7,5},{11,9},{15,13},{19,17},{23,21},{27,25},{31,29}} | collective-permute-start | bytes 393224 | tf_op jit(solution)/shard_map/ppermute | solution.py:421
  14.1 2.9 %shard_map.68 = (bf16[16,4096]{1,0:T(8,128)(2,1)S(1)}, bf16[16,4096]{1,0:T(8,128)(2,1)S(1)}, bf16[16,4096]{1,0:T(8,128)(2,1)S(1)}, bf16[16,4096]{1,0:T(8,128)(2,...) custom-call(bf16[512,1536]{1,0:T(8,128)(2,1)S(1)} %get-tuple-element., ...), custom_call_target="tpu_custom_call" | custom-call | flops 2415919104 | bytes 6291456 | tf_op jit(solution)/shard_map/pallas_call | solution.py:355
  17.0 0.1 collective-permute-start
  17.1 12.0 %collective-permute-done.5.refs_6_ = bf16[16,4096]{1,0:T(8,128)(2,1)S(1)} collective-permute-done((bf16[16,4096]{1,0:T(8,128)(2,1)S(1)}, bf16[16,4096]{1,0:T(8,128)(2,1)S(1)}, u32[]{:S(2)}, u32[]{:S(2)}) %collective-permute-start.5) | collective-permute-done | bytes 131104 | tf_op jit(solution)/shard_map/ppermute | solution.py:421
  29.1 0.0 collective-permute-start.1
  29.1 0.0 collective-permute-done.6.refs_7_
  29.1 2.4 %collective-permute-start.2 = (bf16[16,4096]{1,0:T(8,128)(2,1)S(1)}, bf16[16,4096]{1,0:T(8,128)(2,1)S(1)}, u32[]{:S(2)}, u32[]{:S(2)}) collective-permute-start(bf16[16,4096]{1,0:T(8,128)(2,1)S(1)} %get-tuple-element.30), channel_id=1, source_target_pairs={{0,3},{1,0},{2,1},{3,2},{4,7},{5,4},{6,5},{7,6},{8,11},{9,8},{10,9... | collective-permute-start | bytes 393224 | tf_op jit(solution)/shard_map/ppermute | solution.py:418
  31.5 0.0 collective-permute-done.3.refs_4_
  31.5 0.0 collective-permute-done.4.refs_5_
  31.5 0.2 shard_map.69
  31.7 2.0 %collective-permute-start.7 = (bf16[16,4096]{1,0:T(8,128)(2,1)S(1)}, bf16[16,4096]{1,0:T(8,128)(2,1)S(1)}, u32[]{:S(2)}, u32[]{:S(2)}) collective-permute-start(bf16[16,4096]{1,0:T(8,128)(2,1)S(1)} %get-tuple-element.40), channel_id=1, source_target_pairs={{0,3},{1,0},{2,1},{3,2},{4,7},{5,4},{6,5},{7,6},{8,11},{9,8},{10,9... | collective-permute-start | bytes 393224 | tf_op jit(solution)/shard_map/ppermute | solution.py:418
  33.8 1.3 %collective-permute-start.8 = (bf16[16,4096]{1,0:T(8,128)(2,1)S(1)}, bf16[16,4096]{1,0:T(8,128)(2,1)S(1)}, u32[]{:S(2)}, u32[]{:S(2)}) collective-permute-start(bf16[16,4096]{1,0:T(8,128)(2,1)S(1)} %get-tuple-element.42), channel_id=1, source_target_pairs={{1,2},{2,3},{3,0},{5,6},{6,7},{7,4},{9,10},{10,11},{11,8},{13,14},... | collective-permute-start | bytes 393224 | tf_op jit(solution)/shard_map/ppermute | solution.py:418
  35.0 0.0 collective-permute-done.refs_1_
  35.1 4.0 %collective-permute-done.1.refs_2_ = bf16[16,4096]{1,0:T(8,128)(2,1)S(1)} collective-permute-done((bf16[16,4096]{1,0:T(8,128)(2,1)S(1)}, bf16[16,4096]{1,0:T(8,128)(2,1)S(1)}, u32[]{:S(2)}, u32[]{:S(2)}) %collective-permute-start.1) | collective-permute-done | bytes 131104 | tf_op jit(solution)/shard_map/ppermute | solution.py:418
  39.0 0.4 collective-permute-done.2.refs_3_
  39.4 1.9 %collective-permute-done.7.refs_5_ = bf16[16,4096]{1,0:T(8,128)(2,1)S(1)} collective-permute-done((bf16[16,4096]{1,0:T(8,128)(2,1)S(1)}, bf16[16,4096]{1,0:T(8,128)(2,1)S(1)}, u32[]{:S(2)}, u32[]{:S(2)}) %collective-permute-start.7) | collective-permute-done | bytes 131104 | tf_op jit(solution)/shard_map/ppermute | solution.py:418
  41.4 3.3 %collective-permute-done.8.refs_7_ = bf16[16,4096]{1,0:T(8,128)(2,1)S(1)} collective-permute-done((bf16[16,4096]{1,0:T(8,128)(2,1)S(1)}, bf16[16,4096]{1,0:T(8,128)(2,1)S(1)}, u32[]{:S(2)}, u32[]{:S(2)}) %collective-permute-start.8) | collective-permute-done | bytes 131104 | tf_op jit(solution)/shard_map/ppermute | solution.py:418
  44.7 0.0 copy-done
  44.7 0.0 copy-done.2
  44.7 1.2 %shard_map.70 = f32[8,128]{1,0:T(8,128)S(1)} custom-call(f32[8]{0:T(128)S(1)} %copy-done.2, s32[1,1024]{1,0:T(1,128)S(1)} %bitcast.4, bf16[16,4096]{1,0:T(8,128)(2,1)S(1)} %get-tuple-element.27.refs_0_, bf16[16,4096]{1,0:T(8,128)(2,1)S(1)} %collective-permute-done.refs_1_, bf16[16,4096]{1,0:T(8,128)(2,1)S(1)} %collective-permute-done.1.refs_2_, ...), custom_call_target="tpu_custom_call" | custom-call | flops 134217728 | bytes 2097152 | tf_op jit(solution)/shard_map/pallas_call | solution.py:355
  45.9 9.1 %all-gather = f32[64,128]{1,0:T(8,128)S(1)} all-gather(f32[8,128]{1,0:T(8,128)S(1)} %shard_map.70), channel_id=2, replica_groups=mesh['pts'=8,'blk'=4] {'pts'}, dimensions={0}, use_global_device_ids=true | all-gather | bytes 36864 | tf_op jit(solution)/shard_map/all_gather | solution.py:446
  55.0 1.8 %shard_map.71 = (f32[8,2,8,8]{3,2,1,0:T(8,128)}, f32[1,8]{1,0:T(1,128)}, f32[8,2,4,1024]{3,2,1,0:T(4,128)}) custom-call(f32[8,8,128]{2,1,0:T(8,128)S(1)} %bitcast.3, bf16[16,4096]{1,0:T(8,128)(2,1)S(1)} %get-tuple-element.27.refs_0_, bf16[16,4096]{1,0:T(8,128)(2,1)S(1)} %collective-permute-done.refs_1_, bf16[16,4096]{1,0:T(8,128)(2,1)S(1)} %collective-permute-done.1.refs_2_, ...), custom_call_target="tpu_custom_call" | custom-call | flops 33554432 | bytes 1048576 | tf_op jit(solution)/shard_map/pallas_call | solution.py:355
Async XLA Ops:
  0.6 0.7 %copy-start.1 = (s32[32]{0:T(128)S(1)}, s32[32]{0:T(128)}, u32[]{:S(2)}) copy-start(s32[32]{0:T(128)} %freqs.1) | copy-start | bytes 388
  5.6 39.1 %copy-start = (s32[1024]{0:T(1024)S(1)}, s32[1024]{0:T(1024)}, u32[]{:S(2)}) copy-start(s32[1024]{0:T(1024)} %param.6) | copy-start | bytes 12292
  5.6 39.1 %copy-start.2 = (f32[8]{0:T(128)S(1)}, f32[8]{0:T(128)}, u32[]{:S(2)}) copy-start(f32[8]{0:T(128)} %weights.1) | copy-start | bytes 100
  5.6 26.0 %collective-permute-start.3 = (f32[32,4096]{1,0:T(8,128)S(1)}, f32[32,4096]{1,0:T(8,128)S(1)}, u32[]{:S(2)}, u32[]{:S(2)}) collective-permute-start(f32[32,4096]{1,0:T(8,128)S(1)} %get-tuple-element.35), channel_id=1, source_target_pairs={{1,2},{2,1},{5,6},{6,5},{9,10},{10,9},{13,14},{14,13},{17,18},{18,... | collective-permute-start | bytes 1572872 | tf_op jit(solution)/shard_map/ppermute | solution.py:400
  6.3 25.3 %collective-permute-start.4 = (f32[32,4096]{1,0:T(8,128)S(1)}, f32[32,4096]{1,0:T(8,128)S(1)}, u32[]{:S(2)}, u32[]{:S(2)}) collective-permute-start(f32[32,4096]{1,0:T(8,128)S(1)} %get-tuple-element.36), channel_id=1, source_target_pairs={{0,1},{2,3},{1,0},{3,2},{4,5},{6,7},{5,4},{7,6},{8,9},{10,11},{9,8... | collective-permute-start | bytes 1572872 | tf_op jit(solution)/shard_map/ppermute | solution.py:400
  12.2 17.0 %collective-permute-start.5 = (bf16[16,4096]{1,0:T(8,128)(2,1)S(1)}, bf16[16,4096]{1,0:T(8,128)(2,1)S(1)}, u32[]{:S(2)}, u32[]{:S(2)}) collective-permute-start(bf16[16,4096]{1,0:T(8,128)(2,1)S(1)} %get-tuple-element.37), channel_id=1, source_target_pairs={{3,0},{7,4},{11,8},{15,12},{19,16},{23,20},{27,24},{31,28}} | collective-permute-start | bytes 393224 | tf_op jit(solution)/shard_map/ppermute | solution.py:421
  13.5 15.7 %collective-permute-start.6 = (bf16[16,4096]{1,0:T(8,128)(2,1)S(1)}, bf16[16,4096]{1,0:T(8,128)(2,1)S(1)}, u32[]{:S(2)}, u32[]{:S(2)}) collective-permute-start(bf16[16,4096]{1,0:T(8,128)(2,1)S(1)} %get-tuple-element.38), channel_id=1, source_target_pairs={{3,1},{7,5},{11,9},{15,13},{19,17},{23,21},{27,25},{31,29}} | collective-permute-start | bytes 393224 | tf_op jit(solution)/shard_map/ppermute | solution.py:421
  17.0 18.0 %collective-permute-start = (bf16[16,4096]{1,0:T(8,128)(2,1)S(1)}, bf16[16,4096]{1,0:T(8,128)(2,1)S(1)}, u32[]{:S(2)}, u32[]{:S(2)}) collective-permute-start(bf16[16,4096]{1,0:T(8,128)(2,1)S(1)} %get-tuple-element.28), channel_id=1, source_target_pairs={{0,1},{1,2},{2,3},{3,0},{4,5},{5,6},{6,7},{7,4},{8,9},{9,10},{10,1... | collective-permute-start | bytes 393224 | tf_op jit(solution)/shard_map/ppermute | solution.py:418
  29.1 9.9 %collective-permute-start.1 = (bf16[16,4096]{1,0:T(8,128)(2,1)S(1)}, bf16[16,4096]{1,0:T(8,128)(2,1)S(1)}, u32[]{:S(2)}, u32[]{:S(2)}) collective-permute-start(bf16[16,4096]{1,0:T(8,128)(2,1)S(1)} %get-tuple-element.29), channel_id=1, source_target_pairs={{0,2},{1,3},{2,0},{3,1},{4,6},{5,7},{6,4},{7,5},{8,10},{9,11},{10,... | collective-permute-start | bytes 393224 | tf_op jit(solution)/shard_map/ppermute | solution.py:418
  29.1 10.3 %collective-permute-start.2 = (bf16[16,4096]{1,0:T(8,128)(2,1)S(1)}, bf16[16,4096]{1,0:T(8,128)(2,1)S(1)}, u32[]{:S(2)}, u32[]{:S(2)}) collective-permute-start(bf16[16,4096]{1,0:T(8,128)(2,1)S(1)} %get-tuple-element.30), channel_id=1, source_target_pairs={{0,3},{1,0},{2,1},{3,2},{4,7},{5,4},{6,5},{7,6},{8,11},{9,8},{10,9... | collective-permute-start | bytes 393224 | tf_op jit(solution)/shard_map/ppermute | solution.py:418
  31.7 9.7 %collective-permute-start.7 = (bf16[16,4096]{1,0:T(8,128)(2,1)S(1)}, bf16[16,4096]{1,0:T(8,128)(2,1)S(1)}, u32[]{:S(2)}, u32[]{:S(2)}) collective-permute-start(bf16[16,4096]{1,0:T(8,128)(2,1)S(1)} %get-tuple-element.40), channel_id=1, source_target_pairs={{0,3},{1,0},{2,1},{3,2},{4,7},{5,4},{6,5},{7,6},{8,11},{9,8},{10,9... | collective-permute-start | bytes 393224 | tf_op jit(solution)/shard_map/ppermute | solution.py:418
  33.8 10.9 %collective-permute-start.8 = (bf16[16,4096]{1,0:T(8,128)(2,1)S(1)}, bf16[16,4096]{1,0:T(8,128)(2,1)S(1)}, u32[]{:S(2)}, u32[]{:S(2)}) collective-permute-start(bf16[16,4096]{1,0:T(8,128)(2,1)S(1)} %get-tuple-element.42), channel_id=1, source_target_pairs={{1,2},{2,3},{3,0},{5,6},{6,7},{7,4},{9,10},{10,11},{11,8},{13,14},... | collective-permute-start | bytes 393224 | tf_op jit(solution)/shard_map/ppermute | solution.py:418

commit v6 on v5

--- a/solution.py
+++ b/solution.py
@@ -102,8 +102,26 @@
     return jnp.concatenate(parts, axis=1)
 
 
+def encode(values, coded):
+    rows, features = values.shape
+    largest = jnp.max(jnp.abs(values[...]), axis=1, keepdims=True)
+    largest = jnp.maximum(largest, 1e-30)
+    exponent = jnp.floor(jnp.log2(32000.0 / largest))
+    steps = values[...] * jnp.exp2(exponent)
+    coded[:, :features] = jnp.round(steps).astype(jnp.int32).astype(jnp.int16)
+    tail = jnp.broadcast_to(exponent, (rows, LANES))
+    coded[:, features:] = tail.astype(jnp.int32).astype(jnp.int16)
+
+
+def decode(coded, low, high):
+    features = coded.shape[1] - LANES
+    exponent = coded[low:high, features:].astype(jnp.int32).astype(F32)[:, :1]
+    steps = coded[low:high, :features].astype(jnp.int32).astype(F32)
+    return steps * (1.0 / jnp.exp2(exponent))
+
+
 def halo_kernel(slots, group, var_count, points, freqs, x_hbm, inner, outer, lhs, held, *refs):
-    last, sems = (refs[:-1], refs[-1])
+    first, second, sems = refs
     copies = []
     for j in range(held.shape[0]):
         for i in range(2):
@@ -136,10 +154,10 @@
             low = v * points + j * LANES
             lower = down[v * wide : (v + 1) * wide]
             upper = up[v * wide : (v + 1) * wide]
-            inner[:, low : low + 2 * LANES] = jnp.where(odd, upper, lower)
-            outer[:, low : low + 2 * LANES] = jnp.where(odd, lower, upper)
-            for i, target in enumerate(last):
-                target[:, low : low + 2 * LANES] = upper[i * group : (i + 1) * group].astype(BF16)
+            first[:, low : low + 2 * LANES] = jnp.where(odd, upper, lower)
+            second[:, low : low + 2 * LANES] = jnp.where(odd, lower, upper)
+    encode(first, inner)
+    encode(second, outer)
 
 
 def block_kernel(slots, keep, var_count, points, lhs, held, *outs):
@@ -180,33 +198,18 @@
     lead = refs[:half_slots]
     trail = refs[half_slots : 2 * half_slots]
     inner, outer = refs[2 * half_slots : 2 * half_slots + 2]
-    last = refs[2 * half_slots + 2 : 3 * half_slots + 2]
-    outs = refs[3 * half_slots + 2 :]
+    outs = refs[2 * half_slots + 2 :]
     me = lax.axis_index("blk")
     odd = lax.rem(me, 2) == 1
     for i in range(half_slots):
         above = (i + half_slots - 1) % half_slots
-        rows = slice(above * group, (above + 1) * group)
-        from_above = jnp.where(odd, inner[rows, :], outer[rows, :])
+        rows = (above * group, (above + 1) * group)
+        from_above = jnp.where(odd, decode(inner, *rows), decode(outer, *rows))
         outs[i][...] = (lead[i][...] + from_above).astype(BF16)
-        rows = slice(i * group, (i + 1) * group)
-        from_below = jnp.where(odd, outer[rows, :], inner[rows, :])
-        joined = (trail[i][...] + from_below).astype(BF16)
-        if i == 0:
-            outs[half_slots][...] = jnp.where(me == 0, last[0][...], joined)
-        else:
-            outs[half_slots + i][...] = joined
-            outs[2 * half_slots + i - 1][...] = last[i][...]
-
-
-def gather_pieces(refs, slots, me):
-    half_slots = slots // 2
-    found = [ref[...] for ref in refs[: slots + half_slots + 1]]
-    for i in range(1, half_slots):
-        below = refs[slots + half_slots + i][...]
-        last = refs[2 * slots + i - 1][...]
-        found.append(jnp.where(me == i, last, below))
-    return found
+        rows = (i * group, (i + 1) * group)
+        from_below = jnp.where(odd, decode(outer, *rows), decode(inner, *rows))
+        own = jnp.where(me == 0, 0.0, trail[i][...])
+        outs[half_slots + i][...] = (own + from_below).astype(BF16)
 
 
 def gram_kernel(slots, group, var_count, points, weights, classes, *refs):
@@ -217,7 +220,7 @@
     for k in range(weights.shape[0]):
         picked = picked + jnp.where(classes[...] == k, weights[k], jnp.float32(0.0))
     wide = jnp.concatenate([picked] * var_count, axis=1)
-    left = jnp.concatenate(gather_pieces(refs[:-1], slots, me), axis=0)
+    left = jnp.concatenate([ref[...] for ref in refs[:-1]], axis=0)
     right = (left.astype(F32) * wide).astype(BF16)
     gram = lax.dot_general(
         left, right, (((1,), (1,)), ((), ())), preferred_element_type=F32
@@ -247,14 +250,12 @@
     packed[...] = out
 
 
-def mode_kernel(slots, var_count, points, scaling, feature_count, sums, *refs):
+def mode_kernel(slots, var_count, points, scaling, feature_count, a_ref, b_ref, *refs):
     csd, eig, modes = refs[-3:]
     blocks = 2 * slots
     me = lax.axis_index("blk")
-    spectra = gather_pieces(refs[:-3], slots, me)
-    raw = sums[0]
-    for i in range(1, sums.shape[0]):
-        raw = raw + sums[i]
+    spectra = [ref[...] for ref in refs[:-3]]
+    raw = a_ref[...] + b_ref[...]
     freqs, width = raw.shape
     group = 2 * freqs
     size = blocks * group
@@ -379,28 +380,31 @@
 
     wide = half_slots * group
     groups = points // LANES
-    inner, outer, lhs, held, *last = call(
+    inner, outer, lhs, held = call(
         functools.partial(halo_kernel, slots, group, var_count, points),
         [
-            shape((wide, features), F32),
-            shape((wide, features), F32),
+            shape((wide, features + LANES), jnp.int16),
+            shape((wide, features + LANES), jnp.int16),
             shape((2 * slots * group * var_count, HALF * var_count), BF16),
             shape((groups, row_count, var_count, LANES), BF16),
-        ]
-        + [shape((group, features), BF16)] * half_slots,
+        ],
         [smem, hbm],
         (freq_index, pltpu.with_memory_space_constraint(snapshots, pltpu.HBM)),
-        [pltpu.SemaphoreType.DMA((groups, 2))],
+        [
+            pltpu.VMEM((wide, features), F32),
+            pltpu.VMEM((wide, features), F32),
+            pltpu.SemaphoreType.DMA((groups, 2)),
+        ],
         2 * 2 * wide * HALF * features * var_count,
         2 * row_count * features,
     )
 
-    def swap(x, first):
+    def swap(x, first, also):
         pairs = [(i, i + 1) for i in range(first, slots - 1, 2)]
-        return lax.ppermute(x, "blk", pairs + [(b, a) for a, b in pairs])
-
-    from_outer = swap(outer, 0)
-    swapped = (swap(inner, 1), from_outer)
+        return lax.ppermute(x, "blk", pairs + [(b, a) for a, b in pairs] + also)
+
+    from_outer = swap(outer, 0, [])
+    swapped = (swap(inner, 1, [(slots - 1, 0)]), from_outer)
     keep = [0] + list(range(half_slots + 1, slots))
     piece = shape((group, features), BF16)
     wide_piece = shape((group, features), F32)
@@ -414,25 +418,24 @@
         2 * row_count * features,
     )
 
-    def shift(x, s, first):
-        return lax.ppermute(x, "blk", [(i, (i + s) % slots) for i in range(first, slots)])
-
-    even = [pieces[0]] + [shift(pieces[s], s, 0) for s in range(1, slots)]
-    last = [lax.ppermute(x, "blk", [(slots - 1, i)]) for i, x in enumerate(last)]
+    def shift(x, s):
+        return lax.ppermute(x, "blk", [(i, (i + s) % slots) for i in range(slots)])
+
+    even = [pieces[0]] + [shift(pieces[s], s) for s in range(1, slots)]
     odd = call(
         functools.partial(join_kernel, half_slots, group),
-        [piece] * (slots + half_slots - 1),
-        [vmem] * (slots + 2 + half_slots),
-        (*pieces[slots:], *swapped, *last),
+        [piece] * slots,
+        [vmem] * (slots + 2),
+        (*pieces[slots:], *swapped),
         [],
         slots * group * features,
         10 * slots * group * features,
     )
 
-    above = [odd[0]] + [shift(odd[i], s, 0) for i, s in enumerate(keep) if i]
-    under = [odd[half_slots]] + [shift(odd[half_slots + i], i, 1) for i in range(1, half_slots)]
+    above = [odd[0]] + [shift(odd[i], s) for i, s in enumerate(keep) if i]
+    under = [odd[half_slots]] + [shift(odd[half_slots + i], i) for i in range(1, half_slots)]
     width = 2 * blocks * blocks
-    spectra = (*even, *above, *under, *odd[slots:])
+    spectra = (*even, *above, *under)
     packed = call(
         functools.partial(gram_kernel, slots, group, var_count, points),
         shape((freqs, width), F32),
@@ -443,7 +446,13 @@
         4 * blocks * group * features,
     )
     devices = lax.axis_size("pts")
-    packed = lax.all_gather(packed, "pts")
+    step = 1
+    other = None
+    while step < devices:
+        if other is not None:
+            packed = packed + other
+        other = lax.ppermute(packed, "pts", [(i, i ^ step) for i in range(devices)])
+        step *= 2
     total_features = features * devices
     csd, eigval, modes = call(
         functools.partial(
@@ -459,8 +468,8 @@
             shape((1, freqs), F32),
             shape((freqs, 2, var_count, points), F32),
         ],
-        [vmem] * (1 + len(spectra)),
-        (packed, *spectra),
+        [vmem] * (2 + len(spectra)),
+        (packed, other, *spectra),
         [],
         2 * 2 * blocks * group * group * features,
         2 * blocks * group * features,

time: 57.7 us -> 50.3 us (0.87); the launches traced: 56.8 us -> 50.2 us
  blocking collectives: 9.08 us -> 0 us
  starting transfers between devices: 14.3 us -> 16.7 us
    all_gather x1 -> x0, blocking collectives: 9.08 us -> none  [on_device(): packed = lax.all_gather(packed, 'pts')]
    ppermute x9 -> x10, starting transfers between devices: 14.3 us -> 16.7 us  [the longest x2 6.57 us: swap(): return lax.ppermute(x, 'blk', pairs + [(b, a) for a, b in pairs] + also)]
    ppermute x9 -> x10, waiting for transfers between devices: 21.7 us -> 21.3 us  [the longest x5 8.87 us: shift(): return lax.ppermute(x, 'blk', [(i, (i + s) % slots) for i in range(slots)])]
  transfers between devices with their start and end apart: 9 -> 10, of which waited for: 5 -> 8; matrix products, arithmetic and copies ran while one was open for 0% -> 0% of each run, Pallas kernels for 5% -> 7%
where the time goes in v6:
time: 50.3 us; the launch traced here: 50.2 us
  waiting for transfers between devices  21.3 us (42%)
  starting transfers between devices  16.7 us (33%)
  Pallas kernels  10.8 us (21%)
  between operations  0.71 us (1%)
  local copies, waits for them, and re-layouts  0.66 us (1%)
    pallas_call x5, Pallas kernels, call(): pl.pallas_call(kernel, out_shape=outs, in_specs=ins, out_specs=jax.tree.m...  10.8 us
    ppermute x5, waiting for transfers between devices, shift(): return lax.ppermute(x, 'blk', [(i, (i + s) % slots) for i in range(slots)])  8.87 us
    ppermute x2, waiting for transfers between devices, swap(): return lax.ppermute(x, 'blk', pairs + [(b, a) for a, b in pairs] + also)  8.1 us
    ppermute x2, starting transfers between devices, swap(): return lax.ppermute(x, 'blk', pairs + [(b, a) for a, b in pairs] + also)  6.57 us
    ppermute x5, starting transfers between devices, shift(): return lax.ppermute(x, 'blk', [(i, (i + s) % slots) for i in range(slots)])  5.95 us
    ppermute x3, waiting for transfers between devices, on_device(): other = lax.ppermute(packed, 'pts', [(i, i ^ step) for i in range(devices)])  4.32 us
    ppermute x3, starting transfers between devices, on_device(): other = lax.ppermute(packed, 'pts', [(i, i ^ step) for i in range(devices)])  4.15 us
  transfers between devices with their start and end apart: 10, of which 8 were waited for; matrix products, arithmetic and copies ran while one was open for 0% of the time, Pallas kernels for 7%

profile of v6, /device:TPU:0, one launch (start us, length us, event | category | flops | bytes accessed | tf_op | source)
XLA Modules:
  0.0 50.2 jit_solution(12991959565146165343)
XLA Ops:
  0.6 0.0 copy-start.1
  0.6 0.6 %copy-done.1 = s32[32]{0:T(128)S(1)} copy-done((s32[32]{0:T(128)S(1)}, s32[32]{0:T(128)}, u32[]{:S(2)}) %copy-start.1) | copy-done | bytes 152
  1.3 4.5 %shard_map.67 = (s16[32,4224]{1,0:T(8,128)(2,1)S(1)}, s16[32,4224]{1,0:T(8,128)(2,1)S(1)}, bf16[512,1536]{1,0:T(8,128)(2,1)S(1)}, bf16[8,768,4,128]{3,2,1,0:T(4,128)(2,1)S(1)}) custom-call(s32[32]{0:T(128)S(1)} %copy-done.1, bf16[768,4,1024]{2,1,0:T(4,128)(2,1)} %x_hbm.1), custom_call_target="tpu_custom_call" | custom-call | flops 805306368 | bytes 6291456 | tf_op jit(solution)/shard_map/pallas_call | solution.py:356
  5.8 0.0 copy-start
  5.8 0.0 copy-start.2
  5.8 1.3 %collective-permute-start.3 = (s16[32,4224]{1,0:T(8,128)(2,1)S(1)}, s16[32,4224]{1,0:T(8,128)(2,1)S(1)}, u32[]{:S(2)}, u32[]{:S(2)}) collective-permute-start(s16[32,4224]{1,0:T(8,128)(2,1)S(1)} %get-tuple-element.32), channel_id=1, source_target_pairs={{1,2},{2,1},{3,0},{5,6},{6,5},{7,4},{9,10},{10,9},{11,8},{13,14},{... | collective-permute-start | bytes 811016 | tf_op jit(solution)/shard_map/ppermute | solution.py:404
  7.1 5.3 %collective-permute-start.4 = (s16[32,4224]{1,0:T(8,128)(2,1)S(1)}, s16[32,4224]{1,0:T(8,128)(2,1)S(1)}, u32[]{:S(2)}, u32[]{:S(2)}) collective-permute-start(s16[32,4224]{1,0:T(8,128)(2,1)S(1)} %get-tuple-element.33), channel_id=1, source_target_pairs={{0,1},{2,3},{1,0},{3,2},{4,5},{6,7},{5,4},{7,6},{8,9},{10,11},{9,8... | collective-permute-start | bytes 811016 | tf_op jit(solution)/shard_map/ppermute | solution.py:404
  12.4 2.9 %shard_map.68 = (bf16[16,4096]{1,0:T(8,128)(2,1)S(1)}, bf16[16,4096]{1,0:T(8,128)(2,1)S(1)}, bf16[16,4096]{1,0:T(8,128)(2,1)S(1)}, bf16[16,4096]{1,0:T(8,128)(2,...) custom-call(bf16[512,1536]{1,0:T(8,128)(2,1)S(1)} %get-tuple-element., ...), custom_call_target="tpu_custom_call" | custom-call | flops 2415919104 | bytes 6291456 | tf_op jit(solution)/shard_map/pallas_call | solution.py:356
  15.3 0.1 collective-permute-start
  15.3 1.9 %collective-permute-start.1 = (bf16[16,4096]{1,0:T(8,128)(2,1)S(1)}, bf16[16,4096]{1,0:T(8,128)(2,1)S(1)}, u32[]{:S(2)}, u32[]{:S(2)}) collective-permute-start(bf16[16,4096]{1,0:T(8,128)(2,1)S(1)} %get-tuple-element.26), channel_id=1, source_target_pairs={{0,2},{1,3},{2,0},{3,1},{4,6},{5,7},{6,4},{7,5},{8,10},{9,11},{10,... | collective-permute-start | bytes 393224 | tf_op jit(solution)/shard_map/ppermute | solution.py:422
  17.2 1.9 %collective-permute-start.2 = (bf16[16,4096]{1,0:T(8,128)(2,1)S(1)}, bf16[16,4096]{1,0:T(8,128)(2,1)S(1)}, u32[]{:S(2)}, u32[]{:S(2)}) collective-permute-start(bf16[16,4096]{1,0:T(8,128)(2,1)S(1)} %get-tuple-element.27), channel_id=1, source_target_pairs={{0,3},{1,0},{2,1},{3,2},{4,7},{5,4},{6,5},{7,6},{8,11},{9,8},{10,9... | collective-permute-start | bytes 393224 | tf_op jit(solution)/shard_map/ppermute | solution.py:422
  19.1 0.3 collective-permute-done.3.refs_4_
  19.5 7.8 %collective-permute-done.4.refs_5_ = s16[32,4224]{1,0:T(8,128)(2,1)S(1)} collective-permute-done((s16[32,4224]{1,0:T(8,128)(2,1)S(1)}, s16[32,4224]{1,0:T(8,128)(2,1)S(1)}, u32[]{:S(2)}, u32[]{:S(2)}) %collective-permute-start.4) | collective-permute-done | bytes 270368 | tf_op jit(solution)/shard_map/ppermute | solution.py:404
  27.2 0.4 shard_map.69
  27.7 0.1 collective-permute-start.5
  27.7 2.0 %collective-permute-start.6 = (bf16[16,4096]{1,0:T(8,128)(2,1)S(1)}, bf16[16,4096]{1,0:T(8,128)(2,1)S(1)}, u32[]{:S(2)}, u32[]{:S(2)}) collective-permute-start(bf16[16,4096]{1,0:T(8,128)(2,1)S(1)} %get-tuple-element.37), channel_id=1, source_target_pairs={{0,1},{1,2},{2,3},{3,0},{4,5},{5,6},{6,7},{7,4},{8,9},{9,10},{10,1... | collective-permute-start | bytes 393224 | tf_op jit(solution)/shard_map/ppermute | solution.py:422
  29.7 0.0 collective-permute-done.refs_1_
  29.8 3.2 %collective-permute-done.1.refs_2_ = bf16[16,4096]{1,0:T(8,128)(2,1)S(1)} collective-permute-done((bf16[16,4096]{1,0:T(8,128)(2,1)S(1)}, bf16[16,4096]{1,0:T(8,128)(2,1)S(1)}, u32[]{:S(2)}, u32[]{:S(2)}) %collective-permute-start.1) | collective-permute-done | bytes 131104 | tf_op jit(solution)/shard_map/ppermute | solution.py:422
  32.9 0.0 collective-permute-done.2.refs_3_
  33.0 3.4 %collective-permute-done.5.refs_5_ = bf16[16,4096]{1,0:T(8,128)(2,1)S(1)} collective-permute-done((bf16[16,4096]{1,0:T(8,128)(2,1)S(1)}, bf16[16,4096]{1,0:T(8,128)(2,1)S(1)}, u32[]{:S(2)}, u32[]{:S(2)}) %collective-permute-start.5) | collective-permute-done | bytes 131104 | tf_op jit(solution)/shard_map/ppermute | solution.py:422
  36.3 2.3 %collective-permute-done.6.refs_7_ = bf16[16,4096]{1,0:T(8,128)(2,1)S(1)} collective-permute-done((bf16[16,4096]{1,0:T(8,128)(2,1)S(1)}, bf16[16,4096]{1,0:T(8,128)(2,1)S(1)}, u32[]{:S(2)}, u32[]{:S(2)}) %collective-permute-start.6) | collective-permute-done | bytes 131104 | tf_op jit(solution)/shard_map/ppermute | solution.py:422
  38.6 0.0 copy-done
  38.6 0.0 copy-done.2
  38.6 1.2 %shard_map.70 = f32[8,128]{1,0:T(8,128)S(1)} custom-call(f32[8]{0:T(128)S(1)} %copy-done.2, s32[1,1024]{1,0:T(1,128)S(1)} %bitcast.2, bf16[16,4096]{1,0:T(8,128)(2,1)S(1)} %get-tuple-element.24.refs_0_, bf16[16,4096]{1,0:T(8,128)(2,1)S(1)} %collective-permute-done.refs_1_, bf16[16,4096]{1,0:T(8,128)(2,1)S(1)} %collective-permute-done.1.refs_2_, ...), custom_call_target="tpu_custom_call" | custom-call | flops 134217728 | bytes 2097152 | tf_op jit(solution)/shard_map/pallas_call | solution.py:356
  39.9 0.0 collective-permute-start.7
  39.9 1.2 %collective-permute-done.7 = f32[8,128]{1,0:T(8,128)S(1)} collective-permute-done((f32[8,128]{1,0:T(8,128)S(1)}, f32[8,128]{1,0:T(8,128)S(1)}, u32[]{:S(2)}, u32[]{:S(2)}) %collective-permute-start.7) | collective-permute-done | bytes 4128 | tf_op jit(solution)/shard_map/ppermute | solution.py:454
  41.1 2.0 %collective-permute-start.8 = (f32[8,128]{1,0:T(8,128)S(1)}, f32[8,128]{1,0:T(8,128)S(1)}, u32[]{:S(2)}, u32[]{:S(2)}) collective-permute-start(f32[8,128]{1,0:T(8,128)S(1)} %add.6), channel_id=1, source_target_pairs={{0,8},{4,12},{8,0},{12,4},{16,24},{20,28},{24,16},{28,20},{1,9},{5... | collective-permute-start | bytes 12296 | tf_op jit(solution)/shard_map/ppermute | solution.py:454
  43.1 1.6 %collective-permute-done.8 = f32[8,128]{1,0:T(8,128)S(1)} collective-permute-done((f32[8,128]{1,0:T(8,128)S(1)}, f32[8,128]{1,0:T(8,128)S(1)}, u32[]{:S(2)}, u32[]{:S(2)}) %collective-permute-start.8) | collective-permute-done | bytes 4128 | tf_op jit(solution)/shard_map/ppermute | solution.py:454
  44.7 2.1 %collective-permute-start.9 = (f32[8,128]{1,0:T(8,128)S(1)}, f32[8,128]{1,0:T(8,128)S(1)}, u32[]{:S(2)}, u32[]{:S(2)}) collective-permute-start(f32[8,128]{1,0:T(8,128)S(1)} %add.7.a_ref), channel_id=1, source_target_pairs={{0,16},{4,20},{8,24},{12,28},{16,0},{20,4},{24,8},{28,12},{1,17},{... | collective-permute-start | bytes 12296 | tf_op jit(solution)/shard_map/ppermute | solution.py:454
  46.8 1.6 %collective-permute-done.9.b_ref = f32[8,128]{1,0:T(8,128)S(1)} collective-permute-done((f32[8,128]{1,0:T(8,128)S(1)}, f32[8,128]{1,0:T(8,128)S(1)}, u32[]{:S(2)}, u32[]{:S(2)}) %collective-permute-start.9) | collective-permute-done | bytes 4128 | tf_op jit(solution)/shard_map/ppermute | solution.py:454
  48.4 1.8 %shard_map.71 = (f32[8,2,8,8]{3,2,1,0:T(8,128)}, f32[1,8]{1,0:T(1,128)}, f32[8,2,4,1024]{3,2,1,0:T(4,128)}) custom-call(f32[8,128]{1,0:T(8,128)S(1)} %add.7.a_ref, f32[8,128]{1,0:T(8,128)S(1)} %collective-permute-done.9.b_ref, bf16[16,4096]{1,0:T(8,128)(2,1)S(1)} %get-tuple-element.24.refs_0_, bf16[16,4096]{1,0:T(8,128)(2,1)S(1)} %collective-permute-done.refs_1_, ...), custom_call_target="tpu_custom_call" | custom-call | flops 33554432 | bytes 1048576 | tf_op jit(solution)/shard_map/pallas_call | solution.py:356
  (2 shorter events, 0.0 us)
Async XLA Ops:
  0.6 0.7 %copy-start.1 = (s32[32]{0:T(128)S(1)}, s32[32]{0:T(128)}, u32[]{:S(2)}) copy-start(s32[32]{0:T(128)} %freqs.1) | copy-start | bytes 388
  5.8 32.9 %copy-start = (s32[1024]{0:T(1024)S(1)}, s32[1024]{0:T(1024)}, u32[]{:S(2)}) copy-start(s32[1024]{0:T(1024)} %param.6) | copy-start | bytes 12292
  5.8 32.9 %copy-start.2 = (f32[8]{0:T(128)S(1)}, f32[8]{0:T(128)}, u32[]{:S(2)}) copy-start(f32[8]{0:T(128)} %weights.1) | copy-start | bytes 100
  5.8 13.7 %collective-permute-start.3 = (s16[32,4224]{1,0:T(8,128)(2,1)S(1)}, s16[32,4224]{1,0:T(8,128)(2,1)S(1)}, u32[]{:S(2)}, u32[]{:S(2)}) collective-permute-start(s16[32,4224]{1,0:T(8,128)(2,1)S(1)} %get-tuple-element.32), channel_id=1, source_target_pairs={{1,2},{2,1},{3,0},{5,6},{6,5},{7,4},{9,10},{10,9},{11,8},{13,14},{... | collective-permute-start | bytes 811016 | tf_op jit(solution)/shard_map/ppermute | solution.py:404
  7.1 20.2 %collective-permute-start.4 = (s16[32,4224]{1,0:T(8,128)(2,1)S(1)}, s16[32,4224]{1,0:T(8,128)(2,1)S(1)}, u32[]{:S(2)}, u32[]{:S(2)}) collective-permute-start(s16[32,4224]{1,0:T(8,128)(2,1)S(1)} %get-tuple-element.33), channel_id=1, source_target_pairs={{0,1},{2,3},{1,0},{3,2},{4,5},{6,7},{5,4},{7,6},{8,9},{10,11},{9,8... | collective-permute-start | bytes 811016 | tf_op jit(solution)/shard_map/ppermute | solution.py:404
  15.3 14.5 %collective-permute-start = (bf16[16,4096]{1,0:T(8,128)(2,1)S(1)}, bf16[16,4096]{1,0:T(8,128)(2,1)S(1)}, u32[]{:S(2)}, u32[]{:S(2)}) collective-permute-start(bf16[16,4096]{1,0:T(8,128)(2,1)S(1)} %get-tuple-element.25), channel_id=1, source_target_pairs={{0,1},{1,2},{2,3},{3,0},{4,5},{5,6},{6,7},{7,4},{8,9},{9,10},{10,1... | collective-permute-start | bytes 393224 | tf_op jit(solution)/shard_map/ppermute | solution.py:422
  15.3 17.6 %collective-permute-start.1 = (bf16[16,4096]{1,0:T(8,128)(2,1)S(1)}, bf16[16,4096]{1,0:T(8,128)(2,1)S(1)}, u32[]{:S(2)}, u32[]{:S(2)}) collective-permute-start(bf16[16,4096]{1,0:T(8,128)(2,1)S(1)} %get-tuple-element.26), channel_id=1, source_target_pairs={{0,2},{1,3},{2,0},{3,1},{4,6},{5,7},{6,4},{7,5},{8,10},{9,11},{10,... | collective-permute-start | bytes 393224 | tf_op jit(solution)/shard_map/ppermute | solution.py:422
  17.2 15.7 %collective-permute-start.2 = (bf16[16,4096]{1,0:T(8,128)(2,1)S(1)}, bf16[16,4096]{1,0:T(8,128)(2,1)S(1)}, u32[]{:S(2)}, u32[]{:S(2)}) collective-permute-start(bf16[16,4096]{1,0:T(8,128)(2,1)S(1)} %get-tuple-element.27), channel_id=1, source_target_pairs={{0,3},{1,0},{2,1},{3,2},{4,7},{5,4},{6,5},{7,6},{8,11},{9,8},{10,9... | collective-permute-start | bytes 393224 | tf_op jit(solution)/shard_map/ppermute | solution.py:422
  27.7 8.6 %collective-permute-start.5 = (bf16[16,4096]{1,0:T(8,128)(2,1)S(1)}, bf16[16,4096]{1,0:T(8,128)(2,1)S(1)}, u32[]{:S(2)}, u32[]{:S(2)}) collective-permute-start(bf16[16,4096]{1,0:T(8,128)(2,1)S(1)} %get-tuple-element.35), channel_id=1, source_target_pairs={{0,3},{1,0},{2,1},{3,2},{4,7},{5,4},{6,5},{7,6},{8,11},{9,8},{10,9... | collective-permute-start | bytes 393224 | tf_op jit(solution)/shard_map/ppermute | solution.py:422
  27.7 10.9 %collective-permute-start.6 = (bf16[16,4096]{1,0:T(8,128)(2,1)S(1)}, bf16[16,4096]{1,0:T(8,128)(2,1)S(1)}, u32[]{:S(2)}, u32[]{:S(2)}) collective-permute-start(bf16[16,4096]{1,0:T(8,128)(2,1)S(1)} %get-tuple-element.37), channel_id=1, source_target_pairs={{0,1},{1,2},{2,3},{3,0},{4,5},{5,6},{6,7},{7,4},{8,9},{9,10},{10,1... | collective-permute-start | bytes 393224 | tf_op jit(solution)/shard_map/ppermute | solution.py:422
  39.9 1.2 %collective-permute-start.7 = (f32[8,128]{1,0:T(8,128)S(1)}, f32[8,128]{1,0:T(8,128)S(1)}, u32[]{:S(2)}, u32[]{:S(2)}) collective-permute-start(f32[8,128]{1,0:T(8,128)S(1)} %shard_map.70), channel_id=1, source_target_pairs={{0,4},{4,0},{8,12},{12,8},{16,20},{20,16},{24,28},{28,24},{1,5},{5... | collective-permute-start | bytes 12296 | tf_op jit(solution)/shard_map/ppermute | solution.py:454
  41.1 3.6 %collective-permute-start.8 = (f32[8,128]{1,0:T(8,128)S(1)}, f32[8,128]{1,0:T(8,128)S(1)}, u32[]{:S(2)}, u32[]{:S(2)}) collective-permute-start(f32[8,128]{1,0:T(8,128)S(1)} %add.6), channel_id=1, source_target_pairs={{0,8},{4,12},{8,0},{12,4},{16,24},{20,28},{24,16},{28,20},{1,9},{5... | collective-permute-start | bytes 12296 | tf_op jit(solution)/shard_map/ppermute | solution.py:454
  44.7 3.6 %collective-permute-start.9 = (f32[8,128]{1,0:T(8,128)S(1)}, f32[8,128]{1,0:T(8,128)S(1)}, u32[]{:S(2)}, u32[]{:S(2)}) collective-permute-start(f32[8,128]{1,0:T(8,128)S(1)} %add.7.a_ref), channel_id=1, source_target_pairs={{0,16},{4,20},{8,24},{12,28},{16,0},{20,4},{24,8},{28,12},{1,17},{... | collective-permute-start | bytes 12296 | tf_op jit(solution)/shard_map/ppermute | solution.py:454

commit v7 on v6

--- a/solution.py
+++ b/solution.py
@@ -19,6 +19,14 @@
 
 def iota(shape, axis):
     return lax.broadcasted_iota(jnp.int32, shape, axis)
+
+
+def div(x, n):
+    return x >> (n.bit_length() - 1) if n & (n - 1) == 0 else x // n
+
+
+def rem(x, n):
+    return x & (n - 1) if n & (n - 1) == 0 else x % n
 
 
 def mm(a, b):
@@ -66,13 +74,13 @@
     return (real_part, imag_part)
 
 
-def transform_rows(freqs, me, slots, group, start):
+def transform_rows(freqs, me, wanted, slots, group, start):
     count = group // 2
     times = start + iota((count, HALF), 1)
     window = 0.5 - 0.5 * trig(times)[0]
     row = iota((count, HALF), 0)
     out = []
-    for s in range(slots):
+    for s in wanted:
         owner = lax.rem(me + s, slots)
         freq = jnp.zeros((count, HALF), jnp.int32)
         for f in range(count):
@@ -87,9 +95,10 @@
 
 def spread(rows, var_count):
     width = HALF * var_count
-    pick = one_hot(iota((HALF, width), 1) // var_count == iota((HALF, width), 0))
+    lane = iota((1, width), 1)
+    pick = one_hot(div(lane, var_count) == iota((HALF, width), 0))
     wide = mm(rows, pick)
-    owner = iota(wide.shape, 1) % var_count
+    owner = rem(lane, var_count)
     return [jnp.where(owner == v, wide, 0.0).astype(BF16) for v in range(var_count)]
 
 
@@ -102,10 +111,9 @@
     return jnp.concatenate(parts, axis=1)
 
 
-def encode(values, coded):
+def encode(values, largest, coded):
     rows, features = values.shape
-    largest = jnp.max(jnp.abs(values[...]), axis=1, keepdims=True)
-    largest = jnp.maximum(largest, 1e-30)
+    largest = jnp.maximum(jnp.max(largest, axis=1, keepdims=True), 1e-30)
     exponent = jnp.floor(jnp.log2(32000.0 / largest))
     steps = values[...] * jnp.exp2(exponent)
     coded[:, :features] = jnp.round(steps).astype(jnp.int32).astype(jnp.int16)
@@ -120,47 +128,57 @@
     return steps * (1.0 / jnp.exp2(exponent))
 
 
-def halo_kernel(slots, group, var_count, points, freqs, x_hbm, inner, outer, lhs, held, *refs):
-    first, second, sems = refs
-    copies = []
-    for j in range(held.shape[0]):
-        for i in range(2):
-            rows = pl.ds(i * HALF, HALF)
-            copy = pltpu.make_async_copy(
-                x_hbm.at[rows, :, pl.ds(j * LANES, LANES)], held.at[j, rows], sems.at[j, i]
-            )
-            copy.start()
-            copies.append(copy)
+def bins_copy(bins, freqs, sem):
+    return pltpu.make_async_copy(bins, freqs, sem)
+
+
+def halo_kernel(slots, group, var_count, points, bins, x_hbm, inner, outer, held, *refs):
+    freqs, lhs, first, second, bins_sem, sems = refs
+    fetch = bins_copy(bins, freqs, bins_sem)
+    fetch.start()
+    copies = [
+        pltpu.make_async_copy(x_hbm.at[:, :, pl.ds(j * LANES, LANES)], held.at[j], sems.at[j])
+        for j in range(held.shape[0])
+    ]
+    for copy in copies:
+        copy.start()
     me = lax.axis_index("blk")
     odd = lax.rem(me, 2) == 1
-    full = slots * group
-    wide = full // 2
-    rows = [transform_rows(freqs, me, slots, group, start) for start in (0, HALF)]
-    for v, part in enumerate(spread(jnp.concatenate(rows, axis=0), var_count)):
-        lhs[2 * v * full : 2 * (v + 1) * full, :] = part
-
-    def some(low):
-        return jnp.concatenate(
-            [lhs[2 * v * full + low : 2 * v * full + low + wide, :] for v in range(var_count)],
-            axis=0,
-        )
-
+    half_slots = slots // 2
+    wide = half_slots * group
+    fetch.wait()
+    down_rows = transform_rows(freqs, me, range(half_slots, slots), slots, group, HALF)
+    up_rows = transform_rows(freqs, me, range(1, half_slots + 1), slots, group, 0)
+    parts = spread(jnp.concatenate([down_rows, up_rows], axis=0), var_count)
+    size = wide * var_count
+    for v, part in enumerate(parts):
+        lhs[v * wide : (v + 1) * wide, :] = part[:wide]
+        lhs[size + v * wide : size + (v + 1) * wide, :] = part[wide:]
+    most_first = jnp.zeros((wide, 2 * LANES), F32)
+    most_second = most_first
     for j in range(0, held.shape[0], 2):
-        for copy in copies[2 * j : 2 * j + 4]:
-            copy.wait()
-        down = mm(some(full + wide), columns(held, j, 0, var_count))
-        up = mm(some(group), columns(held, j, 1, var_count))
+        copies[j].wait()
+        copies[j + 1].wait()
+        down = mm(lhs[:size, :], columns(held, j, 0, var_count))
+        up = mm(lhs[size:, :], columns(held, j, 1, var_count))
         for v in range(var_count):
             low = v * points + j * LANES
             lower = down[v * wide : (v + 1) * wide]
             upper = up[v * wide : (v + 1) * wide]
-            first[:, low : low + 2 * LANES] = jnp.where(odd, upper, lower)
-            second[:, low : low + 2 * LANES] = jnp.where(odd, lower, upper)
-    encode(first, inner)
-    encode(second, outer)
-
-
-def block_kernel(slots, keep, var_count, points, lhs, held, *outs):
+            mine = jnp.where(odd, upper, lower)
+            other = jnp.where(odd, lower, upper)
+            most_first = jnp.maximum(most_first, jnp.abs(mine))
+            most_second = jnp.maximum(most_second, jnp.abs(other))
+            first[:, low : low + 2 * LANES] = mine
+            second[:, low : low + 2 * LANES] = other
+    encode(first, most_first, inner)
+    encode(second, most_second, outer)
+
+
+def block_kernel(slots, keep, var_count, points, bins, held, *refs):
+    outs, (freqs, lhs, bins_sem) = (refs[:-3], refs[-3:])
+    fetch = bins_copy(bins, freqs, bins_sem)
+    fetch.start()
     half_slots = slots // 2
     even = outs[:slots]
     lead = outs[slots : slots + half_slots]
@@ -168,6 +186,13 @@
     group = even[0].shape[0]
     full = slots * group
     short = full + half_slots * group
+    me = lax.axis_index("blk")
+    fetch.wait()
+    rows = [
+        transform_rows(freqs, me, range(slots), slots, group, start) for start in (0, HALF)
+    ]
+    for v, part in enumerate(spread(jnp.concatenate(rows, axis=0), var_count)):
+        lhs[2 * v * full : 2 * (v + 1) * full, :] = part
 
     def some(v, low, high):
         return lhs[2 * v * full + low : 2 * v * full + high, :]
@@ -227,22 +252,22 @@
     )
     size = blocks * group
     freqs = group // 2
-    same = iota((size, size), 0) % freqs == iota((size, size), 1) % freqs
+    same = rem(iota((size, size), 0), freqs) == rem(iota((1, size), 1), freqs)
     gram = jnp.where(same, gram, 0.0).reshape(blocks, 2, freqs, size)
     rows_re = gram[:, 0].reshape(blocks * freqs, size)
     rows_im = gram[:, 1].reshape(blocks * freqs, size)
     width = 2 * blocks * blocks
-    row, lane = (iota((size, width), 0), iota((size, width), 1))
-    fits = block_of(row // group, me, slots) == lane % blocks
-    row_part = row // freqs % 2
-    lane_part = lane // blocks % 2
+    row, lane = (iota((size, 1), 0), iota((1, width), 1))
+    fits = block_of(div(row, group), me, slots) == rem(lane, blocks)
+    row_part = rem(div(row, freqs), 2)
+    lane_part = rem(div(lane, blocks), 2)
     from_re = one_hot(fits & (row_part == lane_part))
     sign = jnp.where(lane_part == 0, 1.0, -1.0)
     from_im = jnp.where(fits & (row_part != lane_part), sign, 0.0).astype(BF16)
     total = jnp.zeros((blocks * freqs, width), F32)
     for part_re, part_im in zip(split3(rows_re), split3(rows_im)):
         total = total + (mm(part_re, from_re) + mm(part_im, from_im))
-    mine = iota((freqs, width), 1) // (2 * blocks)
+    mine = div(iota((freqs, width), 1), 2 * blocks)
     out = jnp.zeros((freqs, width), F32)
     for b in range(blocks):
         block = block_of(jnp.int32(b), me, slots)
@@ -250,20 +275,23 @@
     packed[...] = out
 
 
-def mode_kernel(slots, var_count, points, scaling, feature_count, a_ref, b_ref, *refs):
+def mode_kernel(slots, var_count, points, scaling, feature_count, sums, *refs):
     csd, eig, modes = refs[-3:]
+    tiles, refs = ([ref[...] for ref in refs[:sums]], refs[sums:])
     blocks = 2 * slots
     me = lax.axis_index("blk")
     spectra = [ref[...] for ref in refs[:-3]]
-    raw = a_ref[...] + b_ref[...]
+    raw = tiles[0] + tiles[1]
+    if sums == 4:
+        raw = raw + (tiles[2] + tiles[3])
     freqs, width = raw.shape
     group = 2 * freqs
     size = blocks * group
     mat = scaling * raw
-    lane_part = iota((freqs, width), 1) // blocks % 2
+    lane_part = rem(div(iota((freqs, width), 1), blocks), 2)
     is_re = lane_part == 0
     gather = one_hot(
-        iota((width, width), 0) // (2 * blocks) == iota((width, width), 1) % blocks
+        div(iota((width, width), 0), 2 * blocks) == rem(iota((1, width), 1), blocks)
     )
 
     def apply(matrix, vec_re, vec_im):
@@ -295,17 +323,17 @@
     out_re, out_im = apply(raw, low_re.astype(F32), low_im.astype(F32))
     normsq = over_blocks(low_re.astype(F32) * out_re + low_im.astype(F32) * out_im)
     scale = jnp.sqrt(jnp.float32(feature_count) / normsq)
-    row, lane = (iota((width, size), 0), iota((width, size), 1))
-    expand = one_hot(row == block_of(lane // group, me, slots))
+    lane = iota((1, size), 1)
+    expand = one_hot(iota((width, size), 0) == block_of(div(lane, group), me, slots))
     wide = mm(jnp.concatenate([vec_re, vec_im], axis=0).astype(BF16), expand)
     wide_re, wide_im = (wide[:freqs], wide[freqs:])
-    part = iota((freqs, size), 1) // freqs % 2
-    mine = iota((freqs, size), 1) % freqs == iota((freqs, size), 0)
+    part = rem(div(lane, freqs), 2)
+    mine = rem(lane, freqs) == iota((freqs, size), 0)
     coef_re = jnp.where(mine, jnp.where(part == 0, wide_re, -wide_im), 0.0)
     coef_im = jnp.where(mine, jnp.where(part == 0, wide_im, wide_re), 0.0)
     rows = 2 * var_count
     upper = iota((rows, size), 0) < var_count
-    var = iota((rows, size), 0) % var_count
+    var = rem(iota((rows, size), 0), var_count)
     tall = []
     for f in range(freqs):
         both = jnp.where(
@@ -330,10 +358,10 @@
         block = phi[f * rows : (f + 1) * rows] * scale[f : f + 1, :]
         for k in range(2):
             modes[f, k] = block[k * var_count : (k + 1) * var_count]
-    tiles = jnp.concatenate(
+    split_rows = jnp.concatenate(
         [
             jnp.where(
-                iota((blocks, width), 1) // (2 * blocks) == iota((blocks, width), 0),
+                div(iota((blocks, width), 1), 2 * blocks) == iota((blocks, width), 0),
                 jnp.broadcast_to(mat[f : f + 1], (blocks, width)),
                 0.0,
             )
@@ -343,9 +371,9 @@
     )
     for k in range(2):
         row, lane = (iota((width, blocks), 0), iota((width, blocks), 1))
-        fold = one_hot(row % (2 * blocks) == lane + k * blocks)
+        fold = one_hot(rem(row, 2 * blocks) == lane + k * blocks)
         got = jnp.zeros((freqs * blocks, blocks), F32)
-        for piece in split3(tiles):
+        for piece in split3(split_rows):
             got = got + mm(piece, fold)
         for f in range(freqs):
             csd[f, k] = got[f * blocks : (f + 1) * blocks]
@@ -380,20 +408,24 @@
 
     wide = half_slots * group
     groups = points // LANES
-    inner, outer, lhs, held = call(
+    bins = pltpu.with_memory_space_constraint(freq_index, pltpu.HBM)
+    bins_smem = pltpu.SMEM(freq_index.shape, jnp.int32)
+    inner, outer, held = call(
         functools.partial(halo_kernel, slots, group, var_count, points),
         [
             shape((wide, features + LANES), jnp.int16),
             shape((wide, features + LANES), jnp.int16),
-            shape((2 * slots * group * var_count, HALF * var_count), BF16),
             shape((groups, row_count, var_count, LANES), BF16),
         ],
-        [smem, hbm],
-        (freq_index, pltpu.with_memory_space_constraint(snapshots, pltpu.HBM)),
+        [hbm, hbm],
+        (bins, pltpu.with_memory_space_constraint(snapshots, pltpu.HBM)),
         [
+            bins_smem,
+            pltpu.VMEM((2 * wide * var_count, HALF * var_count), BF16),
             pltpu.VMEM((wide, features), F32),
             pltpu.VMEM((wide, features), F32),
-            pltpu.SemaphoreType.DMA((groups, 2)),
+            pltpu.SemaphoreType.DMA,
+            pltpu.SemaphoreType.DMA((groups,)),
         ],
         2 * 2 * wide * HALF * features * var_count,
         2 * row_count * features,
@@ -411,9 +443,13 @@
     pieces = call(
         functools.partial(block_kernel, slots, keep, var_count, points),
         [piece] * slots + [wide_piece] * (2 * half_slots),
-        [vmem, vmem],
-        (lhs, held),
-        [],
+        [hbm, vmem],
+        (bins, held),
+        [
+            bins_smem,
+            pltpu.VMEM((2 * slots * group * var_count, HALF * var_count), BF16),
+            pltpu.SemaphoreType.DMA,
+        ],
         2 * 3 * slots * group * HALF * features * var_count,
         2 * row_count * features,
     )
@@ -446,13 +482,19 @@
         4 * blocks * group * features,
     )
     devices = lax.axis_size("pts")
+    def from_peer(x, step):
+        return lax.ppermute(x, "pts", [(i, i ^ step) for i in range(devices)])
+
+    parts = [packed]
     step = 1
-    other = None
     while step < devices:
-        if other is not None:
-            packed = packed + other
-        other = lax.ppermute(packed, "pts", [(i, i ^ step) for i in range(devices)])
-        step *= 2
+        total = functools.reduce(jnp.add, parts[:2])
+        if len(parts) == 4:
+            total = total + (parts[2] + parts[3])
+        by_four = step > 1 and 4 * step <= devices
+        steps = (step, 2 * step, 3 * step) if by_four else (step,)
+        parts = [total] + [from_peer(total, i) for i in steps]
+        step *= 4 if by_four else 2
     total_features = features * devices
     csd, eigval, modes = call(
         functools.partial(
@@ -462,14 +504,15 @@
             points,
             1.0 / (total_features * (3.0 * NFFT / 8.0)),
             total_features,
+            len(parts),
         ),
         [
             shape((freqs, 2, blocks, blocks), F32),
             shape((1, freqs), F32),
             shape((freqs, 2, var_count, points), F32),
         ],
-        [vmem] * (2 + len(spectra)),
-        (packed, other, *spectra),
+        [vmem] * (len(parts) + len(spectra)),
+        (*parts, *spectra),
         [],
         2 * 2 * blocks * group * group * features,
         2 * blocks * group * features,

time: 50.3 us -> 48.8 us (0.970)
  waiting for transfers between devices: 21.3 us -> 20.5 us
  local copies, waits for them, and re-layouts: 0.66 us -> 0.01 us
    ppermute x2, waiting for transfers between devices: 8.1 us -> 7.05 us  [swap(): return lax.ppermute(x, 'blk', pairs + [(b, a) for a, b in pairs] + also)]
    unnamed x6 -> x4, local copies, waits for them, and re-layouts: 0.66 us -> 0.01 us
    ppermute x3 -> x4, starting transfers between devices: 4.15 us -> 3.66 us  [from_peer(): return lax.ppermute(x, 'pts', [(i, i ^ step) for i in range(devices)])]
    ppermute x3 -> x4, waiting for transfers between devices: 4.32 us -> 4.66 us  [from_peer(): return lax.ppermute(x, 'pts', [(i, i ^ step) for i in range(devices)])]
  transfers between devices with their start and end apart: 10 -> 11, of which waited for: 8 -> 8; matrix products, arithmetic and copies ran while one was open for 0% -> 0% of each run, Pallas kernels for 7% -> 9%
where the time goes in v7:
time: 48.8 us; the launch traced here: 48.7 us
  waiting for transfers between devices  20.5 us (42%)
  starting transfers between devices  16.2 us (33%)
  Pallas kernels  11.3 us (23%)
  between operations  0.71 us (1%)
    pallas_call x5, Pallas kernels, call(): pl.pallas_call(kernel, out_shape=outs, in_specs=ins, out_specs=jax.tree.m...  11.3 us
    ppermute x5, waiting for transfers between devices, shift(): return lax.ppermute(x, 'blk', [(i, (i + s) % slots) for i in range(slots)])  8.79 us
    ppermute x2, waiting for transfers between devices, swap(): return lax.ppermute(x, 'blk', pairs + [(b, a) for a, b in pairs] + also)  7.05 us
    ppermute x2, starting transfers between devices, swap(): return lax.ppermute(x, 'blk', pairs + [(b, a) for a, b in pairs] + also)  6.58 us
    ppermute x5, starting transfers between devices, shift(): return lax.ppermute(x, 'blk', [(i, (i + s) % slots) for i in range(slots)])  5.95 us
    ppermute x4, waiting for transfers between devices, from_peer(): return lax.ppermute(x, 'pts', [(i, i ^ step) for i in range(devices)])  4.66 us
    ppermute x4, starting transfers between devices, from_peer(): return lax.ppermute(x, 'pts', [(i, i ^ step) for i in range(devices)])  3.66 us
  transfers between devices with their start and end apart: 11, of which 8 were waited for; matrix products, arithmetic and copies ran while one was open for 0% of the time, Pallas kernels for 9%

profile of v7, /device:TPU:0, one launch (start us, length us, event | category | flops | bytes accessed | tf_op | source)
XLA Modules:
  0.0 48.7 jit_solution(5618581646637788844)
XLA Ops:
  0.6 3.8 %shard_map.67 = (s16[32,4224]{1,0:T(8,128)(2,1)S(1)}, s16[32,4224]{1,0:T(8,128)(2,1)S(1)}, bf16[8,768,4,128]{3,2,1,0:T(4,128)(2,1)S(1)}) custom-call(s32[32]{0:T(128)} %bins.3, bf16[768,4,1024]{2,1,0:T(4,128)(2,1)} %x_hbm.1), custom_call_target="tpu_custom_call" | custom-call | flops 805306368 | bytes 6291456 | tf_op jit(solution)/shard_map/pallas_call | solution.py:384
  4.4 0.0 copy-start
  4.4 0.0 copy-start.1
  4.4 1.3 %collective-permute-start.3 = (s16[32,4224]{1,0:T(8,128)(2,1)S(1)}, s16[32,4224]{1,0:T(8,128)(2,1)S(1)}, u32[]{:S(2)}, u32[]{:S(2)}) collective-permute-start(s16[32,4224]{1,0:T(8,128)(2,1)S(1)} %get-tuple-element.30), channel_id=1, source_target_pairs={{1,2},{2,1},{3,0},{5,6},{6,5},{7,4},{9,10},{10,9},{11,8},{13,14},{... | collective-permute-start | bytes 811016 | tf_op jit(solution)/shard_map/ppermute | solution.py:436
  5.7 5.3 %collective-permute-start.4 = (s16[32,4224]{1,0:T(8,128)(2,1)S(1)}, s16[32,4224]{1,0:T(8,128)(2,1)S(1)}, u32[]{:S(2)}, u32[]{:S(2)}) collective-permute-start(s16[32,4224]{1,0:T(8,128)(2,1)S(1)} %get-tuple-element.31), channel_id=1, source_target_pairs={{0,1},{2,3},{1,0},{3,2},{4,5},{6,7},{5,4},{7,6},{8,9},{10,11},{9,8... | collective-permute-start | bytes 811016 | tf_op jit(solution)/shard_map/ppermute | solution.py:436
  11.0 4.0 %shard_map.68 = (bf16[16,4096]{1,0:T(8,128)(2,1)S(1)}, bf16[16,4096]{1,0:T(8,128)(2,1)S(1)}, bf16[16,4096]{1,0:T(8,128)(2,1)S(1)}, bf16[16,4096]{1,0:T(8,128)(2,...) custom-call(s32[32]{0:T(128)} %bins.3, ...), custom_call_target="tpu_custom_call" | custom-call | flops 2415919104 | bytes 6291456 | tf_op jit(solution)/shard_map/pallas_call | solution.py:384
  15.0 0.1 collective-permute-start
  15.1 1.9 %collective-permute-start.1 = (bf16[16,4096]{1,0:T(8,128)(2,1)S(1)}, bf16[16,4096]{1,0:T(8,128)(2,1)S(1)}, u32[]{:S(2)}, u32[]{:S(2)}) collective-permute-start(bf16[16,4096]{1,0:T(8,128)(2,1)S(1)} %get-tuple-element.24), channel_id=1, source_target_pairs={{0,2},{1,3},{2,0},{3,1},{4,6},{5,7},{6,4},{7,5},{8,10},{9,11},{10,... | collective-permute-start | bytes 393224 | tf_op jit(solution)/shard_map/ppermute | solution.py:458
  17.0 1.9 %collective-permute-start.2 = (bf16[16,4096]{1,0:T(8,128)(2,1)S(1)}, bf16[16,4096]{1,0:T(8,128)(2,1)S(1)}, u32[]{:S(2)}, u32[]{:S(2)}) collective-permute-start(bf16[16,4096]{1,0:T(8,128)(2,1)S(1)} %get-tuple-element.25), channel_id=1, source_target_pairs={{0,3},{1,0},{2,1},{3,2},{4,7},{5,4},{6,5},{7,6},{8,11},{9,8},{10,9... | collective-permute-start | bytes 393224 | tf_op jit(solution)/shard_map/ppermute | solution.py:458
  18.9 0.0 collective-permute-done.3.refs_4_
  18.9 7.0 %collective-permute-done.4.refs_5_ = s16[32,4224]{1,0:T(8,128)(2,1)S(1)} collective-permute-done((s16[32,4224]{1,0:T(8,128)(2,1)S(1)}, s16[32,4224]{1,0:T(8,128)(2,1)S(1)}, u32[]{:S(2)}, u32[]{:S(2)}) %collective-permute-start.4) | collective-permute-done | bytes 270368 | tf_op jit(solution)/shard_map/ppermute | solution.py:436
  26.0 0.4 shard_map.69
  26.4 0.1 collective-permute-start.5
  26.5 2.0 %collective-permute-start.6 = (bf16[16,4096]{1,0:T(8,128)(2,1)S(1)}, bf16[16,4096]{1,0:T(8,128)(2,1)S(1)}, u32[]{:S(2)}, u32[]{:S(2)}) collective-permute-start(bf16[16,4096]{1,0:T(8,128)(2,1)S(1)} %get-tuple-element.35), channel_id=1, source_target_pairs={{0,1},{1,2},{2,3},{3,0},{4,5},{5,6},{6,7},{7,4},{8,9},{9,10},{10,1... | collective-permute-start | bytes 393224 | tf_op jit(solution)/shard_map/ppermute | solution.py:458
  28.5 0.0 collective-permute-done.refs_1_.refs_5_
  28.5 3.1 %collective-permute-done.1.refs_2_.refs_6_ = bf16[16,4096]{1,0:T(8,128)(2,1)S(1)} collective-permute-done((bf16[16,4096]{1,0:T(8,128)(2,1)S(1)}, bf16[16,4096]{1,0:T(8,128)(2,1)S(1)}, u32[]{:S(2)}, u32[]{:S(2)}) %collective-permute-start.1) | collective-permute-done | bytes 131104 | tf_op jit(solution)/shard_map/ppermute | solution.py:458
  31.6 0.0 collective-permute-done.2.refs_3_.refs_7_
  31.6 3.3 %collective-permute-done.5.refs_5_.refs_9_ = bf16[16,4096]{1,0:T(8,128)(2,1)S(1)} collective-permute-done((bf16[16,4096]{1,0:T(8,128)(2,1)S(1)}, bf16[16,4096]{1,0:T(8,128)(2,1)S(1)}, u32[]{:S(2)}, u32[]{:S(2)}) %collective-permute-start.5) | collective-permute-done | bytes 131104 | tf_op jit(solution)/shard_map/ppermute | solution.py:458
  34.9 2.3 %collective-permute-done.6.refs_7_.refs_11_ = bf16[16,4096]{1,0:T(8,128)(2,1)S(1)} collective-permute-done((bf16[16,4096]{1,0:T(8,128)(2,1)S(1)}, bf16[16,4096]{1,0:T(8,128)(2,1)S(1)}, u32[]{:S(2)}, u32[]{:S(2)}) %collective-permute-start.6) | collective-permute-done | bytes 131104 | tf_op jit(solution)/shard_map/ppermute | solution.py:458
  37.3 0.0 copy-done
  37.3 0.0 copy-done.1
  37.3 1.2 %shard_map.70 = f32[8,128]{1,0:T(8,128)S(1)} custom-call(f32[8]{0:T(128)S(1)} %copy-done.1, s32[1,1024]{1,0:T(1,128)S(1)} %bitcast.2, bf16[16,4096]{1,0:T(8,128)(2,1)S(1)} %get-tuple-element.22.refs_0_.refs_4_, bf16[16,4096]{1,0:T(8,128)(2,1)S(1)} %collective-permute-done.refs_1_.refs_5_, bf16[16,4096]{1,0:T(8,128)(2,1)S(1)} %collective-permute-done.1.refs_2_.refs_6_, ...), custom_call_target="tpu_custom_call" | custom-call | flops 134217728 | bytes 2097152 | tf_op jit(solution)/shard_map/pallas_call | solution.py:384
  38.5 0.1 collective-permute-start.7
  38.6 1.2 %collective-permute-done.7 = f32[8,128]{1,0:T(8,128)S(1)} collective-permute-done((f32[8,128]{1,0:T(8,128)S(1)}, f32[8,128]{1,0:T(8,128)S(1)}, u32[]{:S(2)}, u32[]{:S(2)}) %collective-permute-start.7) | collective-permute-done | bytes 4128 | tf_op jit(solution)/shard_map/ppermute | solution.py:486
  39.7 3.0 %collective-permute-start.10 = (f32[8,128]{1,0:T(8,128)S(1)}, f32[8,128]{1,0:T(8,128)S(1)}, u32[]{:S(2)}, u32[]{:S(2)}) collective-permute-start(f32[8,128]{1,0:T(8,128)S(1)} %add.3.refs_0_), channel_id=1, source_target_pairs={{0,24},{4,28},{8,16},{12,20},{16,8},{20,12},{24,0},{28,4},{1,25},{... | collective-permute-start | bytes 12296 | tf_op jit(solution)/shard_map/ppermute | solution.py:486
  42.8 0.5 collective-permute-start.9
  43.2 0.1 collective-permute-start.8
  43.3 1.0 %collective-permute-done.10.refs_3_ = f32[8,128]{1,0:T(8,128)S(1)} collective-permute-done((f32[8,128]{1,0:T(8,128)S(1)}, f32[8,128]{1,0:T(8,128)S(1)}, u32[]{:S(2)}, u32[]{:S(2)}) %collective-permute-start.10) | collective-permute-done | bytes 4128 | tf_op jit(solution)/shard_map/ppermute | solution.py:486
  44.3 2.0 %collective-permute-done.9.refs_2_ = f32[8,128]{1,0:T(8,128)S(1)} collective-permute-done((f32[8,128]{1,0:T(8,128)S(1)}, f32[8,128]{1,0:T(8,128)S(1)}, u32[]{:S(2)}, u32[]{:S(2)}) %collective-permute-start.9) | collective-permute-done | bytes 4128 | tf_op jit(solution)/shard_map/ppermute | solution.py:486
  46.4 0.5 collective-permute-done.8.refs_1_
  46.8 1.8 %shard_map.71 = (f32[8,2,8,8]{3,2,1,0:T(8,128)}, f32[1,8]{1,0:T(1,128)}, f32[8,2,4,1024]{3,2,1,0:T(4,128)}) custom-call(f32[8,128]{1,0:T(8,128)S(1)} %add.3.refs_0_, f32[8,128]{1,0:T(8,128)S(1)} %collective-permute-done.8.refs_1_, f32[8,128]{1,0:T(8,128)S(1)} %collective-permute-done.9.refs_2_, f32[8,128]{1,0:T(8,128)S(1)} %collective-permute-done.10.refs_3_, ...), custom_call_target="tpu_custom_call" | custom-call | flops 33554432 | bytes 1048576 | tf_op jit(solution)/shard_map/pallas_call | solution.py:384
  (1 shorter events, 0.0 us)
Async XLA Ops:
  4.4 32.9 %copy-start = (s32[1024]{0:T(1024)S(1)}, s32[1024]{0:T(1024)}, u32[]{:S(2)}) copy-start(s32[1024]{0:T(1024)} %param.6) | copy-start | bytes 12292
  4.4 32.9 %copy-start.1 = (f32[8]{0:T(128)S(1)}, f32[8]{0:T(128)}, u32[]{:S(2)}) copy-start(f32[8]{0:T(128)} %weights.1) | copy-start | bytes 100
  4.4 14.5 %collective-permute-start.3 = (s16[32,4224]{1,0:T(8,128)(2,1)S(1)}, s16[32,4224]{1,0:T(8,128)(2,1)S(1)}, u32[]{:S(2)}, u32[]{:S(2)}) collective-permute-start(s16[32,4224]{1,0:T(8,128)(2,1)S(1)} %get-tuple-element.30), channel_id=1, source_target_pairs={{1,2},{2,1},{3,0},{5,6},{6,5},{7,4},{9,10},{10,9},{11,8},{13,14},{... | collective-permute-start | bytes 811016 | tf_op jit(solution)/shard_map/ppermute | solution.py:436
  5.7 20.2 %collective-permute-start.4 = (s16[32,4224]{1,0:T(8,128)(2,1)S(1)}, s16[32,4224]{1,0:T(8,128)(2,1)S(1)}, u32[]{:S(2)}, u32[]{:S(2)}) collective-permute-start(s16[32,4224]{1,0:T(8,128)(2,1)S(1)} %get-tuple-element.31), channel_id=1, source_target_pairs={{0,1},{2,3},{1,0},{3,2},{4,5},{6,7},{5,4},{7,6},{8,9},{10,11},{9,8... | collective-permute-start | bytes 811016 | tf_op jit(solution)/shard_map/ppermute | solution.py:436
  15.0 13.4 %collective-permute-start = (bf16[16,4096]{1,0:T(8,128)(2,1)S(1)}, bf16[16,4096]{1,0:T(8,128)(2,1)S(1)}, u32[]{:S(2)}, u32[]{:S(2)}) collective-permute-start(bf16[16,4096]{1,0:T(8,128)(2,1)S(1)} %get-tuple-element.23), channel_id=1, source_target_pairs={{0,1},{1,2},{2,3},{3,0},{4,5},{5,6},{6,7},{7,4},{8,9},{9,10},{10,1... | collective-permute-start | bytes 393224 | tf_op jit(solution)/shard_map/ppermute | solution.py:458
  15.1 16.5 %collective-permute-start.1 = (bf16[16,4096]{1,0:T(8,128)(2,1)S(1)}, bf16[16,4096]{1,0:T(8,128)(2,1)S(1)}, u32[]{:S(2)}, u32[]{:S(2)}) collective-permute-start(bf16[16,4096]{1,0:T(8,128)(2,1)S(1)} %get-tuple-element.24), channel_id=1, source_target_pairs={{0,2},{1,3},{2,0},{3,1},{4,6},{5,7},{6,4},{7,5},{8,10},{9,11},{10,... | collective-permute-start | bytes 393224 | tf_op jit(solution)/shard_map/ppermute | solution.py:458
  17.0 14.6 %collective-permute-start.2 = (bf16[16,4096]{1,0:T(8,128)(2,1)S(1)}, bf16[16,4096]{1,0:T(8,128)(2,1)S(1)}, u32[]{:S(2)}, u32[]{:S(2)}) collective-permute-start(bf16[16,4096]{1,0:T(8,128)(2,1)S(1)} %get-tuple-element.25), channel_id=1, source_target_pairs={{0,3},{1,0},{2,1},{3,2},{4,7},{5,4},{6,5},{7,6},{8,11},{9,8},{10,9... | collective-permute-start | bytes 393224 | tf_op jit(solution)/shard_map/ppermute | solution.py:458
  26.4 8.5 %collective-permute-start.5 = (bf16[16,4096]{1,0:T(8,128)(2,1)S(1)}, bf16[16,4096]{1,0:T(8,128)(2,1)S(1)}, u32[]{:S(2)}, u32[]{:S(2)}) collective-permute-start(bf16[16,4096]{1,0:T(8,128)(2,1)S(1)} %get-tuple-element.33), channel_id=1, source_target_pairs={{0,3},{1,0},{2,1},{3,2},{4,7},{5,4},{6,5},{7,6},{8,11},{9,8},{10,9... | collective-permute-start | bytes 393224 | tf_op jit(solution)/shard_map/ppermute | solution.py:458
  26.5 10.8 %collective-permute-start.6 = (bf16[16,4096]{1,0:T(8,128)(2,1)S(1)}, bf16[16,4096]{1,0:T(8,128)(2,1)S(1)}, u32[]{:S(2)}, u32[]{:S(2)}) collective-permute-start(bf16[16,4096]{1,0:T(8,128)(2,1)S(1)} %get-tuple-element.35), channel_id=1, source_target_pairs={{0,1},{1,2},{2,3},{3,0},{4,5},{5,6},{6,7},{7,4},{8,9},{9,10},{10,1... | collective-permute-start | bytes 393224 | tf_op jit(solution)/shard_map/ppermute | solution.py:458
  38.5 1.2 %collective-permute-start.7 = (f32[8,128]{1,0:T(8,128)S(1)}, f32[8,128]{1,0:T(8,128)S(1)}, u32[]{:S(2)}, u32[]{:S(2)}) collective-permute-start(f32[8,128]{1,0:T(8,128)S(1)} %shard_map.70), channel_id=1, source_target_pairs={{0,4},{4,0},{8,12},{12,8},{16,20},{20,16},{24,28},{28,24},{1,5},{5... | collective-permute-start | bytes 12296 | tf_op jit(solution)/shard_map/ppermute | solution.py:486
  39.7 4.6 %collective-permute-start.10 = (f32[8,128]{1,0:T(8,128)S(1)}, f32[8,128]{1,0:T(8,128)S(1)}, u32[]{:S(2)}, u32[]{:S(2)}) collective-permute-start(f32[8,128]{1,0:T(8,128)S(1)} %add.3.refs_0_), channel_id=1, source_target_pairs={{0,24},{4,28},{8,16},{12,20},{16,8},{20,12},{24,0},{28,4},{1,25},{... | collective-permute-start | bytes 12296 | tf_op jit(solution)/shard_map/ppermute | solution.py:486
  42.8 3.6 %collective-permute-start.9 = (f32[8,128]{1,0:T(8,128)S(1)}, f32[8,128]{1,0:T(8,128)S(1)}, u32[]{:S(2)}, u32[]{:S(2)}) collective-permute-start(f32[8,128]{1,0:T(8,128)S(1)} %add.3.refs_0_), channel_id=1, source_target_pairs={{0,16},{4,20},{8,24},{12,28},{16,0},{20,4},{24,8},{28,12},{1,17},{... | collective-permute-start | bytes 12296 | tf_op jit(solution)/shard_map/ppermute | solution.py:486
  43.2 3.6 %collective-permute-start.8 = (f32[8,128]{1,0:T(8,128)S(1)}, f32[8,128]{1,0:T(8,128)S(1)}, u32[]{:S(2)}, u32[]{:S(2)}) collective-permute-start(f32[8,128]{1,0:T(8,128)S(1)} %add.3.refs_0_), channel_id=1, source_target_pairs={{0,8},{4,12},{8,0},{12,4},{16,24},{20,28},{24,16},{28,20},{1,9},{5... | collective-permute-start | bytes 12296 | tf_op jit(solution)/shard_map/ppermute | solution.py:486

commit v8 on v7

--- a/solution.py
+++ b/solution.py
@@ -102,13 +102,18 @@
     return [jnp.where(owner == v, wide, 0.0).astype(BF16) for v in range(var_count)]
 
 
-def columns(held, j, half, var_count):
+def columns(held, j, var_count):
     rows = HALF * var_count
-    parts = [
-        held.at[j + i].reshape(2 * rows, LANES)[half * rows : (half + 1) * rows, :]
-        for i in range(2)
+    parts = [held.at[j + i].reshape(rows, LANES)[...] for i in range(2)]
+    return jnp.concatenate(parts, axis=1)
+
+
+def load_copies(x_hbm, half, held, sems):
+    rows = pl.ds(half * HALF, HALF)
+    return [
+        pltpu.make_async_copy(x_hbm.at[rows, :, pl.ds(j * LANES, LANES)], held.at[j], sems.at[j])
+        for j in range(held.shape[0])
     ]
-    return jnp.concatenate(parts, axis=1)
 
 
 def encode(values, largest, coded):
@@ -132,109 +137,132 @@
     return pltpu.make_async_copy(bins, freqs, sem)
 
 
-def halo_kernel(slots, group, var_count, points, bins, x_hbm, inner, outer, held, *refs):
-    freqs, lhs, first, second, bins_sem, sems = refs
+def inner_kernel(slots, group, var_count, points, bins, x_hbm, inner, near, *refs):
+    freqs, lhs, raw, bins_sem, sems = refs
     fetch = bins_copy(bins, freqs, bins_sem)
     fetch.start()
-    copies = [
-        pltpu.make_async_copy(x_hbm.at[:, :, pl.ds(j * LANES, LANES)], held.at[j], sems.at[j])
-        for j in range(held.shape[0])
-    ]
+    me = lax.axis_index("blk")
+    odd = lax.rem(me, 2)
+    copies = load_copies(x_hbm, odd, near, sems)
     for copy in copies:
         copy.start()
-    me = lax.axis_index("blk")
-    odd = lax.rem(me, 2) == 1
     half_slots = slots // 2
     wide = half_slots * group
+    first = jnp.where(odd == 1, 1, half_slots)
     fetch.wait()
-    down_rows = transform_rows(freqs, me, range(half_slots, slots), slots, group, HALF)
-    up_rows = transform_rows(freqs, me, range(1, half_slots + 1), slots, group, 0)
-    parts = spread(jnp.concatenate([down_rows, up_rows], axis=0), var_count)
-    size = wide * var_count
-    for v, part in enumerate(parts):
-        lhs[v * wide : (v + 1) * wide, :] = part[:wide]
-        lhs[size + v * wide : size + (v + 1) * wide, :] = part[wide:]
-    most_first = jnp.zeros((wide, 2 * LANES), F32)
-    most_second = most_first
-    for j in range(0, held.shape[0], 2):
+    wanted = [first + i for i in range(half_slots)]
+    rows = transform_rows(freqs, me, wanted, slots, group, (1 - odd) * HALF)
+    for v, part in enumerate(spread(rows, var_count)):
+        lhs[v * wide : (v + 1) * wide, :] = part
+    most = jnp.zeros((wide, 2 * LANES), F32)
+    for j in range(0, near.shape[0], 2):
         copies[j].wait()
         copies[j + 1].wait()
-        down = mm(lhs[:size, :], columns(held, j, 0, var_count))
-        up = mm(lhs[size:, :], columns(held, j, 1, var_count))
+        got = mm(lhs[...], columns(near, j, var_count))
         for v in range(var_count):
             low = v * points + j * LANES
-            lower = down[v * wide : (v + 1) * wide]
-            upper = up[v * wide : (v + 1) * wide]
-            mine = jnp.where(odd, upper, lower)
-            other = jnp.where(odd, lower, upper)
-            most_first = jnp.maximum(most_first, jnp.abs(mine))
-            most_second = jnp.maximum(most_second, jnp.abs(other))
-            first[:, low : low + 2 * LANES] = mine
-            second[:, low : low + 2 * LANES] = other
-    encode(first, most_first, inner)
-    encode(second, most_second, outer)
-
-
-def block_kernel(slots, keep, var_count, points, bins, held, *refs):
-    outs, (freqs, lhs, bins_sem) = (refs[:-3], refs[-3:])
+            mine = got[v * wide : (v + 1) * wide]
+            most = jnp.maximum(most, jnp.abs(mine))
+            raw[:, low : low + 2 * LANES] = mine
+    encode(raw, most, inner)
+
+
+def block_kernel(slots, keep, group, var_count, points, bins, x_hbm, near, *refs):
+    outs, (freqs, lhs, far, raw, bins_sem, sems) = (refs[:-6], refs[-6:])
     fetch = bins_copy(bins, freqs, bins_sem)
     fetch.start()
+    me = lax.axis_index("blk")
+    odd = lax.rem(me, 2)
+    copies = load_copies(x_hbm, 1 - odd, far, sems)
+    for copy in copies:
+        copy.start()
     half_slots = slots // 2
-    even = outs[:slots]
-    lead = outs[slots : slots + half_slots]
-    trail = outs[slots + half_slots :]
-    group = even[0].shape[0]
+    outer = outs[0]
+    even = outs[1 : 1 + slots]
+    lead = outs[1 + slots : 1 + slots + half_slots]
+    trail = outs[1 + slots + half_slots :]
     full = slots * group
     short = full + half_slots * group
-    me = lax.axis_index("blk")
     fetch.wait()
     rows = [
-        transform_rows(freqs, me, range(slots), slots, group, start) for start in (0, HALF)
+        transform_rows(freqs, me, range(slots), slots, group, start * HALF)
+        for start in (odd, 1 - odd)
     ]
     for v, part in enumerate(spread(jnp.concatenate(rows, axis=0), var_count)):
         lhs[2 * v * full : 2 * (v + 1) * full, :] = part
-
-    def some(v, low, high):
-        return lhs[2 * v * full + low : 2 * v * full + high, :]
-
-    for j in range(0, held.shape[0], 2):
-        parts = [some(v, 0, short) for v in range(var_count)]
-        first = mm(jnp.concatenate(parts, axis=0), columns(held, j, 0, var_count))
-        parts = []
-        for v in range(var_count):
-            parts.append(some(v, full, 2 * full))
-            parts.extend(some(v, s * group, (s + 1) * group) for s in keep)
-        second = mm(jnp.concatenate(parts, axis=0), columns(held, j, 1, var_count))
+    is_odd = odd == 1
+    near_parts = []
+    far_parts = []
+    for v in range(var_count):
+        base = 2 * v * full
+        near_parts.append((base, full))
+        for i, s in enumerate(keep):
+            slot = jnp.where(is_odd, s, i)
+            near_parts.append((pl.multiple_of(base + full + slot * group, group), group))
+        far_parts.append((base + full, full))
+        far_parts.append((base, full))
+
+    def rows_of(parts):
+        return jnp.concatenate([lhs[pl.ds(low, size), :] for low, size in parts], axis=0)
+
+    most = jnp.zeros((half_slots * group, 2 * LANES), F32)
+    for j in range(0, far.shape[0], 2):
+        from_near = mm(rows_of(near_parts), columns(near, j, var_count))
+        copies[j].wait()
+        copies[j + 1].wait()
+        from_far = mm(rows_of(far_parts), columns(far, j, var_count))
         for v in range(var_count):
             low = v * points + j * LANES
             high = low + 2 * LANES
-            top = first[v * short : (v + 1) * short]
-            bottom = second[v * short : (v + 1) * short]
+            top = from_near[v * short : (v + 1) * short]
+            bottom = from_far[2 * v * full : 2 * (v + 1) * full]
             whole = (top[:full] + bottom[:full]).astype(BF16)
+            other = bottom[full:]
             for s in range(slots):
                 even[s][:, low:high] = whole[s * group : (s + 1) * group]
-            for i in range(half_slots):
-                rows = slice(full + i * group, full + (i + 1) * group)
-                lead[i][:, low:high] = bottom[rows]
-                trail[i][:, low:high] = top[rows]
-
-
-def join_kernel(half_slots, group, *refs):
+            for i, s in enumerate(keep):
+                mine = top[full + i * group : full + (i + 1) * group]
+                begun = other[s * group : (s + 1) * group]
+                ended = other[i * group : (i + 1) * group]
+                lead[i][:, low:high] = jnp.where(is_odd, mine, begun)
+                trail[i][:, low:high] = jnp.where(is_odd, ended, mine)
+            sent = jnp.where(
+                is_odd, other[half_slots * group :], other[group : (half_slots + 1) * group]
+            )
+            most = jnp.maximum(most, jnp.abs(sent))
+            raw[:, low:high] = sent
+    encode(raw, most, outer)
+
+
+def inner_join_kernel(half_slots, group, *refs):
     lead = refs[:half_slots]
     trail = refs[half_slots : 2 * half_slots]
-    inner, outer = refs[2 * half_slots : 2 * half_slots + 2]
-    outs = refs[2 * half_slots + 2 :]
+    inner = refs[2 * half_slots]
+    joined = refs[2 * half_slots + 1 :]
     me = lax.axis_index("blk")
     odd = lax.rem(me, 2) == 1
     for i in range(half_slots):
         above = (i + half_slots - 1) % half_slots
-        rows = (above * group, (above + 1) * group)
-        from_above = jnp.where(odd, decode(inner, *rows), decode(outer, *rows))
-        outs[i][...] = (lead[i][...] + from_above).astype(BF16)
-        rows = (i * group, (i + 1) * group)
-        from_below = jnp.where(odd, decode(outer, *rows), decode(inner, *rows))
+        begun = lead[i][...] + decode(inner, above * group, (above + 1) * group)
         own = jnp.where(me == 0, 0.0, trail[i][...])
-        outs[half_slots + i][...] = (own + from_below).astype(BF16)
+        ended = own + decode(inner, i * group, (i + 1) * group)
+        joined[i][...] = jnp.where(odd, begun, ended).astype(BF16)
+
+
+def outer_join_kernel(half_slots, group, *refs):
+    lead = refs[:half_slots]
+    trail = refs[half_slots : 2 * half_slots]
+    outer = refs[2 * half_slots]
+    joined = refs[2 * half_slots + 1 : 3 * half_slots + 1]
+    outs = refs[3 * half_slots + 1 :]
+    odd = lax.rem(lax.axis_index("blk"), 2) == 1
+    for i in range(half_slots):
+        above = (i + half_slots - 1) % half_slots
+        begun = lead[i][...] + decode(outer, above * group, (above + 1) * group)
+        ended = trail[i][...] + decode(outer, i * group, (i + 1) * group)
+        other = jnp.where(odd, ended, begun).astype(BF16)
+        outs[i][...] = jnp.where(odd, joined[i][...], other)
+        outs[half_slots + i][...] = jnp.where(odd, other, joined[i][...])
 
 
 def gram_kernel(slots, group, var_count, points, weights, classes, *refs):
@@ -410,71 +438,77 @@
     groups = points // LANES
     bins = pltpu.with_memory_space_constraint(freq_index, pltpu.HBM)
     bins_smem = pltpu.SMEM(freq_index.shape, jnp.int32)
-    inner, outer, held = call(
-        functools.partial(halo_kernel, slots, group, var_count, points),
-        [
-            shape((wide, features + LANES), jnp.int16),
-            shape((wide, features + LANES), jnp.int16),
-            shape((groups, row_count, var_count, LANES), BF16),
-        ],
+    source = pltpu.with_memory_space_constraint(snapshots, pltpu.HBM)
+    half_block = (groups, HALF, var_count, LANES)
+    payload = shape((wide, features + LANES), jnp.int16)
+    width = HALF * var_count
+    sems = [pltpu.SemaphoreType.DMA, pltpu.SemaphoreType.DMA((groups,))]
+    raw = pltpu.VMEM((wide, features), F32)
+    inner, near = call(
+        functools.partial(inner_kernel, slots, group, var_count, points),
+        [payload, shape(half_block, BF16)],
         [hbm, hbm],
-        (bins, pltpu.with_memory_space_constraint(snapshots, pltpu.HBM)),
-        [
-            bins_smem,
-            pltpu.VMEM((2 * wide * var_count, HALF * var_count), BF16),
-            pltpu.VMEM((wide, features), F32),
-            pltpu.VMEM((wide, features), F32),
-            pltpu.SemaphoreType.DMA,
-            pltpu.SemaphoreType.DMA((groups,)),
-        ],
-        2 * 2 * wide * HALF * features * var_count,
-        2 * row_count * features,
+        (bins, source),
+        [bins_smem, pltpu.VMEM((wide * var_count, width), BF16), raw, *sems],
+        2 * wide * features * width,
+        row_count * features,
     )
 
     def swap(x, first, also):
         pairs = [(i, i + 1) for i in range(first, slots - 1, 2)]
         return lax.ppermute(x, "blk", pairs + [(b, a) for a, b in pairs] + also)
 
-    from_outer = swap(outer, 0, [])
-    swapped = (swap(inner, 1, [(slots - 1, 0)]), from_outer)
     keep = [0] + list(range(half_slots + 1, slots))
     piece = shape((group, features), BF16)
     wide_piece = shape((group, features), F32)
-    pieces = call(
-        functools.partial(block_kernel, slots, keep, var_count, points),
-        [piece] * slots + [wide_piece] * (2 * half_slots),
-        [hbm, vmem],
-        (bins, held),
+    outer, *pieces = call(
+        functools.partial(block_kernel, slots, keep, group, var_count, points),
+        [payload] + [piece] * slots + [wide_piece] * (2 * half_slots),
+        [hbm, hbm, vmem],
+        (bins, source, near),
         [
             bins_smem,
-            pltpu.VMEM((2 * slots * group * var_count, HALF * var_count), BF16),
-            pltpu.SemaphoreType.DMA,
+            pltpu.VMEM((2 * slots * group * var_count, width), BF16),
+            pltpu.VMEM(half_block, BF16),
+            raw,
+            *sems,
         ],
-        2 * 3 * slots * group * HALF * features * var_count,
-        2 * row_count * features,
-    )
+        2 * 4 * slots * group * features * width,
+        row_count * features,
+    )
+    from_outer = swap(outer, 0, [])
+    from_inner = swap(inner, 1, [(slots - 1, 0)])
 
     def shift(x, s):
         return lax.ppermute(x, "blk", [(i, (i + s) % slots) for i in range(slots)])
 
     even = [pieces[0]] + [shift(pieces[s], s) for s in range(1, slots)]
-    odd = call(
-        functools.partial(join_kernel, half_slots, group),
-        [piece] * slots,
-        [vmem] * (slots + 2),
-        (*pieces[slots:], *swapped),
+    halves = pieces[slots:]
+    joined = call(
+        functools.partial(inner_join_kernel, half_slots, group),
+        [piece] * half_slots,
+        [vmem] * (slots + 1),
+        (*halves, from_inner),
         [],
         slots * group * features,
         10 * slots * group * features,
     )
-
+    odd = call(
+        functools.partial(outer_join_kernel, half_slots, group),
+        [piece] * slots,
+        [vmem] * (slots + half_slots + 1),
+        (*halves, from_outer, *joined),
+        [],
+        slots * group * features,
+        10 * slots * group * features,
+    )
     above = [odd[0]] + [shift(odd[i], s) for i, s in enumerate(keep) if i]
     under = [odd[half_slots]] + [shift(odd[half_slots + i], i) for i in range(1, half_slots)]
-    width = 2 * blocks * blocks
+    tile = 2 * blocks * blocks
     spectra = (*even, *above, *under)
     packed = call(
         functools.partial(gram_kernel, slots, group, var_count, points),
-        shape((freqs, width), F32),
+        shape((freqs, tile), F32),
         [smem, vmem] + [vmem] * len(spectra),
         (class_weight, weight_class.reshape(1, points), *spectra),
         [],

time: 48.8 us -> 48.7 us (level)
  Pallas kernels: 11.3 us -> 12.7 us
  waiting for transfers between devices: 20.5 us -> 19.1 us
    ppermute x5, waiting for transfers between devices: 8.79 us -> 6.9 us  [shift(): return lax.ppermute(x, 'blk', [(i, (i + s) % slots) for i in range(slots)])]
    pallas_call x5 -> x6, Pallas kernels: 11.3 us -> 12.7 us  [call(): pl.pallas_call(kernel, out_shape=outs, in_specs=ins, out_specs=jax.tree.m...]
    ppermute x2, waiting for transfers between devices: 7.05 us -> 8 us  [swap(): return lax.ppermute(x, 'blk', pairs + [(b, a) for a, b in pairs] + also)]
  transfers between devices with their start and end apart: 11 -> 11, of which waited for: 8 -> 8; matrix products, arithmetic and copies ran while one was open for 0% -> 0% of each run, Pallas kernels for 9% -> 14%
where the time goes in v8:
time: 48.7 us; the launch traced here: 48.5 us
  waiting for transfers between devices  19.1 us (39%)
  starting transfers between devices  16 us (33%)
  Pallas kernels  12.7 us (26%)
  between operations  0.71 us (1%)
    pallas_call x6, Pallas kernels, call(): pl.pallas_call(kernel, out_shape=outs, in_specs=ins, out_specs=jax.tree.m...  12.7 us
    ppermute x2, waiting for transfers between devices, swap(): return lax.ppermute(x, 'blk', pairs + [(b, a) for a, b in pairs] + also)  8 us
    ppermute x5, waiting for transfers between devices, shift(): return lax.ppermute(x, 'blk', [(i, (i + s) % slots) for i in range(slots)])  6.9 us
    ppermute x2, starting transfers between devices, swap(): return lax.ppermute(x, 'blk', pairs + [(b, a) for a, b in pairs] + also)  6.57 us
    ppermute x5, starting transfers between devices, shift(): return lax.ppermute(x, 'blk', [(i, (i + s) % slots) for i in range(slots)])  5.9 us
    ppermute x4, waiting for transfers between devices, from_peer(): return lax.ppermute(x, 'pts', [(i, i ^ step) for i in range(devices)])  4.23 us
    ppermute x4, starting transfers between devices, from_peer(): return lax.ppermute(x, 'pts', [(i, i ^ step) for i in range(devices)])  3.54 us
  transfers between devices with their start and end apart: 11, of which 8 were waited for; matrix products, arithmetic and copies ran while one was open for 0% of the time, Pallas kernels for 14%

profile of v8, /device:TPU:0, one launch (start us, length us, event | category | flops | bytes accessed | tf_op | source)
XLA Modules:
  0.0 48.5 jit_solution(8856338346622688456)
XLA Ops:
  0.6 2.9 %shard_map.67 = (s16[32,4224]{1,0:T(8,128)(2,1)S(1)}, bf16[8,384,4,128]{3,2,1,0:T(4,128)(2,1)S(1)}) custom-call(s32[32]{0:T(128)} %bins.3, bf16[768,4,1024]{2,1,0:T(4,128)(2,1)} %x_hbm.3), custom_call_target="tpu_custom_call" | custom-call | flops 402653184 | bytes 3145728 | tf_op jit(solution)/shard_map/pallas_call | solution.py:412
  3.5 1.3 %collective-permute-start.4 = (s16[32,4224]{1,0:T(8,128)(2,1)S(1)}, s16[32,4224]{1,0:T(8,128)(2,1)S(1)}, u32[]{:S(2)}, u32[]{:S(2)}) collective-permute-start(s16[32,4224]{1,0:T(8,128)(2,1)S(1)} %get-tuple-element.33), channel_id=1, source_target_pairs={{1,2},{2,1},{3,0},{5,6},{6,5},{7,4},{9,10},{10,9},{11,8},{13,14},{... | collective-permute-start | bytes 811016 | tf_op jit(solution)/shard_map/ppermute | solution.py:459
  4.8 0.0 copy-start
  4.8 0.0 copy-start.1
  4.9 6.1 %shard_map.68 = (s16[32,4224]{1,0:T(8,128)(2,1)S(1)}, bf16[16,4096]{1,0:T(8,128)(2,1)S(1)}, bf16[16,4096]{1,0:T(8,128)(2,1)S(1)}, bf16[16,4096]{1,0:T(8,128)(2,1...) custom-call(s32[32]{0:T(128)} %bins.3, ...), custom_call_target="tpu_custom_call" | custom-call | flops 3221225472 | bytes 3145728 | tf_op jit(solution)/shard_map/pallas_call | solution.py:412
  10.9 5.3 %collective-permute-start.3 = (s16[32,4224]{1,0:T(8,128)(2,1)S(1)}, s16[32,4224]{1,0:T(8,128)(2,1)S(1)}, u32[]{:S(2)}, u32[]{:S(2)}) collective-permute-start(s16[32,4224]{1,0:T(8,128)(2,1)S(1)} %get-tuple-element.32), channel_id=1, source_target_pairs={{0,1},{2,3},{1,0},{3,2},{4,5},{6,7},{5,4},{7,6},{8,9},{10,11},{9,8... | collective-permute-start | bytes 811016 | tf_op jit(solution)/shard_map/ppermute | solution.py:459
  16.2 0.1 collective-permute-start
  16.3 1.8 %collective-permute-start.1 = (bf16[16,4096]{1,0:T(8,128)(2,1)S(1)}, bf16[16,4096]{1,0:T(8,128)(2,1)S(1)}, u32[]{:S(2)}, u32[]{:S(2)}) collective-permute-start(bf16[16,4096]{1,0:T(8,128)(2,1)S(1)} %get-tuple-element.26), channel_id=1, source_target_pairs={{0,2},{1,3},{2,0},{3,1},{4,6},{5,7},{6,4},{7,5},{8,10},{9,11},{10,... | collective-permute-start | bytes 393224 | tf_op jit(solution)/shard_map/ppermute | solution.py:483
  18.1 1.9 %collective-permute-start.2 = (bf16[16,4096]{1,0:T(8,128)(2,1)S(1)}, bf16[16,4096]{1,0:T(8,128)(2,1)S(1)}, u32[]{:S(2)}, u32[]{:S(2)}) collective-permute-start(bf16[16,4096]{1,0:T(8,128)(2,1)S(1)} %get-tuple-element.27), channel_id=1, source_target_pairs={{0,3},{1,0},{2,1},{3,2},{4,7},{5,4},{6,5},{7,6},{8,11},{9,8},{10,9... | collective-permute-start | bytes 393224 | tf_op jit(solution)/shard_map/ppermute | solution.py:483
  20.0 0.0 collective-permute-done.4.refs_4_
  20.1 0.3 shard_map.69
  20.3 8.0 %collective-permute-done.3.refs_4_ = s16[32,4224]{1,0:T(8,128)(2,1)S(1)} collective-permute-done((s16[32,4224]{1,0:T(8,128)(2,1)S(1)}, s16[32,4224]{1,0:T(8,128)(2,1)S(1)}, u32[]{:S(2)}, u32[]{:S(2)}) %collective-permute-start.3) | collective-permute-done | bytes 270368 | tf_op jit(solution)/shard_map/ppermute | solution.py:459
  28.3 0.4 shard_map.70
  28.7 0.1 collective-permute-start.5
  28.8 2.0 %collective-permute-start.6 = (bf16[16,4096]{1,0:T(8,128)(2,1)S(1)}, bf16[16,4096]{1,0:T(8,128)(2,1)S(1)}, u32[]{:S(2)}, u32[]{:S(2)}) collective-permute-start(bf16[16,4096]{1,0:T(8,128)(2,1)S(1)} %get-tuple-element.39), channel_id=1, source_target_pairs={{0,1},{1,2},{2,3},{3,0},{4,5},{5,6},{6,7},{7,4},{8,9},{9,10},{10,1... | collective-permute-start | bytes 393224 | tf_op jit(solution)/shard_map/ppermute | solution.py:483
  30.8 0.0 collective-permute-done.refs_1_.refs_5_
  30.8 0.0 collective-permute-done.1.refs_2_.refs_6_
  30.8 1.2 %collective-permute-done.2.refs_3_.refs_7_ = bf16[16,4096]{1,0:T(8,128)(2,1)S(1)} collective-permute-done((bf16[16,4096]{1,0:T(8,128)(2,1)S(1)}, bf16[16,4096]{1,0:T(8,128)(2,1)S(1)}, u32[]{:S(2)}, u32[]{:S(2)}) %collective-permute-start.2) | collective-permute-done | bytes 131104 | tf_op jit(solution)/shard_map/ppermute | solution.py:483
  32.0 2.4 %collective-permute-done.5.refs_5_.refs_9_ = bf16[16,4096]{1,0:T(8,128)(2,1)S(1)} collective-permute-done((bf16[16,4096]{1,0:T(8,128)(2,1)S(1)}, bf16[16,4096]{1,0:T(8,128)(2,1)S(1)}, u32[]{:S(2)}, u32[]{:S(2)}) %collective-permute-start.5) | collective-permute-done | bytes 131104 | tf_op jit(solution)/shard_map/ppermute | solution.py:483
  34.4 3.3 %collective-permute-done.6.refs_7_.refs_11_ = bf16[16,4096]{1,0:T(8,128)(2,1)S(1)} collective-permute-done((bf16[16,4096]{1,0:T(8,128)(2,1)S(1)}, bf16[16,4096]{1,0:T(8,128)(2,1)S(1)}, u32[]{:S(2)}, u32[]{:S(2)}) %collective-permute-start.6) | collective-permute-done | bytes 131104 | tf_op jit(solution)/shard_map/ppermute | solution.py:483
  37.7 0.0 copy-done
  37.7 0.0 copy-done.1
  37.7 1.3 %shard_map.71 = f32[8,128]{1,0:T(8,128)S(1)} custom-call(f32[8]{0:T(128)S(1)} %copy-done.1, s32[1,1024]{1,0:T(1,128)S(1)} %bitcast.2, bf16[16,4096]{1,0:T(8,128)(2,1)S(1)} %get-tuple-element.24.refs_0_.refs_4_, bf16[16,4096]{1,0:T(8,128)(2,1)S(1)} %collective-permute-done.refs_1_.refs_5_, bf16[16,4096]{1,0:T(8,128)(2,1)S(1)} %collective-permute-done.1.refs_2_.refs_6_, ...), custom_call_target="tpu_custom_call" | custom-call | flops 134217728 | bytes 2097152 | tf_op jit(solution)/shard_map/pallas_call | solution.py:412
  38.9 0.1 collective-permute-start.7
  39.0 1.2 %collective-permute-done.7 = f32[8,128]{1,0:T(8,128)S(1)} collective-permute-done((f32[8,128]{1,0:T(8,128)S(1)}, f32[8,128]{1,0:T(8,128)S(1)}, u32[]{:S(2)}, u32[]{:S(2)}) %collective-permute-start.7) | collective-permute-done | bytes 4128 | tf_op jit(solution)/shard_map/ppermute | solution.py:520
  40.2 2.4 %collective-permute-start.10 = (f32[8,128]{1,0:T(8,128)S(1)}, f32[8,128]{1,0:T(8,128)S(1)}, u32[]{:S(2)}, u32[]{:S(2)}) collective-permute-start(f32[8,128]{1,0:T(8,128)S(1)} %add.3.refs_0_), channel_id=1, source_target_pairs={{0,24},{4,28},{8,16},{12,20},{16,8},{20,12},{24,0},{28,4},{1,25},{... | collective-permute-start | bytes 12296 | tf_op jit(solution)/shard_map/ppermute | solution.py:520
  42.6 0.5 %collective-permute-start.9 = (f32[8,128]{1,0:T(8,128)S(1)}, f32[8,128]{1,0:T(8,128)S(1)}, u32[]{:S(2)}, u32[]{:S(2)}) collective-permute-start(f32[8,128]{1,0:T(8,128)S(1)} %add.3.refs_0_), channel_id=1, source_target_pairs={{0,16},{4,20},{8,24},{12,28},{16,0},{20,4},{24,8},{28,12},{1,17},{... | collective-permute-start | bytes 12296 | tf_op jit(solution)/shard_map/ppermute | solution.py:520
  43.1 0.5 %collective-permute-start.8 = (f32[8,128]{1,0:T(8,128)S(1)}, f32[8,128]{1,0:T(8,128)S(1)}, u32[]{:S(2)}, u32[]{:S(2)}) collective-permute-start(f32[8,128]{1,0:T(8,128)S(1)} %add.3.refs_0_), channel_id=1, source_target_pairs={{0,8},{4,12},{8,0},{12,4},{16,24},{20,28},{24,16},{28,20},{1,9},{5... | collective-permute-start | bytes 12296 | tf_op jit(solution)/shard_map/ppermute | solution.py:520
  43.6 1.0 %collective-permute-done.10.refs_3_ = f32[8,128]{1,0:T(8,128)S(1)} collective-permute-done((f32[8,128]{1,0:T(8,128)S(1)}, f32[8,128]{1,0:T(8,128)S(1)}, u32[]{:S(2)}, u32[]{:S(2)}) %collective-permute-start.10) | collective-permute-done | bytes 4128 | tf_op jit(solution)/shard_map/ppermute | solution.py:520
  44.7 1.5 %collective-permute-done.9.refs_2_ = f32[8,128]{1,0:T(8,128)S(1)} collective-permute-done((f32[8,128]{1,0:T(8,128)S(1)}, f32[8,128]{1,0:T(8,128)S(1)}, u32[]{:S(2)}, u32[]{:S(2)}) %collective-permute-start.9) | collective-permute-done | bytes 4128 | tf_op jit(solution)/shard_map/ppermute | solution.py:520
  46.2 0.5 %collective-permute-done.8.refs_1_ = f32[8,128]{1,0:T(8,128)S(1)} collective-permute-done((f32[8,128]{1,0:T(8,128)S(1)}, f32[8,128]{1,0:T(8,128)S(1)}, u32[]{:S(2)}, u32[]{:S(2)}) %collective-permute-start.8) | collective-permute-done | bytes 4128 | tf_op jit(solution)/shard_map/ppermute | solution.py:520
  46.7 1.8 %shard_map.72 = (f32[8,2,8,8]{3,2,1,0:T(8,128)}, f32[1,8]{1,0:T(1,128)}, f32[8,2,4,1024]{3,2,1,0:T(4,128)}) custom-call(f32[8,128]{1,0:T(8,128)S(1)} %add.3.refs_0_, f32[8,128]{1,0:T(8,128)S(1)} %collective-permute-done.8.refs_1_, f32[8,128]{1,0:T(8,128)S(1)} %collective-permute-done.9.refs_2_, f32[8,128]{1,0:T(8,128)S(1)} %collective-permute-done.10.refs_3_, ...), custom_call_target="tpu_custom_call" | custom-call | flops 33554432 | bytes 1048576 | tf_op jit(solution)/shard_map/pallas_call | solution.py:412
  (1 shorter events, 0.0 us)
Async XLA Ops:
  3.5 16.5 %collective-permute-start.4 = (s16[32,4224]{1,0:T(8,128)(2,1)S(1)}, s16[32,4224]{1,0:T(8,128)(2,1)S(1)}, u32[]{:S(2)}, u32[]{:S(2)}) collective-permute-start(s16[32,4224]{1,0:T(8,128)(2,1)S(1)} %get-tuple-element.33), channel_id=1, source_target_pairs={{1,2},{2,1},{3,0},{5,6},{6,5},{7,4},{9,10},{10,9},{11,8},{13,14},{... | collective-permute-start | bytes 811016 | tf_op jit(solution)/shard_map/ppermute | solution.py:459
  4.8 32.8 %copy-start = (s32[1024]{0:T(1024)S(1)}, s32[1024]{0:T(1024)}, u32[]{:S(2)}) copy-start(s32[1024]{0:T(1024)} %param.6) | copy-start | bytes 12292
  4.8 32.8 %copy-start.1 = (f32[8]{0:T(128)S(1)}, f32[8]{0:T(128)}, u32[]{:S(2)}) copy-start(f32[8]{0:T(128)} %weights.1) | copy-start | bytes 100
  10.9 17.4 %collective-permute-start.3 = (s16[32,4224]{1,0:T(8,128)(2,1)S(1)}, s16[32,4224]{1,0:T(8,128)(2,1)S(1)}, u32[]{:S(2)}, u32[]{:S(2)}) collective-permute-start(s16[32,4224]{1,0:T(8,128)(2,1)S(1)} %get-tuple-element.32), channel_id=1, source_target_pairs={{0,1},{2,3},{1,0},{3,2},{4,5},{6,7},{5,4},{7,6},{8,9},{10,11},{9,8... | collective-permute-start | bytes 811016 | tf_op jit(solution)/shard_map/ppermute | solution.py:459
  16.2 14.6 %collective-permute-start = (bf16[16,4096]{1,0:T(8,128)(2,1)S(1)}, bf16[16,4096]{1,0:T(8,128)(2,1)S(1)}, u32[]{:S(2)}, u32[]{:S(2)}) collective-permute-start(bf16[16,4096]{1,0:T(8,128)(2,1)S(1)} %get-tuple-element.25), channel_id=1, source_target_pairs={{0,1},{1,2},{2,3},{3,0},{4,5},{5,6},{6,7},{7,4},{8,9},{9,10},{10,1... | collective-permute-start | bytes 393224 | tf_op jit(solution)/shard_map/ppermute | solution.py:483
  16.3 14.5 %collective-permute-start.1 = (bf16[16,4096]{1,0:T(8,128)(2,1)S(1)}, bf16[16,4096]{1,0:T(8,128)(2,1)S(1)}, u32[]{:S(2)}, u32[]{:S(2)}) collective-permute-start(bf16[16,4096]{1,0:T(8,128)(2,1)S(1)} %get-tuple-element.26), channel_id=1, source_target_pairs={{0,2},{1,3},{2,0},{3,1},{4,6},{5,7},{6,4},{7,5},{8,10},{9,11},{10,... | collective-permute-start | bytes 393224 | tf_op jit(solution)/shard_map/ppermute | solution.py:483
  18.1 13.9 %collective-permute-start.2 = (bf16[16,4096]{1,0:T(8,128)(2,1)S(1)}, bf16[16,4096]{1,0:T(8,128)(2,1)S(1)}, u32[]{:S(2)}, u32[]{:S(2)}) collective-permute-start(bf16[16,4096]{1,0:T(8,128)(2,1)S(1)} %get-tuple-element.27), channel_id=1, source_target_pairs={{0,3},{1,0},{2,1},{3,2},{4,7},{5,4},{6,5},{7,6},{8,11},{9,8},{10,9... | collective-permute-start | bytes 393224 | tf_op jit(solution)/shard_map/ppermute | solution.py:483
  28.7 5.7 %collective-permute-start.5 = (bf16[16,4096]{1,0:T(8,128)(2,1)S(1)}, bf16[16,4096]{1,0:T(8,128)(2,1)S(1)}, u32[]{:S(2)}, u32[]{:S(2)}) collective-permute-start(bf16[16,4096]{1,0:T(8,128)(2,1)S(1)} %get-tuple-element.37), channel_id=1, source_target_pairs={{0,3},{1,0},{2,1},{3,2},{4,7},{5,4},{6,5},{7,6},{8,11},{9,8},{10,9... | collective-permute-start | bytes 393224 | tf_op jit(solution)/shard_map/ppermute | solution.py:483
  28.8 8.9 %collective-permute-start.6 = (bf16[16,4096]{1,0:T(8,128)(2,1)S(1)}, bf16[16,4096]{1,0:T(8,128)(2,1)S(1)}, u32[]{:S(2)}, u32[]{:S(2)}) collective-permute-start(bf16[16,4096]{1,0:T(8,128)(2,1)S(1)} %get-tuple-element.39), channel_id=1, source_target_pairs={{0,1},{1,2},{2,3},{3,0},{4,5},{5,6},{6,7},{7,4},{8,9},{9,10},{10,1... | collective-permute-start | bytes 393224 | tf_op jit(solution)/shard_map/ppermute | solution.py:483
  38.9 1.2 %collective-permute-start.7 = (f32[8,128]{1,0:T(8,128)S(1)}, f32[8,128]{1,0:T(8,128)S(1)}, u32[]{:S(2)}, u32[]{:S(2)}) collective-permute-start(f32[8,128]{1,0:T(8,128)S(1)} %shard_map.71), channel_id=1, source_target_pairs={{0,4},{4,0},{8,12},{12,8},{16,20},{20,16},{24,28},{28,24},{1,5},{5... | collective-permute-start | bytes 12296 | tf_op jit(solution)/shard_map/ppermute | solution.py:520
  40.2 4.5 %collective-permute-start.10 = (f32[8,128]{1,0:T(8,128)S(1)}, f32[8,128]{1,0:T(8,128)S(1)}, u32[]{:S(2)}, u32[]{:S(2)}) collective-permute-start(f32[8,128]{1,0:T(8,128)S(1)} %add.3.refs_0_), channel_id=1, source_target_pairs={{0,24},{4,28},{8,16},{12,20},{16,8},{20,12},{24,0},{28,4},{1,25},{... | collective-permute-start | bytes 12296 | tf_op jit(solution)/shard_map/ppermute | solution.py:520
  42.6 3.6 %collective-permute-start.9 = (f32[8,128]{1,0:T(8,128)S(1)}, f32[8,128]{1,0:T(8,128)S(1)}, u32[]{:S(2)}, u32[]{:S(2)}) collective-permute-start(f32[8,128]{1,0:T(8,128)S(1)} %add.3.refs_0_), channel_id=1, source_target_pairs={{0,16},{4,20},{8,24},{12,28},{16,0},{20,4},{24,8},{28,12},{1,17},{... | collective-permute-start | bytes 12296 | tf_op jit(solution)/shard_map/ppermute | solution.py:520
  43.1 3.6 %collective-permute-start.8 = (f32[8,128]{1,0:T(8,128)S(1)}, f32[8,128]{1,0:T(8,128)S(1)}, u32[]{:S(2)}, u32[]{:S(2)}) collective-permute-start(f32[8,128]{1,0:T(8,128)S(1)} %add.3.refs_0_), channel_id=1, source_target_pairs={{0,8},{4,12},{8,0},{12,4},{16,24},{20,28},{24,16},{28,20},{1,9},{5... | collective-permute-start | bytes 12296 | tf_op jit(solution)/shard_map/ppermute | solution.py:520

commit v9 on v8

--- a/solution.py
+++ b/solution.py
@@ -94,11 +94,11 @@
 
 
 def spread(rows, var_count):
-    width = HALF * var_count
-    lane = iota((1, width), 1)
-    pick = one_hot(div(lane, var_count) == iota((HALF, width), 0))
-    wide = mm(rows, pick)
-    owner = rem(lane, var_count)
+    lane = iota((1, LANES * var_count), 1)
+    pick = one_hot(div(lane, var_count) == iota((LANES, LANES * var_count), 0))
+    pieces = [mm(rows[:, t : t + LANES], pick) for t in range(0, HALF, LANES)]
+    wide = jnp.concatenate(pieces, axis=1)
+    owner = rem(iota((1, HALF * var_count), 1), var_count)
     return [jnp.where(owner == v, wide, 0.0).astype(BF16) for v in range(var_count)]
 
 

time: 48.7 us -> 48.4 us (level)
  transfers between devices with their start and end apart: 11 -> 11, of which waited for: 8 -> 9; matrix products, arithmetic and copies ran while one was open for 0% -> 0% of each run, Pallas kernels for 14% -> 14%
where the time goes in v9:
time: 48.4 us; the launch traced here: 48.3 us
  waiting for transfers between devices  19.1 us (39%)
  starting transfers between devices  16 us (33%)
  Pallas kernels  12.4 us (26%)
  between operations  0.7 us (1%)
    pallas_call x6, Pallas kernels, call(): pl.pallas_call(kernel, out_shape=outs, in_specs=ins, out_specs=jax.tree.m...  12.4 us
    ppermute x2, waiting for transfers between devices, swap(): return lax.ppermute(x, 'blk', pairs + [(b, a) for a, b in pairs] + also)  7.66 us
    ppermute x5, waiting for transfers between devices, shift(): return lax.ppermute(x, 'blk', [(i, (i + s) % slots) for i in range(slots)])  7.24 us
    ppermute x2, starting transfers between devices, swap(): return lax.ppermute(x, 'blk', pairs + [(b, a) for a, b in pairs] + also)  6.57 us
    ppermute x5, starting transfers between devices, shift(): return lax.ppermute(x, 'blk', [(i, (i + s) % slots) for i in range(slots)])  5.9 us
    ppermute x4, waiting for transfers between devices, from_peer(): return lax.ppermute(x, 'pts', [(i, i ^ step) for i in range(devices)])  4.23 us
    ppermute x4, starting transfers between devices, from_peer(): return lax.ppermute(x, 'pts', [(i, i ^ step) for i in range(devices)])  3.54 us
  transfers between devices with their start and end apart: 11, of which 9 were waited for; matrix products, arithmetic and copies ran while one was open for 0% of the time, Pallas kernels for 14%

profile of v9, /device:TPU:0, one launch (start us, length us, event | category | flops | bytes accessed | tf_op | source)
XLA Modules:
  0.0 48.3 jit_solution(10186839485194941486)
XLA Ops:
  0.6 2.8 %shard_map.67 = (s16[32,4224]{1,0:T(8,128)(2,1)S(1)}, bf16[8,384,4,128]{3,2,1,0:T(4,128)(2,1)S(1)}) custom-call(s32[32]{0:T(128)} %bins.3, bf16[768,4,1024]{2,1,0:T(4,128)(2,1)} %x_hbm.3), custom_call_target="tpu_custom_call" | custom-call | flops 402653184 | bytes 3145728 | tf_op jit(solution)/shard_map/pallas_call | solution.py:412
  3.5 1.3 %collective-permute-start.4 = (s16[32,4224]{1,0:T(8,128)(2,1)S(1)}, s16[32,4224]{1,0:T(8,128)(2,1)S(1)}, u32[]{:S(2)}, u32[]{:S(2)}) collective-permute-start(s16[32,4224]{1,0:T(8,128)(2,1)S(1)} %get-tuple-element.33), channel_id=1, source_target_pairs={{1,2},{2,1},{3,0},{5,6},{6,5},{7,4},{9,10},{10,9},{11,8},{13,14},{... | collective-permute-start | bytes 811016 | tf_op jit(solution)/shard_map/ppermute | solution.py:459
  4.8 0.0 copy-start
  4.8 0.0 copy-start.1
  4.8 5.9 %shard_map.68 = (s16[32,4224]{1,0:T(8,128)(2,1)S(1)}, bf16[16,4096]{1,0:T(8,128)(2,1)S(1)}, bf16[16,4096]{1,0:T(8,128)(2,1)S(1)}, bf16[16,4096]{1,0:T(8,128)(2,1...) custom-call(s32[32]{0:T(128)} %bins.3, ...), custom_call_target="tpu_custom_call" | custom-call | flops 3221225472 | bytes 3145728 | tf_op jit(solution)/shard_map/pallas_call | solution.py:412
  10.7 5.3 %collective-permute-start.3 = (s16[32,4224]{1,0:T(8,128)(2,1)S(1)}, s16[32,4224]{1,0:T(8,128)(2,1)S(1)}, u32[]{:S(2)}, u32[]{:S(2)}) collective-permute-start(s16[32,4224]{1,0:T(8,128)(2,1)S(1)} %get-tuple-element.32), channel_id=1, source_target_pairs={{0,1},{2,3},{1,0},{3,2},{4,5},{6,7},{5,4},{7,6},{8,9},{10,11},{9,8... | collective-permute-start | bytes 811016 | tf_op jit(solution)/shard_map/ppermute | solution.py:459
  16.0 0.1 collective-permute-start
  16.0 1.8 %collective-permute-start.1 = (bf16[16,4096]{1,0:T(8,128)(2,1)S(1)}, bf16[16,4096]{1,0:T(8,128)(2,1)S(1)}, u32[]{:S(2)}, u32[]{:S(2)}) collective-permute-start(bf16[16,4096]{1,0:T(8,128)(2,1)S(1)} %get-tuple-element.26), channel_id=1, source_target_pairs={{0,2},{1,3},{2,0},{3,1},{4,6},{5,7},{6,4},{7,5},{8,10},{9,11},{10,... | collective-permute-start | bytes 393224 | tf_op jit(solution)/shard_map/ppermute | solution.py:483
  17.9 1.9 %collective-permute-start.2 = (bf16[16,4096]{1,0:T(8,128)(2,1)S(1)}, bf16[16,4096]{1,0:T(8,128)(2,1)S(1)}, u32[]{:S(2)}, u32[]{:S(2)}) collective-permute-start(bf16[16,4096]{1,0:T(8,128)(2,1)S(1)} %get-tuple-element.27), channel_id=1, source_target_pairs={{0,3},{1,0},{2,1},{3,2},{4,7},{5,4},{6,5},{7,6},{8,11},{9,8},{10,9... | collective-permute-start | bytes 393224 | tf_op jit(solution)/shard_map/ppermute | solution.py:483
  19.8 0.0 collective-permute-done.4.refs_4_
  19.8 0.3 shard_map.69
  20.1 7.7 %collective-permute-done.3.refs_4_ = s16[32,4224]{1,0:T(8,128)(2,1)S(1)} collective-permute-done((s16[32,4224]{1,0:T(8,128)(2,1)S(1)}, s16[32,4224]{1,0:T(8,128)(2,1)S(1)}, u32[]{:S(2)}, u32[]{:S(2)}) %collective-permute-start.3) | collective-permute-done | bytes 270368 | tf_op jit(solution)/shard_map/ppermute | solution.py:459
  27.7 0.4 shard_map.70
  28.1 0.3 collective-permute-start.5
  28.4 1.8 %collective-permute-start.6 = (bf16[16,4096]{1,0:T(8,128)(2,1)S(1)}, bf16[16,4096]{1,0:T(8,128)(2,1)S(1)}, u32[]{:S(2)}, u32[]{:S(2)}) collective-permute-start(bf16[16,4096]{1,0:T(8,128)(2,1)S(1)} %get-tuple-element.39), channel_id=1, source_target_pairs={{0,1},{1,2},{2,3},{3,0},{4,5},{5,6},{6,7},{7,4},{8,9},{9,10},{10,1... | collective-permute-start | bytes 393224 | tf_op jit(solution)/shard_map/ppermute | solution.py:483
  30.2 0.0 collective-permute-done.refs_1_.refs_5_
  30.2 0.4 collective-permute-done.1.refs_2_.refs_6_
  30.6 1.2 %collective-permute-done.2.refs_3_.refs_7_ = bf16[16,4096]{1,0:T(8,128)(2,1)S(1)} collective-permute-done((bf16[16,4096]{1,0:T(8,128)(2,1)S(1)}, bf16[16,4096]{1,0:T(8,128)(2,1)S(1)}, u32[]{:S(2)}, u32[]{:S(2)}) %collective-permute-start.2) | collective-permute-done | bytes 131104 | tf_op jit(solution)/shard_map/ppermute | solution.py:483
  31.8 2.4 %collective-permute-done.5.refs_5_.refs_9_ = bf16[16,4096]{1,0:T(8,128)(2,1)S(1)} collective-permute-done((bf16[16,4096]{1,0:T(8,128)(2,1)S(1)}, bf16[16,4096]{1,0:T(8,128)(2,1)S(1)}, u32[]{:S(2)}, u32[]{:S(2)}) %collective-permute-start.5) | collective-permute-done | bytes 131104 | tf_op jit(solution)/shard_map/ppermute | solution.py:483
  34.2 3.3 %collective-permute-done.6.refs_7_.refs_11_ = bf16[16,4096]{1,0:T(8,128)(2,1)S(1)} collective-permute-done((bf16[16,4096]{1,0:T(8,128)(2,1)S(1)}, bf16[16,4096]{1,0:T(8,128)(2,1)S(1)}, u32[]{:S(2)}, u32[]{:S(2)}) %collective-permute-start.6) | collective-permute-done | bytes 131104 | tf_op jit(solution)/shard_map/ppermute | solution.py:483
  37.4 0.0 copy-done
  37.4 0.0 copy-done.1
  37.4 1.2 %shard_map.71 = f32[8,128]{1,0:T(8,128)S(1)} custom-call(f32[8]{0:T(128)S(1)} %copy-done.1, s32[1,1024]{1,0:T(1,128)S(1)} %bitcast.2, bf16[16,4096]{1,0:T(8,128)(2,1)S(1)} %get-tuple-element.24.refs_0_.refs_4_, bf16[16,4096]{1,0:T(8,128)(2,1)S(1)} %collective-permute-done.refs_1_.refs_5_, bf16[16,4096]{1,0:T(8,128)(2,1)S(1)} %collective-permute-done.1.refs_2_.refs_6_, ...), custom_call_target="tpu_custom_call" | custom-call | flops 134217728 | bytes 2097152 | tf_op jit(solution)/shard_map/pallas_call | solution.py:412
  38.7 0.1 collective-permute-start.7
  38.7 1.2 %collective-permute-done.7 = f32[8,128]{1,0:T(8,128)S(1)} collective-permute-done((f32[8,128]{1,0:T(8,128)S(1)}, f32[8,128]{1,0:T(8,128)S(1)}, u32[]{:S(2)}, u32[]{:S(2)}) %collective-permute-start.7) | collective-permute-done | bytes 4128 | tf_op jit(solution)/shard_map/ppermute | solution.py:520
  39.9 2.5 %collective-permute-start.10 = (f32[8,128]{1,0:T(8,128)S(1)}, f32[8,128]{1,0:T(8,128)S(1)}, u32[]{:S(2)}, u32[]{:S(2)}) collective-permute-start(f32[8,128]{1,0:T(8,128)S(1)} %add.3.refs_0_), channel_id=1, source_target_pairs={{0,24},{4,28},{8,16},{12,20},{16,8},{20,12},{24,0},{28,4},{1,25},{... | collective-permute-start | bytes 12296 | tf_op jit(solution)/shard_map/ppermute | solution.py:520
  42.4 0.5 %collective-permute-start.9 = (f32[8,128]{1,0:T(8,128)S(1)}, f32[8,128]{1,0:T(8,128)S(1)}, u32[]{:S(2)}, u32[]{:S(2)}) collective-permute-start(f32[8,128]{1,0:T(8,128)S(1)} %add.3.refs_0_), channel_id=1, source_target_pairs={{0,16},{4,20},{8,24},{12,28},{16,0},{20,4},{24,8},{28,12},{1,17},{... | collective-permute-start | bytes 12296 | tf_op jit(solution)/shard_map/ppermute | solution.py:520
  42.9 0.5 %collective-permute-start.8 = (f32[8,128]{1,0:T(8,128)S(1)}, f32[8,128]{1,0:T(8,128)S(1)}, u32[]{:S(2)}, u32[]{:S(2)}) collective-permute-start(f32[8,128]{1,0:T(8,128)S(1)} %add.3.refs_0_), channel_id=1, source_target_pairs={{0,8},{4,12},{8,0},{12,4},{16,24},{20,28},{24,16},{28,20},{1,9},{5... | collective-permute-start | bytes 12296 | tf_op jit(solution)/shard_map/ppermute | solution.py:520
  43.4 1.0 %collective-permute-done.10.refs_3_ = f32[8,128]{1,0:T(8,128)S(1)} collective-permute-done((f32[8,128]{1,0:T(8,128)S(1)}, f32[8,128]{1,0:T(8,128)S(1)}, u32[]{:S(2)}, u32[]{:S(2)}) %collective-permute-start.10) | collective-permute-done | bytes 4128 | tf_op jit(solution)/shard_map/ppermute | solution.py:520
  44.4 1.6 %collective-permute-done.9.refs_2_ = f32[8,128]{1,0:T(8,128)S(1)} collective-permute-done((f32[8,128]{1,0:T(8,128)S(1)}, f32[8,128]{1,0:T(8,128)S(1)}, u32[]{:S(2)}, u32[]{:S(2)}) %collective-permute-start.9) | collective-permute-done | bytes 4128 | tf_op jit(solution)/shard_map/ppermute | solution.py:520
  46.0 0.5 %collective-permute-done.8.refs_1_ = f32[8,128]{1,0:T(8,128)S(1)} collective-permute-done((f32[8,128]{1,0:T(8,128)S(1)}, f32[8,128]{1,0:T(8,128)S(1)}, u32[]{:S(2)}, u32[]{:S(2)}) %collective-permute-start.8) | collective-permute-done | bytes 4128 | tf_op jit(solution)/shard_map/ppermute | solution.py:520
  46.5 1.8 %shard_map.72 = (f32[8,2,8,8]{3,2,1,0:T(8,128)}, f32[1,8]{1,0:T(1,128)}, f32[8,2,4,1024]{3,2,1,0:T(4,128)}) custom-call(f32[8,128]{1,0:T(8,128)S(1)} %add.3.refs_0_, f32[8,128]{1,0:T(8,128)S(1)} %collective-permute-done.8.refs_1_, f32[8,128]{1,0:T(8,128)S(1)} %collective-permute-done.9.refs_2_, f32[8,128]{1,0:T(8,128)S(1)} %collective-permute-done.10.refs_3_, ...), custom_call_target="tpu_custom_call" | custom-call | flops 33554432 | bytes 1048576 | tf_op jit(solution)/shard_map/pallas_call | solution.py:412
  (1 shorter events, 0.0 us)
Async XLA Ops:
  3.5 16.3 %collective-permute-start.4 = (s16[32,4224]{1,0:T(8,128)(2,1)S(1)}, s16[32,4224]{1,0:T(8,128)(2,1)S(1)}, u32[]{:S(2)}, u32[]{:S(2)}) collective-permute-start(s16[32,4224]{1,0:T(8,128)(2,1)S(1)} %get-tuple-element.33), channel_id=1, source_target_pairs={{1,2},{2,1},{3,0},{5,6},{6,5},{7,4},{9,10},{10,9},{11,8},{13,14},{... | collective-permute-start | bytes 811016 | tf_op jit(solution)/shard_map/ppermute | solution.py:459
  4.8 32.7 %copy-start = (s32[1024]{0:T(1024)S(1)}, s32[1024]{0:T(1024)}, u32[]{:S(2)}) copy-start(s32[1024]{0:T(1024)} %param.6) | copy-start | bytes 12292
  4.8 32.7 %copy-start.1 = (f32[8]{0:T(128)S(1)}, f32[8]{0:T(128)}, u32[]{:S(2)}) copy-start(f32[8]{0:T(128)} %weights.1) | copy-start | bytes 100
  10.7 17.1 %collective-permute-start.3 = (s16[32,4224]{1,0:T(8,128)(2,1)S(1)}, s16[32,4224]{1,0:T(8,128)(2,1)S(1)}, u32[]{:S(2)}, u32[]{:S(2)}) collective-permute-start(s16[32,4224]{1,0:T(8,128)(2,1)S(1)} %get-tuple-element.32), channel_id=1, source_target_pairs={{0,1},{2,3},{1,0},{3,2},{4,5},{6,7},{5,4},{7,6},{8,9},{10,11},{9,8... | collective-permute-start | bytes 811016 | tf_op jit(solution)/shard_map/ppermute | solution.py:459
  16.0 14.2 %collective-permute-start = (bf16[16,4096]{1,0:T(8,128)(2,1)S(1)}, bf16[16,4096]{1,0:T(8,128)(2,1)S(1)}, u32[]{:S(2)}, u32[]{:S(2)}) collective-permute-start(bf16[16,4096]{1,0:T(8,128)(2,1)S(1)} %get-tuple-element.25), channel_id=1, source_target_pairs={{0,1},{1,2},{2,3},{3,0},{4,5},{5,6},{6,7},{7,4},{8,9},{9,10},{10,1... | collective-permute-start | bytes 393224 | tf_op jit(solution)/shard_map/ppermute | solution.py:483
  16.0 14.5 %collective-permute-start.1 = (bf16[16,4096]{1,0:T(8,128)(2,1)S(1)}, bf16[16,4096]{1,0:T(8,128)(2,1)S(1)}, u32[]{:S(2)}, u32[]{:S(2)}) collective-permute-start(bf16[16,4096]{1,0:T(8,128)(2,1)S(1)} %get-tuple-element.26), channel_id=1, source_target_pairs={{0,2},{1,3},{2,0},{3,1},{4,6},{5,7},{6,4},{7,5},{8,10},{9,11},{10,... | collective-permute-start | bytes 393224 | tf_op jit(solution)/shard_map/ppermute | solution.py:483
  17.9 13.9 %collective-permute-start.2 = (bf16[16,4096]{1,0:T(8,128)(2,1)S(1)}, bf16[16,4096]{1,0:T(8,128)(2,1)S(1)}, u32[]{:S(2)}, u32[]{:S(2)}) collective-permute-start(bf16[16,4096]{1,0:T(8,128)(2,1)S(1)} %get-tuple-element.27), channel_id=1, source_target_pairs={{0,3},{1,0},{2,1},{3,2},{4,7},{5,4},{6,5},{7,6},{8,11},{9,8},{10,9... | collective-permute-start | bytes 393224 | tf_op jit(solution)/shard_map/ppermute | solution.py:483
  28.1 6.1 %collective-permute-start.5 = (bf16[16,4096]{1,0:T(8,128)(2,1)S(1)}, bf16[16,4096]{1,0:T(8,128)(2,1)S(1)}, u32[]{:S(2)}, u32[]{:S(2)}) collective-permute-start(bf16[16,4096]{1,0:T(8,128)(2,1)S(1)} %get-tuple-element.37), channel_id=1, source_target_pairs={{0,3},{1,0},{2,1},{3,2},{4,7},{5,4},{6,5},{7,6},{8,11},{9,8},{10,9... | collective-permute-start | bytes 393224 | tf_op jit(solution)/shard_map/ppermute | solution.py:483
  28.4 9.0 %collective-permute-start.6 = (bf16[16,4096]{1,0:T(8,128)(2,1)S(1)}, bf16[16,4096]{1,0:T(8,128)(2,1)S(1)}, u32[]{:S(2)}, u32[]{:S(2)}) collective-permute-start(bf16[16,4096]{1,0:T(8,128)(2,1)S(1)} %get-tuple-element.39), channel_id=1, source_target_pairs={{0,1},{1,2},{2,3},{3,0},{4,5},{5,6},{6,7},{7,4},{8,9},{9,10},{10,1... | collective-permute-start | bytes 393224 | tf_op jit(solution)/shard_map/ppermute | solution.py:483
  38.7 1.2 %collective-permute-start.7 = (f32[8,128]{1,0:T(8,128)S(1)}, f32[8,128]{1,0:T(8,128)S(1)}, u32[]{:S(2)}, u32[]{:S(2)}) collective-permute-start(f32[8,128]{1,0:T(8,128)S(1)} %shard_map.71), channel_id=1, source_target_pairs={{0,4},{4,0},{8,12},{12,8},{16,20},{20,16},{24,28},{28,24},{1,5},{5... | collective-permute-start | bytes 12296 | tf_op jit(solution)/shard_map/ppermute | solution.py:520
  39.9 4.5 %collective-permute-start.10 = (f32[8,128]{1,0:T(8,128)S(1)}, f32[8,128]{1,0:T(8,128)S(1)}, u32[]{:S(2)}, u32[]{:S(2)}) collective-permute-start(f32[8,128]{1,0:T(8,128)S(1)} %add.3.refs_0_), channel_id=1, source_target_pairs={{0,24},{4,28},{8,16},{12,20},{16,8},{20,12},{24,0},{28,4},{1,25},{... | collective-permute-start | bytes 12296 | tf_op jit(solution)/shard_map/ppermute | solution.py:520
  42.4 3.6 %collective-permute-start.9 = (f32[8,128]{1,0:T(8,128)S(1)}, f32[8,128]{1,0:T(8,128)S(1)}, u32[]{:S(2)}, u32[]{:S(2)}) collective-permute-start(f32[8,128]{1,0:T(8,128)S(1)} %add.3.refs_0_), channel_id=1, source_target_pairs={{0,16},{4,20},{8,24},{12,28},{16,0},{20,4},{24,8},{28,12},{1,17},{... | collective-permute-start | bytes 12296 | tf_op jit(solution)/shard_map/ppermute | solution.py:520
  42.9 3.6 %collective-permute-start.8 = (f32[8,128]{1,0:T(8,128)S(1)}, f32[8,128]{1,0:T(8,128)S(1)}, u32[]{:S(2)}, u32[]{:S(2)}) collective-permute-start(f32[8,128]{1,0:T(8,128)S(1)} %add.3.refs_0_), channel_id=1, source_target_pairs={{0,8},{4,12},{8,0},{12,4},{16,24},{20,28},{24,16},{28,20},{1,9},{5... | collective-permute-start | bytes 12296 | tf_op jit(solution)/shard_map/ppermute | solution.py:520

commit v10 on v9

--- a/solution.py
+++ b/solution.py
@@ -238,7 +238,11 @@
     lead = refs[:half_slots]
     trail = refs[half_slots : 2 * half_slots]
     inner = refs[2 * half_slots]
-    joined = refs[2 * half_slots + 1 :]
+    later = 2 * half_slots - 2
+    held_back = refs[2 * half_slots + 1 : 2 * half_slots + 1 + later]
+    joined = refs[2 * half_slots + 1 + later :]
+    for source, target in zip(held_back, joined[half_slots:]):
+        target[...] = source[...]
     me = lax.axis_index("blk")
     odd = lax.rem(me, 2) == 1
     for i in range(half_slots):
@@ -482,22 +486,27 @@
     def shift(x, s):
         return lax.ppermute(x, "blk", [(i, (i + s) % slots) for i in range(slots)])
 
-    even = [pieces[0]] + [shift(pieces[s], s) for s in range(1, slots)]
+    later = [s for s in range(1, slots) if s != half_slots]
     halves = pieces[slots:]
     joined = call(
         functools.partial(inner_join_kernel, half_slots, group),
-        [piece] * half_slots,
-        [vmem] * (slots + 1),
-        (*halves, from_inner),
+        [piece] * (half_slots + len(later)),
+        [vmem] * (slots + 1 + len(later)),
+        (*halves, from_inner, *[pieces[s] for s in later]),
         [],
         slots * group * features,
         10 * slots * group * features,
     )
+    even = {s: shift(x, s) for s, x in zip(later, joined[half_slots:])}
+    even = [
+        pieces[0] if s == 0 else shift(pieces[s], s) if s == half_slots else even[s]
+        for s in range(slots)
+    ]
     odd = call(
         functools.partial(outer_join_kernel, half_slots, group),
         [piece] * slots,
         [vmem] * (slots + half_slots + 1),
-        (*halves, from_outer, *joined),
+        (*halves, from_outer, *joined[:half_slots]),
         [],
         slots * group * features,
         10 * slots * group * features,

time: 48.4 us -> 48.4 us (level)
  waiting for transfers between devices: 19.1 us -> 13.2 us
  starting transfers between devices: 16 us -> 21.9 us
    ppermute x2, waiting for transfers between devices: 7.66 us -> 0.01 us  [swap(): return lax.ppermute(x, 'blk', pairs + [(b, a) for a, b in pairs] + also)]
    ppermute x5, starting transfers between devices: 5.9 us -> 11.8 us  [shift(): return lax.ppermute(x, 'blk', [(i, (i + s) % slots) for i in range(slots)])]
    ppermute x5, waiting for transfers between devices: 7.24 us -> 9.01 us  [shift(): return lax.ppermute(x, 'blk', [(i, (i + s) % slots) for i in range(slots)])]
  transfers between devices with their start and end apart: 11 -> 11, of which waited for: 9 -> 8; matrix products, arithmetic and copies ran while one was open for 0% -> 0% of each run, Pallas kernels for 14% -> 14%
where the time goes in v10:
time: 48.4 us; the launch traced here: 48.3 us
  starting transfers between devices  21.9 us (45%)
  waiting for transfers between devices  13.2 us (27%)
  Pallas kernels  12.4 us (26%)
  between operations  0.7 us (1%)
    pallas_call x6, Pallas kernels, call(): pl.pallas_call(kernel, out_shape=outs, in_specs=ins, out_specs=jax.tree.m...  12.4 us
    ppermute x5, starting transfers between devices, shift(): return lax.ppermute(x, 'blk', [(i, (i + s) % slots) for i in range(slots)])  11.8 us
    ppermute x5, waiting for transfers between devices, shift(): return lax.ppermute(x, 'blk', [(i, (i + s) % slots) for i in range(slots)])  9.01 us
    ppermute x2, starting transfers between devices, swap(): return lax.ppermute(x, 'blk', pairs + [(b, a) for a, b in pairs] + also)  6.57 us
    ppermute x4, waiting for transfers between devices, from_peer(): return lax.ppermute(x, 'pts', [(i, i ^ step) for i in range(devices)])  4.23 us
    ppermute x4, starting transfers between devices, from_peer(): return lax.ppermute(x, 'pts', [(i, i ^ step) for i in range(devices)])  3.54 us
  transfers between devices with their start and end apart: 11, of which 8 were waited for; matrix products, arithmetic and copies ran while one was open for 0% of the time, Pallas kernels for 14%

profile of v10, /device:TPU:0, one launch (start us, length us, event | category | flops | bytes accessed | tf_op | source)
XLA Modules:
  0.0 48.3 jit_solution(11968828427389725574)
XLA Ops:
  0.6 2.8 %shard_map.67 = (s16[32,4224]{1,0:T(8,128)(2,1)S(1)}, bf16[8,384,4,128]{3,2,1,0:T(4,128)(2,1)S(1)}) custom-call(s32[32]{0:T(128)} %bins.3, bf16[768,4,1024]{2,1,0:T(4,128)(2,1)} %x_hbm.3), custom_call_target="tpu_custom_call" | custom-call | flops 402653184 | bytes 3145728 | tf_op jit(solution)/shard_map/pallas_call | solution.py:416
  3.5 1.3 %collective-permute-start = (s16[32,4224]{1,0:T(8,128)(2,1)S(1)}, s16[32,4224]{1,0:T(8,128)(2,1)S(1)}, u32[]{:S(2)}, u32[]{:S(2)}) collective-permute-start(s16[32,4224]{1,0:T(8,128)(2,1)S(1)} %get-tuple-element.31), channel_id=1, source_target_pairs={{1,2},{2,1},{3,0},{5,6},{6,5},{7,4},{9,10},{10,9},{11,8},{13,14},{... | collective-permute-start | bytes 811016 | tf_op jit(solution)/shard_map/ppermute | solution.py:463
  4.8 0.0 copy-start
  4.8 0.0 copy-start.1
  4.8 5.9 %shard_map.68 = (s16[32,4224]{1,0:T(8,128)(2,1)S(1)}, bf16[16,4096]{1,0:T(8,128)(2,1)S(1)}, bf16[16,4096]{1,0:T(8,128)(2,1)S(1)}, bf16[16,4096]{1,0:T(8,128)(2,1...) custom-call(s32[32]{0:T(128)} %bins.3, ...), custom_call_target="tpu_custom_call" | custom-call | flops 3221225472 | bytes 3145728 | tf_op jit(solution)/shard_map/pallas_call | solution.py:416
  10.7 5.3 %collective-permute-start.4 = (s16[32,4224]{1,0:T(8,128)(2,1)S(1)}, s16[32,4224]{1,0:T(8,128)(2,1)S(1)}, u32[]{:S(2)}, u32[]{:S(2)}) collective-permute-start(s16[32,4224]{1,0:T(8,128)(2,1)S(1)} %get-tuple-element.37), channel_id=1, source_target_pairs={{0,1},{2,3},{1,0},{3,2},{4,5},{6,7},{5,4},{7,6},{8,9},{10,11},{9,8... | collective-permute-start | bytes 811016 | tf_op jit(solution)/shard_map/ppermute | solution.py:463
  16.0 0.4 collective-permute-start.2
  16.4 0.0 collective-permute-done.refs_4_
  16.4 0.3 shard_map.69
  16.7 6.8 %collective-permute-start.1 = (bf16[16,4096]{1,0:T(8,128)(2,1)S(1)}, bf16[16,4096]{1,0:T(8,128)(2,1)S(1)}, u32[]{:S(2)}, u32[]{:S(2)}) collective-permute-start(bf16[16,4096]{1,0:T(8,128)(2,1)S(1)} %get-tuple-element.34), channel_id=1, source_target_pairs={{0,1},{1,2},{2,3},{3,0},{4,5},{5,6},{6,7},{7,4},{8,9},{9,10},{10,1... | collective-permute-start | bytes 393224 | tf_op jit(solution)/shard_map/ppermute | solution.py:487
  23.5 0.0 collective-permute-start.3
  23.5 0.0 collective-permute-done.4.refs_4_
  23.5 0.4 shard_map.70
  23.8 4.6 %collective-permute-start.5 = (bf16[16,4096]{1,0:T(8,128)(2,1)S(1)}, bf16[16,4096]{1,0:T(8,128)(2,1)S(1)}, u32[]{:S(2)}, u32[]{:S(2)}) collective-permute-start(bf16[16,4096]{1,0:T(8,128)(2,1)S(1)} %get-tuple-element.41), channel_id=1, source_target_pairs={{0,3},{1,0},{2,1},{3,2},{4,7},{5,4},{6,5},{7,6},{8,11},{9,8},{10,9... | collective-permute-start | bytes 393224 | tf_op jit(solution)/shard_map/ppermute | solution.py:487
  28.4 0.0 collective-permute-start.6
  28.4 2.2 %collective-permute-done.2.refs_2_.refs_6_ = bf16[16,4096]{1,0:T(8,128)(2,1)S(1)} collective-permute-done((bf16[16,4096]{1,0:T(8,128)(2,1)S(1)}, bf16[16,4096]{1,0:T(8,128)(2,1)S(1)}, u32[]{:S(2)}, u32[]{:S(2)}) %collective-permute-start.2) | collective-permute-done | bytes 131104 | tf_op jit(solution)/shard_map/ppermute | solution.py:487
  30.6 0.0 collective-permute-done.1.refs_1_.refs_5_
  30.6 2.2 %collective-permute-done.3.refs_3_.refs_7_ = bf16[16,4096]{1,0:T(8,128)(2,1)S(1)} collective-permute-done((bf16[16,4096]{1,0:T(8,128)(2,1)S(1)}, bf16[16,4096]{1,0:T(8,128)(2,1)S(1)}, u32[]{:S(2)}, u32[]{:S(2)}) %collective-permute-start.3) | collective-permute-done | bytes 131104 | tf_op jit(solution)/shard_map/ppermute | solution.py:487
  32.8 3.1 %collective-permute-done.5.refs_5_.refs_9_ = bf16[16,4096]{1,0:T(8,128)(2,1)S(1)} collective-permute-done((bf16[16,4096]{1,0:T(8,128)(2,1)S(1)}, bf16[16,4096]{1,0:T(8,128)(2,1)S(1)}, u32[]{:S(2)}, u32[]{:S(2)}) %collective-permute-start.5) | collective-permute-done | bytes 131104 | tf_op jit(solution)/shard_map/ppermute | solution.py:487
  35.9 1.5 %collective-permute-done.6.refs_7_.refs_11_ = bf16[16,4096]{1,0:T(8,128)(2,1)S(1)} collective-permute-done((bf16[16,4096]{1,0:T(8,128)(2,1)S(1)}, bf16[16,4096]{1,0:T(8,128)(2,1)S(1)}, u32[]{:S(2)}, u32[]{:S(2)}) %collective-permute-start.6) | collective-permute-done | bytes 131104 | tf_op jit(solution)/shard_map/ppermute | solution.py:487
  37.4 0.0 copy-done
  37.4 0.0 copy-done.1
  37.4 1.2 %shard_map.71 = f32[8,128]{1,0:T(8,128)S(1)} custom-call(f32[8]{0:T(128)S(1)} %copy-done.1, s32[1,1024]{1,0:T(1,128)S(1)} %bitcast.2, bf16[16,4096]{1,0:T(8,128)(2,1)S(1)} %get-tuple-element.26.refs_0_.refs_4_, bf16[16,4096]{1,0:T(8,128)(2,1)S(1)} %collective-permute-done.1.refs_1_.refs_5_, bf16[16,4096]{1,0:T(8,128)(2,1)S(1)} %collective-permute-done.2.refs_2_.refs_6_, ...), custom_call_target="tpu_custom_call" | custom-call | flops 134217728 | bytes 2097152 | tf_op jit(solution)/shard_map/pallas_call | solution.py:416
  38.7 0.1 collective-permute-start.7
  38.7 1.2 %collective-permute-done.7 = f32[8,128]{1,0:T(8,128)S(1)} collective-permute-done((f32[8,128]{1,0:T(8,128)S(1)}, f32[8,128]{1,0:T(8,128)S(1)}, u32[]{:S(2)}, u32[]{:S(2)}) %collective-permute-start.7) | collective-permute-done | bytes 4128 | tf_op jit(solution)/shard_map/ppermute | solution.py:529
  39.9 2.5 %collective-permute-start.10 = (f32[8,128]{1,0:T(8,128)S(1)}, f32[8,128]{1,0:T(8,128)S(1)}, u32[]{:S(2)}, u32[]{:S(2)}) collective-permute-start(f32[8,128]{1,0:T(8,128)S(1)} %add.3.refs_0_), channel_id=1, source_target_pairs={{0,24},{4,28},{8,16},{12,20},{16,8},{20,12},{24,0},{28,4},{1,25},{... | collective-permute-start | bytes 12296 | tf_op jit(solution)/shard_map/ppermute | solution.py:529
  42.4 0.5 %collective-permute-start.9 = (f32[8,128]{1,0:T(8,128)S(1)}, f32[8,128]{1,0:T(8,128)S(1)}, u32[]{:S(2)}, u32[]{:S(2)}) collective-permute-start(f32[8,128]{1,0:T(8,128)S(1)} %add.3.refs_0_), channel_id=1, source_target_pairs={{0,16},{4,20},{8,24},{12,28},{16,0},{20,4},{24,8},{28,12},{1,17},{... | collective-permute-start | bytes 12296 | tf_op jit(solution)/shard_map/ppermute | solution.py:529
  42.9 0.5 %collective-permute-start.8 = (f32[8,128]{1,0:T(8,128)S(1)}, f32[8,128]{1,0:T(8,128)S(1)}, u32[]{:S(2)}, u32[]{:S(2)}) collective-permute-start(f32[8,128]{1,0:T(8,128)S(1)} %add.3.refs_0_), channel_id=1, source_target_pairs={{0,8},{4,12},{8,0},{12,4},{16,24},{20,28},{24,16},{28,20},{1,9},{5... | collective-permute-start | bytes 12296 | tf_op jit(solution)/shard_map/ppermute | solution.py:529
  43.4 1.0 %collective-permute-done.10.refs_3_ = f32[8,128]{1,0:T(8,128)S(1)} collective-permute-done((f32[8,128]{1,0:T(8,128)S(1)}, f32[8,128]{1,0:T(8,128)S(1)}, u32[]{:S(2)}, u32[]{:S(2)}) %collective-permute-start.10) | collective-permute-done | bytes 4128 | tf_op jit(solution)/shard_map/ppermute | solution.py:529
  44.4 1.6 %collective-permute-done.9.refs_2_ = f32[8,128]{1,0:T(8,128)S(1)} collective-permute-done((f32[8,128]{1,0:T(8,128)S(1)}, f32[8,128]{1,0:T(8,128)S(1)}, u32[]{:S(2)}, u32[]{:S(2)}) %collective-permute-start.9) | collective-permute-done | bytes 4128 | tf_op jit(solution)/shard_map/ppermute | solution.py:529
  46.0 0.5 %collective-permute-done.8.refs_1_ = f32[8,128]{1,0:T(8,128)S(1)} collective-permute-done((f32[8,128]{1,0:T(8,128)S(1)}, f32[8,128]{1,0:T(8,128)S(1)}, u32[]{:S(2)}, u32[]{:S(2)}) %collective-permute-start.8) | collective-permute-done | bytes 4128 | tf_op jit(solution)/shard_map/ppermute | solution.py:529
  46.5 1.8 %shard_map.72 = (f32[8,2,8,8]{3,2,1,0:T(8,128)}, f32[1,8]{1,0:T(1,128)}, f32[8,2,4,1024]{3,2,1,0:T(4,128)}) custom-call(f32[8,128]{1,0:T(8,128)S(1)} %add.3.refs_0_, f32[8,128]{1,0:T(8,128)S(1)} %collective-permute-done.8.refs_1_, f32[8,128]{1,0:T(8,128)S(1)} %collective-permute-done.9.refs_2_, f32[8,128]{1,0:T(8,128)S(1)} %collective-permute-done.10.refs_3_, ...), custom_call_target="tpu_custom_call" | custom-call | flops 33554432 | bytes 1048576 | tf_op jit(solution)/shard_map/pallas_call | solution.py:416
  (1 shorter events, 0.0 us)
Async XLA Ops:
  3.5 12.9 %collective-permute-start = (s16[32,4224]{1,0:T(8,128)(2,1)S(1)}, s16[32,4224]{1,0:T(8,128)(2,1)S(1)}, u32[]{:S(2)}, u32[]{:S(2)}) collective-permute-start(s16[32,4224]{1,0:T(8,128)(2,1)S(1)} %get-tuple-element.31), channel_id=1, source_target_pairs={{1,2},{2,1},{3,0},{5,6},{6,5},{7,4},{9,10},{10,9},{11,8},{13,14},{... | collective-permute-start | bytes 811016 | tf_op jit(solution)/shard_map/ppermute | solution.py:463
  4.8 32.7 %copy-start = (s32[1024]{0:T(1024)S(1)}, s32[1024]{0:T(1024)}, u32[]{:S(2)}) copy-start(s32[1024]{0:T(1024)} %param.6) | copy-start | bytes 12292
  4.8 32.7 %copy-start.1 = (f32[8]{0:T(128)S(1)}, f32[8]{0:T(128)}, u32[]{:S(2)}) copy-start(f32[8]{0:T(128)} %weights.1) | copy-start | bytes 100
  10.7 12.8 %collective-permute-start.4 = (s16[32,4224]{1,0:T(8,128)(2,1)S(1)}, s16[32,4224]{1,0:T(8,128)(2,1)S(1)}, u32[]{:S(2)}, u32[]{:S(2)}) collective-permute-start(s16[32,4224]{1,0:T(8,128)(2,1)S(1)} %get-tuple-element.37), channel_id=1, source_target_pairs={{0,1},{2,3},{1,0},{3,2},{4,5},{6,7},{5,4},{7,6},{8,9},{10,11},{9,8... | collective-permute-start | bytes 811016 | tf_op jit(solution)/shard_map/ppermute | solution.py:463
  16.0 14.6 %collective-permute-start.2 = (bf16[16,4096]{1,0:T(8,128)(2,1)S(1)}, bf16[16,4096]{1,0:T(8,128)(2,1)S(1)}, u32[]{:S(2)}, u32[]{:S(2)}) collective-permute-start(bf16[16,4096]{1,0:T(8,128)(2,1)S(1)} %get-tuple-element.35), channel_id=1, source_target_pairs={{0,2},{1,3},{2,0},{3,1},{4,6},{5,7},{6,4},{7,5},{8,10},{9,11},{10,... | collective-permute-start | bytes 393224 | tf_op jit(solution)/shard_map/ppermute | solution.py:487
  16.7 13.9 %collective-permute-start.1 = (bf16[16,4096]{1,0:T(8,128)(2,1)S(1)}, bf16[16,4096]{1,0:T(8,128)(2,1)S(1)}, u32[]{:S(2)}, u32[]{:S(2)}) collective-permute-start(bf16[16,4096]{1,0:T(8,128)(2,1)S(1)} %get-tuple-element.34), channel_id=1, source_target_pairs={{0,1},{1,2},{2,3},{3,0},{4,5},{5,6},{6,7},{7,4},{8,9},{9,10},{10,1... | collective-permute-start | bytes 393224 | tf_op jit(solution)/shard_map/ppermute | solution.py:487
  23.5 9.4 %collective-permute-start.3 = (bf16[16,4096]{1,0:T(8,128)(2,1)S(1)}, bf16[16,4096]{1,0:T(8,128)(2,1)S(1)}, u32[]{:S(2)}, u32[]{:S(2)}) collective-permute-start(bf16[16,4096]{1,0:T(8,128)(2,1)S(1)} %get-tuple-element.36), channel_id=1, source_target_pairs={{0,3},{1,0},{2,1},{3,2},{4,7},{5,4},{6,5},{7,6},{8,11},{9,8},{10,9... | collective-permute-start | bytes 393224 | tf_op jit(solution)/shard_map/ppermute | solution.py:487
  23.8 12.1 %collective-permute-start.5 = (bf16[16,4096]{1,0:T(8,128)(2,1)S(1)}, bf16[16,4096]{1,0:T(8,128)(2,1)S(1)}, u32[]{:S(2)}, u32[]{:S(2)}) collective-permute-start(bf16[16,4096]{1,0:T(8,128)(2,1)S(1)} %get-tuple-element.41), channel_id=1, source_target_pairs={{0,3},{1,0},{2,1},{3,2},{4,7},{5,4},{6,5},{7,6},{8,11},{9,8},{10,9... | collective-permute-start | bytes 393224 | tf_op jit(solution)/shard_map/ppermute | solution.py:487
  28.4 9.0 %collective-permute-start.6 = (bf16[16,4096]{1,0:T(8,128)(2,1)S(1)}, bf16[16,4096]{1,0:T(8,128)(2,1)S(1)}, u32[]{:S(2)}, u32[]{:S(2)}) collective-permute-start(bf16[16,4096]{1,0:T(8,128)(2,1)S(1)} %get-tuple-element.43), channel_id=1, source_target_pairs={{0,1},{1,2},{2,3},{3,0},{4,5},{5,6},{6,7},{7,4},{8,9},{9,10},{10,1... | collective-permute-start | bytes 393224 | tf_op jit(solution)/shard_map/ppermute | solution.py:487
  38.7 1.2 %collective-permute-start.7 = (f32[8,128]{1,0:T(8,128)S(1)}, f32[8,128]{1,0:T(8,128)S(1)}, u32[]{:S(2)}, u32[]{:S(2)}) collective-permute-start(f32[8,128]{1,0:T(8,128)S(1)} %shard_map.71), channel_id=1, source_target_pairs={{0,4},{4,0},{8,12},{12,8},{16,20},{20,16},{24,28},{28,24},{1,5},{5... | collective-permute-start | bytes 12296 | tf_op jit(solution)/shard_map/ppermute | solution.py:529
  39.9 4.5 %collective-permute-start.10 = (f32[8,128]{1,0:T(8,128)S(1)}, f32[8,128]{1,0:T(8,128)S(1)}, u32[]{:S(2)}, u32[]{:S(2)}) collective-permute-start(f32[8,128]{1,0:T(8,128)S(1)} %add.3.refs_0_), channel_id=1, source_target_pairs={{0,24},{4,28},{8,16},{12,20},{16,8},{20,12},{24,0},{28,4},{1,25},{... | collective-permute-start | bytes 12296 | tf_op jit(solution)/shard_map/ppermute | solution.py:529
  42.4 3.6 %collective-permute-start.9 = (f32[8,128]{1,0:T(8,128)S(1)}, f32[8,128]{1,0:T(8,128)S(1)}, u32[]{:S(2)}, u32[]{:S(2)}) collective-permute-start(f32[8,128]{1,0:T(8,128)S(1)} %add.3.refs_0_), channel_id=1, source_target_pairs={{0,16},{4,20},{8,24},{12,28},{16,0},{20,4},{24,8},{28,12},{1,17},{... | collective-permute-start | bytes 12296 | tf_op jit(solution)/shard_map/ppermute | solution.py:529
  42.9 3.6 %collective-permute-start.8 = (f32[8,128]{1,0:T(8,128)S(1)}, f32[8,128]{1,0:T(8,128)S(1)}, u32[]{:S(2)}, u32[]{:S(2)}) collective-permute-start(f32[8,128]{1,0:T(8,128)S(1)} %add.3.refs_0_), channel_id=1, source_target_pairs={{0,8},{4,12},{8,0},{12,4},{16,24},{20,28},{24,16},{28,20},{1,9},{5... | collective-permute-start | bytes 12296 | tf_op jit(solution)/shard_map/ppermute | solution.py:529

commit v11 on v9

--- a/solution.py
+++ b/solution.py
@@ -39,6 +39,11 @@
     mid = rest.astype(BF16)
     low = (rest - mid.astype(F32)).astype(BF16)
     return (high, mid, low)
+
+
+def sum_thirds(x):
+    rows = x.shape[0] // 3
+    return x[:rows] + (x[rows : 2 * rows] + x[2 * rows :])
 
 
 def one_hot(condition):
@@ -272,12 +277,15 @@
     picked = jnp.zeros(classes.shape, F32)
     for k in range(weights.shape[0]):
         picked = picked + jnp.where(classes[...] == k, weights[k], jnp.float32(0.0))
-    wide = jnp.concatenate([picked] * var_count, axis=1)
-    left = jnp.concatenate([ref[...] for ref in refs[:-1]], axis=0)
-    right = (left.astype(F32) * wide).astype(BF16)
-    gram = lax.dot_general(
-        left, right, (((1,), (1,)), ((), ())), preferred_element_type=F32
-    )
+    gram = None
+    for v in range(var_count):
+        part = slice(v * points, (v + 1) * points)
+        left = jnp.concatenate([ref[:, part] for ref in refs[:-1]], axis=0)
+        right = (left.astype(F32) * picked).astype(BF16)
+        product = lax.dot_general(
+            left, right, (((1,), (1,)), ((), ())), preferred_element_type=F32
+        )
+        gram = product if gram is None else gram + product
     size = blocks * group
     freqs = group // 2
     same = rem(iota((size, size), 0), freqs) == rem(iota((1, size), 1), freqs)
@@ -292,9 +300,9 @@
     from_re = one_hot(fits & (row_part == lane_part))
     sign = jnp.where(lane_part == 0, 1.0, -1.0)
     from_im = jnp.where(fits & (row_part != lane_part), sign, 0.0).astype(BF16)
-    total = jnp.zeros((blocks * freqs, width), F32)
-    for part_re, part_im in zip(split3(rows_re), split3(rows_im)):
-        total = total + (mm(part_re, from_re) + mm(part_im, from_im))
+    total = mm(jnp.concatenate(split3(rows_re), axis=0), from_re)
+    total = total + mm(jnp.concatenate(split3(rows_im), axis=0), from_im)
+    total = sum_thirds(total)
     mine = div(iota((freqs, width), 1), 2 * blocks)
     out = jnp.zeros((freqs, width), F32)
     for b in range(blocks):
@@ -322,14 +330,14 @@
         div(iota((width, width), 0), 2 * blocks) == rem(iota((1, width), 1), blocks)
     )
 
-    def apply(matrix, vec_re, vec_im):
-        top = matrix * jnp.where(is_re, vec_re, -vec_im)
-        bottom = matrix * jnp.where(is_re, vec_im, vec_re)
-        both = jnp.concatenate([top, bottom], axis=0)
-        parts = jnp.concatenate([p.astype(F32) for p in split3(both)], axis=0).astype(BF16)
-        got = mm(parts, gather)
-        got = got[: 2 * freqs] + got[2 * freqs : 4 * freqs] + got[4 * freqs :]
-        return (got[:freqs], got[freqs:])
+    def apply(*items):
+        rows = []
+        for matrix, vec_re, vec_im in items:
+            rows.append(matrix * jnp.where(is_re, vec_re, -vec_im))
+            rows.append(matrix * jnp.where(is_re, vec_im, vec_re))
+        both = jnp.concatenate(rows, axis=0)
+        got = sum_thirds(mm(jnp.concatenate(split3(both), axis=0), gather))
+        return [got[i * freqs : (i + 1) * freqs] for i in range(2 * len(items))]
 
     def over_blocks(x):
         return jnp.sum(x, axis=1, keepdims=True) * jnp.float32(1.0 / (2 * blocks))
@@ -337,19 +345,18 @@
     vec_re = jnp.full((freqs, width), 1.0 / math.sqrt(blocks), F32)
     vec_im = jnp.zeros((freqs, width), F32)
     for _ in range(ITERS):
-        out_re, out_im = apply(mat, vec_re, vec_im)
+        out_re, out_im = apply((mat, vec_re, vec_im))
         length = jnp.sqrt(over_blocks(out_re * out_re + out_im * out_im))
         vec_re, vec_im = (out_re / length, out_im / length)
-    out_re, out_im = apply(mat, vec_re, vec_im)
+    low_re = vec_re.astype(BF16).astype(F32)
+    low_im = vec_im.astype(BF16).astype(F32)
+    out_re, out_im, low_out_re, low_out_im = apply((mat, vec_re, vec_im), (raw, low_re, low_im))
     value = over_blocks(vec_re * out_re + vec_im * out_im)
     diagonal = iota((freqs, freqs), 0) == iota((freqs, freqs), 1)
     eig[...] = jnp.sum(
         jnp.where(diagonal, jnp.broadcast_to(value, (freqs, freqs)), 0.0), axis=0, keepdims=True
     )
-    low_re = vec_re.astype(BF16)
-    low_im = vec_im.astype(BF16)
-    out_re, out_im = apply(raw, low_re.astype(F32), low_im.astype(F32))
-    normsq = over_blocks(low_re.astype(F32) * out_re + low_im.astype(F32) * out_im)
+    normsq = over_blocks(low_re * low_out_re + low_im * low_out_im)
     scale = jnp.sqrt(jnp.float32(feature_count) / normsq)
     lane = iota((1, size), 1)
     expand = one_hot(iota((width, size), 0) == block_of(div(lane, group), me, slots))
@@ -397,12 +404,11 @@
         ],
         axis=0,
     )
+    thirds = jnp.concatenate(split3(split_rows), axis=0)
     for k in range(2):
         row, lane = (iota((width, blocks), 0), iota((width, blocks), 1))
         fold = one_hot(rem(row, 2 * blocks) == lane + k * blocks)
-        got = jnp.zeros((freqs * blocks, blocks), F32)
-        for piece in split3(split_rows):
-            got = got + mm(piece, fold)
+        got = sum_thirds(mm(thirds, fold))
         for f in range(freqs):
             csd[f, k] = got[f * blocks : (f + 1) * blocks]
 

time: 48.4 us -> 48.4 us (level)
  no operation moved by 1% of the time
where the time goes in v11:
time: 48.4 us; the launch traced here: 48.2 us
  waiting for transfers between devices  19.1 us (39%)
  starting transfers between devices  16 us (33%)
  Pallas kernels  12.3 us (25%)
  between operations  0.7 us (1%)
    pallas_call x6, Pallas kernels, call(): pl.pallas_call(kernel, out_shape=outs, in_specs=ins, out_specs=jax.tree.m...  12.3 us
    ppermute x2, waiting for transfers between devices, swap(): return lax.ppermute(x, 'blk', pairs + [(b, a) for a, b in pairs] + also)  7.66 us
    ppermute x5, waiting for transfers between devices, shift(): return lax.ppermute(x, 'blk', [(i, (i + s) % slots) for i in range(slots)])  7.24 us
    ppermute x2, starting transfers between devices, swap(): return lax.ppermute(x, 'blk', pairs + [(b, a) for a, b in pairs] + also)  6.57 us
    ppermute x5, starting transfers between devices, shift(): return lax.ppermute(x, 'blk', [(i, (i + s) % slots) for i in range(slots)])  5.9 us
    ppermute x4, waiting for transfers between devices, from_peer(): return lax.ppermute(x, 'pts', [(i, i ^ step) for i in range(devices)])  4.23 us
    ppermute x4, starting transfers between devices, from_peer(): return lax.ppermute(x, 'pts', [(i, i ^ step) for i in range(devices)])  3.56 us
  transfers between devices with their start and end apart: 11, of which 9 were waited for; matrix products, arithmetic and copies ran while one was open for 0% of the time, Pallas kernels for 14%

profile of v11, /device:TPU:0, one launch (start us, length us, event | category | flops | bytes accessed | tf_op | source)
XLA Modules:
  0.0 48.2 jit_solution(2006726201815382901)
XLA Ops:
  0.6 2.8 %shard_map.67 = (s16[32,4224]{1,0:T(8,128)(2,1)S(1)}, bf16[8,384,4,128]{3,2,1,0:T(4,128)(2,1)S(1)}) custom-call(s32[32]{0:T(128)} %bins.3, bf16[768,4,1024]{2,1,0:T(4,128)(2,1)} %x_hbm.3), custom_call_target="tpu_custom_call" | custom-call | flops 402653184 | bytes 3145728 | tf_op jit(solution)/shard_map/pallas_call | solution.py:418
  3.5 1.3 %collective-permute-start.4 = (s16[32,4224]{1,0:T(8,128)(2,1)S(1)}, s16[32,4224]{1,0:T(8,128)(2,1)S(1)}, u32[]{:S(2)}, u32[]{:S(2)}) collective-permute-start(s16[32,4224]{1,0:T(8,128)(2,1)S(1)} %get-tuple-element.33), channel_id=1, source_target_pairs={{1,2},{2,1},{3,0},{5,6},{6,5},{7,4},{9,10},{10,9},{11,8},{13,14},{... | collective-permute-start | bytes 811016 | tf_op jit(solution)/shard_map/ppermute | solution.py:465
  4.8 0.0 copy-start
  4.8 0.0 copy-start.1
  4.8 5.9 %shard_map.68 = (s16[32,4224]{1,0:T(8,128)(2,1)S(1)}, bf16[16,4096]{1,0:T(8,128)(2,1)S(1)}, bf16[16,4096]{1,0:T(8,128)(2,1)S(1)}, bf16[16,4096]{1,0:T(8,128)(2,1...) custom-call(s32[32]{0:T(128)} %bins.3, ...), custom_call_target="tpu_custom_call" | custom-call | flops 3221225472 | bytes 3145728 | tf_op jit(solution)/shard_map/pallas_call | solution.py:418
  10.7 5.3 %collective-permute-start.3 = (s16[32,4224]{1,0:T(8,128)(2,1)S(1)}, s16[32,4224]{1,0:T(8,128)(2,1)S(1)}, u32[]{:S(2)}, u32[]{:S(2)}) collective-permute-start(s16[32,4224]{1,0:T(8,128)(2,1)S(1)} %get-tuple-element.32), channel_id=1, source_target_pairs={{0,1},{2,3},{1,0},{3,2},{4,5},{6,7},{5,4},{7,6},{8,9},{10,11},{9,8... | collective-permute-start | bytes 811016 | tf_op jit(solution)/shard_map/ppermute | solution.py:465
  16.0 0.1 collective-permute-start
  16.0 1.8 %collective-permute-start.1 = (bf16[16,4096]{1,0:T(8,128)(2,1)S(1)}, bf16[16,4096]{1,0:T(8,128)(2,1)S(1)}, u32[]{:S(2)}, u32[]{:S(2)}) collective-permute-start(bf16[16,4096]{1,0:T(8,128)(2,1)S(1)} %get-tuple-element.26), channel_id=1, source_target_pairs={{0,2},{1,3},{2,0},{3,1},{4,6},{5,7},{6,4},{7,5},{8,10},{9,11},{10,... | collective-permute-start | bytes 393224 | tf_op jit(solution)/shard_map/ppermute | solution.py:489
  17.9 1.9 %collective-permute-start.2 = (bf16[16,4096]{1,0:T(8,128)(2,1)S(1)}, bf16[16,4096]{1,0:T(8,128)(2,1)S(1)}, u32[]{:S(2)}, u32[]{:S(2)}) collective-permute-start(bf16[16,4096]{1,0:T(8,128)(2,1)S(1)} %get-tuple-element.27), channel_id=1, source_target_pairs={{0,3},{1,0},{2,1},{3,2},{4,7},{5,4},{6,5},{7,6},{8,11},{9,8},{10,9... | collective-permute-start | bytes 393224 | tf_op jit(solution)/shard_map/ppermute | solution.py:489
  19.8 0.0 collective-permute-done.4.refs_4_
  19.8 0.3 shard_map.69
  20.1 7.7 %collective-permute-done.3.refs_4_ = s16[32,4224]{1,0:T(8,128)(2,1)S(1)} collective-permute-done((s16[32,4224]{1,0:T(8,128)(2,1)S(1)}, s16[32,4224]{1,0:T(8,128)(2,1)S(1)}, u32[]{:S(2)}, u32[]{:S(2)}) %collective-permute-start.3) | collective-permute-done | bytes 270368 | tf_op jit(solution)/shard_map/ppermute | solution.py:465
  27.7 0.4 shard_map.70
  28.1 0.3 collective-permute-start.5
  28.4 1.8 %collective-permute-start.6 = (bf16[16,4096]{1,0:T(8,128)(2,1)S(1)}, bf16[16,4096]{1,0:T(8,128)(2,1)S(1)}, u32[]{:S(2)}, u32[]{:S(2)}) collective-permute-start(bf16[16,4096]{1,0:T(8,128)(2,1)S(1)} %get-tuple-element.39), channel_id=1, source_target_pairs={{0,1},{1,2},{2,3},{3,0},{4,5},{5,6},{6,7},{7,4},{8,9},{9,10},{10,1... | collective-permute-start | bytes 393224 | tf_op jit(solution)/shard_map/ppermute | solution.py:489
  30.2 0.0 collective-permute-done.refs_1_.refs_5_
  30.2 0.4 collective-permute-done.1.refs_2_.refs_6_
  30.6 1.2 %collective-permute-done.2.refs_3_.refs_7_ = bf16[16,4096]{1,0:T(8,128)(2,1)S(1)} collective-permute-done((bf16[16,4096]{1,0:T(8,128)(2,1)S(1)}, bf16[16,4096]{1,0:T(8,128)(2,1)S(1)}, u32[]{:S(2)}, u32[]{:S(2)}) %collective-permute-start.2) | collective-permute-done | bytes 131104 | tf_op jit(solution)/shard_map/ppermute | solution.py:489
  31.8 2.4 %collective-permute-done.5.refs_5_.refs_9_ = bf16[16,4096]{1,0:T(8,128)(2,1)S(1)} collective-permute-done((bf16[16,4096]{1,0:T(8,128)(2,1)S(1)}, bf16[16,4096]{1,0:T(8,128)(2,1)S(1)}, u32[]{:S(2)}, u32[]{:S(2)}) %collective-permute-start.5) | collective-permute-done | bytes 131104 | tf_op jit(solution)/shard_map/ppermute | solution.py:489
  34.2 3.3 %collective-permute-done.6.refs_7_.refs_11_ = bf16[16,4096]{1,0:T(8,128)(2,1)S(1)} collective-permute-done((bf16[16,4096]{1,0:T(8,128)(2,1)S(1)}, bf16[16,4096]{1,0:T(8,128)(2,1)S(1)}, u32[]{:S(2)}, u32[]{:S(2)}) %collective-permute-start.6) | collective-permute-done | bytes 131104 | tf_op jit(solution)/shard_map/ppermute | solution.py:489
  37.4 0.0 copy-done
  37.4 0.0 copy-done.1
  37.4 1.2 %shard_map.71 = f32[8,128]{1,0:T(8,128)S(1)} custom-call(f32[8]{0:T(128)S(1)} %copy-done.1, s32[1,1024]{1,0:T(1,128)S(1)} %bitcast.2, bf16[16,4096]{1,0:T(8,128)(2,1)S(1)} %get-tuple-element.24.refs_0_.refs_4_, bf16[16,4096]{1,0:T(8,128)(2,1)S(1)} %collective-permute-done.refs_1_.refs_5_, bf16[16,4096]{1,0:T(8,128)(2,1)S(1)} %collective-permute-done.1.refs_2_.refs_6_, ...), custom_call_target="tpu_custom_call" | custom-call | flops 134217728 | bytes 2097152 | tf_op jit(solution)/shard_map/pallas_call | solution.py:418
  38.6 0.1 collective-permute-start.7
  38.7 1.2 %collective-permute-done.7 = f32[8,128]{1,0:T(8,128)S(1)} collective-permute-done((f32[8,128]{1,0:T(8,128)S(1)}, f32[8,128]{1,0:T(8,128)S(1)}, u32[]{:S(2)}, u32[]{:S(2)}) %collective-permute-start.7) | collective-permute-done | bytes 4128 | tf_op jit(solution)/shard_map/ppermute | solution.py:526
  39.8 2.5 %collective-permute-start.10 = (f32[8,128]{1,0:T(8,128)S(1)}, f32[8,128]{1,0:T(8,128)S(1)}, u32[]{:S(2)}, u32[]{:S(2)}) collective-permute-start(f32[8,128]{1,0:T(8,128)S(1)} %add.3.refs_0_), channel_id=1, source_target_pairs={{0,24},{4,28},{8,16},{12,20},{16,8},{20,12},{24,0},{28,4},{1,25},{... | collective-permute-start | bytes 12296 | tf_op jit(solution)/shard_map/ppermute | solution.py:526
  42.3 0.5 %collective-permute-start.9 = (f32[8,128]{1,0:T(8,128)S(1)}, f32[8,128]{1,0:T(8,128)S(1)}, u32[]{:S(2)}, u32[]{:S(2)}) collective-permute-start(f32[8,128]{1,0:T(8,128)S(1)} %add.3.refs_0_), channel_id=1, source_target_pairs={{0,16},{4,20},{8,24},{12,28},{16,0},{20,4},{24,8},{28,12},{1,17},{... | collective-permute-start | bytes 12296 | tf_op jit(solution)/shard_map/ppermute | solution.py:526
  42.8 0.5 %collective-permute-start.8 = (f32[8,128]{1,0:T(8,128)S(1)}, f32[8,128]{1,0:T(8,128)S(1)}, u32[]{:S(2)}, u32[]{:S(2)}) collective-permute-start(f32[8,128]{1,0:T(8,128)S(1)} %add.3.refs_0_), channel_id=1, source_target_pairs={{0,8},{4,12},{8,0},{12,4},{16,24},{20,28},{24,16},{28,20},{1,9},{5... | collective-permute-start | bytes 12296 | tf_op jit(solution)/shard_map/ppermute | solution.py:526
  43.3 1.0 %collective-permute-done.10.refs_3_ = f32[8,128]{1,0:T(8,128)S(1)} collective-permute-done((f32[8,128]{1,0:T(8,128)S(1)}, f32[8,128]{1,0:T(8,128)S(1)}, u32[]{:S(2)}, u32[]{:S(2)}) %collective-permute-start.10) | collective-permute-done | bytes 4128 | tf_op jit(solution)/shard_map/ppermute | solution.py:526
  44.4 1.6 %collective-permute-done.9.refs_2_ = f32[8,128]{1,0:T(8,128)S(1)} collective-permute-done((f32[8,128]{1,0:T(8,128)S(1)}, f32[8,128]{1,0:T(8,128)S(1)}, u32[]{:S(2)}, u32[]{:S(2)}) %collective-permute-start.9) | collective-permute-done | bytes 4128 | tf_op jit(solution)/shard_map/ppermute | solution.py:526
  45.9 0.5 %collective-permute-done.8.refs_1_ = f32[8,128]{1,0:T(8,128)S(1)} collective-permute-done((f32[8,128]{1,0:T(8,128)S(1)}, f32[8,128]{1,0:T(8,128)S(1)}, u32[]{:S(2)}, u32[]{:S(2)}) %collective-permute-start.8) | collective-permute-done | bytes 4128 | tf_op jit(solution)/shard_map/ppermute | solution.py:526
  46.4 1.8 %shard_map.72 = (f32[8,2,8,8]{3,2,1,0:T(8,128)}, f32[1,8]{1,0:T(1,128)}, f32[8,2,4,1024]{3,2,1,0:T(4,128)}) custom-call(f32[8,128]{1,0:T(8,128)S(1)} %add.3.refs_0_, f32[8,128]{1,0:T(8,128)S(1)} %collective-permute-done.8.refs_1_, f32[8,128]{1,0:T(8,128)S(1)} %collective-permute-done.9.refs_2_, f32[8,128]{1,0:T(8,128)S(1)} %collective-permute-done.10.refs_3_, ...), custom_call_target="tpu_custom_call" | custom-call | flops 33554432 | bytes 1048576 | tf_op jit(solution)/shard_map/pallas_call | solution.py:418
  (1 shorter events, 0.0 us)
Async XLA Ops:
  3.5 16.3 %collective-permute-start.4 = (s16[32,4224]{1,0:T(8,128)(2,1)S(1)}, s16[32,4224]{1,0:T(8,128)(2,1)S(1)}, u32[]{:S(2)}, u32[]{:S(2)}) collective-permute-start(s16[32,4224]{1,0:T(8,128)(2,1)S(1)} %get-tuple-element.33), channel_id=1, source_target_pairs={{1,2},{2,1},{3,0},{5,6},{6,5},{7,4},{9,10},{10,9},{11,8},{13,14},{... | collective-permute-start | bytes 811016 | tf_op jit(solution)/shard_map/ppermute | solution.py:465
  4.8 32.7 %copy-start = (s32[1024]{0:T(1024)S(1)}, s32[1024]{0:T(1024)}, u32[]{:S(2)}) copy-start(s32[1024]{0:T(1024)} %param.6) | copy-start | bytes 12292
  4.8 32.7 %copy-start.1 = (f32[8]{0:T(128)S(1)}, f32[8]{0:T(128)}, u32[]{:S(2)}) copy-start(f32[8]{0:T(128)} %weights.1) | copy-start | bytes 100
  10.7 17.1 %collective-permute-start.3 = (s16[32,4224]{1,0:T(8,128)(2,1)S(1)}, s16[32,4224]{1,0:T(8,128)(2,1)S(1)}, u32[]{:S(2)}, u32[]{:S(2)}) collective-permute-start(s16[32,4224]{1,0:T(8,128)(2,1)S(1)} %get-tuple-element.32), channel_id=1, source_target_pairs={{0,1},{2,3},{1,0},{3,2},{4,5},{6,7},{5,4},{7,6},{8,9},{10,11},{9,8... | collective-permute-start | bytes 811016 | tf_op jit(solution)/shard_map/ppermute | solution.py:465
  16.0 14.2 %collective-permute-start = (bf16[16,4096]{1,0:T(8,128)(2,1)S(1)}, bf16[16,4096]{1,0:T(8,128)(2,1)S(1)}, u32[]{:S(2)}, u32[]{:S(2)}) collective-permute-start(bf16[16,4096]{1,0:T(8,128)(2,1)S(1)} %get-tuple-element.25), channel_id=1, source_target_pairs={{0,1},{1,2},{2,3},{3,0},{4,5},{5,6},{6,7},{7,4},{8,9},{9,10},{10,1... | collective-permute-start | bytes 393224 | tf_op jit(solution)/shard_map/ppermute | solution.py:489
  16.0 14.5 %collective-permute-start.1 = (bf16[16,4096]{1,0:T(8,128)(2,1)S(1)}, bf16[16,4096]{1,0:T(8,128)(2,1)S(1)}, u32[]{:S(2)}, u32[]{:S(2)}) collective-permute-start(bf16[16,4096]{1,0:T(8,128)(2,1)S(1)} %get-tuple-element.26), channel_id=1, source_target_pairs={{0,2},{1,3},{2,0},{3,1},{4,6},{5,7},{6,4},{7,5},{8,10},{9,11},{10,... | collective-permute-start | bytes 393224 | tf_op jit(solution)/shard_map/ppermute | solution.py:489
  17.9 13.9 %collective-permute-start.2 = (bf16[16,4096]{1,0:T(8,128)(2,1)S(1)}, bf16[16,4096]{1,0:T(8,128)(2,1)S(1)}, u32[]{:S(2)}, u32[]{:S(2)}) collective-permute-start(bf16[16,4096]{1,0:T(8,128)(2,1)S(1)} %get-tuple-element.27), channel_id=1, source_target_pairs={{0,3},{1,0},{2,1},{3,2},{4,7},{5,4},{6,5},{7,6},{8,11},{9,8},{10,9... | collective-permute-start | bytes 393224 | tf_op jit(solution)/shard_map/ppermute | solution.py:489
  28.1 6.1 %collective-permute-start.5 = (bf16[16,4096]{1,0:T(8,128)(2,1)S(1)}, bf16[16,4096]{1,0:T(8,128)(2,1)S(1)}, u32[]{:S(2)}, u32[]{:S(2)}) collective-permute-start(bf16[16,4096]{1,0:T(8,128)(2,1)S(1)} %get-tuple-element.37), channel_id=1, source_target_pairs={{0,3},{1,0},{2,1},{3,2},{4,7},{5,4},{6,5},{7,6},{8,11},{9,8},{10,9... | collective-permute-start | bytes 393224 | tf_op jit(solution)/shard_map/ppermute | solution.py:489
  28.4 9.0 %collective-permute-start.6 = (bf16[16,4096]{1,0:T(8,128)(2,1)S(1)}, bf16[16,4096]{1,0:T(8,128)(2,1)S(1)}, u32[]{:S(2)}, u32[]{:S(2)}) collective-permute-start(bf16[16,4096]{1,0:T(8,128)(2,1)S(1)} %get-tuple-element.39), channel_id=1, source_target_pairs={{0,1},{1,2},{2,3},{3,0},{4,5},{5,6},{6,7},{7,4},{8,9},{9,10},{10,1... | collective-permute-start | bytes 393224 | tf_op jit(solution)/shard_map/ppermute | solution.py:489
  38.6 1.2 %collective-permute-start.7 = (f32[8,128]{1,0:T(8,128)S(1)}, f32[8,128]{1,0:T(8,128)S(1)}, u32[]{:S(2)}, u32[]{:S(2)}) collective-permute-start(f32[8,128]{1,0:T(8,128)S(1)} %shard_map.71), channel_id=1, source_target_pairs={{0,4},{4,0},{8,12},{12,8},{16,20},{20,16},{24,28},{28,24},{1,5},{5... | collective-permute-start | bytes 12296 | tf_op jit(solution)/shard_map/ppermute | solution.py:526
  39.8 4.5 %collective-permute-start.10 = (f32[8,128]{1,0:T(8,128)S(1)}, f32[8,128]{1,0:T(8,128)S(1)}, u32[]{:S(2)}, u32[]{:S(2)}) collective-permute-start(f32[8,128]{1,0:T(8,128)S(1)} %add.3.refs_0_), channel_id=1, source_target_pairs={{0,24},{4,28},{8,16},{12,20},{16,8},{20,12},{24,0},{28,4},{1,25},{... | collective-permute-start | bytes 12296 | tf_op jit(solution)/shard_map/ppermute | solution.py:526
  42.3 3.6 %collective-permute-start.9 = (f32[8,128]{1,0:T(8,128)S(1)}, f32[8,128]{1,0:T(8,128)S(1)}, u32[]{:S(2)}, u32[]{:S(2)}) collective-permute-start(f32[8,128]{1,0:T(8,128)S(1)} %add.3.refs_0_), channel_id=1, source_target_pairs={{0,16},{4,20},{8,24},{12,28},{16,0},{20,4},{24,8},{28,12},{1,17},{... | collective-permute-start | bytes 12296 | tf_op jit(solution)/shard_map/ppermute | solution.py:526
  42.8 3.6 %collective-permute-start.8 = (f32[8,128]{1,0:T(8,128)S(1)}, f32[8,128]{1,0:T(8,128)S(1)}, u32[]{:S(2)}, u32[]{:S(2)}) collective-permute-start(f32[8,128]{1,0:T(8,128)S(1)} %add.3.refs_0_), channel_id=1, source_target_pairs={{0,8},{4,12},{8,0},{12,4},{16,24},{20,28},{24,16},{28,20},{1,9},{5... | collective-permute-start | bytes 12296 | tf_op jit(solution)/shard_map/ppermute | solution.py:526

commit v12 on v11

--- a/solution.py
+++ b/solution.py
@@ -312,7 +312,8 @@
 
 
 def mode_kernel(slots, var_count, points, scaling, feature_count, sums, *refs):
-    csd, eig, modes = refs[-3:]
+    csd_out, eig, modes_out, csd, modes, sems = refs[-6:]
+    refs = refs[:-3]
     tiles, refs = ([ref[...] for ref in refs[:sums]], refs[sums:])
     blocks = 2 * slots
     me = lax.axis_index("blk")
@@ -329,6 +330,27 @@
     gather = one_hot(
         div(iota((width, width), 0), 2 * blocks) == rem(iota((1, width), 1), blocks)
     )
+
+    split_rows = jnp.concatenate(
+        [
+            jnp.where(
+                div(iota((blocks, width), 1), 2 * blocks) == iota((blocks, width), 0),
+                jnp.broadcast_to(mat[f : f + 1], (blocks, width)),
+                0.0,
+            )
+            for f in range(freqs)
+        ],
+        axis=0,
+    )
+    thirds = jnp.concatenate(split3(split_rows), axis=0)
+    for k in range(2):
+        row, lane = (iota((width, blocks), 0), iota((width, blocks), 1))
+        fold = one_hot(rem(row, 2 * blocks) == lane + k * blocks)
+        got = sum_thirds(mm(thirds, fold))
+        for f in range(freqs):
+            csd[f, k] = got[f * blocks : (f + 1) * blocks]
+    copies = [pltpu.make_async_copy(csd, csd_out, sems.at[0])]
+    copies[0].start()
 
     def apply(*items):
         rows = []
@@ -388,38 +410,30 @@
         ],
         axis=0,
     )
-    phi = mm(coef, stacked)
-    for f in range(freqs):
-        block = phi[f * rows : (f + 1) * rows] * scale[f : f + 1, :]
-        for k in range(2):
-            modes[f, k] = block[k * var_count : (k + 1) * var_count]
-    split_rows = jnp.concatenate(
-        [
-            jnp.where(
-                div(iota((blocks, width), 1), 2 * blocks) == iota((blocks, width), 0),
-                jnp.broadcast_to(mat[f : f + 1], (blocks, width)),
-                0.0,
-            )
-            for f in range(freqs)
-        ],
-        axis=0,
-    )
-    thirds = jnp.concatenate(split3(split_rows), axis=0)
-    for k in range(2):
-        row, lane = (iota((width, blocks), 0), iota((width, blocks), 1))
-        fold = one_hot(rem(row, 2 * blocks) == lane + k * blocks)
-        got = sum_thirds(mm(thirds, fold))
+    for i in range(2):
+        part = slice(i * points // 2, (i + 1) * points // 2)
+        phi = mm(coef, stacked[:, part])
         for f in range(freqs):
-            csd[f, k] = got[f * blocks : (f + 1) * blocks]
-
-
-def call(kernel, outs, ins, inputs, scratch, flops, moved):
+            block = phi[f * rows : (f + 1) * rows] * scale[f : f + 1, :]
+            for k in range(2):
+                modes[f, k, :, part] = block[k * var_count : (k + 1) * var_count]
+        lanes = pl.ds(i * points // 2, points // 2)
+        copy = pltpu.make_async_copy(
+            modes.at[:, :, :, lanes], modes_out.at[:, :, :, lanes], sems.at[1 + i]
+        )
+        copy.start()
+        copies.append(copy)
+    for copy in copies:
+        copy.wait()
+
+
+def call(kernel, outs, ins, inputs, scratch, flops, moved, places=None):
     vmem = pl.BlockSpec(memory_space=pltpu.VMEM)
     return pl.pallas_call(
         kernel,
         out_shape=outs,
         in_specs=ins,
-        out_specs=jax.tree.map(lambda _: vmem, outs),
+        out_specs=places or jax.tree.map(lambda _: vmem, outs),
         scratch_shapes=scratch,
         compiler_params=pltpu.CompilerParams(vmem_limit_bytes=VMEM_LIMIT),
         cost_estimate=pl.CostEstimate(flops=flops, bytes_accessed=moved, transcendentals=0),
@@ -553,9 +567,14 @@
         ],
         [vmem] * (len(parts) + len(spectra)),
         (*parts, *spectra),
-        [],
+        [
+            pltpu.VMEM((freqs, 2, blocks, blocks), F32),
+            pltpu.VMEM((freqs, 2, var_count, points), F32),
+            pltpu.SemaphoreType.DMA((3,)),
+        ],
         2 * 2 * blocks * group * group * features,
         2 * blocks * group * features,
+        [hbm, vmem, hbm],
     )
     return (csd, eigval.reshape(freqs), modes)
 

time: 48.4 us -> 48.9 us (1.010)
  Pallas kernels: 12.3 us -> 12.8 us
    pallas_call x6, Pallas kernels: 12.3 us -> 12.8 us  [call(): pl.pallas_call(kernel, out_shape=outs, in_specs=ins, out_specs=places or...]
  transfers between devices with their start and end apart: 11 -> 11, of which waited for: 9 -> 9; matrix products, arithmetic and copies ran while one was open for 0% -> 0% of each run, Pallas kernels for 14% -> 13%
where the time goes in v12:
time: 48.9 us; the launch traced here: 48.7 us
  waiting for transfers between devices  19.1 us (39%)
  starting transfers between devices  16 us (33%)
  Pallas kernels  12.8 us (26%)
  between operations  0.7 us (1%)
    pallas_call x6, Pallas kernels, call(): pl.pallas_call(kernel, out_shape=outs, in_specs=ins, out_specs=places or...  12.8 us
    ppermute x2, waiting for transfers between devices, swap(): return lax.ppermute(x, 'blk', pairs + [(b, a) for a, b in pairs] + also)  7.66 us
    ppermute x5, waiting for transfers between devices, shift(): return lax.ppermute(x, 'blk', [(i, (i + s) % slots) for i in range(slots)])  7.24 us
    ppermute x2, starting transfers between devices, swap(): return lax.ppermute(x, 'blk', pairs + [(b, a) for a, b in pairs] + also)  6.57 us
    ppermute x5, starting transfers between devices, shift(): return lax.ppermute(x, 'blk', [(i, (i + s) % slots) for i in range(slots)])  5.9 us
    ppermute x4, waiting for transfers between devices, from_peer(): return lax.ppermute(x, 'pts', [(i, i ^ step) for i in range(devices)])  4.23 us
    ppermute x4, starting transfers between devices, from_peer(): return lax.ppermute(x, 'pts', [(i, i ^ step) for i in range(devices)])  3.56 us
  transfers between devices with their start and end apart: 11, of which 9 were waited for; matrix products, arithmetic and copies ran while one was open for 0% of the time, Pallas kernels for 13%

profile of v12, /device:TPU:0, one launch (start us, length us, event | category | flops | bytes accessed | tf_op | source)
XLA Modules:
  0.0 48.7 jit_solution(286959128944177803)
XLA Ops:
  0.6 2.8 %shard_map.67 = (s16[32,4224]{1,0:T(8,128)(2,1)S(1)}, bf16[8,384,4,128]{3,2,1,0:T(4,128)(2,1)S(1)}) custom-call(s32[32]{0:T(128)} %bins.3, bf16[768,4,1024]{2,1,0:T(4,128)(2,1)} %x_hbm.3), custom_call_target="tpu_custom_call" | custom-call | flops 402653184 | bytes 3145728 | tf_op jit(solution)/shard_map/pallas_call | solution.py:432
  3.5 1.3 %collective-permute-start.4 = (s16[32,4224]{1,0:T(8,128)(2,1)S(1)}, s16[32,4224]{1,0:T(8,128)(2,1)S(1)}, u32[]{:S(2)}, u32[]{:S(2)}) collective-permute-start(s16[32,4224]{1,0:T(8,128)(2,1)S(1)} %get-tuple-element.33), channel_id=1, source_target_pairs={{1,2},{2,1},{3,0},{5,6},{6,5},{7,4},{9,10},{10,9},{11,8},{13,14},{... | collective-permute-start | bytes 811016 | tf_op jit(solution)/shard_map/ppermute | solution.py:479
  4.8 0.0 copy-start
  4.8 0.0 copy-start.1
  4.8 5.9 %shard_map.68 = (s16[32,4224]{1,0:T(8,128)(2,1)S(1)}, bf16[16,4096]{1,0:T(8,128)(2,1)S(1)}, bf16[16,4096]{1,0:T(8,128)(2,1)S(1)}, bf16[16,4096]{1,0:T(8,128)(2,1...) custom-call(s32[32]{0:T(128)} %bins.3, ...), custom_call_target="tpu_custom_call" | custom-call | flops 3221225472 | bytes 3145728 | tf_op jit(solution)/shard_map/pallas_call | solution.py:432
  10.7 5.3 %collective-permute-start.3 = (s16[32,4224]{1,0:T(8,128)(2,1)S(1)}, s16[32,4224]{1,0:T(8,128)(2,1)S(1)}, u32[]{:S(2)}, u32[]{:S(2)}) collective-permute-start(s16[32,4224]{1,0:T(8,128)(2,1)S(1)} %get-tuple-element.32), channel_id=1, source_target_pairs={{0,1},{2,3},{1,0},{3,2},{4,5},{6,7},{5,4},{7,6},{8,9},{10,11},{9,8... | collective-permute-start | bytes 811016 | tf_op jit(solution)/shard_map/ppermute | solution.py:479
  16.0 0.1 collective-permute-start
  16.0 1.8 %collective-permute-start.1 = (bf16[16,4096]{1,0:T(8,128)(2,1)S(1)}, bf16[16,4096]{1,0:T(8,128)(2,1)S(1)}, u32[]{:S(2)}, u32[]{:S(2)}) collective-permute-start(bf16[16,4096]{1,0:T(8,128)(2,1)S(1)} %get-tuple-element.26), channel_id=1, source_target_pairs={{0,2},{1,3},{2,0},{3,1},{4,6},{5,7},{6,4},{7,5},{8,10},{9,11},{10,... | collective-permute-start | bytes 393224 | tf_op jit(solution)/shard_map/ppermute | solution.py:503
  17.9 1.9 %collective-permute-start.2 = (bf16[16,4096]{1,0:T(8,128)(2,1)S(1)}, bf16[16,4096]{1,0:T(8,128)(2,1)S(1)}, u32[]{:S(2)}, u32[]{:S(2)}) collective-permute-start(bf16[16,4096]{1,0:T(8,128)(2,1)S(1)} %get-tuple-element.27), channel_id=1, source_target_pairs={{0,3},{1,0},{2,1},{3,2},{4,7},{5,4},{6,5},{7,6},{8,11},{9,8},{10,9... | collective-permute-start | bytes 393224 | tf_op jit(solution)/shard_map/ppermute | solution.py:503
  19.8 0.0 collective-permute-done.4.refs_4_
  19.8 0.3 shard_map.69
  20.1 7.7 %collective-permute-done.3.refs_4_ = s16[32,4224]{1,0:T(8,128)(2,1)S(1)} collective-permute-done((s16[32,4224]{1,0:T(8,128)(2,1)S(1)}, s16[32,4224]{1,0:T(8,128)(2,1)S(1)}, u32[]{:S(2)}, u32[]{:S(2)}) %collective-permute-start.3) | collective-permute-done | bytes 270368 | tf_op jit(solution)/shard_map/ppermute | solution.py:479
  27.7 0.4 shard_map.70
  28.1 0.3 collective-permute-start.5
  28.4 1.8 %collective-permute-start.6 = (bf16[16,4096]{1,0:T(8,128)(2,1)S(1)}, bf16[16,4096]{1,0:T(8,128)(2,1)S(1)}, u32[]{:S(2)}, u32[]{:S(2)}) collective-permute-start(bf16[16,4096]{1,0:T(8,128)(2,1)S(1)} %get-tuple-element.39), channel_id=1, source_target_pairs={{0,1},{1,2},{2,3},{3,0},{4,5},{5,6},{6,7},{7,4},{8,9},{9,10},{10,1... | collective-permute-start | bytes 393224 | tf_op jit(solution)/shard_map/ppermute | solution.py:503
  30.2 0.0 collective-permute-done.refs_1_.refs_5_
  30.2 0.4 collective-permute-done.1.refs_2_.refs_6_
  30.6 1.2 %collective-permute-done.2.refs_3_.refs_7_ = bf16[16,4096]{1,0:T(8,128)(2,1)S(1)} collective-permute-done((bf16[16,4096]{1,0:T(8,128)(2,1)S(1)}, bf16[16,4096]{1,0:T(8,128)(2,1)S(1)}, u32[]{:S(2)}, u32[]{:S(2)}) %collective-permute-start.2) | collective-permute-done | bytes 131104 | tf_op jit(solution)/shard_map/ppermute | solution.py:503
  31.8 2.4 %collective-permute-done.5.refs_5_.refs_9_ = bf16[16,4096]{1,0:T(8,128)(2,1)S(1)} collective-permute-done((bf16[16,4096]{1,0:T(8,128)(2,1)S(1)}, bf16[16,4096]{1,0:T(8,128)(2,1)S(1)}, u32[]{:S(2)}, u32[]{:S(2)}) %collective-permute-start.5) | collective-permute-done | bytes 131104 | tf_op jit(solution)/shard_map/ppermute | solution.py:503
  34.2 3.3 %collective-permute-done.6.refs_7_.refs_11_ = bf16[16,4096]{1,0:T(8,128)(2,1)S(1)} collective-permute-done((bf16[16,4096]{1,0:T(8,128)(2,1)S(1)}, bf16[16,4096]{1,0:T(8,128)(2,1)S(1)}, u32[]{:S(2)}, u32[]{:S(2)}) %collective-permute-start.6) | collective-permute-done | bytes 131104 | tf_op jit(solution)/shard_map/ppermute | solution.py:503
  37.4 0.0 copy-done
  37.4 0.0 copy-done.1
  37.4 1.2 %shard_map.71 = f32[8,128]{1,0:T(8,128)S(1)} custom-call(f32[8]{0:T(128)S(1)} %copy-done.1, s32[1,1024]{1,0:T(1,128)S(1)} %bitcast.2, bf16[16,4096]{1,0:T(8,128)(2,1)S(1)} %get-tuple-element.24.refs_0_.refs_4_, bf16[16,4096]{1,0:T(8,128)(2,1)S(1)} %collective-permute-done.refs_1_.refs_5_, bf16[16,4096]{1,0:T(8,128)(2,1)S(1)} %collective-permute-done.1.refs_2_.refs_6_, ...), custom_call_target="tpu_custom_call" | custom-call | flops 134217728 | bytes 2097152 | tf_op jit(solution)/shard_map/pallas_call | solution.py:432
  38.6 0.1 collective-permute-start.7
  38.7 1.2 %collective-permute-done.7 = f32[8,128]{1,0:T(8,128)S(1)} collective-permute-done((f32[8,128]{1,0:T(8,128)S(1)}, f32[8,128]{1,0:T(8,128)S(1)}, u32[]{:S(2)}, u32[]{:S(2)}) %collective-permute-start.7) | collective-permute-done | bytes 4128 | tf_op jit(solution)/shard_map/ppermute | solution.py:540
  39.8 2.5 %collective-permute-start.10 = (f32[8,128]{1,0:T(8,128)S(1)}, f32[8,128]{1,0:T(8,128)S(1)}, u32[]{:S(2)}, u32[]{:S(2)}) collective-permute-start(f32[8,128]{1,0:T(8,128)S(1)} %add.3.refs_0_), channel_id=1, source_target_pairs={{0,24},{4,28},{8,16},{12,20},{16,8},{20,12},{24,0},{28,4},{1,25},{... | collective-permute-start | bytes 12296 | tf_op jit(solution)/shard_map/ppermute | solution.py:540
  42.3 0.5 %collective-permute-start.9 = (f32[8,128]{1,0:T(8,128)S(1)}, f32[8,128]{1,0:T(8,128)S(1)}, u32[]{:S(2)}, u32[]{:S(2)}) collective-permute-start(f32[8,128]{1,0:T(8,128)S(1)} %add.3.refs_0_), channel_id=1, source_target_pairs={{0,16},{4,20},{8,24},{12,28},{16,0},{20,4},{24,8},{28,12},{1,17},{... | collective-permute-start | bytes 12296 | tf_op jit(solution)/shard_map/ppermute | solution.py:540
  42.8 0.5 %collective-permute-start.8 = (f32[8,128]{1,0:T(8,128)S(1)}, f32[8,128]{1,0:T(8,128)S(1)}, u32[]{:S(2)}, u32[]{:S(2)}) collective-permute-start(f32[8,128]{1,0:T(8,128)S(1)} %add.3.refs_0_), channel_id=1, source_target_pairs={{0,8},{4,12},{8,0},{12,4},{16,24},{20,28},{24,16},{28,20},{1,9},{5... | collective-permute-start | bytes 12296 | tf_op jit(solution)/shard_map/ppermute | solution.py:540
  43.3 1.0 %collective-permute-done.10.refs_3_ = f32[8,128]{1,0:T(8,128)S(1)} collective-permute-done((f32[8,128]{1,0:T(8,128)S(1)}, f32[8,128]{1,0:T(8,128)S(1)}, u32[]{:S(2)}, u32[]{:S(2)}) %collective-permute-start.10) | collective-permute-done | bytes 4128 | tf_op jit(solution)/shard_map/ppermute | solution.py:540
  44.4 1.6 %collective-permute-done.9.refs_2_ = f32[8,128]{1,0:T(8,128)S(1)} collective-permute-done((f32[8,128]{1,0:T(8,128)S(1)}, f32[8,128]{1,0:T(8,128)S(1)}, u32[]{:S(2)}, u32[]{:S(2)}) %collective-permute-start.9) | collective-permute-done | bytes 4128 | tf_op jit(solution)/shard_map/ppermute | solution.py:540
  45.9 0.5 %collective-permute-done.8.refs_1_ = f32[8,128]{1,0:T(8,128)S(1)} collective-permute-done((f32[8,128]{1,0:T(8,128)S(1)}, f32[8,128]{1,0:T(8,128)S(1)}, u32[]{:S(2)}, u32[]{:S(2)}) %collective-permute-start.8) | collective-permute-done | bytes 4128 | tf_op jit(solution)/shard_map/ppermute | solution.py:540
  46.4 2.3 %shard_map.72 = (f32[8,2,8,8]{3,2,1,0:T(8,128)}, f32[1,8]{1,0:T(1,128)}, f32[8,2,4,1024]{3,2,1,0:T(4,128)}) custom-call(f32[8,128]{1,0:T(8,128)S(1)} %add.3.refs_0_, f32[8,128]{1,0:T(8,128)S(1)} %collective-permute-done.8.refs_1_, f32[8,128]{1,0:T(8,128)S(1)} %collective-permute-done.9.refs_2_, f32[8,128]{1,0:T(8,128)S(1)} %collective-permute-done.10.refs_3_, ...), custom_call_target="tpu_custom_call" | custom-call | flops 33554432 | bytes 1048576 | tf_op jit(solution)/shard_map/pallas_call | solution.py:432
  (1 shorter events, 0.0 us)
Async XLA Ops:
  3.5 16.3 %collective-permute-start.4 = (s16[32,4224]{1,0:T(8,128)(2,1)S(1)}, s16[32,4224]{1,0:T(8,128)(2,1)S(1)}, u32[]{:S(2)}, u32[]{:S(2)}) collective-permute-start(s16[32,4224]{1,0:T(8,128)(2,1)S(1)} %get-tuple-element.33), channel_id=1, source_target_pairs={{1,2},{2,1},{3,0},{5,6},{6,5},{7,4},{9,10},{10,9},{11,8},{13,14},{... | collective-permute-start | bytes 811016 | tf_op jit(solution)/shard_map/ppermute | solution.py:479
  4.8 32.7 %copy-start = (s32[1024]{0:T(1024)S(1)}, s32[1024]{0:T(1024)}, u32[]{:S(2)}) copy-start(s32[1024]{0:T(1024)} %param.6) | copy-start | bytes 12292
  4.8 32.7 %copy-start.1 = (f32[8]{0:T(128)S(1)}, f32[8]{0:T(128)}, u32[]{:S(2)}) copy-start(f32[8]{0:T(128)} %weights.1) | copy-start | bytes 100
  10.7 17.1 %collective-permute-start.3 = (s16[32,4224]{1,0:T(8,128)(2,1)S(1)}, s16[32,4224]{1,0:T(8,128)(2,1)S(1)}, u32[]{:S(2)}, u32[]{:S(2)}) collective-permute-start(s16[32,4224]{1,0:T(8,128)(2,1)S(1)} %get-tuple-element.32), channel_id=1, source_target_pairs={{0,1},{2,3},{1,0},{3,2},{4,5},{6,7},{5,4},{7,6},{8,9},{10,11},{9,8... | collective-permute-start | bytes 811016 | tf_op jit(solution)/shard_map/ppermute | solution.py:479
  16.0 14.2 %collective-permute-start = (bf16[16,4096]{1,0:T(8,128)(2,1)S(1)}, bf16[16,4096]{1,0:T(8,128)(2,1)S(1)}, u32[]{:S(2)}, u32[]{:S(2)}) collective-permute-start(bf16[16,4096]{1,0:T(8,128)(2,1)S(1)} %get-tuple-element.25), channel_id=1, source_target_pairs={{0,1},{1,2},{2,3},{3,0},{4,5},{5,6},{6,7},{7,4},{8,9},{9,10},{10,1... | collective-permute-start | bytes 393224 | tf_op jit(solution)/shard_map/ppermute | solution.py:503
  16.0 14.5 %collective-permute-start.1 = (bf16[16,4096]{1,0:T(8,128)(2,1)S(1)}, bf16[16,4096]{1,0:T(8,128)(2,1)S(1)}, u32[]{:S(2)}, u32[]{:S(2)}) collective-permute-start(bf16[16,4096]{1,0:T(8,128)(2,1)S(1)} %get-tuple-element.26), channel_id=1, source_target_pairs={{0,2},{1,3},{2,0},{3,1},{4,6},{5,7},{6,4},{7,5},{8,10},{9,11},{10,... | collective-permute-start | bytes 393224 | tf_op jit(solution)/shard_map/ppermute | solution.py:503
  17.9 13.9 %collective-permute-start.2 = (bf16[16,4096]{1,0:T(8,128)(2,1)S(1)}, bf16[16,4096]{1,0:T(8,128)(2,1)S(1)}, u32[]{:S(2)}, u32[]{:S(2)}) collective-permute-start(bf16[16,4096]{1,0:T(8,128)(2,1)S(1)} %get-tuple-element.27), channel_id=1, source_target_pairs={{0,3},{1,0},{2,1},{3,2},{4,7},{5,4},{6,5},{7,6},{8,11},{9,8},{10,9... | collective-permute-start | bytes 393224 | tf_op jit(solution)/shard_map/ppermute | solution.py:503
  28.1 6.1 %collective-permute-start.5 = (bf16[16,4096]{1,0:T(8,128)(2,1)S(1)}, bf16[16,4096]{1,0:T(8,128)(2,1)S(1)}, u32[]{:S(2)}, u32[]{:S(2)}) collective-permute-start(bf16[16,4096]{1,0:T(8,128)(2,1)S(1)} %get-tuple-element.37), channel_id=1, source_target_pairs={{0,3},{1,0},{2,1},{3,2},{4,7},{5,4},{6,5},{7,6},{8,11},{9,8},{10,9... | collective-permute-start | bytes 393224 | tf_op jit(solution)/shard_map/ppermute | solution.py:503
  28.4 9.0 %collective-permute-start.6 = (bf16[16,4096]{1,0:T(8,128)(2,1)S(1)}, bf16[16,4096]{1,0:T(8,128)(2,1)S(1)}, u32[]{:S(2)}, u32[]{:S(2)}) collective-permute-start(bf16[16,4096]{1,0:T(8,128)(2,1)S(1)} %get-tuple-element.39), channel_id=1, source_target_pairs={{0,1},{1,2},{2,3},{3,0},{4,5},{5,6},{6,7},{7,4},{8,9},{9,10},{10,1... | collective-permute-start | bytes 393224 | tf_op jit(solution)/shard_map/ppermute | solution.py:503
  38.6 1.2 %collective-permute-start.7 = (f32[8,128]{1,0:T(8,128)S(1)}, f32[8,128]{1,0:T(8,128)S(1)}, u32[]{:S(2)}, u32[]{:S(2)}) collective-permute-start(f32[8,128]{1,0:T(8,128)S(1)} %shard_map.71), channel_id=1, source_target_pairs={{0,4},{4,0},{8,12},{12,8},{16,20},{20,16},{24,28},{28,24},{1,5},{5... | collective-permute-start | bytes 12296 | tf_op jit(solution)/shard_map/ppermute | solution.py:540
  39.8 4.5 %collective-permute-start.10 = (f32[8,128]{1,0:T(8,128)S(1)}, f32[8,128]{1,0:T(8,128)S(1)}, u32[]{:S(2)}, u32[]{:S(2)}) collective-permute-start(f32[8,128]{1,0:T(8,128)S(1)} %add.3.refs_0_), channel_id=1, source_target_pairs={{0,24},{4,28},{8,16},{12,20},{16,8},{20,12},{24,0},{28,4},{1,25},{... | collective-permute-start | bytes 12296 | tf_op jit(solution)/shard_map/ppermute | solution.py:540
  42.3 3.6 %collective-permute-start.9 = (f32[8,128]{1,0:T(8,128)S(1)}, f32[8,128]{1,0:T(8,128)S(1)}, u32[]{:S(2)}, u32[]{:S(2)}) collective-permute-start(f32[8,128]{1,0:T(8,128)S(1)} %add.3.refs_0_), channel_id=1, source_target_pairs={{0,16},{4,20},{8,24},{12,28},{16,0},{20,4},{24,8},{28,12},{1,17},{... | collective-permute-start | bytes 12296 | tf_op jit(solution)/shard_map/ppermute | solution.py:540
  42.8 3.6 %collective-permute-start.8 = (f32[8,128]{1,0:T(8,128)S(1)}, f32[8,128]{1,0:T(8,128)S(1)}, u32[]{:S(2)}, u32[]{:S(2)}) collective-permute-start(f32[8,128]{1,0:T(8,128)S(1)} %add.3.refs_0_), channel_id=1, source_target_pairs={{0,8},{4,12},{8,0},{12,4},{16,24},{20,28},{24,16},{28,20},{1,9},{5... | collective-permute-start | bytes 12296 | tf_op jit(solution)/shard_map/ppermute | solution.py:540

commit v13 on v11

--- a/solution.py
+++ b/solution.py
@@ -525,16 +525,19 @@
     def from_peer(x, step):
         return lax.ppermute(x, "pts", [(i, i ^ step) for i in range(devices)])
 
+    groups_of = []
+    step = 2
+    while step < devices:
+        by_four = 4 * step <= devices
+        groups_of.append((step, 2 * step, 3 * step) if by_four else (step,))
+        step *= 4 if by_four else 2
+    groups_of.append((1,))
     parts = [packed]
-    step = 1
-    while step < devices:
+    for steps in groups_of:
         total = functools.reduce(jnp.add, parts[:2])
         if len(parts) == 4:
             total = total + (parts[2] + parts[3])
-        by_four = step > 1 and 4 * step <= devices
-        steps = (step, 2 * step, 3 * step) if by_four else (step,)
         parts = [total] + [from_peer(total, i) for i in steps]
-        step *= 4 if by_four else 2
     total_features = features * devices
     csd, eigval, modes = call(
         functools.partial(

time: 48.4 us -> 48.4 us (level)
  no operation moved by 1% of the time
where the time goes in v13:
time: 48.4 us; the launch traced here: 48.2 us
  waiting for transfers between devices  19.1 us (39%)
  starting transfers between devices  16 us (33%)
  Pallas kernels  12.3 us (25%)
  between operations  0.69 us (1%)
    pallas_call x6, Pallas kernels, call(): pl.pallas_call(kernel, out_shape=outs, in_specs=ins, out_specs=jax.tree.m...  12.3 us
    ppermute x2, waiting for transfers between devices, swap(): return lax.ppermute(x, 'blk', pairs + [(b, a) for a, b in pairs] + also)  7.66 us
    ppermute x5, waiting for transfers between devices, shift(): return lax.ppermute(x, 'blk', [(i, (i + s) % slots) for i in range(slots)])  7.24 us
    ppermute x2, starting transfers between devices, swap(): return lax.ppermute(x, 'blk', pairs + [(b, a) for a, b in pairs] + also)  6.57 us
    ppermute x5, starting transfers between devices, shift(): return lax.ppermute(x, 'blk', [(i, (i + s) % slots) for i in range(slots)])  5.9 us
    ppermute x4, waiting for transfers between devices, from_peer(): return lax.ppermute(x, 'pts', [(i, i ^ step) for i in range(devices)])  4.24 us
    ppermute x4, starting transfers between devices, from_peer(): return lax.ppermute(x, 'pts', [(i, i ^ step) for i in range(devices)])  3.56 us
  transfers between devices with their start and end apart: 11, of which 9 were waited for; matrix products, arithmetic and copies ran while one was open for 0% of the time, Pallas kernels for 14%

profile of v13, /device:TPU:0, one launch (start us, length us, event | category | flops | bytes accessed | tf_op | source)
XLA Modules:
  0.0 48.2 jit_solution(5128291932570564981)
XLA Ops:
  0.6 2.8 %shard_map.67 = (s16[32,4224]{1,0:T(8,128)(2,1)S(1)}, bf16[8,384,4,128]{3,2,1,0:T(4,128)(2,1)S(1)}) custom-call(s32[32]{0:T(128)} %bins.3, bf16[768,4,1024]{2,1,0:T(4,128)(2,1)} %x_hbm.3), custom_call_target="tpu_custom_call" | custom-call | flops 402653184 | bytes 3145728 | tf_op jit(solution)/shard_map/pallas_call | solution.py:418
  3.5 1.3 %collective-permute-start.4 = (s16[32,4224]{1,0:T(8,128)(2,1)S(1)}, s16[32,4224]{1,0:T(8,128)(2,1)S(1)}, u32[]{:S(2)}, u32[]{:S(2)}) collective-permute-start(s16[32,4224]{1,0:T(8,128)(2,1)S(1)} %get-tuple-element.33), channel_id=1, source_target_pairs={{1,2},{2,1},{3,0},{5,6},{6,5},{7,4},{9,10},{10,9},{11,8},{13,14},{... | collective-permute-start | bytes 811016 | tf_op jit(solution)/shard_map/ppermute | solution.py:465
  4.8 0.0 copy-start
  4.8 0.0 copy-start.1
  4.8 5.9 %shard_map.68 = (s16[32,4224]{1,0:T(8,128)(2,1)S(1)}, bf16[16,4096]{1,0:T(8,128)(2,1)S(1)}, bf16[16,4096]{1,0:T(8,128)(2,1)S(1)}, bf16[16,4096]{1,0:T(8,128)(2,1...) custom-call(s32[32]{0:T(128)} %bins.3, ...), custom_call_target="tpu_custom_call" | custom-call | flops 3221225472 | bytes 3145728 | tf_op jit(solution)/shard_map/pallas_call | solution.py:418
  10.7 5.3 %collective-permute-start.3 = (s16[32,4224]{1,0:T(8,128)(2,1)S(1)}, s16[32,4224]{1,0:T(8,128)(2,1)S(1)}, u32[]{:S(2)}, u32[]{:S(2)}) collective-permute-start(s16[32,4224]{1,0:T(8,128)(2,1)S(1)} %get-tuple-element.32), channel_id=1, source_target_pairs={{0,1},{2,3},{1,0},{3,2},{4,5},{6,7},{5,4},{7,6},{8,9},{10,11},{9,8... | collective-permute-start | bytes 811016 | tf_op jit(solution)/shard_map/ppermute | solution.py:465
  16.0 0.1 collective-permute-start
  16.0 1.8 %collective-permute-start.1 = (bf16[16,4096]{1,0:T(8,128)(2,1)S(1)}, bf16[16,4096]{1,0:T(8,128)(2,1)S(1)}, u32[]{:S(2)}, u32[]{:S(2)}) collective-permute-start(bf16[16,4096]{1,0:T(8,128)(2,1)S(1)} %get-tuple-element.26), channel_id=1, source_target_pairs={{0,2},{1,3},{2,0},{3,1},{4,6},{5,7},{6,4},{7,5},{8,10},{9,11},{10,... | collective-permute-start | bytes 393224 | tf_op jit(solution)/shard_map/ppermute | solution.py:489
  17.9 1.9 %collective-permute-start.2 = (bf16[16,4096]{1,0:T(8,128)(2,1)S(1)}, bf16[16,4096]{1,0:T(8,128)(2,1)S(1)}, u32[]{:S(2)}, u32[]{:S(2)}) collective-permute-start(bf16[16,4096]{1,0:T(8,128)(2,1)S(1)} %get-tuple-element.27), channel_id=1, source_target_pairs={{0,3},{1,0},{2,1},{3,2},{4,7},{5,4},{6,5},{7,6},{8,11},{9,8},{10,9... | collective-permute-start | bytes 393224 | tf_op jit(solution)/shard_map/ppermute | solution.py:489
  19.8 0.0 collective-permute-done.4.refs_4_
  19.8 0.3 shard_map.69
  20.1 7.7 %collective-permute-done.3.refs_4_ = s16[32,4224]{1,0:T(8,128)(2,1)S(1)} collective-permute-done((s16[32,4224]{1,0:T(8,128)(2,1)S(1)}, s16[32,4224]{1,0:T(8,128)(2,1)S(1)}, u32[]{:S(2)}, u32[]{:S(2)}) %collective-permute-start.3) | collective-permute-done | bytes 270368 | tf_op jit(solution)/shard_map/ppermute | solution.py:465
  27.7 0.4 shard_map.70
  28.1 0.3 collective-permute-start.5
  28.4 1.8 %collective-permute-start.6 = (bf16[16,4096]{1,0:T(8,128)(2,1)S(1)}, bf16[16,4096]{1,0:T(8,128)(2,1)S(1)}, u32[]{:S(2)}, u32[]{:S(2)}) collective-permute-start(bf16[16,4096]{1,0:T(8,128)(2,1)S(1)} %get-tuple-element.39), channel_id=1, source_target_pairs={{0,1},{1,2},{2,3},{3,0},{4,5},{5,6},{6,7},{7,4},{8,9},{9,10},{10,1... | collective-permute-start | bytes 393224 | tf_op jit(solution)/shard_map/ppermute | solution.py:489
  30.2 0.0 collective-permute-done.refs_1_.refs_3_
  30.2 0.4 collective-permute-done.1.refs_2_.refs_4_
  30.6 1.2 %collective-permute-done.2.refs_3_.refs_5_ = bf16[16,4096]{1,0:T(8,128)(2,1)S(1)} collective-permute-done((bf16[16,4096]{1,0:T(8,128)(2,1)S(1)}, bf16[16,4096]{1,0:T(8,128)(2,1)S(1)}, u32[]{:S(2)}, u32[]{:S(2)}) %collective-permute-start.2) | collective-permute-done | bytes 131104 | tf_op jit(solution)/shard_map/ppermute | solution.py:489
  31.8 2.4 %collective-permute-done.5.refs_5_.refs_7_ = bf16[16,4096]{1,0:T(8,128)(2,1)S(1)} collective-permute-done((bf16[16,4096]{1,0:T(8,128)(2,1)S(1)}, bf16[16,4096]{1,0:T(8,128)(2,1)S(1)}, u32[]{:S(2)}, u32[]{:S(2)}) %collective-permute-start.5) | collective-permute-done | bytes 131104 | tf_op jit(solution)/shard_map/ppermute | solution.py:489
  34.2 3.3 %collective-permute-done.6.refs_7_.refs_9_ = bf16[16,4096]{1,0:T(8,128)(2,1)S(1)} collective-permute-done((bf16[16,4096]{1,0:T(8,128)(2,1)S(1)}, bf16[16,4096]{1,0:T(8,128)(2,1)S(1)}, u32[]{:S(2)}, u32[]{:S(2)}) %collective-permute-start.6) | collective-permute-done | bytes 131104 | tf_op jit(solution)/shard_map/ppermute | solution.py:489
  37.4 0.0 copy-done
  37.4 0.0 copy-done.1
  37.4 1.2 %shard_map.71 = f32[8,128]{1,0:T(8,128)S(1)} custom-call(f32[8]{0:T(128)S(1)} %copy-done.1, s32[1,1024]{1,0:T(1,128)S(1)} %bitcast.2, bf16[16,4096]{1,0:T(8,128)(2,1)S(1)} %get-tuple-element.24.refs_0_.refs_2_, bf16[16,4096]{1,0:T(8,128)(2,1)S(1)} %collective-permute-done.refs_1_.refs_3_, bf16[16,4096]{1,0:T(8,128)(2,1)S(1)} %collective-permute-done.1.refs_2_.refs_4_, ...), custom_call_target="tpu_custom_call" | custom-call | flops 134217728 | bytes 2097152 | tf_op jit(solution)/shard_map/pallas_call | solution.py:418
  38.6 2.5 %collective-permute-start.9 = (f32[8,128]{1,0:T(8,128)S(1)}, f32[8,128]{1,0:T(8,128)S(1)}, u32[]{:S(2)}, u32[]{:S(2)}) collective-permute-start(f32[8,128]{1,0:T(8,128)S(1)} %shard_map.71), channel_id=1, source_target_pairs={{0,24},{4,28},{8,16},{12,20},{16,8},{20,12},{24,0},{28,4},{1,25},{... | collective-permute-start | bytes 12296 | tf_op jit(solution)/shard_map/ppermute | solution.py:526
  41.1 0.5 %collective-permute-start.8 = (f32[8,128]{1,0:T(8,128)S(1)}, f32[8,128]{1,0:T(8,128)S(1)}, u32[]{:S(2)}, u32[]{:S(2)}) collective-permute-start(f32[8,128]{1,0:T(8,128)S(1)} %shard_map.71), channel_id=1, source_target_pairs={{0,16},{4,20},{8,24},{12,28},{16,0},{20,4},{24,8},{28,12},{1,17},{... | collective-permute-start | bytes 12296 | tf_op jit(solution)/shard_map/ppermute | solution.py:526
  41.6 0.5 %collective-permute-start.7 = (f32[8,128]{1,0:T(8,128)S(1)}, f32[8,128]{1,0:T(8,128)S(1)}, u32[]{:S(2)}, u32[]{:S(2)}) collective-permute-start(f32[8,128]{1,0:T(8,128)S(1)} %shard_map.71), channel_id=1, source_target_pairs={{0,8},{4,12},{8,0},{12,4},{16,24},{20,28},{24,16},{28,20},{1,9},{5... | collective-permute-start | bytes 12296 | tf_op jit(solution)/shard_map/ppermute | solution.py:526
  42.2 1.0 %collective-permute-done.9 = f32[8,128]{1,0:T(8,128)S(1)} collective-permute-done((f32[8,128]{1,0:T(8,128)S(1)}, f32[8,128]{1,0:T(8,128)S(1)}, u32[]{:S(2)}, u32[]{:S(2)}) %collective-permute-start.9) | collective-permute-done | bytes 4128 | tf_op jit(solution)/shard_map/ppermute | solution.py:526
  43.2 1.6 %collective-permute-done.8 = f32[8,128]{1,0:T(8,128)S(1)} collective-permute-done((f32[8,128]{1,0:T(8,128)S(1)}, f32[8,128]{1,0:T(8,128)S(1)}, u32[]{:S(2)}, u32[]{:S(2)}) %collective-permute-start.8) | collective-permute-done | bytes 4128 | tf_op jit(solution)/shard_map/ppermute | solution.py:526
  44.7 0.5 %collective-permute-done.7 = f32[8,128]{1,0:T(8,128)S(1)} collective-permute-done((f32[8,128]{1,0:T(8,128)S(1)}, f32[8,128]{1,0:T(8,128)S(1)}, u32[]{:S(2)}, u32[]{:S(2)}) %collective-permute-start.7) | collective-permute-done | bytes 4128 | tf_op jit(solution)/shard_map/ppermute | solution.py:526
  45.3 0.0 collective-permute-start.10
  45.3 1.2 %collective-permute-done.10.refs_1_ = f32[8,128]{1,0:T(8,128)S(1)} collective-permute-done((f32[8,128]{1,0:T(8,128)S(1)}, f32[8,128]{1,0:T(8,128)S(1)}, u32[]{:S(2)}, u32[]{:S(2)}) %collective-permute-start.10) | collective-permute-done | bytes 4128 | tf_op jit(solution)/shard_map/ppermute | solution.py:526
  46.4 1.8 %shard_map.72 = (f32[8,2,8,8]{3,2,1,0:T(8,128)}, f32[1,8]{1,0:T(1,128)}, f32[8,2,4,1024]{3,2,1,0:T(4,128)}) custom-call(f32[8,128]{1,0:T(8,128)S(1)} %add_add_fusion.refs_0_, f32[8,128]{1,0:T(8,128)S(1)} %collective-permute-done.10.refs_1_, bf16[16,4096]{1,0:T(8,128)(2,1)S(1)} %get-tuple-element.24.refs_0_.refs_2_, ...), custom_call_target="tpu_custom_call" | custom-call | flops 33554432 | bytes 1048576 | tf_op jit(solution)/shard_map/pallas_call | solution.py:418
  (1 shorter events, 0.0 us)
Async XLA Ops:
  3.5 16.3 %collective-permute-start.4 = (s16[32,4224]{1,0:T(8,128)(2,1)S(1)}, s16[32,4224]{1,0:T(8,128)(2,1)S(1)}, u32[]{:S(2)}, u32[]{:S(2)}) collective-permute-start(s16[32,4224]{1,0:T(8,128)(2,1)S(1)} %get-tuple-element.33), channel_id=1, source_target_pairs={{1,2},{2,1},{3,0},{5,6},{6,5},{7,4},{9,10},{10,9},{11,8},{13,14},{... | collective-permute-start | bytes 811016 | tf_op jit(solution)/shard_map/ppermute | solution.py:465
  4.8 32.7 %copy-start = (s32[1024]{0:T(1024)S(1)}, s32[1024]{0:T(1024)}, u32[]{:S(2)}) copy-start(s32[1024]{0:T(1024)} %param.6) | copy-start | bytes 12292
  4.8 32.7 %copy-start.1 = (f32[8]{0:T(128)S(1)}, f32[8]{0:T(128)}, u32[]{:S(2)}) copy-start(f32[8]{0:T(128)} %weights.1) | copy-start | bytes 100
  10.7 17.1 %collective-permute-start.3 = (s16[32,4224]{1,0:T(8,128)(2,1)S(1)}, s16[32,4224]{1,0:T(8,128)(2,1)S(1)}, u32[]{:S(2)}, u32[]{:S(2)}) collective-permute-start(s16[32,4224]{1,0:T(8,128)(2,1)S(1)} %get-tuple-element.32), channel_id=1, source_target_pairs={{0,1},{2,3},{1,0},{3,2},{4,5},{6,7},{5,4},{7,6},{8,9},{10,11},{9,8... | collective-permute-start | bytes 811016 | tf_op jit(solution)/shard_map/ppermute | solution.py:465
  16.0 14.2 %collective-permute-start = (bf16[16,4096]{1,0:T(8,128)(2,1)S(1)}, bf16[16,4096]{1,0:T(8,128)(2,1)S(1)}, u32[]{:S(2)}, u32[]{:S(2)}) collective-permute-start(bf16[16,4096]{1,0:T(8,128)(2,1)S(1)} %get-tuple-element.25), channel_id=1, source_target_pairs={{0,1},{1,2},{2,3},{3,0},{4,5},{5,6},{6,7},{7,4},{8,9},{9,10},{10,1... | collective-permute-start | bytes 393224 | tf_op jit(solution)/shard_map/ppermute | solution.py:489
  16.0 14.5 %collective-permute-start.1 = (bf16[16,4096]{1,0:T(8,128)(2,1)S(1)}, bf16[16,4096]{1,0:T(8,128)(2,1)S(1)}, u32[]{:S(2)}, u32[]{:S(2)}) collective-permute-start(bf16[16,4096]{1,0:T(8,128)(2,1)S(1)} %get-tuple-element.26), channel_id=1, source_target_pairs={{0,2},{1,3},{2,0},{3,1},{4,6},{5,7},{6,4},{7,5},{8,10},{9,11},{10,... | collective-permute-start | bytes 393224 | tf_op jit(solution)/shard_map/ppermute | solution.py:489
  17.9 13.9 %collective-permute-start.2 = (bf16[16,4096]{1,0:T(8,128)(2,1)S(1)}, bf16[16,4096]{1,0:T(8,128)(2,1)S(1)}, u32[]{:S(2)}, u32[]{:S(2)}) collective-permute-start(bf16[16,4096]{1,0:T(8,128)(2,1)S(1)} %get-tuple-element.27), channel_id=1, source_target_pairs={{0,3},{1,0},{2,1},{3,2},{4,7},{5,4},{6,5},{7,6},{8,11},{9,8},{10,9... | collective-permute-start | bytes 393224 | tf_op jit(solution)/shard_map/ppermute | solution.py:489
  28.1 6.1 %collective-permute-start.5 = (bf16[16,4096]{1,0:T(8,128)(2,1)S(1)}, bf16[16,4096]{1,0:T(8,128)(2,1)S(1)}, u32[]{:S(2)}, u32[]{:S(2)}) collective-permute-start(bf16[16,4096]{1,0:T(8,128)(2,1)S(1)} %get-tuple-element.37), channel_id=1, source_target_pairs={{0,3},{1,0},{2,1},{3,2},{4,7},{5,4},{6,5},{7,6},{8,11},{9,8},{10,9... | collective-permute-start | bytes 393224 | tf_op jit(solution)/shard_map/ppermute | solution.py:489
  28.4 9.0 %collective-permute-start.6 = (bf16[16,4096]{1,0:T(8,128)(2,1)S(1)}, bf16[16,4096]{1,0:T(8,128)(2,1)S(1)}, u32[]{:S(2)}, u32[]{:S(2)}) collective-permute-start(bf16[16,4096]{1,0:T(8,128)(2,1)S(1)} %get-tuple-element.39), channel_id=1, source_target_pairs={{0,1},{1,2},{2,3},{3,0},{4,5},{5,6},{6,7},{7,4},{8,9},{9,10},{10,1... | collective-permute-start | bytes 393224 | tf_op jit(solution)/shard_map/ppermute | solution.py:489
  38.6 4.6 %collective-permute-start.9 = (f32[8,128]{1,0:T(8,128)S(1)}, f32[8,128]{1,0:T(8,128)S(1)}, u32[]{:S(2)}, u32[]{:S(2)}) collective-permute-start(f32[8,128]{1,0:T(8,128)S(1)} %shard_map.71), channel_id=1, source_target_pairs={{0,24},{4,28},{8,16},{12,20},{16,8},{20,12},{24,0},{28,4},{1,25},{... | collective-permute-start | bytes 12296 | tf_op jit(solution)/shard_map/ppermute | solution.py:526
  41.1 3.6 %collective-permute-start.8 = (f32[8,128]{1,0:T(8,128)S(1)}, f32[8,128]{1,0:T(8,128)S(1)}, u32[]{:S(2)}, u32[]{:S(2)}) collective-permute-start(f32[8,128]{1,0:T(8,128)S(1)} %shard_map.71), channel_id=1, source_target_pairs={{0,16},{4,20},{8,24},{12,28},{16,0},{20,4},{24,8},{28,12},{1,17},{... | collective-permute-start | bytes 12296 | tf_op jit(solution)/shard_map/ppermute | solution.py:526
  41.6 3.6 %collective-permute-start.7 = (f32[8,128]{1,0:T(8,128)S(1)}, f32[8,128]{1,0:T(8,128)S(1)}, u32[]{:S(2)}, u32[]{:S(2)}) collective-permute-start(f32[8,128]{1,0:T(8,128)S(1)} %shard_map.71), channel_id=1, source_target_pairs={{0,8},{4,12},{8,0},{12,4},{16,24},{20,28},{24,16},{28,20},{1,9},{5... | collective-permute-start | bytes 12296 | tf_op jit(solution)/shard_map/ppermute | solution.py:526
  45.3 1.2 %collective-permute-start.10 = (f32[8,128]{1,0:T(8,128)S(1)}, f32[8,128]{1,0:T(8,128)S(1)}, u32[]{:S(2)}, u32[]{:S(2)}) collective-permute-start(f32[8,128]{1,0:T(8,128)S(1)} %add_add_fusion.refs_0_), channel_id=1, source_target_pairs={{0,4},{4,0},{8,12},{12,8},{16,20},{20,16},{24,28},{28,24},{1,5},{5... | collective-permute-start | bytes 12296 | tf_op jit(solution)/shard_map/ppermute | solution.py:526
